TPU v7x, 32 devices: a whole 2x2x4 slice. The times are simulated.
32 devices in a mesh: seq: 16 (over z, y, core), head: 2 (over x).
Axes of the slice: x: 2, y: 2, z: 4, core: 2. Of those that a mesh axis runs over, the one named last changes fastest.
Arguments:
- queries: bfloat16 [4096, 4096], P('seq', 'head'), may hold values from -0.29882812 to 0.29882812
- keys: bfloat16 [4096, 4096], P('seq', 'head'), may hold values from -0.29882812 to 0.29882812
- values: bfloat16 [4096, 4096], P('seq', 'head'), may hold values from -0.59765625 to 0.59765625
- out_grad: bfloat16 [4096, 4096], P('seq', 'head'), may hold values from -6 to 6
- doc_lengths: int32 [8], replicated, may hold values from 1 to 1024, 4096 in all
Outputs:
- query_grad: bfloat16 [4096, 4096], P(('seq', 'head'))
- key_grad: bfloat16 [4096, 4096], P(('seq', 'head'))
- value_grad: bfloat16 [4096, 4096], P(('seq', 'head'))
Inputs may be any that keep to these rules, and one draw needn't show every extreme that they name: `doc_lengths`: the lengths sum to 4096 and the largest equals 1024.
All inputs are finite; a program needn't handle non-finite values.
Results may differ from a plain program's by a relative error of at most 0.0033.
Values may be sent and summed in bfloat16 or wider, within the bound.
No kernel may reach another device: no remote copies, remote signals or barrier semaphores. Data moves between devices by JAX's collectives and lax.ppermute only.
A program may use at most 128 MiB of HBM per device.

v0:
```python
import functools

import jax
import jax.numpy as jnp
from jax import lax
from jax.experimental import pallas as pl
from jax.experimental.pallas import tpu as pltpu
from jax.sharding import PartitionSpec as P

HEAD_DIM = 128
MOST = 1024
GROUP = 4
CHUNK = 4
PAD = 16
LINK = jnp.bfloat16
VMEM_LIMIT = 16 * 1024 * 1024
GRAD_LIMIT = 40 * 1024 * 1024
FIRST_LIMIT = 53 * 1024 * 1024
SECOND_LIMIT = 52 * 1024 * 1024
NT = (((1,), (1,)), ((), ()))
TN = (((0,), (0,)), ((), ()))
NN = (((1,), (0,)), ((), ()))


def dot(a, b, dims):
    return lax.dot_general(a, b, dims, preferred_element_type=jnp.float32)


def doc_at(meta, ndocs, position):
    start, begin, end = jnp.int32(0), jnp.int32(0), jnp.int32(0)
    for i in range(ndocs):
        stop = start + meta[i]
        begin = jnp.where(start <= position, start, begin)
        end = jnp.where(start <= position, stop, end)
        start = stop
    return begin, end


def block_range(meta, ndocs, base, rows):
    begin0, end0 = doc_at(meta, ndocs, base)
    begin1, end1 = doc_at(meta, ndocs, base + rows - 1)
    first = jnp.where(begin0 < base, end0, base) - base
    return begin0, end0, begin1, end1, first, begin1 - base


def state_kernel(lengths, q, k, v, g, *rest, ndocs, rows, offset, heads, group, kinds):
    outs, held, sems, known, got = rest[-4 - len(kinds):-4], rest[-4], rest[-3], rest[-2], rest[-1]
    gw = group * HEAD_DIM
    place = lax.axis_index("seq")
    first_core = lax.rem(place, 2) == 0

    def copy(n, c, i, ref):
        src = ref.at[:, pl.ds(offset + c * gw, gw)]
        return pltpu.make_async_copy(src, held.at[n, i, :, pl.ds(c * gw, gw)], sems.at[n, c, i])

    fetch = pltpu.make_async_copy(lengths, known, got)
    fetch.start()
    for n, kind in enumerate(kinds):
        tails = first_core if kind == "kept" else jnp.logical_not(first_core)
        for c in range(heads // group):

            @pl.when(tails)
            def _():
                copy(n, c, 0, k).start()
                copy(n, c, 1, v).start()

            @pl.when(jnp.logical_not(tails))
            def _():
                copy(n, c, 0, q).start()
                copy(n, c, 1, g).start()

    fetch.wait()
    _, _, _, _, first, last = block_range(known, ndocs, place * rows, rows)
    order = lax.broadcasted_iota(jnp.int32, (rows, HEAD_DIM), 0)
    zero = jnp.zeros((), held.dtype)
    for n, (kind, out) in enumerate(zip(kinds, outs)):
        tails = first_core if kind == "kept" else jnp.logical_not(first_core)
        low, high = jnp.where(tails, last, 0), jnp.where(tails, rows, first)
        here = (order >= low) & (order < high)
        for h in range(heads):
            if h % group == 0:
                copy(n, h // group, 0, k).wait()
                copy(n, h // group, 1, v).wait()
            cols = slice(h * HEAD_DIM, (h + 1) * HEAD_DIM)
            out[h] = dot(jnp.where(here, held[n, 0, :, cols], zero), held[n, 1, :, cols], TN)


def pair_kernel(lengths, kept, got, *rest, ndocs, rows, hops):
    sent = rest[-hops:]
    place = lax.axis_index("seq")
    first_core = lax.rem(place, 2) == 0
    even = (place - lax.rem(place, 2)) * rows
    odd = even + rows
    _, even_e0 = doc_at(lengths, ndocs, even)
    odd_b1, _ = doc_at(lengths, ndocs, odd + rows - 1)
    joins = jnp.where(jnp.where(first_core, odd_b1 < odd, even_e0 > odd), 1.0, 0.0)
    size = kept.shape[0] * HEAD_DIM
    total = (got[...] + joins * kept[...]).astype(LINK).reshape(size, HEAD_DIM)
    for out in sent:
        out[:size] = total
        if out.shape[0] > size:
            out[size:] = jnp.zeros((out.shape[0] - size, HEAD_DIM), LINK)


def join_kernel(lengths, other, *rest, ndocs, rows, counts, hops):
    came, mine, theirs = rest[:hops], rest[-2 * len(counts):-len(counts)], rest[-len(counts):]
    place = lax.axis_index("seq")
    first_core = lax.rem(place, 2) == 0
    even = (place - lax.rem(place, 2)) * rows
    odd = even + rows
    even_b0, _ = doc_at(lengths, ndocs, even)
    _, even_e1 = doc_at(lengths, ndocs, odd - 1)
    odd_b0, _ = doc_at(lengths, ndocs, odd)
    _, odd_e1 = doc_at(lengths, ndocs, odd + rows - 1)

    def one(if_first, if_second):
        return jnp.where(jnp.where(first_core, if_first, if_second), 1.0, 0.0)

    weights = [
        one(odd + rows + hop * 2 * rows < odd_e1, even - hop * 2 * rows > even_b0) for hop in range(hops)
    ]
    from_other, from_pair = one(odd < even_e1, odd > odd_b0), one(odd + rows < even_e1, even > odd_b0)
    for c, count in enumerate(counts):
        at = slice(sum(counts[:c]), sum(counts[:c + 1]))
        lines = slice(at.start * HEAD_DIM, at.stop * HEAD_DIM)
        total = weights[0] * came[0][lines].astype(jnp.float32)
        for hop in range(1, hops):
            total = total + weights[hop] * came[hop][lines].astype(jnp.float32)
        total = total.reshape(count, HEAD_DIM, HEAD_DIM)
        theirs[c][...] = total
        mine[c][...] = from_other * other[at] + from_pair * total


def split(a, axis):
    high = a.astype(jnp.bfloat16)
    return jnp.concatenate([high, (a - high.astype(jnp.float32)).astype(jnp.bfloat16)], axis=axis)


def mask_kernel(lengths, *rest, ndocs, rows):
    lower, upper = rest[-2:]
    line = lax.broadcasted_iota(jnp.int32, (rows, rows), 0)
    across = lax.broadcasted_iota(jnp.int32, (rows, rows), 1)
    begin_line = jnp.zeros((rows, rows), jnp.int32)
    begin_across = jnp.zeros((rows, rows), jnp.int32)
    start = jnp.int32(0) - lax.axis_index("seq") * rows
    for i in range(ndocs):
        begin_line = jnp.where(line >= start, start, begin_line)
        begin_across = jnp.where(across >= start, start, begin_across)
        start = start + lengths[i]
    lower[...] = jnp.where((across <= line) & (across >= begin_line), 1.0, 0.0)
    upper[...] = jnp.where((line <= across) & (line >= begin_across), 1.0, 0.0)


def own_range(lengths, ndocs, rows):
    place = lax.axis_index("seq")
    _, _, _, _, first, last = block_range(lengths, ndocs, place * rows, rows)
    order = lax.broadcasted_iota(jnp.int32, (rows, HEAD_DIM), 0)
    return lax.rem(place, 2) == 0, order < first, order >= last


def local_part(q, k, v, g, lower, upper, at):
    qh, kh, vh, gh = (ref[:, at] for ref in (q, k, v, g))
    weight_gv = (dot(gh, vh, NT) * lower[...]).astype(jnp.bfloat16)
    weight_vg = (dot(vh, gh, NT) * upper[...]).astype(jnp.bfloat16)
    weight_kq = (dot(kh, qh, NT) * upper[...]).astype(jnp.bfloat16)
    return dot(weight_gv, kh, NN), dot(weight_vg, qh, NN), dot(weight_kq, gh, NN)


def twice(ref, at):
    return jnp.concatenate([ref[:, at]] * 2, axis=1)


def carry_of_state(g, state, first_rows, at):
    return jnp.where(first_rows, dot(twice(g, at), split(state, 1), NT), 0.0)


def carries_of_grad(k, v, grad, last_rows, at):
    carry_k = jnp.where(last_rows, dot(twice(v, at), split(grad, 1), NT), 0.0)
    return carry_k, jnp.where(last_rows, dot(twice(k, at), split(grad, 0), NN), 0.0)


def deal(done, outs, rows, groups):
    part, column = rows // groups, lax.axis_index("head")
    for j in range(groups):
        at = pl.ds(pl.multiple_of(lax.rem(column + j, groups) * part, part), part)
        for i in range(3):
            outs[j][i] = done[i, at, :]


def grad_kernel(lengths, q, k, v, g, lower, upper, mine, got, *rest, ndocs, rows, offset, heads, groups):
    outs, done = rest[-1 - groups:-1], rest[-1]
    first_core, first_rows, last_rows = own_range(lengths, ndocs, rows)
    for h in range(heads):
        cols = slice(h * HEAD_DIM, (h + 1) * HEAD_DIM)
        at = slice(offset + h * HEAD_DIM, offset + (h + 1) * HEAD_DIM)
        state = jnp.where(first_core, got[h], mine[h])
        grad = jnp.where(first_core, mine[h], got[h])
        near = local_part(q, k, v, g, lower, upper, at)
        carries = (carry_of_state(g, state, first_rows, at), *carries_of_grad(k, v, grad, last_rows, at))
        for i in range(3):
            done[i, :, cols] = (near[i] + carries[i]).astype(jnp.bfloat16)
    deal(done, outs, rows, groups)


def begin_kernel(lengths, q, k, v, g, lower, upper, mine, *rest, ndocs, rows, offset, heads):
    near = rest[-1]
    first_core, first_rows, last_rows = own_range(lengths, ndocs, rows)
    for h in range(heads):
        cols = slice(h * HEAD_DIM, (h + 1) * HEAD_DIM)
        at = slice(offset + h * HEAD_DIM, offset + (h + 1) * HEAD_DIM)
        for i, value in enumerate(local_part(q, k, v, g, lower, upper, at)):
            near[i, :, cols] = value

    @pl.when(first_core)
    def _():
        for h in range(heads):
            cols = slice(h * HEAD_DIM, (h + 1) * HEAD_DIM)
            at = slice(offset + h * HEAD_DIM, offset + (h + 1) * HEAD_DIM)
            carry_k, carry_v = carries_of_grad(k, v, mine[h], last_rows, at)
            near[1, :, cols] += carry_k
            near[2, :, cols] += carry_v

    @pl.when(jnp.logical_not(first_core))
    def _():
        for h in range(heads):
            cols = slice(h * HEAD_DIM, (h + 1) * HEAD_DIM)
            at = slice(offset + h * HEAD_DIM, offset + (h + 1) * HEAD_DIM)
            near[0, :, cols] += carry_of_state(g, mine[h], first_rows, at)


def end_kernel(lengths, k, v, g, near, got, *rest, ndocs, rows, offset, heads, groups):
    outs, done = rest[-1 - groups:-1], rest[-1]
    first_core, first_rows, last_rows = own_range(lengths, ndocs, rows)

    @pl.when(first_core)
    def _():
        for h in range(heads):
            cols = slice(h * HEAD_DIM, (h + 1) * HEAD_DIM)
            at = slice(offset + h * HEAD_DIM, offset + (h + 1) * HEAD_DIM)
            done[0, :, cols] = (near[0, :, cols] + carry_of_state(g, got[h], first_rows, at)).astype(jnp.bfloat16)
            done[1, :, cols] = near[1, :, cols].astype(jnp.bfloat16)
            done[2, :, cols] = near[2, :, cols].astype(jnp.bfloat16)

    @pl.when(jnp.logical_not(first_core))
    def _():
        for h in range(heads):
            cols = slice(h * HEAD_DIM, (h + 1) * HEAD_DIM)
            at = slice(offset + h * HEAD_DIM, offset + (h + 1) * HEAD_DIM)
            carry_k, carry_v = carries_of_grad(k, v, got[h], last_rows, at)
            done[0, :, cols] = near[0, :, cols].astype(jnp.bfloat16)
            done[1, :, cols] = (near[1, :, cols] + carry_k).astype(jnp.bfloat16)
            done[2, :, cols] = (near[2, :, cols] + carry_v).astype(jnp.bfloat16)

    deal(done, outs, rows, groups)


def place_kernel(*refs, groups, offset, cw, width):
    parts, outs, sems = refs[:groups], refs[-4:-1], refs[-1]
    column = lax.axis_index("head")
    copies = []
    for j in range(groups):
        start = pl.multiple_of(lax.rem(column + groups - j, groups) * width + offset, 128)
        for i in range(3):
            copies.append(pltpu.make_async_copy(parts[j].at[i], outs[i].at[:, pl.ds(start, cw)], sems.at[len(copies)]))
            copies[-1].start()
    for copy in copies:
        copy.wait()


def cuts_of(width):
    heads = width // HEAD_DIM
    size = CHUNK if heads % (2 * CHUNK) == 0 else 2
    cw, half = size * HEAD_DIM, max(heads // 2, size) * HEAD_DIM
    return [(at, half, [(o, cw) for o in range(at, at + half, cw)]) for at in range(0, width, half)]


def shards(queries, keys, values, out_grad, doc_lengths):
    rows, width = queries.shape
    ndocs = doc_lengths.shape[0]
    seq, groups = lax.axis_size("seq"), lax.axis_size("head")
    pairs = seq // 2
    hops = -(-MOST // (2 * rows))
    halves = cuts_of(width)
    part = rows // groups
    anywhere = pl.BlockSpec(memory_space=pl.ANY)
    in_vmem = pl.BlockSpec(memory_space=pltpu.VMEM)
    in_smem = pl.BlockSpec(memory_space=pltpu.SMEM)
    f32, bf16 = jnp.float32, jnp.bfloat16
    inputs = (queries, keys, values, out_grad)
    sizes = dict(ndocs=ndocs, rows=rows)
    cheap = pl.CostEstimate(flops=0, bytes_accessed=1024, transcendentals=0)

    def shape_of(*dims, dtype=f32):
        return jax.ShapeDtypeStruct(dims, dtype)

    def call(name, kernel, args, outs, scratch=(), after=(), limit=VMEM_LIMIT):
        return pl.pallas_call(
            kernel, in_specs=[in_smem] + [in_vmem] * len(args) + [anywhere] * len(after), out_specs=[in_vmem] * len(outs), out_shape=outs,
            scratch_shapes=list(scratch), cost_estimate=cheap,
            compiler_params=pltpu.CompilerParams(vmem_limit_bytes=limit), name=name,
        )(doc_lengths, *args, *after)

    def swap_cores(a):
        return lax.ppermute(a, "seq", [(b, b ^ 1) for b in range(seq)])

    def swap_pairs(sent):
        came = []
        for hop in range(1, hops + 1):
            perm = [(2 * m, 2 * (m + hop) + 1) for m in range(pairs - hop)]
            came.append(lax.ppermute(sent[hop - 1], "seq", perm + [(b, a) for a, b in perm]))
        return came

    def send_rows(outs):
        arrived = list(outs[:1])
        for j in range(1, groups):
            arrived.append(lax.ppermute(outs[j], "head", [(x, (x + j) % groups) for x in range(groups)]))
        return arrived

    square = (HEAD_DIM, HEAD_DIM)

    def states(kinds, offset, half, after):
        heads = half // HEAD_DIM
        group = GROUP if heads % GROUP == 0 else 2
        return pl.pallas_call(
            functools.partial(state_kernel, offset=offset, heads=heads, group=group, kinds=kinds, **sizes),
            in_specs=[anywhere] * (5 + len(after)), out_specs=[in_vmem] * len(kinds),
            out_shape=[shape_of(heads, *square)] * len(kinds),
            scratch_shapes=[
                pltpu.VMEM((len(kinds), 2, rows, half), bf16), pltpu.SemaphoreType.DMA((len(kinds), heads // group, 2)),
                pltpu.SMEM((ndocs,), jnp.int32), pltpu.SemaphoreType.DMA,
            ],
            cost_estimate=cheap, compiler_params=pltpu.CompilerParams(vmem_limit_bytes=SECOND_LIMIT if after else FIRST_LIMIT), name="states",
        )(doc_lengths, *inputs, *after)

    def pair_up(kept, got, after):
        lines = kept.shape[0] * HEAD_DIM
        outs = [shape_of(lines + PAD * (hops - hop), HEAD_DIM, dtype=LINK) for hop in range(1, hops + 1)]
        totals = call("pair", functools.partial(pair_kernel, hops=hops, **sizes), (kept, got), outs, after=after)
        return totals[-1], swap_pairs(totals)

    def join(kept, came, chunks, after):
        counts = [cw // HEAD_DIM for _, cw in chunks]
        joined = call(
            "join", functools.partial(join_kernel, counts=counts, hops=hops, **sizes), (swap_cores(kept), *came),
            [shape_of(n, *square) for n in counts] * 2, after=after,
        )
        return [(mine, swap_cores(theirs)) for mine, theirs in zip(joined[:len(chunks)], joined[len(chunks):])]

    def grads(masks, offset, cw, mine, theirs, after):
        return call(
            "grads", functools.partial(grad_kernel, offset=offset, heads=cw // HEAD_DIM, groups=groups, **sizes),
            (*inputs, *masks, mine, theirs), [shape_of(3, part, cw, dtype=bf16)] * groups,
            [pltpu.VMEM((3, rows, cw), bf16)], after, GRAD_LIMIT,
        )

    def grads_early(masks, offset, cw, mine, theirs):
        more = dict(offset=offset, heads=cw // HEAD_DIM, **sizes)
        near = call(
            "begin", functools.partial(begin_kernel, **more), (*inputs, *masks, mine), [shape_of(3, rows, cw)],
            limit=GRAD_LIMIT,
        )[0]
        return call(
            "end", functools.partial(end_kernel, groups=groups, **more), (*inputs[1:], near, theirs),
            [shape_of(3, part, cw, dtype=bf16)] * groups, [pltpu.VMEM((3, rows, cw), bf16)], limit=GRAD_LIMIT,
        )

    cuts, outs, arrived, totals, masks = [], [], [], [], None
    for start, half, chunks in halves:
        if not totals:
            (sent,) = states(("sent",), start, half, [])
            (kept,) = states(("kept",), start, half, [])
        else:
            kept, sent = states(("kept", "sent"), start, half, totals)
        total, came = pair_up(kept, swap_cores(sent), [made[0] for made in outs[:1]])
        totals = [total]
        masks = masks or call("masks", functools.partial(mask_kernel, **sizes), (), [shape_of(rows, rows)] * 2, after=totals)
        joined = join(kept, came, chunks, [parts[1] for parts in arrived[:1]] or masks[:1])
        for (offset, cw), (mine, theirs) in zip(chunks, joined):
            after = [made[0] for made in outs[-1:]] + [parts[1] for parts in arrived[1:-1]][-1:]
            if outs:
                outs.append(grads(masks, offset, cw, mine, theirs, after))
            else:
                outs.append(grads_early(masks, offset, cw, mine, theirs))
            arrived.append(send_rows(outs[-1]))
        cuts += chunks

    placed = []
    for c, (offset, cw) in enumerate(cuts):
        placed = pl.pallas_call(
            functools.partial(place_kernel, groups=groups, offset=offset, cw=cw, width=width),
            grid_spec=pl.GridSpec(
                grid=(1,), in_specs=[anywhere] * (groups + len(placed)), out_specs=[anywhere] * 3,
                scratch_shapes=[pltpu.SemaphoreType.DMA((3 * groups,))],
            ),
            out_shape=[shape_of(part, width * groups, dtype=bf16)] * 3,
            input_output_aliases={groups + i: i for i in range(len(placed))},
            cost_estimate=cheap,
            compiler_params=pltpu.CompilerParams(vmem_limit_bytes=VMEM_LIMIT), name="place",
        )(*arrived[c], *placed)
    return tuple(placed)


def solution(mesh):
    return jax.shard_map(
        shards,
        mesh=mesh,
        in_specs=(P("seq", "head"), P("seq", "head"), P("seq", "head"), P("seq", "head"), P()),
        out_specs=(P(("seq", "head"), None), P(("seq", "head"), None), P(("seq", "head"), None)),
        check_vma=False,
    )
```

profile of v0, /device:TPU:0, one launch (start us, length us, event | category | flops | bytes accessed | tf_op | source)
XLA Modules:
  0.0 61.3 jit_solution(926370518072588869)
XLA Ops:
  0.6 0.0 copy-start.4
  0.6 0.6 %copy-done.4 = s32[8]{0:T(128)S(1)} copy-done((s32[8]{0:T(128)S(1)}, s32[8]{0:T(128)}, u32[]{:S(2)}) %copy-start.4) | copy-done | bytes 56
  1.3 1.6 %states.4 = f32[8,128,128]{2,1,0:T(8,128)S(1)} custom-call(s32[8]{0:T(128)S(1)} %copy-done.4, bf16[256,2048]{1,0:T(8,128)(2,1)} %q.13, bf16[256,2048]{1,0:T(8,128)(2,1)} %k.15, bf16[256,2048]{1,0:T(8,128)(2,1)} %v.15, bf16[256,2048]{1,0:T(8,128)(2,1)} %g.15), custom_call_target="tpu_custom_call" | custom-call | bytes 1024 | tf_op jit(solution)/shard_map/states/pallas_call | solution.py:324
  2.9 0.0 copy-start.5
  2.9 0.5 collective-permute-start
  3.5 1.6 %states.3.kept = f32[8,128,128]{2,1,0:T(8,128)S(1)} custom-call(s32[8]{0:T(128)S(1)} %copy-done.4, bf16[256,2048]{1,0:T(8,128)(2,1)} %q.13, bf16[256,2048]{1,0:T(8,128)(2,1)} %k.15, bf16[256,2048]{1,0:T(8,128)(2,1)} %v.15, bf16[256,2048]{1,0:T(8,128)(2,1)} %g.15), custom_call_target="tpu_custom_call" | custom-call | bytes 1024 | tf_op jit(solution)/shard_map/states/pallas_call | solution.py:324
  5.1 0.1 collective-permute-start.3
  5.2 0.0 collective-permute-done.got
  5.2 0.6 %pair.2 = (bf16[1040,128]{1,0:T(8,128)(2,1)S(1)}, bf16[1024,128]{1,0:T(8,128)(2,1)S(1)}) custom-call(s32[8]{0:T(128)S(1)} %copy-done.4, f32[8,128,128]{2,1,0:T(8,128)S(1)} %states.3.kept, f32[8,128,128]{2,1,0:T(8,128)S(1)} %collective-permute-done.got), custom_call_target="tpu_custom_call" | custom-call | bytes 1024 | tf_op jit(solution)/shard_map/pair/pallas_call | solution.py:297
  5.9 4.5 %collective-permute-start.4 = (bf16[1040,128]{1,0:T(8,128)(2,1)S(1)}, bf16[1040,128]{1,0:T(8,128)(2,1)S(1)}, u32[]{:S(2)}, u32[]{:S(2)}) collective-permute-start(bf16[1040,128]{1,0:T(8,128)(2,1)S(1)} %get-tuple-element.41), channel_id=1, source_target_pairs={{0,6},{4,10},{8,14},{12,18},{16,22},{20,26},{24,30},{6,0},{10,4},{... | collective-permute-start | bytes 798728 | tf_op jit(solution)/shard_map/ppermute | solution.py:310
  10.4 3.5 %collective-permute-start.5 = (bf16[1024,128]{1,0:T(8,128)(2,1)S(1)}, bf16[1024,128]{1,0:T(8,128)(2,1)S(1)}, u32[]{:S(2)}, u32[]{:S(2)}) collective-permute-start(bf16[1024,128]{1,0:T(8,128)(2,1)S(1)} %get-tuple-element.36.rest_0_), channel_id=1, source_target_pairs={{0,10},{4,14},{8,18},{12,22},{16,26},{20,30},{10,0},{14,4},{18,8},... | collective-permute-start | bytes 786440 | tf_op jit(solution)/shard_map/ppermute | solution.py:310
  13.9 0.0 copy-done.5
  13.9 0.0 copy-start.1
  13.9 0.0 copy-start.2
  13.9 0.0 copy-start.3
  13.9 2.4 %states.5 = (f32[8,128,128]{2,1,0:T(8,128)S(1)}, f32[8,128,128]{2,1,0:T(8,128)S(1)}) custom-call(s32[8]{0:T(128)S(1)} %copy-done.5, bf16[256,2048]{1,0:T(8,128)(2,1)} %q.13, bf16[256,2048]{1,0:T(8,128)(2,1)} %k.15, bf16[256,2048]{1,0:T(8,128)(2,1)} %v.15, bf16[256,2048]{1,0:T(8,128)(2,1)} %g.15, bf16[1024,128]{1,0:T(8,128)(2,1)S(1)} %get-tuple-element.36.rest_0_), custom_call_target="tpu_custom_call" | custom-call | bytes 1024 | tf_op jit(solution)/shard_map/states/pallas_call | solution.py:324
  16.3 0.0 copy-start
  16.3 0.1 collective-permute-start.2
  16.4 0.7 %masks.1 = (f32[256,256]{1,0:T(8,128)S(1)}, f32[256,256]{1,0:T(8,128)S(1)}) custom-call(s32[8]{0:T(128)S(1)} %copy-done.5, bf16[1024,128]{1,0:T(8,128)(2,1)S(1)} %get-tuple-element.36.rest_0_), custom_call_target="tpu_custom_call" | custom-call | bytes 1024 | tf_op jit(solution)/shard_map/masks/pallas_call | solution.py:297
  17.1 0.0 collective-permute-done.3.other
  17.1 1.8 %collective-permute-done.5.rest_1_ = bf16[1024,128]{1,0:T(8,128)(2,1)S(1)} collective-permute-done((bf16[1024,128]{1,0:T(8,128)(2,1)S(1)}, bf16[1024,128]{1,0:T(8,128)(2,1)S(1)}, u32[]{:S(2)}, u32[]{:S(2)}) %collective-permute-start.5) | collective-permute-done | bytes 262176 | tf_op jit(solution)/shard_map/ppermute | solution.py:310
  18.9 0.0 collective-permute-done.4.rest_0_
  18.9 0.7 %join.2 = (f32[4,128,128]{2,1,0:T(8,128)S(1)}, f32[4,128,128]{2,1,0:T(8,128)S(1)}, f32[4,128,128]{2,1,0:T(8,128)S(1)}, f32[4,128,128]{2,1,0:T(8,128)S(1)}) custom-call(s32[8]{0:T(128)S(1)} %copy-done.5, f32[8,128,128]{2,1,0:T(8,128)S(1)} %collective-permute-done.3.other, bf16[1040,128]{1,0:T(8,128)(2,1)S(1)} %collective-permute-done.4.rest_0_, ...), custom_call_target="tpu_custom_call" | custom-call | bytes 1024 | tf_op jit(solution)/shard_map/join/pallas_call | solution.py:297
  19.6 0.1 collective-permute-start.6
  19.7 0.5 collective-permute-start.1
  20.2 0.0 copy-done.1
  20.2 0.0 copy-done.2
  20.2 0.0 copy-done.3
  20.2 0.0 copy-done
  20.2 2.1 %begin.1.near = f32[3,256,512]{2,1,0:T(8,128)S(1)} custom-call(s32[8]{0:T(128)S(1)} %copy-done.5, bf16[256,2048]{1,0:T(8,128)(2,1)S(1)} %copy-done.3, bf16[256,2048]{1,0:T(8,128)(2,1)S(1)} %copy-done, bf16[256,2048]{1,0:T(8,128)(2,1)S(1)} %copy-done.1, bf16[256,2048]{1,0:T(8,128)(2,1)S(1)} %copy-done.2, f32[256,256]{1,0:T(8,128)S(1)} %get-tuple-element.37.rest_2_.lower, ...), custom_call_target="tpu_custom_call" | custom-call | bytes 1024 | tf_op jit(solution)/shard_map/begin/pallas_call | solution.py:297
  22.3 0.0 collective-permute-done.6.got
  22.3 1.0 %end.1 = (bf16[3,128,512]{2,1,0:T(8,128)(2,1)S(1)}, bf16[3,128,512]{2,1,0:T(8,128)(2,1)S(1)}) custom-call(s32[8]{0:T(128)S(1)} %copy-done.5, bf16[256,2048]{1,0:T(8,128)(2,1)S(1)} %copy-done, bf16[256,2048]{1,0:T(8,128)(2,1)S(1)} %copy-done.1, bf16[256,2048]{1,0:T(8,128)(2,1)S(1)} %copy-done.2, f32[3,256,512]{2,1,0:T(8,128)S(1)} %begin.1.near, ...), custom_call_target="tpu_custom_call" | custom-call | bytes 1024 | tf_op jit(solution)/shard_map/end/pallas_call | solution.py:297
  23.3 1.6 %collective-permute-start.9 = (bf16[3,128,512]{2,1,0:T(8,128)(2,1)S(1)}, bf16[3,128,512]{2,1,0:T(8,128)(2,1)S(1)}, u32[]{:S(2)}, u32[]{:S(2)}) collective-permute-start(bf16[3,128,512]{2,1,0:T(8,128)(2,1)S(1)} %get-tuple-element.47), channel_id=1, source_target_pairs={{0,1},{1,0},{2,3},{3,2},{4,5},{5,4},{6,7},{7,6},{8,9},{9,8},{10,11... | collective-permute-start | bytes 1179656 | tf_op jit(solution)/shard_map/ppermute | solution.py:316
  24.8 0.0 collective-permute-start.12
  24.8 0.0 collective-permute-done.2.got
  24.8 0.6 %pair.3 = (bf16[1040,128]{1,0:T(8,128)(2,1)S(1)}, bf16[1024,128]{1,0:T(8,128)(2,1)S(1)}) custom-call(s32[8]{0:T(128)S(1)} %copy-done.5, f32[8,128,128]{2,1,0:T(8,128)S(1)} %get-tuple-element.39.kept, f32[8,128,128]{2,1,0:T(8,128)S(1)} %collective-permute-done.2.got, bf16[3,128,512]{2,1,0:T(8,128)(2,1)S(1)} %get-tuple-element.44.rest_0_.refs_0_), custom_call_target="tpu_custom_call" | custom-call | bytes 1024 | tf_op jit(solution)/shard_map/pair/pallas_call | solution.py:297
  25.5 2.8 %collective-permute-start.7 = (bf16[1040,128]{1,0:T(8,128)(2,1)S(1)}, bf16[1040,128]{1,0:T(8,128)(2,1)S(1)}, u32[]{:S(2)}, u32[]{:S(2)}) collective-permute-start(bf16[1040,128]{1,0:T(8,128)(2,1)S(1)} %get-tuple-element.45), channel_id=1, source_target_pairs={{0,6},{4,10},{8,14},{12,18},{16,22},{20,26},{24,30},{6,0},{10,4},{... | collective-permute-start | bytes 798728 | tf_op jit(solution)/shard_map/ppermute | solution.py:310
  28.2 3.0 %collective-permute-start.8 = (bf16[1024,128]{1,0:T(8,128)(2,1)S(1)}, bf16[1024,128]{1,0:T(8,128)(2,1)S(1)}, u32[]{:S(2)}, u32[]{:S(2)}) collective-permute-start(bf16[1024,128]{1,0:T(8,128)(2,1)S(1)} %get-tuple-element.46), channel_id=1, source_target_pairs={{0,10},{4,14},{8,18},{12,22},{16,26},{20,30},{10,0},{14,4},{18,8},... | collective-permute-start | bytes 786440 | tf_op jit(solution)/shard_map/ppermute | solution.py:310
  31.2 0.0 collective-permute-done.12.got
  31.2 2.2 %grads.3 = (bf16[3,128,512]{2,1,0:T(8,128)(2,1)S(1)}, bf16[3,128,512]{2,1,0:T(8,128)(2,1)S(1)}) custom-call(s32[8]{0:T(128)S(1)} %copy-done.5, bf16[256,2048]{1,0:T(8,128)(2,1)S(1)} %copy-done.3, bf16[256,2048]{1,0:T(8,128)(2,1)S(1)} %copy-done, bf16[256,2048]{1,0:T(8,128)(2,1)S(1)} %copy-done.1, bf16[256,2048]{1,0:T(8,128)(2,1)S(1)} %copy-done.2, ...), custom_call_target="tpu_custom_call" | custom-call | bytes 1024 | tf_op jit(solution)/shard_map/grads/pallas_call | solution.py:297
  33.4 0.6 %collective-permute-start.13 = (bf16[3,128,512]{2,1,0:T(8,128)(2,1)S(1)}, bf16[3,128,512]{2,1,0:T(8,128)(2,1)S(1)}, u32[]{:S(2)}, u32[]{:S(2)}) collective-permute-start(bf16[3,128,512]{2,1,0:T(8,128)(2,1)S(1)} %get-tuple-element.56), channel_id=1, source_target_pairs={{0,1},{1,0},{2,3},{3,2},{4,5},{5,4},{6,7},{7,6},{8,9},{9,8},{10,11... | collective-permute-start | bytes 1179656 | tf_op jit(solution)/shard_map/ppermute | solution.py:316
  34.0 0.0 collective-permute-done.1.other
  34.0 2.2 %collective-permute-done.8.rest_1_ = bf16[1024,128]{1,0:T(8,128)(2,1)S(1)} collective-permute-done((bf16[1024,128]{1,0:T(8,128)(2,1)S(1)}, bf16[1024,128]{1,0:T(8,128)(2,1)S(1)}, u32[]{:S(2)}, u32[]{:S(2)}) %collective-permute-start.8) | collective-permute-done | bytes 262176 | tf_op jit(solution)/shard_map/ppermute | solution.py:310
  36.2 0.0 collective-permute-done.7.rest_0_
  36.2 0.0 collective-permute-done.9.rest_2_.refs_1_
  36.2 0.7 %join.3 = (f32[4,128,128]{2,1,0:T(8,128)S(1)}, f32[4,128,128]{2,1,0:T(8,128)S(1)}, f32[4,128,128]{2,1,0:T(8,128)S(1)}, f32[4,128,128]{2,1,0:T(8,128)S(1)}) custom-call(s32[8]{0:T(128)S(1)} %copy-done.5, f32[8,128,128]{2,1,0:T(8,128)S(1)} %collective-permute-done.1.other, bf16[1040,128]{1,0:T(8,128)(2,1)S(1)} %collective-permute-done.7.rest_0_, ...), custom_call_target="tpu_custom_call" | custom-call | bytes 1024 | tf_op jit(solution)/shard_map/join/pallas_call | solution.py:297
  36.9 0.1 collective-permute-start.11
  37.0 0.5 collective-permute-start.10
  37.5 1.0 %collective-permute-done.11.got = f32[4,128,128]{2,1,0:T(8,128)S(1)} collective-permute-done((f32[4,128,128]{2,1,0:T(8,128)S(1)}, f32[4,128,128]{2,1,0:T(8,128)S(1)}, u32[]{:S(2)}, u32[]{:S(2)}) %collective-permute-start.11) | collective-permute-done | bytes 262176 | tf_op jit(solution)/shard_map/ppermute | solution.py:304
  38.5 2.2 %grads.4 = (bf16[3,128,512]{2,1,0:T(8,128)(2,1)S(1)}, bf16[3,128,512]{2,1,0:T(8,128)(2,1)S(1)}) custom-call(s32[8]{0:T(128)S(1)} %copy-done.5, bf16[256,2048]{1,0:T(8,128)(2,1)S(1)} %copy-done.3, bf16[256,2048]{1,0:T(8,128)(2,1)S(1)} %copy-done, bf16[256,2048]{1,0:T(8,128)(2,1)S(1)} %copy-done.1, bf16[256,2048]{1,0:T(8,128)(2,1)S(1)} %copy-done.2, ...), custom_call_target="tpu_custom_call" | custom-call | bytes 1024 | tf_op jit(solution)/shard_map/grads/pallas_call | solution.py:297
  40.7 0.6 %collective-permute-start.15 = (bf16[3,128,512]{2,1,0:T(8,128)(2,1)S(1)}, bf16[3,128,512]{2,1,0:T(8,128)(2,1)S(1)}, u32[]{:S(2)}, u32[]{:S(2)}) collective-permute-start(bf16[3,128,512]{2,1,0:T(8,128)(2,1)S(1)} %get-tuple-element.59), channel_id=1, source_target_pairs={{0,1},{1,0},{2,3},{3,2},{4,5},{5,4},{6,7},{7,6},{8,9},{9,8},{10,11... | collective-permute-start | bytes 1179656 | tf_op jit(solution)/shard_map/ppermute | solution.py:316
  41.3 1.5 %collective-permute-done.13.rest_1_.refs_1_ = bf16[3,128,512]{2,1,0:T(8,128)(2,1)S(1)} collective-permute-done((bf16[3,128,512]{2,1,0:T(8,128)(2,1)S(1)}, bf16[3,128,512]{2,1,0:T(8,128)(2,1)S(1)}, u32[]{:S(2)}, u32[]{:S(2)}) %collective-permute-start.13) | collective-permute-done | bytes 393248 | tf_op jit(solution)/shard_map/ppermute | solution.py:316
  42.8 0.0 collective-permute-done.10.got
  42.8 2.2 %grads.5 = (bf16[3,128,512]{2,1,0:T(8,128)(2,1)S(1)}, bf16[3,128,512]{2,1,0:T(8,128)(2,1)S(1)}) custom-call(s32[8]{0:T(128)S(1)} %copy-done.5, bf16[256,2048]{1,0:T(8,128)(2,1)S(1)} %copy-done.3, bf16[256,2048]{1,0:T(8,128)(2,1)S(1)} %copy-done, bf16[256,2048]{1,0:T(8,128)(2,1)S(1)} %copy-done.1, bf16[256,2048]{1,0:T(8,128)(2,1)S(1)} %copy-done.2, ...), custom_call_target="tpu_custom_call" | custom-call | bytes 1024 | tf_op jit(solution)/shard_map/grads/pallas_call | solution.py:297
  45.0 1.7 %collective-permute-start.14 = (bf16[3,128,512]{2,1,0:T(8,128)(2,1)S(1)}, bf16[3,128,512]{2,1,0:T(8,128)(2,1)S(1)}, u32[]{:S(2)}, u32[]{:S(2)}) collective-permute-start(bf16[3,128,512]{2,1,0:T(8,128)(2,1)S(1)} %get-tuple-element.58), channel_id=1, source_target_pairs={{0,1},{1,0},{2,3},{3,2},{4,5},{5,4},{6,7},{7,6},{8,9},{9,8},{10,11... | collective-permute-start | bytes 1179656 | tf_op jit(solution)/shard_map/ppermute | solution.py:316
  46.7 0.9 %place.4 = (bf16[128,4096]{1,0:T(8,128)(2,1)}, bf16[128,4096]{1,0:T(8,128)(2,1)}, bf16[128,4096]{1,0:T(8,128)(2,1)}) custom-call(bf16[3,128,512]{2,1,0:T(8,128)(2,1)S(1)} %get-tuple-element.44.rest_0_.refs_0_, bf16[3,128,512]{2,1,0:T(8,128)(2,1)S(1)} %collective-permute-done.9.rest_2_.refs_1_), custom_call_target="tpu_custom_call" | custom-call | bytes 1024 | tf_op jit(solution)/shard_map/place/pallas_call | solution.py:389
  47.6 0.9 %place.5 = (bf16[128,4096]{1,0:T(8,128)(2,1)}, bf16[128,4096]{1,0:T(8,128)(2,1)}, bf16[128,4096]{1,0:T(8,128)(2,1)}) custom-call(bf16[3,128,512]{2,1,0:T(8,128)(2,1)S(1)} %get-tuple-element.54.rest_0_.refs_0_, bf16[3,128,512]{2,1,0:T(8,128)(2,1)S(1)} %collective-permute-done.13.rest_1_.refs_1_, ...), custom_call_target="tpu_custom_call", output_to_operand_aliasing={{0}: (2, {}), {1}: (3, {}), {2}: (4, {})} | custom-call | bytes 1024 | tf_op jit(solution)/shard_map/place/pallas_call | solution.py:389
  48.6 4.2 %collective-permute-done.15.refs_1_ = bf16[3,128,512]{2,1,0:T(8,128)(2,1)S(1)} collective-permute-done((bf16[3,128,512]{2,1,0:T(8,128)(2,1)S(1)}, bf16[3,128,512]{2,1,0:T(8,128)(2,1)S(1)}, u32[]{:S(2)}, u32[]{:S(2)}) %collective-permute-start.15) | collective-permute-done | bytes 393248 | tf_op jit(solution)/shard_map/ppermute | solution.py:316
  52.7 0.9 %place.6 = (bf16[128,4096]{1,0:T(8,128)(2,1)}, bf16[128,4096]{1,0:T(8,128)(2,1)}, bf16[128,4096]{1,0:T(8,128)(2,1)}) custom-call(bf16[3,128,512]{2,1,0:T(8,128)(2,1)S(1)} %get-tuple-element.55.rest_0_.refs_0_, bf16[3,128,512]{2,1,0:T(8,128)(2,1)S(1)} %collective-permute-done.15.refs_1_, ...), custom_call_target="tpu_custom_call", output_to_operand_aliasing={{0}: (2, {}), {1}: (3, {}), {2}: (4, {})} | custom-call | bytes 1024 | tf_op jit(solution)/shard_map/place/pallas_call | solution.py:389
  53.7 6.7 %collective-permute-done.14.refs_1_ = bf16[3,128,512]{2,1,0:T(8,128)(2,1)S(1)} collective-permute-done((bf16[3,128,512]{2,1,0:T(8,128)(2,1)S(1)}, bf16[3,128,512]{2,1,0:T(8,128)(2,1)S(1)}, u32[]{:S(2)}, u32[]{:S(2)}) %collective-permute-start.14) | collective-permute-done | bytes 393248 | tf_op jit(solution)/shard_map/ppermute | solution.py:316
  60.4 0.9 %place.7 = (bf16[128,4096]{1,0:T(8,128)(2,1)}, bf16[128,4096]{1,0:T(8,128)(2,1)}, bf16[128,4096]{1,0:T(8,128)(2,1)}) custom-call(bf16[3,128,512]{2,1,0:T(8,128)(2,1)S(1)} %get-tuple-element.57.refs_0_, bf16[3,128,512]{2,1,0:T(8,128)(2,1)S(1)} %collective-permute-done.14.refs_1_, ...), custom_call_target="tpu_custom_call", output_to_operand_aliasing={{0}: (2, {}), {1}: (3, {}), {2}: (4, {})} | custom-call | bytes 1024 | tf_op jit(solution)/shard_map/place/pallas_call | solution.py:389
Async XLA Ops:
  0.6 0.7 %copy-start.4 = (s32[8]{0:T(128)S(1)}, s32[8]{0:T(128)}, u32[]{:S(2)}) copy-start(s32[8]{0:T(128)} %lengths.25) | copy-start | bytes 100
  2.9 10.9 %copy-start.5 = (s32[8]{0:T(128)S(1)}, s32[8]{0:T(128)}, u32[]{:S(2)}) copy-start(s32[8]{0:T(128)} %lengths.25) | copy-start | bytes 100
  2.9 2.3 %collective-permute-start = (f32[8,128,128]{2,1,0:T(8,128)S(1)}, f32[8,128,128]{2,1,0:T(8,128)S(1)}, u32[]{:S(2)}, u32[]{:S(2)}) collective-permute-start(f32[8,128,128]{2,1,0:T(8,128)S(1)} %states.4), channel_id=1, source_target_pairs={{0,2},{2,0},{4,6},{6,4},{8,10},{10,8},{12,14},{14,12},{16,18},{18,... | collective-permute-start | bytes 1572872 | tf_op jit(solution)/shard_map/ppermute | solution.py:304
  5.1 12.0 %collective-permute-start.3 = (f32[8,128,128]{2,1,0:T(8,128)S(1)}, f32[8,128,128]{2,1,0:T(8,128)S(1)}, u32[]{:S(2)}, u32[]{:S(2)}) collective-permute-start(f32[8,128,128]{2,1,0:T(8,128)S(1)} %states.3.kept), channel_id=1, source_target_pairs={{0,2},{2,0},{4,6},{6,4},{8,10},{10,8},{12,14},{14,12},{16,18},{18,... | collective-permute-start | bytes 1572872 | tf_op jit(solution)/shard_map/ppermute | solution.py:304
  5.9 13.0 %collective-permute-start.4 = (bf16[1040,128]{1,0:T(8,128)(2,1)S(1)}, bf16[1040,128]{1,0:T(8,128)(2,1)S(1)}, u32[]{:S(2)}, u32[]{:S(2)}) collective-permute-start(bf16[1040,128]{1,0:T(8,128)(2,1)S(1)} %get-tuple-element.41), channel_id=1, source_target_pairs={{0,6},{4,10},{8,14},{12,18},{16,22},{20,26},{24,30},{6,0},{10,4},{... | collective-permute-start | bytes 798728 | tf_op jit(solution)/shard_map/ppermute | solution.py:310
  10.4 8.5 %collective-permute-start.5 = (bf16[1024,128]{1,0:T(8,128)(2,1)S(1)}, bf16[1024,128]{1,0:T(8,128)(2,1)S(1)}, u32[]{:S(2)}, u32[]{:S(2)}) collective-permute-start(bf16[1024,128]{1,0:T(8,128)(2,1)S(1)} %get-tuple-element.36.rest_0_), channel_id=1, source_target_pairs={{0,10},{4,14},{8,18},{12,22},{16,26},{20,30},{10,0},{14,4},{18,8},... | collective-permute-start | bytes 786440 | tf_op jit(solution)/shard_map/ppermute | solution.py:310
  13.9 6.3 %copy-start.1 = (bf16[256,2048]{1,0:T(8,128)(2,1)S(1)}, bf16[256,2048]{1,0:T(8,128)(2,1)}, u32[]{:S(2)}) copy-start(bf16[256,2048]{1,0:T(8,128)(2,1)} %v.15) | copy-start | bytes 3145732
  13.9 6.3 %copy-start.2 = (bf16[256,2048]{1,0:T(8,128)(2,1)S(1)}, bf16[256,2048]{1,0:T(8,128)(2,1)}, u32[]{:S(2)}) copy-start(bf16[256,2048]{1,0:T(8,128)(2,1)} %g.15) | copy-start | bytes 3145732
  13.9 6.3 %copy-start.3 = (bf16[256,2048]{1,0:T(8,128)(2,1)S(1)}, bf16[256,2048]{1,0:T(8,128)(2,1)}, u32[]{:S(2)}) copy-start(bf16[256,2048]{1,0:T(8,128)(2,1)} %q.13) | copy-start | bytes 3145732
  16.3 3.9 %copy-start = (bf16[256,2048]{1,0:T(8,128)(2,1)S(1)}, bf16[256,2048]{1,0:T(8,128)(2,1)}, u32[]{:S(2)}) copy-start(bf16[256,2048]{1,0:T(8,128)(2,1)} %k.15) | copy-start | bytes 3145732
  16.3 8.5 %collective-permute-start.2 = (f32[8,128,128]{2,1,0:T(8,128)S(1)}, f32[8,128,128]{2,1,0:T(8,128)S(1)}, u32[]{:S(2)}, u32[]{:S(2)}) collective-permute-start(f32[8,128,128]{2,1,0:T(8,128)S(1)} %get-tuple-element.40), channel_id=1, source_target_pairs={{0,2},{2,0},{4,6},{6,4},{8,10},{10,8},{12,14},{14,12},{16,18},{18,... | collective-permute-start | bytes 1572872 | tf_op jit(solution)/shard_map/ppermute | solution.py:304
  19.6 2.7 %collective-permute-start.6 = (f32[4,128,128]{2,1,0:T(8,128)S(1)}, f32[4,128,128]{2,1,0:T(8,128)S(1)}, u32[]{:S(2)}, u32[]{:S(2)}) collective-permute-start(f32[4,128,128]{2,1,0:T(8,128)S(1)} %get-tuple-element.43), channel_id=1, source_target_pairs={{0,2},{2,0},{4,6},{6,4},{8,10},{10,8},{12,14},{14,12},{16,18},{18,... | collective-permute-start | bytes 786440 | tf_op jit(solution)/shard_map/ppermute | solution.py:304
  19.7 14.3 %collective-permute-start.1 = (f32[8,128,128]{2,1,0:T(8,128)S(1)}, f32[8,128,128]{2,1,0:T(8,128)S(1)}, u32[]{:S(2)}, u32[]{:S(2)}) collective-permute-start(f32[8,128,128]{2,1,0:T(8,128)S(1)} %get-tuple-element.39.kept), channel_id=1, source_target_pairs={{0,2},{2,0},{4,6},{6,4},{8,10},{10,8},{12,14},{14,12},{16,18},{18,... | collective-permute-start | bytes 1572872 | tf_op jit(solution)/shard_map/ppermute | solution.py:304
  23.3 13.0 %collective-permute-start.9 = (bf16[3,128,512]{2,1,0:T(8,128)(2,1)S(1)}, bf16[3,128,512]{2,1,0:T(8,128)(2,1)S(1)}, u32[]{:S(2)}, u32[]{:S(2)}) collective-permute-start(bf16[3,128,512]{2,1,0:T(8,128)(2,1)S(1)} %get-tuple-element.47), channel_id=1, source_target_pairs={{0,1},{1,0},{2,3},{3,2},{4,5},{5,4},{6,7},{7,6},{8,9},{9,8},{10,11... | collective-permute-start | bytes 1179656 | tf_op jit(solution)/shard_map/ppermute | solution.py:316
  24.8 6.4 %collective-permute-start.12 = (f32[4,128,128]{2,1,0:T(8,128)S(1)}, f32[4,128,128]{2,1,0:T(8,128)S(1)}, u32[]{:S(2)}, u32[]{:S(2)}) collective-permute-start(f32[4,128,128]{2,1,0:T(8,128)S(1)} %get-tuple-element.53), channel_id=1, source_target_pairs={{0,2},{2,0},{4,6},{6,4},{8,10},{10,8},{12,14},{14,12},{16,18},{18,... | collective-permute-start | bytes 786440 | tf_op jit(solution)/shard_map/ppermute | solution.py:304
  25.5 10.8 %collective-permute-start.7 = (bf16[1040,128]{1,0:T(8,128)(2,1)S(1)}, bf16[1040,128]{1,0:T(8,128)(2,1)S(1)}, u32[]{:S(2)}, u32[]{:S(2)}) collective-permute-start(bf16[1040,128]{1,0:T(8,128)(2,1)S(1)} %get-tuple-element.45), channel_id=1, source_target_pairs={{0,6},{4,10},{8,14},{12,18},{16,22},{20,26},{24,30},{6,0},{10,4},{... | collective-permute-start | bytes 798728 | tf_op jit(solution)/shard_map/ppermute | solution.py:310
  28.2 8.0 %collective-permute-start.8 = (bf16[1024,128]{1,0:T(8,128)(2,1)S(1)}, bf16[1024,128]{1,0:T(8,128)(2,1)S(1)}, u32[]{:S(2)}, u32[]{:S(2)}) collective-permute-start(bf16[1024,128]{1,0:T(8,128)(2,1)S(1)} %get-tuple-element.46), channel_id=1, source_target_pairs={{0,10},{4,14},{8,18},{12,22},{16,26},{20,30},{10,0},{14,4},{18,8},... | collective-permute-start | bytes 786440 | tf_op jit(solution)/shard_map/ppermute | solution.py:310
  33.4 9.4 %collective-permute-start.13 = (bf16[3,128,512]{2,1,0:T(8,128)(2,1)S(1)}, bf16[3,128,512]{2,1,0:T(8,128)(2,1)S(1)}, u32[]{:S(2)}, u32[]{:S(2)}) collective-permute-start(bf16[3,128,512]{2,1,0:T(8,128)(2,1)S(1)} %get-tuple-element.56), channel_id=1, source_target_pairs={{0,1},{1,0},{2,3},{3,2},{4,5},{5,4},{6,7},{7,6},{8,9},{9,8},{10,11... | collective-permute-start | bytes 1179656 | tf_op jit(solution)/shard_map/ppermute | solution.py:316
  36.9 1.6 %collective-permute-start.11 = (f32[4,128,128]{2,1,0:T(8,128)S(1)}, f32[4,128,128]{2,1,0:T(8,128)S(1)}, u32[]{:S(2)}, u32[]{:S(2)}) collective-permute-start(f32[4,128,128]{2,1,0:T(8,128)S(1)} %get-tuple-element.51), channel_id=1, source_target_pairs={{0,2},{2,0},{4,6},{6,4},{8,10},{10,8},{12,14},{14,12},{16,18},{18,... | collective-permute-start | bytes 786440 | tf_op jit(solution)/shard_map/ppermute | solution.py:304
  37.0 5.8 %collective-permute-start.10 = (f32[4,128,128]{2,1,0:T(8,128)S(1)}, f32[4,128,128]{2,1,0:T(8,128)S(1)}, u32[]{:S(2)}, u32[]{:S(2)}) collective-permute-start(f32[4,128,128]{2,1,0:T(8,128)S(1)} %get-tuple-element.49), channel_id=1, source_target_pairs={{0,2},{2,0},{4,6},{6,4},{8,10},{10,8},{12,14},{14,12},{16,18},{18,... | collective-permute-start | bytes 786440 | tf_op jit(solution)/shard_map/ppermute | solution.py:304
  40.7 12.0 %collective-permute-start.15 = (bf16[3,128,512]{2,1,0:T(8,128)(2,1)S(1)}, bf16[3,128,512]{2,1,0:T(8,128)(2,1)S(1)}, u32[]{:S(2)}, u32[]{:S(2)}) collective-permute-start(bf16[3,128,512]{2,1,0:T(8,128)(2,1)S(1)} %get-tuple-element.59), channel_id=1, source_target_pairs={{0,1},{1,0},{2,3},{3,2},{4,5},{5,4},{6,7},{7,6},{8,9},{9,8},{10,11... | collective-permute-start | bytes 1179656 | tf_op jit(solution)/shard_map/ppermute | solution.py:316
  45.0 15.4 %collective-permute-start.14 = (bf16[3,128,512]{2,1,0:T(8,128)(2,1)S(1)}, bf16[3,128,512]{2,1,0:T(8,128)(2,1)S(1)}, u32[]{:S(2)}, u32[]{:S(2)}) collective-permute-start(bf16[3,128,512]{2,1,0:T(8,128)(2,1)S(1)} %get-tuple-element.58), channel_id=1, source_target_pairs={{0,1},{1,0},{2,3},{3,2},{4,5},{5,4},{6,7},{7,6},{8,9},{9,8},{10,11... | collective-permute-start | bytes 1179656 | tf_op jit(solution)/shard_map/ppermute | solution.py:316
where the time goes:
time: 61.6 us; the launch traced here: 61.3 us
  Pallas kernels  22.3 us (36%)
  starting transfers between devices  20.1 us (33%)
  waiting for transfers between devices  17.4 us (28%)
  between operations  0.88 us (1%)
  local copies, waits for them, and re-layouts  0.68 us (1%)
    ppermute x4, starting transfers between devices, swap_pairs(): lax.ppermute(sent[hop - 1], 'seq', perm + [(b, a) for a, b in perm])  13.7 us
    pallas_call x10, Pallas kernels, call(): pl.pallas_call(kernel, in_specs=[in_smem] + [in_vmem] * len(args) + [anyw...  12.9 us
    ppermute x4, waiting for transfers between devices, send_rows(): lax.ppermute(outs[j], 'head', [(x, (x + j) % groups) for x in range(group...  12.3 us
    pallas_call x3, Pallas kernels, states(): pl.pallas_call(functools.partial(state_kernel, offset=offset, heads=heads...  5.7 us
    ppermute x4, starting transfers between devices, send_rows(): lax.ppermute(outs[j], 'head', [(x, (x + j) % groups) for x in range(group...  4.53 us
    ppermute x4, waiting for transfers between devices, swap_pairs(): lax.ppermute(sent[hop - 1], 'seq', perm + [(b, a) for a, b in perm])  3.99 us
    pallas_call x4, Pallas kernels, shards(): pl.pallas_call(functools.partial(place_kernel, groups=groups, offset=offs...  3.7 us
    ppermute x8, starting transfers between devices, swap_cores(): return lax.ppermute(a, 'seq', [(b, b ^ 1) for b in range(seq)])  1.85 us
  transfers between devices with their start and end apart: 16, of which 6 were waited for; matrix products, arithmetic and copies ran while one was open for 0% of the time, Pallas kernels for 32%

commit v1 on v0

--- a/solution.py
+++ b/solution.py
@@ -85,8 +85,8 @@
             out[h] = dot(jnp.where(here, held[n, 0, :, cols], zero), held[n, 1, :, cols], TN)
 
 
-def pair_kernel(lengths, kept, got, *rest, ndocs, rows, hops):
-    sent = rest[-hops:]
+def pair_kernel(lengths, kept, got, *rest, ndocs, rows, hops, copies):
+    sent, again = rest[-hops - copies:len(rest) - copies], rest[len(rest) - copies:]
     place = lax.axis_index("seq")
     first_core = lax.rem(place, 2) == 0
     even = (place - lax.rem(place, 2)) * rows
@@ -100,10 +100,14 @@
         out[:size] = total
         if out.shape[0] > size:
             out[size:] = jnp.zeros((out.shape[0] - size, HEAD_DIM), LINK)
-
-
-def join_kernel(lengths, other, *rest, ndocs, rows, counts, hops):
-    came, mine, theirs = rest[:hops], rest[-2 * len(counts):-len(counts)], rest[-len(counts):]
+    for i, out in enumerate(again):
+        count = out.shape[0]
+        out[...] = kept[i * count:(i + 1) * count]
+
+
+def join_kernel(lengths, *rest, ndocs, rows, counts, hops, pieces):
+    others, came = rest[:len(counts)], rest[len(counts):len(counts) + hops]
+    mine, theirs = rest[-pieces - len(counts):-pieces], rest[-pieces:]
     place = lax.axis_index("seq")
     first_core = lax.rem(place, 2) == 0
     even = (place - lax.rem(place, 2)) * rows
@@ -127,8 +131,11 @@
         for hop in range(1, hops):
             total = total + weights[hop] * came[hop][lines].astype(jnp.float32)
         total = total.reshape(count, HEAD_DIM, HEAD_DIM)
-        theirs[c][...] = total
-        mine[c][...] = from_other * other[at] + from_pair * total
+        if pieces == 1:
+            theirs[0][at] = total
+        else:
+            theirs[c][...] = total
+        mine[c][...] = from_other * others[c][...] + from_pair * total
 
 
 def split(a, axis):
@@ -187,14 +194,14 @@
             outs[j][i] = done[i, at, :]
 
 
-def grad_kernel(lengths, q, k, v, g, lower, upper, mine, got, *rest, ndocs, rows, offset, heads, groups):
+def grad_kernel(lengths, q, k, v, g, lower, upper, mine, got, *rest, ndocs, rows, offset, base, heads, groups):
     outs, done = rest[-1 - groups:-1], rest[-1]
     first_core, first_rows, last_rows = own_range(lengths, ndocs, rows)
     for h in range(heads):
         cols = slice(h * HEAD_DIM, (h + 1) * HEAD_DIM)
         at = slice(offset + h * HEAD_DIM, offset + (h + 1) * HEAD_DIM)
-        state = jnp.where(first_core, got[h], mine[h])
-        grad = jnp.where(first_core, mine[h], got[h])
+        state = jnp.where(first_core, got[base + h], mine[h])
+        grad = jnp.where(first_core, mine[h], got[base + h])
         near = local_part(q, k, v, g, lower, upper, at)
         carries = (carry_of_state(g, state, first_rows, at), *carries_of_grad(k, v, grad, last_rows, at))
         for i in range(3):
@@ -332,23 +339,24 @@
             cost_estimate=cheap, compiler_params=pltpu.CompilerParams(vmem_limit_bytes=SECOND_LIMIT if after else FIRST_LIMIT), name="states",
         )(doc_lengths, *inputs, *after)
 
-    def pair_up(kept, got, after):
+    def pair_up(kept, got, counts, after):
         lines = kept.shape[0] * HEAD_DIM
-        outs = [shape_of(lines + PAD * (hops - hop), HEAD_DIM, dtype=LINK) for hop in range(1, hops + 1)]
-        totals = call("pair", functools.partial(pair_kernel, hops=hops, **sizes), (kept, got), outs, after=after)
-        return totals[-1], swap_pairs(totals)
-
-    def join(kept, came, chunks, after):
+        outs = [shape_of(lines + PAD * (hops - hop + 1), HEAD_DIM, dtype=LINK) for hop in range(1, hops + 1)]
+        outs += [shape_of(n, *square) for n in counts]
+        kernel = functools.partial(pair_kernel, hops=hops, copies=len(counts), **sizes)
+        made = call("pair", kernel, (kept, got), outs, after=after)
+        return made[hops - 1], swap_pairs(made[:hops]), [swap_cores(a) for a in made[hops:]]
+
+    def join(others, came, chunks, after, at_once):
         counts = [cw // HEAD_DIM for _, cw in chunks]
-        joined = call(
-            "join", functools.partial(join_kernel, counts=counts, hops=hops, **sizes), (swap_cores(kept), *came),
-            [shape_of(n, *square) for n in counts] * 2, after=after,
-        )
-        return [(mine, swap_cores(theirs)) for mine, theirs in zip(joined[:len(chunks)], joined[len(chunks):])]
-
-    def grads(masks, offset, cw, mine, theirs, after):
+        pieces = [sum(counts)] if at_once else counts
+        kernel = functools.partial(join_kernel, counts=counts, hops=hops, pieces=len(pieces), **sizes)
+        made = call("join", kernel, (*others, *came), [shape_of(n, *square) for n in (*counts, *pieces)], after=after)
+        return made[:len(counts)], [swap_cores(a) for a in made[len(counts):]]
+
+    def grads(masks, offset, base, cw, mine, theirs, after):
         return call(
-            "grads", functools.partial(grad_kernel, offset=offset, heads=cw // HEAD_DIM, groups=groups, **sizes),
+            "grads", functools.partial(grad_kernel, offset=offset, base=base, heads=cw // HEAD_DIM, groups=groups, **sizes),
             (*inputs, *masks, mine, theirs), [shape_of(3, part, cw, dtype=bf16)] * groups,
             [pltpu.VMEM((3, rows, cw), bf16)], after, GRAD_LIMIT,
         )
@@ -364,25 +372,33 @@
             [shape_of(3, part, cw, dtype=bf16)] * groups, [pltpu.VMEM((3, rows, cw), bf16)], limit=GRAD_LIMIT,
         )
 
-    cuts, outs, arrived, totals, masks = [], [], [], [], None
-    for start, half, chunks in halves:
-        if not totals:
-            (sent,) = states(("sent",), start, half, [])
-            (kept,) = states(("kept",), start, half, [])
-        else:
-            kept, sent = states(("kept", "sent"), start, half, totals)
-        total, came = pair_up(kept, swap_cores(sent), [made[0] for made in outs[:1]])
-        totals = [total]
-        masks = masks or call("masks", functools.partial(mask_kernel, **sizes), (), [shape_of(rows, rows)] * 2, after=totals)
-        joined = join(kept, came, chunks, [parts[1] for parts in arrived[:1]] or masks[:1])
-        for (offset, cw), (mine, theirs) in zip(chunks, joined):
+    outs, arrived = [], []
+
+    def half_grads(chunks, joined):
+        mine, theirs = joined
+        base = 0
+        for c, (offset, cw) in enumerate(chunks):
             after = [made[0] for made in outs[-1:]] + [parts[1] for parts in arrived[1:-1]][-1:]
             if outs:
-                outs.append(grads(masks, offset, cw, mine, theirs, after))
+                at = base if len(theirs) == 1 else 0
+                outs.append(grads(masks, offset, at, cw, mine[c], theirs[c % len(theirs)], after))
             else:
-                outs.append(grads_early(masks, offset, cw, mine, theirs))
+                outs.append(grads_early(masks, offset, cw, mine[c], theirs[0]))
             arrived.append(send_rows(outs[-1]))
-        cuts += chunks
+            base += cw // HEAD_DIM
+
+    (start, half, chunks), (second, _, second_chunks) = halves
+    counts = [cw // HEAD_DIM for _, cw in chunks]
+    (sent,) = states(("sent",), start, half, [])
+    (kept,) = states(("kept",), start, half, [])
+    total, came, others = pair_up(kept, swap_cores(sent), counts, [])
+    masks = call("masks", functools.partial(mask_kernel, **sizes), (), [shape_of(rows, rows)] * 2, after=[total])
+    kept, sent = states(("kept", "sent"), second, half, [total])
+    got = swap_cores(sent)
+    half_grads(chunks, join(others, came, chunks, [masks[0], sent], True))
+    _, came, others = pair_up(kept, got, counts, [outs[0][0]])
+    half_grads(second_chunks, join(others, came, second_chunks, [outs[-1][0], arrived[0][1]], False))
+    cuts = chunks + second_chunks
 
     placed = []
     for c, (offset, cw) in enumerate(cuts):

time: 61.6 us -> 63.2 us (1.026)
  waiting for transfers between devices: 17.4 us -> 19.5 us
  starting transfers between devices: 20.1 us -> 19.4 us
    ppermute x4, waiting for transfers between devices: 12.3 us -> 14.9 us  [send_rows(): lax.ppermute(outs[j], 'head', [(x, (x + j) % groups) for x in range(group...]
    ppermute x4, starting transfers between devices: 4.53 us -> 3.36 us  [send_rows(): lax.ppermute(outs[j], 'head', [(x, (x + j) % groups) for x in range(group...]
    ppermute x8 -> x9, starting transfers between devices: 1.85 us -> 2.36 us  [swap_cores(): return lax.ppermute(a, 'seq', [(b, b ^ 1) for b in range(seq)])]
  transfers between devices with their start and end apart: 16 -> 17, of which waited for: 6 -> 6; matrix products, arithmetic and copies ran while one was open for 0% -> 0% of each run, Pallas kernels for 32% -> 29%
where the time goes in v1:
time: 63.2 us; the launch traced here: 62.9 us
  Pallas kernels  22.4 us (35%)
  waiting for transfers between devices  19.5 us (31%)
  starting transfers between devices  19.4 us (31%)
  between operations  0.91 us (1%)
  local copies, waits for them, and re-layouts  0.68 us (1%)
    ppermute x4, waiting for transfers between devices, send_rows(): lax.ppermute(outs[j], 'head', [(x, (x + j) % groups) for x in range(group...  14.9 us
    ppermute x4, starting transfers between devices, swap_pairs(): lax.ppermute(sent[hop - 1], 'seq', perm + [(b, a) for a, b in perm])  13.7 us
    pallas_call x10, Pallas kernels, call(): pl.pallas_call(kernel, in_specs=[in_smem] + [in_vmem] * len(args) + [anyw...  13 us
    pallas_call x3, Pallas kernels, states(): pl.pallas_call(functools.partial(state_kernel, offset=offset, heads=heads...  5.7 us
    pallas_call x4, Pallas kernels, shards(): pl.pallas_call(functools.partial(place_kernel, groups=groups, offset=offs...  3.7 us
    ppermute x4, waiting for transfers between devices, swap_pairs(): lax.ppermute(sent[hop - 1], 'seq', perm + [(b, a) for a, b in perm])  3.57 us
    ppermute x4, starting transfers between devices, send_rows(): lax.ppermute(outs[j], 'head', [(x, (x + j) % groups) for x in range(group...  3.36 us
    ppermute x9, starting transfers between devices, swap_cores(): return lax.ppermute(a, 'seq', [(b, b ^ 1) for b in range(seq)])  2.36 us
  transfers between devices with their start and end apart: 17, of which 6 were waited for; matrix products, arithmetic and copies ran while one was open for 0% of the time, Pallas kernels for 29%

profile of v1, /device:TPU:0, one launch (start us, length us, event | category | flops | bytes accessed | tf_op | source)
XLA Modules:
  0.0 62.9 jit_solution(8131673947814395197)
XLA Ops:
  0.6 0.0 copy-start.4
  0.6 0.6 %copy-done.4 = s32[8]{0:T(128)S(1)} copy-done((s32[8]{0:T(128)S(1)}, s32[8]{0:T(128)}, u32[]{:S(2)}) %copy-start.4) | copy-done | bytes 56
  1.3 1.6 %states.4 = f32[8,128,128]{2,1,0:T(8,128)S(1)} custom-call(s32[8]{0:T(128)S(1)} %copy-done.4, bf16[256,2048]{1,0:T(8,128)(2,1)} %q.13, bf16[256,2048]{1,0:T(8,128)(2,1)} %k.15, bf16[256,2048]{1,0:T(8,128)(2,1)} %v.15, bf16[256,2048]{1,0:T(8,128)(2,1)} %g.15), custom_call_target="tpu_custom_call" | custom-call | bytes 1024 | tf_op jit(solution)/shard_map/states/pallas_call | solution.py:331
  2.9 0.0 copy-start.5
  2.9 0.5 collective-permute-start
  3.5 1.6 %states.3.kept = f32[8,128,128]{2,1,0:T(8,128)S(1)} custom-call(s32[8]{0:T(128)S(1)} %copy-done.4, bf16[256,2048]{1,0:T(8,128)(2,1)} %q.13, bf16[256,2048]{1,0:T(8,128)(2,1)} %k.15, bf16[256,2048]{1,0:T(8,128)(2,1)} %v.15, bf16[256,2048]{1,0:T(8,128)(2,1)} %g.15), custom_call_target="tpu_custom_call" | custom-call | bytes 1024 | tf_op jit(solution)/shard_map/states/pallas_call | solution.py:331
  5.1 0.0 collective-permute-done.got
  5.1 0.6 %pair.2 = (bf16[1056,128]{1,0:T(8,128)(2,1)S(1)}, bf16[1040,128]{1,0:T(8,128)(2,1)S(1)}, f32[4,128,128]{2,1,0:T(8,128)S(1)}, f32[4,128,128]{2,1,0:T(8,128)S(1)}) custom-call(s32[8]{0:T(128)S(1)} %copy-done.4, f32[8,128,128]{2,1,0:T(8,128)S(1)} %states.3.kept, f32[8,128,128]{2,1,0:T(8,128)S(1)} %collective-permute-done.got), custom_call_target="tpu_custom_call" | custom-call | bytes 1024 | tf_op jit(solution)/shard_map/pair/pallas_call | solution.py:304
  5.8 4.5 %collective-permute-start.4 = (bf16[1056,128]{1,0:T(8,128)(2,1)S(1)}, bf16[1056,128]{1,0:T(8,128)(2,1)S(1)}, u32[]{:S(2)}, u32[]{:S(2)}) collective-permute-start(bf16[1056,128]{1,0:T(8,128)(2,1)S(1)} %get-tuple-element.46), channel_id=1, source_target_pairs={{0,6},{4,10},{8,14},{12,18},{16,22},{20,26},{24,30},{6,0},{10,4},{... | collective-permute-start | bytes 811016 | tf_op jit(solution)/shard_map/ppermute | solution.py:317
  10.3 3.2 %collective-permute-start.5 = (bf16[1040,128]{1,0:T(8,128)(2,1)S(1)}, bf16[1040,128]{1,0:T(8,128)(2,1)S(1)}, u32[]{:S(2)}, u32[]{:S(2)}) collective-permute-start(bf16[1040,128]{1,0:T(8,128)(2,1)S(1)} %get-tuple-element.39.rest_0_), channel_id=1, source_target_pairs={{0,10},{4,14},{8,18},{12,22},{16,26},{20,30},{10,0},{14,4},{18,8},... | collective-permute-start | bytes 798728 | tf_op jit(solution)/shard_map/ppermute | solution.py:317
  13.6 0.1 collective-permute-start.2
  13.6 0.5 collective-permute-start.3
  14.1 0.7 %masks.1 = (f32[256,256]{1,0:T(8,128)S(1)}, f32[256,256]{1,0:T(8,128)S(1)}) custom-call(s32[8]{0:T(128)S(1)} %copy-done.4, bf16[1040,128]{1,0:T(8,128)(2,1)S(1)} %get-tuple-element.39.rest_0_), custom_call_target="tpu_custom_call" | custom-call | bytes 1024 | tf_op jit(solution)/shard_map/masks/pallas_call | solution.py:304
  14.8 0.0 copy-done.5
  14.8 0.0 copy-start.1
  14.8 0.0 copy-start.2
  14.8 0.0 copy-start.3
  14.9 2.4 %states.5 = (f32[8,128,128]{2,1,0:T(8,128)S(1)}, f32[8,128,128]{2,1,0:T(8,128)S(1)}) custom-call(s32[8]{0:T(128)S(1)} %copy-done.5, bf16[256,2048]{1,0:T(8,128)(2,1)} %q.13, bf16[256,2048]{1,0:T(8,128)(2,1)} %k.15, bf16[256,2048]{1,0:T(8,128)(2,1)} %v.15, bf16[256,2048]{1,0:T(8,128)(2,1)} %g.15, bf16[1040,128]{1,0:T(8,128)(2,1)S(1)} %get-tuple-element.39.rest_0_), custom_call_target="tpu_custom_call" | custom-call | bytes 1024 | tf_op jit(solution)/shard_map/states/pallas_call | solution.py:331
  17.3 0.0 copy-start
  17.3 0.0 collective-permute-done.2.rest_0_
  17.3 0.0 collective-permute-done.3.rest_1_
  17.3 1.3 %collective-permute-done.5.rest_3_ = bf16[1040,128]{1,0:T(8,128)(2,1)S(1)} collective-permute-done((bf16[1040,128]{1,0:T(8,128)(2,1)S(1)}, bf16[1040,128]{1,0:T(8,128)(2,1)S(1)}, u32[]{:S(2)}, u32[]{:S(2)}) %collective-permute-start.5) | collective-permute-done | bytes 266272 | tf_op jit(solution)/shard_map/ppermute | solution.py:317
  18.7 0.0 collective-permute-done.4.rest_2_
  18.7 0.7 %join.2 = (f32[4,128,128]{2,1,0:T(8,128)S(1)}, f32[4,128,128]{2,1,0:T(8,128)S(1)}, f32[8,128,128]{2,1,0:T(8,128)S(1)}) custom-call(s32[8]{0:T(128)S(1)} %copy-done.5, f32[4,128,128]{2,1,0:T(8,128)S(1)} %collective-permute-done.2.rest_0_, f32[4,128,128]{2,1,0:T(8,128)S(1)} %collective-permute-done.3.rest_1_, ...), custom_call_target="tpu_custom_call" | custom-call | bytes 1024 | tf_op jit(solution)/shard_map/join/pallas_call | solution.py:304
  19.4 0.1 collective-permute-start.6
  19.5 0.5 collective-permute-start.1
  20.0 0.0 copy-done.1
  20.0 0.0 copy-done.2
  20.0 0.0 copy-done.3
  20.0 0.0 copy-done
  20.0 2.1 %begin.1.near = f32[3,256,512]{2,1,0:T(8,128)S(1)} custom-call(s32[8]{0:T(128)S(1)} %copy-done.5, bf16[256,2048]{1,0:T(8,128)(2,1)S(1)} %copy-done.3, bf16[256,2048]{1,0:T(8,128)(2,1)S(1)} %copy-done, bf16[256,2048]{1,0:T(8,128)(2,1)S(1)} %copy-done.1, bf16[256,2048]{1,0:T(8,128)(2,1)S(1)} %copy-done.2, f32[256,256]{1,0:T(8,128)S(1)} %get-tuple-element.40.rest_4_.lower, ...), custom_call_target="tpu_custom_call" | custom-call | bytes 1024 | tf_op jit(solution)/shard_map/begin/pallas_call | solution.py:304
  22.0 0.0 collective-permute-done.6.got
  22.1 1.0 %end.1 = (bf16[3,128,512]{2,1,0:T(8,128)(2,1)S(1)}, bf16[3,128,512]{2,1,0:T(8,128)(2,1)S(1)}) custom-call(s32[8]{0:T(128)S(1)} %copy-done.5, bf16[256,2048]{1,0:T(8,128)(2,1)S(1)} %copy-done, bf16[256,2048]{1,0:T(8,128)(2,1)S(1)} %copy-done.1, bf16[256,2048]{1,0:T(8,128)(2,1)S(1)} %copy-done.2, f32[3,256,512]{2,1,0:T(8,128)S(1)} %begin.1.near, ...), custom_call_target="tpu_custom_call" | custom-call | bytes 1024 | tf_op jit(solution)/shard_map/end/pallas_call | solution.py:304
  23.1 1.6 %collective-permute-start.11 = (bf16[3,128,512]{2,1,0:T(8,128)(2,1)S(1)}, bf16[3,128,512]{2,1,0:T(8,128)(2,1)S(1)}, u32[]{:S(2)}, u32[]{:S(2)}) collective-permute-start(bf16[3,128,512]{2,1,0:T(8,128)(2,1)S(1)} %get-tuple-element.56), channel_id=1, source_target_pairs={{0,1},{1,0},{2,3},{3,2},{4,5},{5,4},{6,7},{7,6},{8,9},{9,8},{10,11... | collective-permute-start | bytes 1179656 | tf_op jit(solution)/shard_map/ppermute | solution.py:323
  24.6 0.0 collective-permute-done.1.got
  24.6 0.7 %pair.3 = (bf16[1056,128]{1,0:T(8,128)(2,1)S(1)}, bf16[1040,128]{1,0:T(8,128)(2,1)S(1)}, f32[4,128,128]{2,1,0:T(8,128)S(1)}, f32[4,128,128]{2,1,0:T(8,128)S(1)}) custom-call(s32[8]{0:T(128)S(1)} %copy-done.5, f32[8,128,128]{2,1,0:T(8,128)S(1)} %get-tuple-element.42.kept, f32[8,128,128]{2,1,0:T(8,128)S(1)} %collective-permute-done.1.got, ...), custom_call_target="tpu_custom_call" | custom-call | bytes 1024 | tf_op jit(solution)/shard_map/pair/pallas_call | solution.py:304
  25.3 0.1 collective-permute-start.7
  25.3 2.9 %collective-permute-start.9 = (bf16[1056,128]{1,0:T(8,128)(2,1)S(1)}, bf16[1056,128]{1,0:T(8,128)(2,1)S(1)}, u32[]{:S(2)}, u32[]{:S(2)}) collective-permute-start(bf16[1056,128]{1,0:T(8,128)(2,1)S(1)} %get-tuple-element.52), channel_id=1, source_target_pairs={{0,6},{4,10},{8,14},{12,18},{16,22},{20,26},{24,30},{6,0},{10,4},{... | collective-permute-start | bytes 811016 | tf_op jit(solution)/shard_map/ppermute | solution.py:317
  28.3 3.0 %collective-permute-start.10 = (bf16[1040,128]{1,0:T(8,128)(2,1)S(1)}, bf16[1040,128]{1,0:T(8,128)(2,1)S(1)}, u32[]{:S(2)}, u32[]{:S(2)}) collective-permute-start(bf16[1040,128]{1,0:T(8,128)(2,1)S(1)} %get-tuple-element.53), channel_id=1, source_target_pairs={{0,10},{4,14},{8,18},{12,22},{16,26},{20,30},{10,0},{14,4},{18,8},... | collective-permute-start | bytes 798728 | tf_op jit(solution)/shard_map/ppermute | solution.py:317
  31.3 0.1 collective-permute-start.8
  31.4 2.2 %grads.3 = (bf16[3,128,512]{2,1,0:T(8,128)(2,1)S(1)}, bf16[3,128,512]{2,1,0:T(8,128)(2,1)S(1)}) custom-call(s32[8]{0:T(128)S(1)} %copy-done.5, bf16[256,2048]{1,0:T(8,128)(2,1)S(1)} %copy-done.3, bf16[256,2048]{1,0:T(8,128)(2,1)S(1)} %copy-done, bf16[256,2048]{1,0:T(8,128)(2,1)S(1)} %copy-done.1, bf16[256,2048]{1,0:T(8,128)(2,1)S(1)} %copy-done.2, ...), custom_call_target="tpu_custom_call" | custom-call | bytes 1024 | tf_op jit(solution)/shard_map/grads/pallas_call | solution.py:304
  33.5 0.0 collective-permute-done.7.rest_0_
  33.6 0.6 collective-permute-start.14
  34.2 0.0 collective-permute-done.8.rest_1_
  34.2 2.2 %collective-permute-done.10.rest_3_ = bf16[1040,128]{1,0:T(8,128)(2,1)S(1)} collective-permute-done((bf16[1040,128]{1,0:T(8,128)(2,1)S(1)}, bf16[1040,128]{1,0:T(8,128)(2,1)S(1)}, u32[]{:S(2)}, u32[]{:S(2)}) %collective-permute-start.10) | collective-permute-done | bytes 266272 | tf_op jit(solution)/shard_map/ppermute | solution.py:317
  36.4 0.0 collective-permute-done.9.rest_2_
  36.4 0.0 collective-permute-done.11.rest_5_.refs_1_
  36.4 0.7 %join.3 = (f32[4,128,128]{2,1,0:T(8,128)S(1)}, f32[4,128,128]{2,1,0:T(8,128)S(1)}, f32[4,128,128]{2,1,0:T(8,128)S(1)}, f32[4,128,128]{2,1,0:T(8,128)S(1)}) custom-call(s32[8]{0:T(128)S(1)} %copy-done.5, f32[4,128,128]{2,1,0:T(8,128)S(1)} %collective-permute-done.7.rest_0_, f32[4,128,128]{2,1,0:T(8,128)S(1)} %collective-permute-done.8.rest_1_, ...), custom_call_target="tpu_custom_call" | custom-call | bytes 1024 | tf_op jit(solution)/shard_map/join/pallas_call | solution.py:304
  37.1 0.1 collective-permute-start.13
  37.2 0.5 collective-permute-start.12
  37.7 1.0 %collective-permute-done.13.got = f32[4,128,128]{2,1,0:T(8,128)S(1)} collective-permute-done((f32[4,128,128]{2,1,0:T(8,128)S(1)}, f32[4,128,128]{2,1,0:T(8,128)S(1)}, u32[]{:S(2)}, u32[]{:S(2)}) %collective-permute-start.13) | collective-permute-done | bytes 262176 | tf_op jit(solution)/shard_map/ppermute | solution.py:311
  38.7 2.2 %grads.4 = (bf16[3,128,512]{2,1,0:T(8,128)(2,1)S(1)}, bf16[3,128,512]{2,1,0:T(8,128)(2,1)S(1)}) custom-call(s32[8]{0:T(128)S(1)} %copy-done.5, bf16[256,2048]{1,0:T(8,128)(2,1)S(1)} %copy-done.3, bf16[256,2048]{1,0:T(8,128)(2,1)S(1)} %copy-done, bf16[256,2048]{1,0:T(8,128)(2,1)S(1)} %copy-done.1, bf16[256,2048]{1,0:T(8,128)(2,1)S(1)} %copy-done.2, ...), custom_call_target="tpu_custom_call" | custom-call | bytes 1024 | tf_op jit(solution)/shard_map/grads/pallas_call | solution.py:304
  40.9 0.6 collective-permute-start.16
  41.5 4.0 %collective-permute-done.14.rest_1_.refs_1_ = bf16[3,128,512]{2,1,0:T(8,128)(2,1)S(1)} collective-permute-done((bf16[3,128,512]{2,1,0:T(8,128)(2,1)S(1)}, bf16[3,128,512]{2,1,0:T(8,128)(2,1)S(1)}, u32[]{:S(2)}, u32[]{:S(2)}) %collective-permute-start.14) | collective-permute-done | bytes 393248 | tf_op jit(solution)/shard_map/ppermute | solution.py:323
  45.5 0.0 collective-permute-done.12.got
  45.5 2.2 %grads.5 = (bf16[3,128,512]{2,1,0:T(8,128)(2,1)S(1)}, bf16[3,128,512]{2,1,0:T(8,128)(2,1)S(1)}) custom-call(s32[8]{0:T(128)S(1)} %copy-done.5, bf16[256,2048]{1,0:T(8,128)(2,1)S(1)} %copy-done.3, bf16[256,2048]{1,0:T(8,128)(2,1)S(1)} %copy-done, bf16[256,2048]{1,0:T(8,128)(2,1)S(1)} %copy-done.1, bf16[256,2048]{1,0:T(8,128)(2,1)S(1)} %copy-done.2, ...), custom_call_target="tpu_custom_call" | custom-call | bytes 1024 | tf_op jit(solution)/shard_map/grads/pallas_call | solution.py:304
  47.7 0.6 collective-permute-start.15
  48.3 0.9 %place.4 = (bf16[128,4096]{1,0:T(8,128)(2,1)}, bf16[128,4096]{1,0:T(8,128)(2,1)}, bf16[128,4096]{1,0:T(8,128)(2,1)}) custom-call(bf16[3,128,512]{2,1,0:T(8,128)(2,1)S(1)} %get-tuple-element.49.rest_0_.refs_0_, bf16[3,128,512]{2,1,0:T(8,128)(2,1)S(1)} %collective-permute-done.11.rest_5_.refs_1_), custom_call_target="tpu_custom_call" | custom-call | bytes 1024 | tf_op jit(solution)/shard_map/place/pallas_call | solution.py:405
  49.2 0.9 %place.5 = (bf16[128,4096]{1,0:T(8,128)(2,1)}, bf16[128,4096]{1,0:T(8,128)(2,1)}, bf16[128,4096]{1,0:T(8,128)(2,1)}) custom-call(bf16[3,128,512]{2,1,0:T(8,128)(2,1)S(1)} %get-tuple-element.55.rest_4_.rest_0_.refs_0_, bf16[3,128,512]{2,1,0:T(8,128)(2,1)S(1)} %collective-permute-done.14.rest_1_.refs_1_, ...), custom_call_target="tpu_custom_call", output_to_operand_aliasing={{0}: (2, {}), {1}: (3, {}), {2}: (4, {})} | custom-call | bytes 1024 | tf_op jit(solution)/shard_map/place/pallas_call | solution.py:405
  50.2 3.8 %collective-permute-done.16.refs_1_ = bf16[3,128,512]{2,1,0:T(8,128)(2,1)S(1)} collective-permute-done((bf16[3,128,512]{2,1,0:T(8,128)(2,1)S(1)}, bf16[3,128,512]{2,1,0:T(8,128)(2,1)S(1)}, u32[]{:S(2)}, u32[]{:S(2)}) %collective-permute-start.16) | collective-permute-done | bytes 393248 | tf_op jit(solution)/shard_map/ppermute | solution.py:323
  54.0 0.9 %place.6 = (bf16[128,4096]{1,0:T(8,128)(2,1)}, bf16[128,4096]{1,0:T(8,128)(2,1)}, bf16[128,4096]{1,0:T(8,128)(2,1)}) custom-call(bf16[3,128,512]{2,1,0:T(8,128)(2,1)S(1)} %get-tuple-element.61.rest_0_.refs_0_, bf16[3,128,512]{2,1,0:T(8,128)(2,1)S(1)} %collective-permute-done.16.refs_1_, ...), custom_call_target="tpu_custom_call", output_to_operand_aliasing={{0}: (2, {}), {1}: (3, {}), {2}: (4, {})} | custom-call | bytes 1024 | tf_op jit(solution)/shard_map/place/pallas_call | solution.py:405
  54.9 7.1 %collective-permute-done.15.refs_1_ = bf16[3,128,512]{2,1,0:T(8,128)(2,1)S(1)} collective-permute-done((bf16[3,128,512]{2,1,0:T(8,128)(2,1)S(1)}, bf16[3,128,512]{2,1,0:T(8,128)(2,1)S(1)}, u32[]{:S(2)}, u32[]{:S(2)}) %collective-permute-start.15) | collective-permute-done | bytes 393248 | tf_op jit(solution)/shard_map/ppermute | solution.py:323
  62.0 0.9 %place.7 = (bf16[128,4096]{1,0:T(8,128)(2,1)}, bf16[128,4096]{1,0:T(8,128)(2,1)}, bf16[128,4096]{1,0:T(8,128)(2,1)}) custom-call(bf16[3,128,512]{2,1,0:T(8,128)(2,1)S(1)} %get-tuple-element.63.refs_0_, bf16[3,128,512]{2,1,0:T(8,128)(2,1)S(1)} %collective-permute-done.15.refs_1_, ...), custom_call_target="tpu_custom_call", output_to_operand_aliasing={{0}: (2, {}), {1}: (3, {}), {2}: (4, {})} | custom-call | bytes 1024 | tf_op jit(solution)/shard_map/place/pallas_call | solution.py:405
Async XLA Ops:
  0.6 0.7 %copy-start.4 = (s32[8]{0:T(128)S(1)}, s32[8]{0:T(128)}, u32[]{:S(2)}) copy-start(s32[8]{0:T(128)} %lengths.25) | copy-start | bytes 100
  2.9 11.9 %copy-start.5 = (s32[8]{0:T(128)S(1)}, s32[8]{0:T(128)}, u32[]{:S(2)}) copy-start(s32[8]{0:T(128)} %lengths.25) | copy-start | bytes 100
  2.9 2.2 %collective-permute-start = (f32[8,128,128]{2,1,0:T(8,128)S(1)}, f32[8,128,128]{2,1,0:T(8,128)S(1)}, u32[]{:S(2)}, u32[]{:S(2)}) collective-permute-start(f32[8,128,128]{2,1,0:T(8,128)S(1)} %states.4), channel_id=1, source_target_pairs={{0,2},{2,0},{4,6},{6,4},{8,10},{10,8},{12,14},{14,12},{16,18},{18,... | collective-permute-start | bytes 1572872 | tf_op jit(solution)/shard_map/ppermute | solution.py:311
  5.8 12.9 %collective-permute-start.4 = (bf16[1056,128]{1,0:T(8,128)(2,1)S(1)}, bf16[1056,128]{1,0:T(8,128)(2,1)S(1)}, u32[]{:S(2)}, u32[]{:S(2)}) collective-permute-start(bf16[1056,128]{1,0:T(8,128)(2,1)S(1)} %get-tuple-element.46), channel_id=1, source_target_pairs={{0,6},{4,10},{8,14},{12,18},{16,22},{20,26},{24,30},{6,0},{10,4},{... | collective-permute-start | bytes 811016 | tf_op jit(solution)/shard_map/ppermute | solution.py:317
  10.3 8.3 %collective-permute-start.5 = (bf16[1040,128]{1,0:T(8,128)(2,1)S(1)}, bf16[1040,128]{1,0:T(8,128)(2,1)S(1)}, u32[]{:S(2)}, u32[]{:S(2)}) collective-permute-start(bf16[1040,128]{1,0:T(8,128)(2,1)S(1)} %get-tuple-element.39.rest_0_), channel_id=1, source_target_pairs={{0,10},{4,14},{8,18},{12,22},{16,26},{20,30},{10,0},{14,4},{18,8},... | collective-permute-start | bytes 798728 | tf_op jit(solution)/shard_map/ppermute | solution.py:317
  13.6 3.7 %collective-permute-start.2 = (f32[4,128,128]{2,1,0:T(8,128)S(1)}, f32[4,128,128]{2,1,0:T(8,128)S(1)}, u32[]{:S(2)}, u32[]{:S(2)}) collective-permute-start(f32[4,128,128]{2,1,0:T(8,128)S(1)} %get-tuple-element.44), channel_id=1, source_target_pairs={{0,2},{2,0},{4,6},{6,4},{8,10},{10,8},{12,14},{14,12},{16,18},{18,... | collective-permute-start | bytes 786440 | tf_op jit(solution)/shard_map/ppermute | solution.py:311
  13.6 3.7 %collective-permute-start.3 = (f32[4,128,128]{2,1,0:T(8,128)S(1)}, f32[4,128,128]{2,1,0:T(8,128)S(1)}, u32[]{:S(2)}, u32[]{:S(2)}) collective-permute-start(f32[4,128,128]{2,1,0:T(8,128)S(1)} %get-tuple-element.45), channel_id=1, source_target_pairs={{0,2},{2,0},{4,6},{6,4},{8,10},{10,8},{12,14},{14,12},{16,18},{18,... | collective-permute-start | bytes 786440 | tf_op jit(solution)/shard_map/ppermute | solution.py:311
  14.8 5.1 %copy-start.1 = (bf16[256,2048]{1,0:T(8,128)(2,1)S(1)}, bf16[256,2048]{1,0:T(8,128)(2,1)}, u32[]{:S(2)}) copy-start(bf16[256,2048]{1,0:T(8,128)(2,1)} %v.15) | copy-start | bytes 3145732
  14.8 5.1 %copy-start.2 = (bf16[256,2048]{1,0:T(8,128)(2,1)S(1)}, bf16[256,2048]{1,0:T(8,128)(2,1)}, u32[]{:S(2)}) copy-start(bf16[256,2048]{1,0:T(8,128)(2,1)} %g.15) | copy-start | bytes 3145732
  14.8 5.1 %copy-start.3 = (bf16[256,2048]{1,0:T(8,128)(2,1)S(1)}, bf16[256,2048]{1,0:T(8,128)(2,1)}, u32[]{:S(2)}) copy-start(bf16[256,2048]{1,0:T(8,128)(2,1)} %q.13) | copy-start | bytes 3145732
  17.3 2.7 %copy-start = (bf16[256,2048]{1,0:T(8,128)(2,1)S(1)}, bf16[256,2048]{1,0:T(8,128)(2,1)}, u32[]{:S(2)}) copy-start(bf16[256,2048]{1,0:T(8,128)(2,1)} %k.15) | copy-start | bytes 3145732
  19.4 2.7 %collective-permute-start.6 = (f32[8,128,128]{2,1,0:T(8,128)S(1)}, f32[8,128,128]{2,1,0:T(8,128)S(1)}, u32[]{:S(2)}, u32[]{:S(2)}) collective-permute-start(f32[8,128,128]{2,1,0:T(8,128)S(1)} %get-tuple-element.48), channel_id=1, source_target_pairs={{0,2},{2,0},{4,6},{6,4},{8,10},{10,8},{12,14},{14,12},{16,18},{18,... | collective-permute-start | bytes 1572872 | tf_op jit(solution)/shard_map/ppermute | solution.py:311
  19.5 5.1 %collective-permute-start.1 = (f32[8,128,128]{2,1,0:T(8,128)S(1)}, f32[8,128,128]{2,1,0:T(8,128)S(1)}, u32[]{:S(2)}, u32[]{:S(2)}) collective-permute-start(f32[8,128,128]{2,1,0:T(8,128)S(1)} %get-tuple-element.43.rest_5_), channel_id=1, source_target_pairs={{0,2},{2,0},{4,6},{6,4},{8,10},{10,8},{12,14},{14,12},{16,18},{18,... | collective-permute-start | bytes 1572872 | tf_op jit(solution)/shard_map/ppermute | solution.py:311
  23.1 13.3 %collective-permute-start.11 = (bf16[3,128,512]{2,1,0:T(8,128)(2,1)S(1)}, bf16[3,128,512]{2,1,0:T(8,128)(2,1)S(1)}, u32[]{:S(2)}, u32[]{:S(2)}) collective-permute-start(bf16[3,128,512]{2,1,0:T(8,128)(2,1)S(1)} %get-tuple-element.56), channel_id=1, source_target_pairs={{0,1},{1,0},{2,3},{3,2},{4,5},{5,4},{6,7},{7,6},{8,9},{9,8},{10,11... | collective-permute-start | bytes 1179656 | tf_op jit(solution)/shard_map/ppermute | solution.py:323
  25.3 8.3 %collective-permute-start.7 = (f32[4,128,128]{2,1,0:T(8,128)S(1)}, f32[4,128,128]{2,1,0:T(8,128)S(1)}, u32[]{:S(2)}, u32[]{:S(2)}) collective-permute-start(f32[4,128,128]{2,1,0:T(8,128)S(1)} %get-tuple-element.50), channel_id=1, source_target_pairs={{0,2},{2,0},{4,6},{6,4},{8,10},{10,8},{12,14},{14,12},{16,18},{18,... | collective-permute-start | bytes 786440 | tf_op jit(solution)/shard_map/ppermute | solution.py:311
  25.3 11.0 %collective-permute-start.9 = (bf16[1056,128]{1,0:T(8,128)(2,1)S(1)}, bf16[1056,128]{1,0:T(8,128)(2,1)S(1)}, u32[]{:S(2)}, u32[]{:S(2)}) collective-permute-start(bf16[1056,128]{1,0:T(8,128)(2,1)S(1)} %get-tuple-element.52), channel_id=1, source_target_pairs={{0,6},{4,10},{8,14},{12,18},{16,22},{20,26},{24,30},{6,0},{10,4},{... | collective-permute-start | bytes 811016 | tf_op jit(solution)/shard_map/ppermute | solution.py:317
  28.3 8.1 %collective-permute-start.10 = (bf16[1040,128]{1,0:T(8,128)(2,1)S(1)}, bf16[1040,128]{1,0:T(8,128)(2,1)S(1)}, u32[]{:S(2)}, u32[]{:S(2)}) collective-permute-start(bf16[1040,128]{1,0:T(8,128)(2,1)S(1)} %get-tuple-element.53), channel_id=1, source_target_pairs={{0,10},{4,14},{8,18},{12,22},{16,26},{20,30},{10,0},{14,4},{18,8},... | collective-permute-start | bytes 798728 | tf_op jit(solution)/shard_map/ppermute | solution.py:317
  31.3 2.9 %collective-permute-start.8 = (f32[4,128,128]{2,1,0:T(8,128)S(1)}, f32[4,128,128]{2,1,0:T(8,128)S(1)}, u32[]{:S(2)}, u32[]{:S(2)}) collective-permute-start(f32[4,128,128]{2,1,0:T(8,128)S(1)} %get-tuple-element.51), channel_id=1, source_target_pairs={{0,2},{2,0},{4,6},{6,4},{8,10},{10,8},{12,14},{14,12},{16,18},{18,... | collective-permute-start | bytes 786440 | tf_op jit(solution)/shard_map/ppermute | solution.py:311
  33.6 12.0 %collective-permute-start.14 = (bf16[3,128,512]{2,1,0:T(8,128)(2,1)S(1)}, bf16[3,128,512]{2,1,0:T(8,128)(2,1)S(1)}, u32[]{:S(2)}, u32[]{:S(2)}) collective-permute-start(bf16[3,128,512]{2,1,0:T(8,128)(2,1)S(1)} %get-tuple-element.62), channel_id=1, source_target_pairs={{0,1},{1,0},{2,3},{3,2},{4,5},{5,4},{6,7},{7,6},{8,9},{9,8},{10,11... | collective-permute-start | bytes 1179656 | tf_op jit(solution)/shard_map/ppermute | solution.py:323
  37.1 1.6 %collective-permute-start.13 = (f32[4,128,128]{2,1,0:T(8,128)S(1)}, f32[4,128,128]{2,1,0:T(8,128)S(1)}, u32[]{:S(2)}, u32[]{:S(2)}) collective-permute-start(f32[4,128,128]{2,1,0:T(8,128)S(1)} %get-tuple-element.60), channel_id=1, source_target_pairs={{0,2},{2,0},{4,6},{6,4},{8,10},{10,8},{12,14},{14,12},{16,18},{18,... | collective-permute-start | bytes 786440 | tf_op jit(solution)/shard_map/ppermute | solution.py:311
  37.2 8.3 %collective-permute-start.12 = (f32[4,128,128]{2,1,0:T(8,128)S(1)}, f32[4,128,128]{2,1,0:T(8,128)S(1)}, u32[]{:S(2)}, u32[]{:S(2)}) collective-permute-start(f32[4,128,128]{2,1,0:T(8,128)S(1)} %get-tuple-element.58), channel_id=1, source_target_pairs={{0,2},{2,0},{4,6},{6,4},{8,10},{10,8},{12,14},{14,12},{16,18},{18,... | collective-permute-start | bytes 786440 | tf_op jit(solution)/shard_map/ppermute | solution.py:311
  40.9 13.1 %collective-permute-start.16 = (bf16[3,128,512]{2,1,0:T(8,128)(2,1)S(1)}, bf16[3,128,512]{2,1,0:T(8,128)(2,1)S(1)}, u32[]{:S(2)}, u32[]{:S(2)}) collective-permute-start(bf16[3,128,512]{2,1,0:T(8,128)(2,1)S(1)} %get-tuple-element.65), channel_id=1, source_target_pairs={{0,1},{1,0},{2,3},{3,2},{4,5},{5,4},{6,7},{7,6},{8,9},{9,8},{10,11... | collective-permute-start | bytes 1179656 | tf_op jit(solution)/shard_map/ppermute | solution.py:323
  47.7 14.3 %collective-permute-start.15 = (bf16[3,128,512]{2,1,0:T(8,128)(2,1)S(1)}, bf16[3,128,512]{2,1,0:T(8,128)(2,1)S(1)}, u32[]{:S(2)}, u32[]{:S(2)}) collective-permute-start(bf16[3,128,512]{2,1,0:T(8,128)(2,1)S(1)} %get-tuple-element.64), channel_id=1, source_target_pairs={{0,1},{1,0},{2,3},{3,2},{4,5},{5,4},{6,7},{7,6},{8,9},{9,8},{10,11... | collective-permute-start | bytes 1179656 | tf_op jit(solution)/shard_map/ppermute | solution.py:323

commit v2 on v0

--- a/solution.py
+++ b/solution.py
@@ -14,9 +14,9 @@
 PAD = 16
 LINK = jnp.bfloat16
 VMEM_LIMIT = 16 * 1024 * 1024
-GRAD_LIMIT = 40 * 1024 * 1024
+GRAD_LIMIT = 32 * 1024 * 1024
 FIRST_LIMIT = 53 * 1024 * 1024
-SECOND_LIMIT = 52 * 1024 * 1024
+SECOND_LIMIT = 40 * 1024 * 1024
 NT = (((1,), (1,)), ((), ()))
 TN = (((0,), (0,)), ((), ()))
 NN = (((1,), (0,)), ((), ()))
@@ -202,55 +202,26 @@
     deal(done, outs, rows, groups)
 
 
-def begin_kernel(lengths, q, k, v, g, lower, upper, mine, *rest, ndocs, rows, offset, heads):
-    near = rest[-1]
-    first_core, first_rows, last_rows = own_range(lengths, ndocs, rows)
+def local_kernel(lengths, q, k, v, g, lower, upper, near, token, *, offset, heads):
+    token[...] = jnp.zeros_like(token)
     for h in range(heads):
         cols = slice(h * HEAD_DIM, (h + 1) * HEAD_DIM)
         at = slice(offset + h * HEAD_DIM, offset + (h + 1) * HEAD_DIM)
         for i, value in enumerate(local_part(q, k, v, g, lower, upper, at)):
             near[i, :, cols] = value
 
-    @pl.when(first_core)
-    def _():
-        for h in range(heads):
-            cols = slice(h * HEAD_DIM, (h + 1) * HEAD_DIM)
-            at = slice(offset + h * HEAD_DIM, offset + (h + 1) * HEAD_DIM)
-            carry_k, carry_v = carries_of_grad(k, v, mine[h], last_rows, at)
-            near[1, :, cols] += carry_k
-            near[2, :, cols] += carry_v
-
-    @pl.when(jnp.logical_not(first_core))
-    def _():
-        for h in range(heads):
-            cols = slice(h * HEAD_DIM, (h + 1) * HEAD_DIM)
-            at = slice(offset + h * HEAD_DIM, offset + (h + 1) * HEAD_DIM)
-            near[0, :, cols] += carry_of_state(g, mine[h], first_rows, at)
-
-
-def end_kernel(lengths, k, v, g, near, got, *rest, ndocs, rows, offset, heads, groups):
+
+def carry_kernel(lengths, k, v, g, near, mine, got, *rest, ndocs, rows, offset, heads, groups):
     outs, done = rest[-1 - groups:-1], rest[-1]
     first_core, first_rows, last_rows = own_range(lengths, ndocs, rows)
-
-    @pl.when(first_core)
-    def _():
-        for h in range(heads):
-            cols = slice(h * HEAD_DIM, (h + 1) * HEAD_DIM)
-            at = slice(offset + h * HEAD_DIM, offset + (h + 1) * HEAD_DIM)
-            done[0, :, cols] = (near[0, :, cols] + carry_of_state(g, got[h], first_rows, at)).astype(jnp.bfloat16)
-            done[1, :, cols] = near[1, :, cols].astype(jnp.bfloat16)
-            done[2, :, cols] = near[2, :, cols].astype(jnp.bfloat16)
-
-    @pl.when(jnp.logical_not(first_core))
-    def _():
-        for h in range(heads):
-            cols = slice(h * HEAD_DIM, (h + 1) * HEAD_DIM)
-            at = slice(offset + h * HEAD_DIM, offset + (h + 1) * HEAD_DIM)
-            carry_k, carry_v = carries_of_grad(k, v, got[h], last_rows, at)
-            done[0, :, cols] = near[0, :, cols].astype(jnp.bfloat16)
-            done[1, :, cols] = (near[1, :, cols] + carry_k).astype(jnp.bfloat16)
-            done[2, :, cols] = (near[2, :, cols] + carry_v).astype(jnp.bfloat16)
-
+    for h in range(heads):
+        cols = slice(h * HEAD_DIM, (h + 1) * HEAD_DIM)
+        at = slice(offset + h * HEAD_DIM, offset + (h + 1) * HEAD_DIM)
+        state = jnp.where(first_core, got[h], mine[h])
+        grad = jnp.where(first_core, mine[h], got[h])
+        carries = (carry_of_state(g, state, first_rows, at), *carries_of_grad(k, v, grad, last_rows, at))
+        for i in range(3):
+            done[i, :, cols] = (near[i, :, cols] + carries[i]).astype(jnp.bfloat16)
     deal(done, outs, rows, groups)
 
 
@@ -353,15 +324,17 @@
             [pltpu.VMEM((3, rows, cw), bf16)], after, GRAD_LIMIT,
         )
 
-    def grads_early(masks, offset, cw, mine, theirs):
-        more = dict(offset=offset, heads=cw // HEAD_DIM, **sizes)
-        near = call(
-            "begin", functools.partial(begin_kernel, **more), (*inputs, *masks, mine), [shape_of(3, rows, cw)],
-            limit=GRAD_LIMIT,
-        )[0]
+    def local(masks, offset, cw):
+        kernel = functools.partial(local_kernel, offset=offset, heads=cw // HEAD_DIM)
         return call(
-            "end", functools.partial(end_kernel, groups=groups, **more), (*inputs[1:], near, theirs),
-            [shape_of(3, part, cw, dtype=bf16)] * groups, [pltpu.VMEM((3, rows, cw), bf16)], limit=GRAD_LIMIT,
+            "local", kernel, (*inputs, *masks), [shape_of(3, rows, cw), shape_of(8, HEAD_DIM)], limit=GRAD_LIMIT,
+        )
+
+    def carry(near, offset, cw, mine, theirs, after):
+        kernel = functools.partial(carry_kernel, offset=offset, heads=cw // HEAD_DIM, groups=groups, **sizes)
+        return call(
+            "carry", kernel, (*inputs[1:], near, mine, theirs), [shape_of(3, part, cw, dtype=bf16)] * groups,
+            [pltpu.VMEM((3, rows, cw), bf16)], after, GRAD_LIMIT,
         )
 
     cuts, outs, arrived, totals, masks = [], [], [], [], None
@@ -370,18 +343,21 @@
             (sent,) = states(("sent",), start, half, [])
             (kept,) = states(("kept",), start, half, [])
         else:
-            kept, sent = states(("kept", "sent"), start, half, totals)
+            kept, sent = states(("kept", "sent"), start, half, [token])
         total, came = pair_up(kept, swap_cores(sent), [made[0] for made in outs[:1]])
-        totals = [total]
-        masks = masks or call("masks", functools.partial(mask_kernel, **sizes), (), [shape_of(rows, rows)] * 2, after=totals)
-        joined = join(kept, came, chunks, [parts[1] for parts in arrived[:1]] or masks[:1])
-        for (offset, cw), (mine, theirs) in zip(chunks, joined):
+        if not totals:
+            masks = call("masks", functools.partial(mask_kernel, **sizes), (), [shape_of(rows, rows)] * 2, after=[total])
+            near = [local(masks, *chunk) for chunk in chunks]
+            token = near[0][1]
+        joined = join(kept, came, chunks, [parts[1] for parts in arrived[:1]] or [made[1] for made in near])
+        for c, ((offset, cw), (mine, theirs)) in enumerate(zip(chunks, joined)):
             after = [made[0] for made in outs[-1:]] + [parts[1] for parts in arrived[1:-1]][-1:]
-            if outs:
+            if totals:
                 outs.append(grads(masks, offset, cw, mine, theirs, after))
             else:
-                outs.append(grads_early(masks, offset, cw, mine, theirs))
+                outs.append(carry(near[c][0], offset, cw, mine, theirs, after))
             arrived.append(send_rows(outs[-1]))
+        totals = [total]
         cuts += chunks
 
     placed = []

time: 61.6 us -> 62 us (level)
    ppermute x8, waiting for transfers between devices: 1.04 us -> 2.12 us  [swap_cores(): return lax.ppermute(a, 'seq', [(b, b ^ 1) for b in range(seq)])]
    ppermute x4, waiting for transfers between devices: 3.99 us -> 3.1 us  [swap_pairs(): lax.ppermute(sent[hop - 1], 'seq', perm + [(b, a) for a, b in perm])]
    pallas_call x10 -> x11, Pallas kernels: 12.9 us -> 13.5 us  [call(): pl.pallas_call(kernel, in_specs=[in_smem] + [in_vmem] * len(args) + [anyw...]
where the time goes in v2:
time: 62 us; the launch traced here: 61.7 us
  Pallas kernels  22.5 us (36%)
  starting transfers between devices  20.5 us (33%)
  waiting for transfers between devices  17.2 us (28%)
  between operations  0.87 us (1%)
  local copies, waits for them, and re-layouts  0.67 us (1%)
    ppermute x4, starting transfers between devices, swap_pairs(): lax.ppermute(sent[hop - 1], 'seq', perm + [(b, a) for a, b in perm])  13.6 us
    pallas_call x11, Pallas kernels, call(): pl.pallas_call(kernel, in_specs=[in_smem] + [in_vmem] * len(args) + [anyw...  13.5 us
    ppermute x4, waiting for transfers between devices, send_rows(): lax.ppermute(outs[j], 'head', [(x, (x + j) % groups) for x in range(group...  12 us
    pallas_call x3, Pallas kernels, states(): pl.pallas_call(functools.partial(state_kernel, offset=offset, heads=heads...  5.25 us
    ppermute x4, starting transfers between devices, send_rows(): lax.ppermute(outs[j], 'head', [(x, (x + j) % groups) for x in range(group...  4.89 us
    pallas_call x4, Pallas kernels, shards(): pl.pallas_call(functools.partial(place_kernel, groups=groups, offset=offs...  3.7 us
    ppermute x4, waiting for transfers between devices, swap_pairs(): lax.ppermute(sent[hop - 1], 'seq', perm + [(b, a) for a, b in perm])  3.1 us
    ppermute x8, waiting for transfers between devices, swap_cores(): return lax.ppermute(a, 'seq', [(b, b ^ 1) for b in range(seq)])  2.12 us
  transfers between devices with their start and end apart: 16, of which 6 were waited for; matrix products, arithmetic and copies ran while one was open for 0% of the time, Pallas kernels for 32%

profile of v2, /device:TPU:0, one launch (start us, length us, event | category | flops | bytes accessed | tf_op | source)
XLA Modules:
  0.0 61.7 jit_solution(1439460555631852863)
XLA Ops:
  0.6 0.0 copy-start.4
  0.6 0.6 %copy-done.4 = s32[8]{0:T(128)S(1)} copy-done((s32[8]{0:T(128)S(1)}, s32[8]{0:T(128)}, u32[]{:S(2)}) %copy-start.4) | copy-done | bytes 56
  1.3 1.6 %states.4 = f32[8,128,128]{2,1,0:T(8,128)S(1)} custom-call(s32[8]{0:T(128)S(1)} %copy-done.4, bf16[256,2048]{1,0:T(8,128)(2,1)} %q.13, bf16[256,2048]{1,0:T(8,128)(2,1)} %k.17, bf16[256,2048]{1,0:T(8,128)(2,1)} %v.17, bf16[256,2048]{1,0:T(8,128)(2,1)} %g.17), custom_call_target="tpu_custom_call" | custom-call | bytes 1024 | tf_op jit(solution)/shard_map/states/pallas_call | solution.py:295
  2.9 0.5 collective-permute-start
  3.5 0.0 copy-start.1
  3.5 0.0 copy-start.2
  3.5 0.0 copy-start.3
  3.5 1.8 %states.3.kept = f32[8,128,128]{2,1,0:T(8,128)S(1)} custom-call(s32[8]{0:T(128)S(1)} %copy-done.4, bf16[256,2048]{1,0:T(8,128)(2,1)} %q.13, bf16[256,2048]{1,0:T(8,128)(2,1)} %k.17, bf16[256,2048]{1,0:T(8,128)(2,1)} %v.17, bf16[256,2048]{1,0:T(8,128)(2,1)} %g.17), custom_call_target="tpu_custom_call" | custom-call | bytes 1024 | tf_op jit(solution)/shard_map/states/pallas_call | solution.py:295
  5.3 0.0 copy-start
  5.3 0.1 collective-permute-start.3
  5.4 0.0 collective-permute-done.got
  5.4 0.6 %pair.2 = (bf16[1040,128]{1,0:T(8,128)(2,1)S(1)}, bf16[1024,128]{1,0:T(8,128)(2,1)S(1)}) custom-call(s32[8]{0:T(128)S(1)} %copy-done.4, f32[8,128,128]{2,1,0:T(8,128)S(1)} %states.3.kept, f32[8,128,128]{2,1,0:T(8,128)S(1)} %collective-permute-done.got), custom_call_target="tpu_custom_call" | custom-call | bytes 1024 | tf_op jit(solution)/shard_map/pair/pallas_call | solution.py:268
  6.0 4.5 %collective-permute-start.4 = (bf16[1040,128]{1,0:T(8,128)(2,1)S(1)}, bf16[1040,128]{1,0:T(8,128)(2,1)S(1)}, u32[]{:S(2)}, u32[]{:S(2)}) collective-permute-start(bf16[1040,128]{1,0:T(8,128)(2,1)S(1)} %get-tuple-element.47), channel_id=1, source_target_pairs={{0,6},{4,10},{8,14},{12,18},{16,22},{20,26},{24,30},{6,0},{10,4},{... | collective-permute-start | bytes 798728 | tf_op jit(solution)/shard_map/ppermute | solution.py:281
  10.6 3.4 %collective-permute-start.5 = (bf16[1024,128]{1,0:T(8,128)(2,1)S(1)}, bf16[1024,128]{1,0:T(8,128)(2,1)S(1)}, u32[]{:S(2)}, u32[]{:S(2)}) collective-permute-start(bf16[1024,128]{1,0:T(8,128)(2,1)S(1)} %get-tuple-element.40.rest_0_), channel_id=1, source_target_pairs={{0,10},{4,14},{8,18},{12,22},{16,26},{20,30},{10,0},{14,4},{18,8},... | collective-permute-start | bytes 786440 | tf_op jit(solution)/shard_map/ppermute | solution.py:281
  14.0 0.7 %masks.1 = (f32[256,256]{1,0:T(8,128)S(1)}, f32[256,256]{1,0:T(8,128)S(1)}) custom-call(s32[8]{0:T(128)S(1)} %copy-done.4, bf16[1024,128]{1,0:T(8,128)(2,1)S(1)} %get-tuple-element.40.rest_0_), custom_call_target="tpu_custom_call" | custom-call | bytes 1024 | tf_op jit(solution)/shard_map/masks/pallas_call | solution.py:268
  14.7 0.0 copy-done.1
  14.7 0.0 copy-done.2
  14.7 0.0 copy-done.3
  14.7 0.0 copy-done
  14.7 1.6 %local.2 = (f32[3,256,512]{2,1,0:T(8,128)S(1)}, f32[8,128]{1,0:T(8,128)S(1)}) custom-call(s32[8]{0:T(128)S(1)} %copy-done.4, bf16[256,2048]{1,0:T(8,128)(2,1)S(1)} %copy-done.3, bf16[256,2048]{1,0:T(8,128)(2,1)S(1)} %copy-done, bf16[256,2048]{1,0:T(8,128)(2,1)S(1)} %copy-done.1, bf16[256,2048]{1,0:T(8,128)(2,1)S(1)} %copy-done.2, ...), custom_call_target="tpu_custom_call" | custom-call | bytes 1024 | tf_op jit(solution)/shard_map/local/pallas_call | solution.py:268
  16.3 1.8 %states.5 = (f32[8,128,128]{2,1,0:T(8,128)S(1)}, f32[8,128,128]{2,1,0:T(8,128)S(1)}) custom-call(s32[8]{0:T(128)S(1)} %copy-done.4, bf16[256,2048]{1,0:T(8,128)(2,1)S(1)} %copy-done.3, bf16[256,2048]{1,0:T(8,128)(2,1)S(1)} %copy-done, bf16[256,2048]{1,0:T(8,128)(2,1)S(1)} %copy-done.1, bf16[256,2048]{1,0:T(8,128)(2,1)S(1)} %copy-done.2, ...), custom_call_target="tpu_custom_call" | custom-call | bytes 1024 | tf_op jit(solution)/shard_map/states/pallas_call | solution.py:295
  18.2 0.1 collective-permute-start.2
  18.2 1.6 %local.3 = (f32[3,256,512]{2,1,0:T(8,128)S(1)}, f32[8,128]{1,0:T(8,128)S(1)}) custom-call(s32[8]{0:T(128)S(1)} %copy-done.4, bf16[256,2048]{1,0:T(8,128)(2,1)S(1)} %copy-done.3, bf16[256,2048]{1,0:T(8,128)(2,1)S(1)} %copy-done, bf16[256,2048]{1,0:T(8,128)(2,1)S(1)} %copy-done.1, bf16[256,2048]{1,0:T(8,128)(2,1)S(1)} %copy-done.2, ...), custom_call_target="tpu_custom_call" | custom-call | bytes 1024 | tf_op jit(solution)/shard_map/local/pallas_call | solution.py:268
  19.9 0.0 collective-permute-done.3.other
  19.9 0.0 collective-permute-done.5.rest_1_
  19.9 0.0 collective-permute-done.4.rest_0_
  19.9 0.7 %join.2 = (f32[4,128,128]{2,1,0:T(8,128)S(1)}, f32[4,128,128]{2,1,0:T(8,128)S(1)}, f32[4,128,128]{2,1,0:T(8,128)S(1)}, f32[4,128,128]{2,1,0:T(8,128)S(1)}) custom-call(s32[8]{0:T(128)S(1)} %copy-done.4, f32[8,128,128]{2,1,0:T(8,128)S(1)} %collective-permute-done.3.other, bf16[1040,128]{1,0:T(8,128)(2,1)S(1)} %collective-permute-done.4.rest_0_, ...), custom_call_target="tpu_custom_call" | custom-call | bytes 1024 | tf_op jit(solution)/shard_map/join/pallas_call | solution.py:268
  20.6 0.6 collective-permute-start.6
  21.2 0.1 collective-permute-start.1
  21.3 1.1 %collective-permute-done.6.got = f32[4,128,128]{2,1,0:T(8,128)S(1)} collective-permute-done((f32[4,128,128]{2,1,0:T(8,128)S(1)}, f32[4,128,128]{2,1,0:T(8,128)S(1)}, u32[]{:S(2)}, u32[]{:S(2)}) %collective-permute-start.6) | collective-permute-done | bytes 262176 | tf_op jit(solution)/shard_map/ppermute | solution.py:275
  22.4 1.3 %carry.2 = (bf16[3,128,512]{2,1,0:T(8,128)(2,1)S(1)}, bf16[3,128,512]{2,1,0:T(8,128)(2,1)S(1)}) custom-call(s32[8]{0:T(128)S(1)} %copy-done.4, bf16[256,2048]{1,0:T(8,128)(2,1)S(1)} %copy-done, bf16[256,2048]{1,0:T(8,128)(2,1)S(1)} %copy-done.1, bf16[256,2048]{1,0:T(8,128)(2,1)S(1)} %copy-done.2, f32[3,256,512]{2,1,0:T(8,128)S(1)} %get-tuple-element.46.near, ...), custom_call_target="tpu_custom_call" | custom-call | bytes 1024 | tf_op jit(solution)/shard_map/carry/pallas_call | solution.py:268
  23.7 1.6 %collective-permute-start.9 = (bf16[3,128,512]{2,1,0:T(8,128)(2,1)S(1)}, bf16[3,128,512]{2,1,0:T(8,128)(2,1)S(1)}, u32[]{:S(2)}, u32[]{:S(2)}) collective-permute-start(bf16[3,128,512]{2,1,0:T(8,128)(2,1)S(1)} %get-tuple-element.54), channel_id=1, source_target_pairs={{0,1},{1,0},{2,3},{3,2},{4,5},{5,4},{6,7},{7,6},{8,9},{9,8},{10,11... | collective-permute-start | bytes 1179656 | tf_op jit(solution)/shard_map/ppermute | solution.py:287
  25.2 0.1 collective-permute-start.12
  25.3 0.0 collective-permute-done.2.got
  25.3 0.6 %pair.3 = (bf16[1040,128]{1,0:T(8,128)(2,1)S(1)}, bf16[1024,128]{1,0:T(8,128)(2,1)S(1)}) custom-call(s32[8]{0:T(128)S(1)} %copy-done.4, f32[8,128,128]{2,1,0:T(8,128)S(1)} %get-tuple-element.44.kept, f32[8,128,128]{2,1,0:T(8,128)S(1)} %collective-permute-done.2.got, bf16[3,128,512]{2,1,0:T(8,128)(2,1)S(1)} %get-tuple-element.51.rest_0_.refs_0_), custom_call_target="tpu_custom_call" | custom-call | bytes 1024 | tf_op jit(solution)/shard_map/pair/pallas_call | solution.py:268
  26.0 2.6 %collective-permute-start.7 = (bf16[1040,128]{1,0:T(8,128)(2,1)S(1)}, bf16[1040,128]{1,0:T(8,128)(2,1)S(1)}, u32[]{:S(2)}, u32[]{:S(2)}) collective-permute-start(bf16[1040,128]{1,0:T(8,128)(2,1)S(1)} %get-tuple-element.52), channel_id=1, source_target_pairs={{0,6},{4,10},{8,14},{12,18},{16,22},{20,26},{24,30},{6,0},{10,4},{... | collective-permute-start | bytes 798728 | tf_op jit(solution)/shard_map/ppermute | solution.py:281
  28.5 3.1 %collective-permute-start.8 = (bf16[1024,128]{1,0:T(8,128)(2,1)S(1)}, bf16[1024,128]{1,0:T(8,128)(2,1)S(1)}, u32[]{:S(2)}, u32[]{:S(2)}) collective-permute-start(bf16[1024,128]{1,0:T(8,128)(2,1)S(1)} %get-tuple-element.53), channel_id=1, source_target_pairs={{0,10},{4,14},{8,18},{12,22},{16,26},{20,30},{10,0},{14,4},{18,8},... | collective-permute-start | bytes 786440 | tf_op jit(solution)/shard_map/ppermute | solution.py:281
  31.6 0.0 collective-permute-done.12.got
  31.6 1.3 %carry.3 = (bf16[3,128,512]{2,1,0:T(8,128)(2,1)S(1)}, bf16[3,128,512]{2,1,0:T(8,128)(2,1)S(1)}) custom-call(s32[8]{0:T(128)S(1)} %copy-done.4, bf16[256,2048]{1,0:T(8,128)(2,1)S(1)} %copy-done, bf16[256,2048]{1,0:T(8,128)(2,1)S(1)} %copy-done.1, bf16[256,2048]{1,0:T(8,128)(2,1)S(1)} %copy-done.2, f32[3,256,512]{2,1,0:T(8,128)S(1)} %get-tuple-element.59.near, ...), custom_call_target="tpu_custom_call" | custom-call | bytes 1024 | tf_op jit(solution)/shard_map/carry/pallas_call | solution.py:268
  32.9 0.6 collective-permute-start.13
  33.5 0.0 collective-permute-done.1.other
  33.5 3.1 %collective-permute-done.8.rest_1_ = bf16[1024,128]{1,0:T(8,128)(2,1)S(1)} collective-permute-done((bf16[1024,128]{1,0:T(8,128)(2,1)S(1)}, bf16[1024,128]{1,0:T(8,128)(2,1)S(1)}, u32[]{:S(2)}, u32[]{:S(2)}) %collective-permute-start.8) | collective-permute-done | bytes 262176 | tf_op jit(solution)/shard_map/ppermute | solution.py:281
  36.6 0.0 collective-permute-done.7.rest_0_
  36.6 0.0 collective-permute-done.9.rest_2_.refs_1_
  36.6 0.7 %join.3 = (f32[4,128,128]{2,1,0:T(8,128)S(1)}, f32[4,128,128]{2,1,0:T(8,128)S(1)}, f32[4,128,128]{2,1,0:T(8,128)S(1)}, f32[4,128,128]{2,1,0:T(8,128)S(1)}) custom-call(s32[8]{0:T(128)S(1)} %copy-done.4, f32[8,128,128]{2,1,0:T(8,128)S(1)} %collective-permute-done.1.other, bf16[1040,128]{1,0:T(8,128)(2,1)S(1)} %collective-permute-done.7.rest_0_, ...), custom_call_target="tpu_custom_call" | custom-call | bytes 1024 | tf_op jit(solution)/shard_map/join/pallas_call | solution.py:268
  37.3 0.1 collective-permute-start.11
  37.4 0.5 collective-permute-start.10
  37.9 1.0 %collective-permute-done.11.got = f32[4,128,128]{2,1,0:T(8,128)S(1)} collective-permute-done((f32[4,128,128]{2,1,0:T(8,128)S(1)}, f32[4,128,128]{2,1,0:T(8,128)S(1)}, u32[]{:S(2)}, u32[]{:S(2)}) %collective-permute-start.11) | collective-permute-done | bytes 262176 | tf_op jit(solution)/shard_map/ppermute | solution.py:275
  38.9 2.2 %grads.2 = (bf16[3,128,512]{2,1,0:T(8,128)(2,1)S(1)}, bf16[3,128,512]{2,1,0:T(8,128)(2,1)S(1)}) custom-call(s32[8]{0:T(128)S(1)} %copy-done.4, bf16[256,2048]{1,0:T(8,128)(2,1)S(1)} %copy-done.3, bf16[256,2048]{1,0:T(8,128)(2,1)S(1)} %copy-done, bf16[256,2048]{1,0:T(8,128)(2,1)S(1)} %copy-done.1, bf16[256,2048]{1,0:T(8,128)(2,1)S(1)} %copy-done.2, ...), custom_call_target="tpu_custom_call" | custom-call | bytes 1024 | tf_op jit(solution)/shard_map/grads/pallas_call | solution.py:268
  41.1 0.6 collective-permute-start.15
  41.7 1.8 %collective-permute-done.13.rest_1_.refs_1_ = bf16[3,128,512]{2,1,0:T(8,128)(2,1)S(1)} collective-permute-done((bf16[3,128,512]{2,1,0:T(8,128)(2,1)S(1)}, bf16[3,128,512]{2,1,0:T(8,128)(2,1)S(1)}, u32[]{:S(2)}, u32[]{:S(2)}) %collective-permute-start.13) | collective-permute-done | bytes 393248 | tf_op jit(solution)/shard_map/ppermute | solution.py:287
  43.6 0.0 collective-permute-done.10.got
  43.6 2.2 %grads.3 = (bf16[3,128,512]{2,1,0:T(8,128)(2,1)S(1)}, bf16[3,128,512]{2,1,0:T(8,128)(2,1)S(1)}) custom-call(s32[8]{0:T(128)S(1)} %copy-done.4, bf16[256,2048]{1,0:T(8,128)(2,1)S(1)} %copy-done.3, bf16[256,2048]{1,0:T(8,128)(2,1)S(1)} %copy-done, bf16[256,2048]{1,0:T(8,128)(2,1)S(1)} %copy-done.1, bf16[256,2048]{1,0:T(8,128)(2,1)S(1)} %copy-done.2, ...), custom_call_target="tpu_custom_call" | custom-call | bytes 1024 | tf_op jit(solution)/shard_map/grads/pallas_call | solution.py:268
  45.7 2.1 %collective-permute-start.14 = (bf16[3,128,512]{2,1,0:T(8,128)(2,1)S(1)}, bf16[3,128,512]{2,1,0:T(8,128)(2,1)S(1)}, u32[]{:S(2)}, u32[]{:S(2)}) collective-permute-start(bf16[3,128,512]{2,1,0:T(8,128)(2,1)S(1)} %get-tuple-element.66), channel_id=1, source_target_pairs={{0,1},{1,0},{2,3},{3,2},{4,5},{5,4},{6,7},{7,6},{8,9},{9,8},{10,11... | collective-permute-start | bytes 1179656 | tf_op jit(solution)/shard_map/ppermute | solution.py:287
  47.8 0.9 %place.4 = (bf16[128,4096]{1,0:T(8,128)(2,1)}, bf16[128,4096]{1,0:T(8,128)(2,1)}, bf16[128,4096]{1,0:T(8,128)(2,1)}) custom-call(bf16[3,128,512]{2,1,0:T(8,128)(2,1)S(1)} %get-tuple-element.51.rest_0_.refs_0_, bf16[3,128,512]{2,1,0:T(8,128)(2,1)S(1)} %collective-permute-done.9.rest_2_.refs_1_), custom_call_target="tpu_custom_call" | custom-call | bytes 1024 | tf_op jit(solution)/shard_map/place/pallas_call | solution.py:365
  48.7 0.9 %place.5 = (bf16[128,4096]{1,0:T(8,128)(2,1)}, bf16[128,4096]{1,0:T(8,128)(2,1)}, bf16[128,4096]{1,0:T(8,128)(2,1)}) custom-call(bf16[3,128,512]{2,1,0:T(8,128)(2,1)S(1)} %get-tuple-element.62.rest_0_.refs_0_, bf16[3,128,512]{2,1,0:T(8,128)(2,1)S(1)} %collective-permute-done.13.rest_1_.refs_1_, ...), custom_call_target="tpu_custom_call", output_to_operand_aliasing={{0}: (2, {}), {1}: (3, {}), {2}: (4, {})} | custom-call | bytes 1024 | tf_op jit(solution)/shard_map/place/pallas_call | solution.py:365
  49.7 3.4 %collective-permute-done.15.refs_1_ = bf16[3,128,512]{2,1,0:T(8,128)(2,1)S(1)} collective-permute-done((bf16[3,128,512]{2,1,0:T(8,128)(2,1)S(1)}, bf16[3,128,512]{2,1,0:T(8,128)(2,1)S(1)}, u32[]{:S(2)}, u32[]{:S(2)}) %collective-permute-start.15) | collective-permute-done | bytes 393248 | tf_op jit(solution)/shard_map/ppermute | solution.py:287
  53.1 0.9 %place.6 = (bf16[128,4096]{1,0:T(8,128)(2,1)}, bf16[128,4096]{1,0:T(8,128)(2,1)}, bf16[128,4096]{1,0:T(8,128)(2,1)}) custom-call(bf16[3,128,512]{2,1,0:T(8,128)(2,1)S(1)} %get-tuple-element.63.rest_0_.refs_0_, bf16[3,128,512]{2,1,0:T(8,128)(2,1)S(1)} %collective-permute-done.15.refs_1_, ...), custom_call_target="tpu_custom_call", output_to_operand_aliasing={{0}: (2, {}), {1}: (3, {}), {2}: (4, {})} | custom-call | bytes 1024 | tf_op jit(solution)/shard_map/place/pallas_call | solution.py:365
  54.1 6.7 %collective-permute-done.14.refs_1_ = bf16[3,128,512]{2,1,0:T(8,128)(2,1)S(1)} collective-permute-done((bf16[3,128,512]{2,1,0:T(8,128)(2,1)S(1)}, bf16[3,128,512]{2,1,0:T(8,128)(2,1)S(1)}, u32[]{:S(2)}, u32[]{:S(2)}) %collective-permute-start.14) | collective-permute-done | bytes 393248 | tf_op jit(solution)/shard_map/ppermute | solution.py:287
  60.8 0.9 %place.7 = (bf16[128,4096]{1,0:T(8,128)(2,1)}, bf16[128,4096]{1,0:T(8,128)(2,1)}, bf16[128,4096]{1,0:T(8,128)(2,1)}) custom-call(bf16[3,128,512]{2,1,0:T(8,128)(2,1)S(1)} %get-tuple-element.65.refs_0_, bf16[3,128,512]{2,1,0:T(8,128)(2,1)S(1)} %collective-permute-done.14.refs_1_, ...), custom_call_target="tpu_custom_call", output_to_operand_aliasing={{0}: (2, {}), {1}: (3, {}), {2}: (4, {})} | custom-call | bytes 1024 | tf_op jit(solution)/shard_map/place/pallas_call | solution.py:365
Async XLA Ops:
  0.6 0.7 %copy-start.4 = (s32[8]{0:T(128)S(1)}, s32[8]{0:T(128)}, u32[]{:S(2)}) copy-start(s32[8]{0:T(128)} %lengths.27) | copy-start | bytes 100
  2.9 2.5 %collective-permute-start = (f32[8,128,128]{2,1,0:T(8,128)S(1)}, f32[8,128,128]{2,1,0:T(8,128)S(1)}, u32[]{:S(2)}, u32[]{:S(2)}) collective-permute-start(f32[8,128,128]{2,1,0:T(8,128)S(1)} %states.4), channel_id=1, source_target_pairs={{0,2},{2,0},{4,6},{6,4},{8,10},{10,8},{12,14},{14,12},{16,18},{18,... | collective-permute-start | bytes 1572872 | tf_op jit(solution)/shard_map/ppermute | solution.py:275
  3.5 11.2 %copy-start.1 = (bf16[256,2048]{1,0:T(8,128)(2,1)S(1)}, bf16[256,2048]{1,0:T(8,128)(2,1)}, u32[]{:S(2)}) copy-start(bf16[256,2048]{1,0:T(8,128)(2,1)} %v.17) | copy-start | bytes 3145732
  3.5 11.2 %copy-start.2 = (bf16[256,2048]{1,0:T(8,128)(2,1)S(1)}, bf16[256,2048]{1,0:T(8,128)(2,1)}, u32[]{:S(2)}) copy-start(bf16[256,2048]{1,0:T(8,128)(2,1)} %g.17) | copy-start | bytes 3145732
  3.5 11.2 %copy-start.3 = (bf16[256,2048]{1,0:T(8,128)(2,1)S(1)}, bf16[256,2048]{1,0:T(8,128)(2,1)}, u32[]{:S(2)}) copy-start(bf16[256,2048]{1,0:T(8,128)(2,1)} %q.13) | copy-start | bytes 3145732
  5.3 9.5 %copy-start = (bf16[256,2048]{1,0:T(8,128)(2,1)S(1)}, bf16[256,2048]{1,0:T(8,128)(2,1)}, u32[]{:S(2)}) copy-start(bf16[256,2048]{1,0:T(8,128)(2,1)} %k.17) | copy-start | bytes 3145732
  5.3 14.6 %collective-permute-start.3 = (f32[8,128,128]{2,1,0:T(8,128)S(1)}, f32[8,128,128]{2,1,0:T(8,128)S(1)}, u32[]{:S(2)}, u32[]{:S(2)}) collective-permute-start(f32[8,128,128]{2,1,0:T(8,128)S(1)} %states.3.kept), channel_id=1, source_target_pairs={{0,2},{2,0},{4,6},{6,4},{8,10},{10,8},{12,14},{14,12},{16,18},{18,... | collective-permute-start | bytes 1572872 | tf_op jit(solution)/shard_map/ppermute | solution.py:275
  6.0 13.9 %collective-permute-start.4 = (bf16[1040,128]{1,0:T(8,128)(2,1)S(1)}, bf16[1040,128]{1,0:T(8,128)(2,1)S(1)}, u32[]{:S(2)}, u32[]{:S(2)}) collective-permute-start(bf16[1040,128]{1,0:T(8,128)(2,1)S(1)} %get-tuple-element.47), channel_id=1, source_target_pairs={{0,6},{4,10},{8,14},{12,18},{16,22},{20,26},{24,30},{6,0},{10,4},{... | collective-permute-start | bytes 798728 | tf_op jit(solution)/shard_map/ppermute | solution.py:281
  10.6 9.3 %collective-permute-start.5 = (bf16[1024,128]{1,0:T(8,128)(2,1)S(1)}, bf16[1024,128]{1,0:T(8,128)(2,1)S(1)}, u32[]{:S(2)}, u32[]{:S(2)}) collective-permute-start(bf16[1024,128]{1,0:T(8,128)(2,1)S(1)} %get-tuple-element.40.rest_0_), channel_id=1, source_target_pairs={{0,10},{4,14},{8,18},{12,22},{16,26},{20,30},{10,0},{14,4},{18,8},... | collective-permute-start | bytes 786440 | tf_op jit(solution)/shard_map/ppermute | solution.py:281
  18.2 7.1 %collective-permute-start.2 = (f32[8,128,128]{2,1,0:T(8,128)S(1)}, f32[8,128,128]{2,1,0:T(8,128)S(1)}, u32[]{:S(2)}, u32[]{:S(2)}) collective-permute-start(f32[8,128,128]{2,1,0:T(8,128)S(1)} %get-tuple-element.45), channel_id=1, source_target_pairs={{0,2},{2,0},{4,6},{6,4},{8,10},{10,8},{12,14},{14,12},{16,18},{18,... | collective-permute-start | bytes 1572872 | tf_op jit(solution)/shard_map/ppermute | solution.py:275
  20.6 1.7 %collective-permute-start.6 = (f32[4,128,128]{2,1,0:T(8,128)S(1)}, f32[4,128,128]{2,1,0:T(8,128)S(1)}, u32[]{:S(2)}, u32[]{:S(2)}) collective-permute-start(f32[4,128,128]{2,1,0:T(8,128)S(1)} %get-tuple-element.50), channel_id=1, source_target_pairs={{0,2},{2,0},{4,6},{6,4},{8,10},{10,8},{12,14},{14,12},{16,18},{18,... | collective-permute-start | bytes 786440 | tf_op jit(solution)/shard_map/ppermute | solution.py:275
  21.2 12.3 %collective-permute-start.1 = (f32[8,128,128]{2,1,0:T(8,128)S(1)}, f32[8,128,128]{2,1,0:T(8,128)S(1)}, u32[]{:S(2)}, u32[]{:S(2)}) collective-permute-start(f32[8,128,128]{2,1,0:T(8,128)S(1)} %get-tuple-element.44.kept), channel_id=1, source_target_pairs={{0,2},{2,0},{4,6},{6,4},{8,10},{10,8},{12,14},{14,12},{16,18},{18,... | collective-permute-start | bytes 1572872 | tf_op jit(solution)/shard_map/ppermute | solution.py:275
  23.7 12.9 %collective-permute-start.9 = (bf16[3,128,512]{2,1,0:T(8,128)(2,1)S(1)}, bf16[3,128,512]{2,1,0:T(8,128)(2,1)S(1)}, u32[]{:S(2)}, u32[]{:S(2)}) collective-permute-start(bf16[3,128,512]{2,1,0:T(8,128)(2,1)S(1)} %get-tuple-element.54), channel_id=1, source_target_pairs={{0,1},{1,0},{2,3},{3,2},{4,5},{5,4},{6,7},{7,6},{8,9},{9,8},{10,11... | collective-permute-start | bytes 1179656 | tf_op jit(solution)/shard_map/ppermute | solution.py:287
  25.2 6.4 %collective-permute-start.12 = (f32[4,128,128]{2,1,0:T(8,128)S(1)}, f32[4,128,128]{2,1,0:T(8,128)S(1)}, u32[]{:S(2)}, u32[]{:S(2)}) collective-permute-start(f32[4,128,128]{2,1,0:T(8,128)S(1)} %get-tuple-element.61), channel_id=1, source_target_pairs={{0,2},{2,0},{4,6},{6,4},{8,10},{10,8},{12,14},{14,12},{16,18},{18,... | collective-permute-start | bytes 786440 | tf_op jit(solution)/shard_map/ppermute | solution.py:275
  26.0 10.6 %collective-permute-start.7 = (bf16[1040,128]{1,0:T(8,128)(2,1)S(1)}, bf16[1040,128]{1,0:T(8,128)(2,1)S(1)}, u32[]{:S(2)}, u32[]{:S(2)}) collective-permute-start(bf16[1040,128]{1,0:T(8,128)(2,1)S(1)} %get-tuple-element.52), channel_id=1, source_target_pairs={{0,6},{4,10},{8,14},{12,18},{16,22},{20,26},{24,30},{6,0},{10,4},{... | collective-permute-start | bytes 798728 | tf_op jit(solution)/shard_map/ppermute | solution.py:281
  28.5 8.1 %collective-permute-start.8 = (bf16[1024,128]{1,0:T(8,128)(2,1)S(1)}, bf16[1024,128]{1,0:T(8,128)(2,1)S(1)}, u32[]{:S(2)}, u32[]{:S(2)}) collective-permute-start(bf16[1024,128]{1,0:T(8,128)(2,1)S(1)} %get-tuple-element.53), channel_id=1, source_target_pairs={{0,10},{4,14},{8,18},{12,22},{16,26},{20,30},{10,0},{14,4},{18,8},... | collective-permute-start | bytes 786440 | tf_op jit(solution)/shard_map/ppermute | solution.py:281
  32.9 10.6 %collective-permute-start.13 = (bf16[3,128,512]{2,1,0:T(8,128)(2,1)S(1)}, bf16[3,128,512]{2,1,0:T(8,128)(2,1)S(1)}, u32[]{:S(2)}, u32[]{:S(2)}) collective-permute-start(bf16[3,128,512]{2,1,0:T(8,128)(2,1)S(1)} %get-tuple-element.64), channel_id=1, source_target_pairs={{0,1},{1,0},{2,3},{3,2},{4,5},{5,4},{6,7},{7,6},{8,9},{9,8},{10,11... | collective-permute-start | bytes 1179656 | tf_op jit(solution)/shard_map/ppermute | solution.py:287
  37.3 1.6 %collective-permute-start.11 = (f32[4,128,128]{2,1,0:T(8,128)S(1)}, f32[4,128,128]{2,1,0:T(8,128)S(1)}, u32[]{:S(2)}, u32[]{:S(2)}) collective-permute-start(f32[4,128,128]{2,1,0:T(8,128)S(1)} %get-tuple-element.58), channel_id=1, source_target_pairs={{0,2},{2,0},{4,6},{6,4},{8,10},{10,8},{12,14},{14,12},{16,18},{18,... | collective-permute-start | bytes 786440 | tf_op jit(solution)/shard_map/ppermute | solution.py:275
  37.4 6.1 %collective-permute-start.10 = (f32[4,128,128]{2,1,0:T(8,128)S(1)}, f32[4,128,128]{2,1,0:T(8,128)S(1)}, u32[]{:S(2)}, u32[]{:S(2)}) collective-permute-start(f32[4,128,128]{2,1,0:T(8,128)S(1)} %get-tuple-element.56), channel_id=1, source_target_pairs={{0,2},{2,0},{4,6},{6,4},{8,10},{10,8},{12,14},{14,12},{16,18},{18,... | collective-permute-start | bytes 786440 | tf_op jit(solution)/shard_map/ppermute | solution.py:275
  41.1 12.0 %collective-permute-start.15 = (bf16[3,128,512]{2,1,0:T(8,128)(2,1)S(1)}, bf16[3,128,512]{2,1,0:T(8,128)(2,1)S(1)}, u32[]{:S(2)}, u32[]{:S(2)}) collective-permute-start(bf16[3,128,512]{2,1,0:T(8,128)(2,1)S(1)} %get-tuple-element.67), channel_id=1, source_target_pairs={{0,1},{1,0},{2,3},{3,2},{4,5},{5,4},{6,7},{7,6},{8,9},{9,8},{10,11... | collective-permute-start | bytes 1179656 | tf_op jit(solution)/shard_map/ppermute | solution.py:287
  45.7 15.0 %collective-permute-start.14 = (bf16[3,128,512]{2,1,0:T(8,128)(2,1)S(1)}, bf16[3,128,512]{2,1,0:T(8,128)(2,1)S(1)}, u32[]{:S(2)}, u32[]{:S(2)}) collective-permute-start(bf16[3,128,512]{2,1,0:T(8,128)(2,1)S(1)} %get-tuple-element.66), channel_id=1, source_target_pairs={{0,1},{1,0},{2,3},{3,2},{4,5},{5,4},{6,7},{7,6},{8,9},{9,8},{10,11... | collective-permute-start | bytes 1179656 | tf_op jit(solution)/shard_map/ppermute | solution.py:287

commit v3 on v2

--- a/solution.py
+++ b/solution.py
@@ -16,7 +16,7 @@
 VMEM_LIMIT = 16 * 1024 * 1024
 GRAD_LIMIT = 32 * 1024 * 1024
 FIRST_LIMIT = 53 * 1024 * 1024
-SECOND_LIMIT = 40 * 1024 * 1024
+KEPT_LIMIT = 53 * 1024 * 1024
 NT = (((1,), (1,)), ((), ()))
 TN = (((0,), (0,)), ((), ()))
 NN = (((1,), (0,)), ((), ()))
@@ -43,46 +43,72 @@
     return begin0, end0, begin1, end1, first, begin1 - base
 
 
-def state_kernel(lengths, q, k, v, g, *rest, ndocs, rows, offset, heads, group, kinds):
-    outs, held, sems, known, got = rest[-4 - len(kinds):-4], rest[-4], rest[-3], rest[-2], rest[-1]
+def make_masks(lengths, lower, upper, ndocs, rows):
+    line = lax.broadcasted_iota(jnp.int32, (rows, rows), 0)
+    across = lax.broadcasted_iota(jnp.int32, (rows, rows), 1)
+    begin_line = jnp.zeros((rows, rows), jnp.int32)
+    begin_across = jnp.zeros((rows, rows), jnp.int32)
+    start = jnp.int32(0) - lax.axis_index("seq") * rows
+    for i in range(ndocs):
+        begin_line = jnp.where(line >= start, start, begin_line)
+        begin_across = jnp.where(across >= start, start, begin_across)
+        start = start + lengths[i]
+    lower[...] = jnp.where((across <= line) & (across >= begin_line), 1.0, 0.0).astype(lower.dtype)
+    upper[...] = jnp.where((line <= across) & (line >= begin_across), 1.0, 0.0).astype(upper.dtype)
+
+
+def state_kernel(lengths, q, k, v, g, out, *rest, ndocs, rows, offset, heads, group, kept):
+    *masks, held, sems, known, got = rest
     gw = group * HEAD_DIM
     place = lax.axis_index("seq")
     first_core = lax.rem(place, 2) == 0
 
-    def copy(n, c, i, ref):
+    tails = first_core if kept else jnp.logical_not(first_core)
+
+    def copy(c, i, ref):
         src = ref.at[:, pl.ds(offset + c * gw, gw)]
-        return pltpu.make_async_copy(src, held.at[n, i, :, pl.ds(c * gw, gw)], sems.at[n, c, i])
+        return pltpu.make_async_copy(src, held.at[i, :, pl.ds(c * gw, gw)], sems.at[c, i])
 
     fetch = pltpu.make_async_copy(lengths, known, got)
     fetch.start()
-    for n, kind in enumerate(kinds):
-        tails = first_core if kind == "kept" else jnp.logical_not(first_core)
-        for c in range(heads // group):
-
-            @pl.when(tails)
-            def _():
-                copy(n, c, 0, k).start()
-                copy(n, c, 1, v).start()
-
-            @pl.when(jnp.logical_not(tails))
-            def _():
-                copy(n, c, 0, q).start()
-                copy(n, c, 1, g).start()
+    for c in range(heads // group):
+
+        @pl.when(tails)
+        def _():
+            copy(c, 0, k).start()
+            copy(c, 1, v).start()
+
+        @pl.when(jnp.logical_not(tails))
+        def _():
+            copy(c, 0, q).start()
+            copy(c, 1, g).start()
 
     fetch.wait()
+    if masks:
+        make_masks(known, *masks, ndocs, rows)
     _, _, _, _, first, last = block_range(known, ndocs, place * rows, rows)
     order = lax.broadcasted_iota(jnp.int32, (rows, HEAD_DIM), 0)
     zero = jnp.zeros((), held.dtype)
-    for n, (kind, out) in enumerate(zip(kinds, outs)):
-        tails = first_core if kind == "kept" else jnp.logical_not(first_core)
-        low, high = jnp.where(tails, last, 0), jnp.where(tails, rows, first)
-        here = (order >= low) & (order < high)
-        for h in range(heads):
-            if h % group == 0:
-                copy(n, h // group, 0, k).wait()
-                copy(n, h // group, 1, v).wait()
-            cols = slice(h * HEAD_DIM, (h + 1) * HEAD_DIM)
-            out[h] = dot(jnp.where(here, held[n, 0, :, cols], zero), held[n, 1, :, cols], TN)
+    low, high = jnp.where(tails, last, 0), jnp.where(tails, rows, first)
+    here = (order >= low) & (order < high)
+    for h in range(heads):
+        if h % group == 0:
+            copy(h // group, 0, k).wait()
+            copy(h // group, 1, v).wait()
+        cols = slice(h * HEAD_DIM, (h + 1) * HEAD_DIM)
+        out[h] = dot(jnp.where(here, held[0, :, cols], zero), held[1, :, cols], TN)
+
+
+def late_state_kernel(lengths, q, k, v, g, *rest, ndocs, rows, offset, heads):
+    kept, sent = rest[-2:]
+    first_core, first_rows, last_rows = own_range(lengths, ndocs, rows)
+    zero = jnp.zeros((), q.dtype)
+    for h in range(heads):
+        at = slice(offset + h * HEAD_DIM, offset + (h + 1) * HEAD_DIM)
+        tail = dot(jnp.where(last_rows, k[:, at], zero), v[:, at], TN)
+        head = dot(jnp.where(first_rows, q[:, at], zero), g[:, at], TN)
+        kept[h] = jnp.where(first_core, tail, head)
+        sent[h] = jnp.where(first_core, head, tail)
 
 
 def pair_kernel(lengths, kept, got, *rest, ndocs, rows, hops):
@@ -136,21 +162,6 @@
     return jnp.concatenate([high, (a - high.astype(jnp.float32)).astype(jnp.bfloat16)], axis=axis)
 
 
-def mask_kernel(lengths, *rest, ndocs, rows):
-    lower, upper = rest[-2:]
-    line = lax.broadcasted_iota(jnp.int32, (rows, rows), 0)
-    across = lax.broadcasted_iota(jnp.int32, (rows, rows), 1)
-    begin_line = jnp.zeros((rows, rows), jnp.int32)
-    begin_across = jnp.zeros((rows, rows), jnp.int32)
-    start = jnp.int32(0) - lax.axis_index("seq") * rows
-    for i in range(ndocs):
-        begin_line = jnp.where(line >= start, start, begin_line)
-        begin_across = jnp.where(across >= start, start, begin_across)
-        start = start + lengths[i]
-    lower[...] = jnp.where((across <= line) & (across >= begin_line), 1.0, 0.0)
-    upper[...] = jnp.where((line <= across) & (line >= begin_across), 1.0, 0.0)
-
-
 def own_range(lengths, ndocs, rows):
     place = lax.axis_index("seq")
     _, _, _, _, first, last = block_range(lengths, ndocs, place * rows, rows)
@@ -160,9 +171,9 @@
 
 def local_part(q, k, v, g, lower, upper, at):
     qh, kh, vh, gh = (ref[:, at] for ref in (q, k, v, g))
-    weight_gv = (dot(gh, vh, NT) * lower[...]).astype(jnp.bfloat16)
-    weight_vg = (dot(vh, gh, NT) * upper[...]).astype(jnp.bfloat16)
-    weight_kq = (dot(kh, qh, NT) * upper[...]).astype(jnp.bfloat16)
+    weight_gv = dot(gh, vh, NT).astype(jnp.bfloat16) * lower[...]
+    weight_vg = dot(vh, gh, NT).astype(jnp.bfloat16) * upper[...]
+    weight_kq = dot(kh, qh, NT).astype(jnp.bfloat16) * upper[...]
     return dot(weight_gv, kh, NN), dot(weight_vg, qh, NN), dot(weight_kq, gh, NN)
 
 
@@ -289,19 +300,26 @@
 
     square = (HEAD_DIM, HEAD_DIM)
 
-    def states(kinds, offset, half, after):
+    def states(kept, offset, half):
         heads = half // HEAD_DIM
         group = GROUP if heads % GROUP == 0 else 2
+        outs = [shape_of(heads, *square)] + [shape_of(rows, rows, dtype=bf16)] * (2 * kept)
         return pl.pallas_call(
-            functools.partial(state_kernel, offset=offset, heads=heads, group=group, kinds=kinds, **sizes),
-            in_specs=[anywhere] * (5 + len(after)), out_specs=[in_vmem] * len(kinds),
-            out_shape=[shape_of(heads, *square)] * len(kinds),
+            functools.partial(state_kernel, offset=offset, heads=heads, group=group, kept=kept, **sizes),
+            in_specs=[anywhere] * 5, out_specs=[in_vmem] * len(outs), out_shape=outs,
             scratch_shapes=[
-                pltpu.VMEM((len(kinds), 2, rows, half), bf16), pltpu.SemaphoreType.DMA((len(kinds), heads // group, 2)),
+                pltpu.VMEM((2, rows, half), bf16), pltpu.SemaphoreType.DMA((heads // group, 2)),
                 pltpu.SMEM((ndocs,), jnp.int32), pltpu.SemaphoreType.DMA,
             ],
-            cost_estimate=cheap, compiler_params=pltpu.CompilerParams(vmem_limit_bytes=SECOND_LIMIT if after else FIRST_LIMIT), name="states",
-        )(doc_lengths, *inputs, *after)
+            cost_estimate=cheap, compiler_params=pltpu.CompilerParams(vmem_limit_bytes=KEPT_LIMIT if kept else FIRST_LIMIT), name="states",
+        )(doc_lengths, *inputs)
+
+    def late_states(offset, half, after):
+        heads = half // HEAD_DIM
+        return call(
+            "states", functools.partial(late_state_kernel, offset=offset, heads=heads, **sizes), inputs,
+            [shape_of(heads, *square)] * 2, after=after, limit=GRAD_LIMIT,
+        )
 
     def pair_up(kept, got, after):
         lines = kept.shape[0] * HEAD_DIM
@@ -340,13 +358,12 @@
     cuts, outs, arrived, totals, masks = [], [], [], [], None
     for start, half, chunks in halves:
         if not totals:
-            (sent,) = states(("sent",), start, half, [])
-            (kept,) = states(("kept",), start, half, [])
+            (sent,) = states(False, start, half)
+            kept, *masks = states(True, start, half)
         else:
-            kept, sent = states(("kept", "sent"), start, half, [token])
+            kept, sent = late_states(start, half, [token])
         total, came = pair_up(kept, swap_cores(sent), [made[0] for made in outs[:1]])
         if not totals:
-            masks = call("masks", functools.partial(mask_kernel, **sizes), (), [shape_of(rows, rows)] * 2, after=[total])
             near = [local(masks, *chunk) for chunk in chunks]
             token = near[0][1]
         joined = join(kept, came, chunks, [parts[1] for parts in arrived[:1]] or [made[1] for made in near])

time: 62 us -> 61 us (0.984)
  Pallas kernels: 22.5 us -> 21.1 us
  waiting for transfers between devices: 17.2 us -> 17.9 us
    pallas_call x3 -> x2, Pallas kernels: 5.25 us -> 3.44 us  [states(): pl.pallas_call(functools.partial(state_kernel, offset=offset, heads=heads...]
  transfers between devices with their start and end apart: 16 -> 16, of which waited for: 6 -> 7; matrix products, arithmetic and copies ran while one was open for 0% -> 0% of each run, Pallas kernels for 32% -> 31%
where the time goes in v3:
time: 61 us; the launch traced here: 60.7 us
  Pallas kernels  21.1 us (35%)
  starting transfers between devices  20.1 us (33%)
  waiting for transfers between devices  17.9 us (29%)
  between operations  0.85 us (1%)
  local copies, waits for them, and re-layouts  0.67 us (1%)
    pallas_call x11, Pallas kernels, call(): pl.pallas_call(kernel, in_specs=[in_smem] + [in_vmem] * len(args) + [anyw...  14 us
    ppermute x4, starting transfers between devices, swap_pairs(): lax.ppermute(sent[hop - 1], 'seq', perm + [(b, a) for a, b in perm])  13.7 us
    ppermute x4, waiting for transfers between devices, send_rows(): lax.ppermute(outs[j], 'head', [(x, (x + j) % groups) for x in range(group...  12.3 us
    ppermute x4, starting transfers between devices, send_rows(): lax.ppermute(outs[j], 'head', [(x, (x + j) % groups) for x in range(group...  4.56 us
    pallas_call x4, Pallas kernels, shards(): pl.pallas_call(functools.partial(place_kernel, groups=groups, offset=offs...  3.7 us
    ppermute x4, waiting for transfers between devices, swap_pairs(): lax.ppermute(sent[hop - 1], 'seq', perm + [(b, a) for a, b in perm])  3.58 us
    pallas_call x2, Pallas kernels, states(): pl.pallas_call(functools.partial(state_kernel, offset=offset, heads=heads...  3.44 us
    ppermute x8, waiting for transfers between devices, swap_cores(): return lax.ppermute(a, 'seq', [(b, b ^ 1) for b in range(seq)])  2.07 us
  transfers between devices with their start and end apart: 16, of which 7 were waited for; matrix products, arithmetic and copies ran while one was open for 0% of the time, Pallas kernels for 31%

profile of v3, /device:TPU:0, one launch (start us, length us, event | category | flops | bytes accessed | tf_op | source)
XLA Modules:
  0.0 60.7 jit_solution(16988614718141048938)
XLA Ops:
  0.6 0.0 copy-start.4
  0.6 0.6 %copy-done.4 = s32[8]{0:T(128)S(1)} copy-done((s32[8]{0:T(128)S(1)}, s32[8]{0:T(128)}, u32[]{:S(2)}) %copy-start.4) | copy-done | bytes 56
  1.3 1.6 %states.5 = f32[8,128,128]{2,1,0:T(8,128)S(1)} custom-call(s32[8]{0:T(128)S(1)} %copy-done.4, bf16[256,2048]{1,0:T(8,128)(2,1)} %q.13, bf16[256,2048]{1,0:T(8,128)(2,1)} %k.17, bf16[256,2048]{1,0:T(8,128)(2,1)} %v.17, bf16[256,2048]{1,0:T(8,128)(2,1)} %g.17), custom_call_target="tpu_custom_call" | custom-call | bytes 1024 | tf_op jit(solution)/shard_map/states/pallas_call | solution.py:307
  2.9 0.5 collective-permute-start.3
  3.5 0.0 copy-start.1
  3.5 0.0 copy-start.2
  3.5 0.0 copy-start.3
  3.5 1.8 %states.3 = (f32[8,128,128]{2,1,0:T(8,128)S(1)}, bf16[256,256]{1,0:T(8,128)(2,1)S(1)}, bf16[256,256]{1,0:T(8,128)(2,1)S(1)}) custom-call(s32[8]{0:T(128)S(1)} %copy-done.4, bf16[256,2048]{1,0:T(8,128)(2,1)} %q.13, bf16[256,2048]{1,0:T(8,128)(2,1)} %k.17, bf16[256,2048]{1,0:T(8,128)(2,1)} %v.17, bf16[256,2048]{1,0:T(8,128)(2,1)} %g.17), custom_call_target="tpu_custom_call" | custom-call | bytes 1024 | tf_op jit(solution)/shard_map/states/pallas_call | solution.py:307
  5.3 0.0 copy-start
  5.3 0.1 collective-permute-start.2
  5.4 0.0 collective-permute-done.3.got
  5.4 0.6 %pair.2 = (bf16[1040,128]{1,0:T(8,128)(2,1)S(1)}, bf16[1024,128]{1,0:T(8,128)(2,1)S(1)}) custom-call(s32[8]{0:T(128)S(1)} %copy-done.4, f32[8,128,128]{2,1,0:T(8,128)S(1)} %get-tuple-element.47.kept, f32[8,128,128]{2,1,0:T(8,128)S(1)} %collective-permute-done.3.got), custom_call_target="tpu_custom_call" | custom-call | bytes 1024 | tf_op jit(solution)/shard_map/pair/pallas_call | solution.py:279
  6.0 4.5 %collective-permute-start.4 = (bf16[1040,128]{1,0:T(8,128)(2,1)S(1)}, bf16[1040,128]{1,0:T(8,128)(2,1)S(1)}, u32[]{:S(2)}, u32[]{:S(2)}) collective-permute-start(bf16[1040,128]{1,0:T(8,128)(2,1)S(1)} %get-tuple-element.48), channel_id=1, source_target_pairs={{0,6},{4,10},{8,14},{12,18},{16,22},{20,26},{24,30},{6,0},{10,4},{... | collective-permute-start | bytes 798728 | tf_op jit(solution)/shard_map/ppermute | solution.py:292
  10.6 3.4 %collective-permute-start.5 = (bf16[1024,128]{1,0:T(8,128)(2,1)S(1)}, bf16[1024,128]{1,0:T(8,128)(2,1)S(1)}, u32[]{:S(2)}, u32[]{:S(2)}) collective-permute-start(bf16[1024,128]{1,0:T(8,128)(2,1)S(1)} %get-tuple-element.49), channel_id=1, source_target_pairs={{0,10},{4,14},{8,18},{12,22},{16,26},{20,30},{10,0},{14,4},{18,8},... | collective-permute-start | bytes 786440 | tf_op jit(solution)/shard_map/ppermute | solution.py:292
  14.0 0.0 copy-done.1
  14.0 0.0 copy-done.2
  14.0 0.0 copy-done.3
  14.0 0.0 copy-done
  14.1 1.6 %local.2 = (f32[3,256,512]{2,1,0:T(8,128)S(1)}, f32[8,128]{1,0:T(8,128)S(1)}) custom-call(s32[8]{0:T(128)S(1)} %copy-done.4, bf16[256,2048]{1,0:T(8,128)(2,1)S(1)} %copy-done.3, bf16[256,2048]{1,0:T(8,128)(2,1)S(1)} %copy-done, bf16[256,2048]{1,0:T(8,128)(2,1)S(1)} %copy-done.1, bf16[256,2048]{1,0:T(8,128)(2,1)S(1)} %copy-done.2, ...), custom_call_target="tpu_custom_call" | custom-call | bytes 1024 | tf_op jit(solution)/shard_map/local/pallas_call | solution.py:279
  15.7 1.2 %states.4 = (f32[8,128,128]{2,1,0:T(8,128)S(1)}, f32[8,128,128]{2,1,0:T(8,128)S(1)}) custom-call(s32[8]{0:T(128)S(1)} %copy-done.4, bf16[256,2048]{1,0:T(8,128)(2,1)S(1)} %copy-done.3, bf16[256,2048]{1,0:T(8,128)(2,1)S(1)} %copy-done, bf16[256,2048]{1,0:T(8,128)(2,1)S(1)} %copy-done.1, bf16[256,2048]{1,0:T(8,128)(2,1)S(1)} %copy-done.2, ...), custom_call_target="tpu_custom_call" | custom-call | bytes 1024 | tf_op jit(solution)/shard_map/states/pallas_call | solution.py:279
  16.8 0.1 collective-permute-start.1
  16.9 1.6 %local.3 = (f32[3,256,512]{2,1,0:T(8,128)S(1)}, f32[8,128]{1,0:T(8,128)S(1)}) custom-call(s32[8]{0:T(128)S(1)} %copy-done.4, bf16[256,2048]{1,0:T(8,128)(2,1)S(1)} %copy-done.3, bf16[256,2048]{1,0:T(8,128)(2,1)S(1)} %copy-done, bf16[256,2048]{1,0:T(8,128)(2,1)S(1)} %copy-done.1, bf16[256,2048]{1,0:T(8,128)(2,1)S(1)} %copy-done.2, ...), custom_call_target="tpu_custom_call" | custom-call | bytes 1024 | tf_op jit(solution)/shard_map/local/pallas_call | solution.py:279
  18.5 0.0 collective-permute-done.2.other
  18.6 0.5 collective-permute-done.5.rest_1_
  19.0 0.0 collective-permute-done.4.rest_0_
  19.0 0.7 %join.2 = (f32[4,128,128]{2,1,0:T(8,128)S(1)}, f32[4,128,128]{2,1,0:T(8,128)S(1)}, f32[4,128,128]{2,1,0:T(8,128)S(1)}, f32[4,128,128]{2,1,0:T(8,128)S(1)}) custom-call(s32[8]{0:T(128)S(1)} %copy-done.4, f32[8,128,128]{2,1,0:T(8,128)S(1)} %collective-permute-done.2.other, bf16[1040,128]{1,0:T(8,128)(2,1)S(1)} %collective-permute-done.4.rest_0_, ...), custom_call_target="tpu_custom_call" | custom-call | bytes 1024 | tf_op jit(solution)/shard_map/join/pallas_call | solution.py:279
  19.8 0.1 collective-permute-start.6
  19.9 0.5 collective-permute-start
  20.3 1.0 %collective-permute-done.6.got = f32[4,128,128]{2,1,0:T(8,128)S(1)} collective-permute-done((f32[4,128,128]{2,1,0:T(8,128)S(1)}, f32[4,128,128]{2,1,0:T(8,128)S(1)}, u32[]{:S(2)}, u32[]{:S(2)}) %collective-permute-start.6) | collective-permute-done | bytes 262176 | tf_op jit(solution)/shard_map/ppermute | solution.py:286
  21.4 1.3 %carry.2 = (bf16[3,128,512]{2,1,0:T(8,128)(2,1)S(1)}, bf16[3,128,512]{2,1,0:T(8,128)(2,1)S(1)}) custom-call(s32[8]{0:T(128)S(1)} %copy-done.4, bf16[256,2048]{1,0:T(8,128)(2,1)S(1)} %copy-done, bf16[256,2048]{1,0:T(8,128)(2,1)S(1)} %copy-done.1, bf16[256,2048]{1,0:T(8,128)(2,1)S(1)} %copy-done.2, f32[3,256,512]{2,1,0:T(8,128)S(1)} %get-tuple-element.46.near, ...), custom_call_target="tpu_custom_call" | custom-call | bytes 1024 | tf_op jit(solution)/shard_map/carry/pallas_call | solution.py:279
  22.7 1.6 %collective-permute-start.9 = (bf16[3,128,512]{2,1,0:T(8,128)(2,1)S(1)}, bf16[3,128,512]{2,1,0:T(8,128)(2,1)S(1)}, u32[]{:S(2)}, u32[]{:S(2)}) collective-permute-start(bf16[3,128,512]{2,1,0:T(8,128)(2,1)S(1)} %get-tuple-element.56), channel_id=1, source_target_pairs={{0,1},{1,0},{2,3},{3,2},{4,5},{5,4},{6,7},{7,6},{8,9},{9,8},{10,11... | collective-permute-start | bytes 1179656 | tf_op jit(solution)/shard_map/ppermute | solution.py:298
  24.2 0.0 collective-permute-start.12
  24.2 0.0 collective-permute-done.1.got
  24.2 0.6 %pair.3 = (bf16[1040,128]{1,0:T(8,128)(2,1)S(1)}, bf16[1024,128]{1,0:T(8,128)(2,1)S(1)}) custom-call(s32[8]{0:T(128)S(1)} %copy-done.4, f32[8,128,128]{2,1,0:T(8,128)S(1)} %get-tuple-element.44.kept, f32[8,128,128]{2,1,0:T(8,128)S(1)} %collective-permute-done.1.got, bf16[3,128,512]{2,1,0:T(8,128)(2,1)S(1)} %get-tuple-element.53.rest_0_.refs_0_), custom_call_target="tpu_custom_call" | custom-call | bytes 1024 | tf_op jit(solution)/shard_map/pair/pallas_call | solution.py:279
  24.9 2.8 %collective-permute-start.7 = (bf16[1040,128]{1,0:T(8,128)(2,1)S(1)}, bf16[1040,128]{1,0:T(8,128)(2,1)S(1)}, u32[]{:S(2)}, u32[]{:S(2)}) collective-permute-start(bf16[1040,128]{1,0:T(8,128)(2,1)S(1)} %get-tuple-element.54), channel_id=1, source_target_pairs={{0,6},{4,10},{8,14},{12,18},{16,22},{20,26},{24,30},{6,0},{10,4},{... | collective-permute-start | bytes 798728 | tf_op jit(solution)/shard_map/ppermute | solution.py:292
  27.6 3.0 %collective-permute-start.8 = (bf16[1024,128]{1,0:T(8,128)(2,1)S(1)}, bf16[1024,128]{1,0:T(8,128)(2,1)S(1)}, u32[]{:S(2)}, u32[]{:S(2)}) collective-permute-start(bf16[1024,128]{1,0:T(8,128)(2,1)S(1)} %get-tuple-element.55), channel_id=1, source_target_pairs={{0,10},{4,14},{8,18},{12,22},{16,26},{20,30},{10,0},{14,4},{18,8},... | collective-permute-start | bytes 786440 | tf_op jit(solution)/shard_map/ppermute | solution.py:292
  30.6 0.0 collective-permute-done.12.got
  30.6 1.3 %carry.3 = (bf16[3,128,512]{2,1,0:T(8,128)(2,1)S(1)}, bf16[3,128,512]{2,1,0:T(8,128)(2,1)S(1)}) custom-call(s32[8]{0:T(128)S(1)} %copy-done.4, bf16[256,2048]{1,0:T(8,128)(2,1)S(1)} %copy-done, bf16[256,2048]{1,0:T(8,128)(2,1)S(1)} %copy-done.1, bf16[256,2048]{1,0:T(8,128)(2,1)S(1)} %copy-done.2, f32[3,256,512]{2,1,0:T(8,128)S(1)} %get-tuple-element.61.near, ...), custom_call_target="tpu_custom_call" | custom-call | bytes 1024 | tf_op jit(solution)/shard_map/carry/pallas_call | solution.py:279
  31.9 0.6 collective-permute-start.13
  32.5 0.0 collective-permute-done.other
  32.5 3.1 %collective-permute-done.8.rest_1_ = bf16[1024,128]{1,0:T(8,128)(2,1)S(1)} collective-permute-done((bf16[1024,128]{1,0:T(8,128)(2,1)S(1)}, bf16[1024,128]{1,0:T(8,128)(2,1)S(1)}, u32[]{:S(2)}, u32[]{:S(2)}) %collective-permute-start.8) | collective-permute-done | bytes 262176 | tf_op jit(solution)/shard_map/ppermute | solution.py:292
  35.6 0.0 collective-permute-done.7.rest_0_
  35.6 0.0 collective-permute-done.9.rest_2_.refs_1_
  35.7 0.7 %join.3 = (f32[4,128,128]{2,1,0:T(8,128)S(1)}, f32[4,128,128]{2,1,0:T(8,128)S(1)}, f32[4,128,128]{2,1,0:T(8,128)S(1)}, f32[4,128,128]{2,1,0:T(8,128)S(1)}) custom-call(s32[8]{0:T(128)S(1)} %copy-done.4, f32[8,128,128]{2,1,0:T(8,128)S(1)} %collective-permute-done.other, bf16[1040,128]{1,0:T(8,128)(2,1)S(1)} %collective-permute-done.7.rest_0_, ...), custom_call_target="tpu_custom_call" | custom-call | bytes 1024 | tf_op jit(solution)/shard_map/join/pallas_call | solution.py:279
  36.4 0.1 collective-permute-start.11
  36.5 0.5 collective-permute-start.10
  37.0 1.0 %collective-permute-done.11.got = f32[4,128,128]{2,1,0:T(8,128)S(1)} collective-permute-done((f32[4,128,128]{2,1,0:T(8,128)S(1)}, f32[4,128,128]{2,1,0:T(8,128)S(1)}, u32[]{:S(2)}, u32[]{:S(2)}) %collective-permute-start.11) | collective-permute-done | bytes 262176 | tf_op jit(solution)/shard_map/ppermute | solution.py:286
  38.0 2.2 %grads.2 = (bf16[3,128,512]{2,1,0:T(8,128)(2,1)S(1)}, bf16[3,128,512]{2,1,0:T(8,128)(2,1)S(1)}) custom-call(s32[8]{0:T(128)S(1)} %copy-done.4, bf16[256,2048]{1,0:T(8,128)(2,1)S(1)} %copy-done.3, bf16[256,2048]{1,0:T(8,128)(2,1)S(1)} %copy-done, bf16[256,2048]{1,0:T(8,128)(2,1)S(1)} %copy-done.1, bf16[256,2048]{1,0:T(8,128)(2,1)S(1)} %copy-done.2, ...), custom_call_target="tpu_custom_call" | custom-call | bytes 1024 | tf_op jit(solution)/shard_map/grads/pallas_call | solution.py:279
  40.1 0.6 collective-permute-start.15
  40.7 1.6 %collective-permute-done.13.rest_1_.refs_1_ = bf16[3,128,512]{2,1,0:T(8,128)(2,1)S(1)} collective-permute-done((bf16[3,128,512]{2,1,0:T(8,128)(2,1)S(1)}, bf16[3,128,512]{2,1,0:T(8,128)(2,1)S(1)}, u32[]{:S(2)}, u32[]{:S(2)}) %collective-permute-start.13) | collective-permute-done | bytes 393248 | tf_op jit(solution)/shard_map/ppermute | solution.py:298
  42.3 0.0 collective-permute-done.10.got
  42.3 2.2 %grads.3 = (bf16[3,128,512]{2,1,0:T(8,128)(2,1)S(1)}, bf16[3,128,512]{2,1,0:T(8,128)(2,1)S(1)}) custom-call(s32[8]{0:T(128)S(1)} %copy-done.4, bf16[256,2048]{1,0:T(8,128)(2,1)S(1)} %copy-done.3, bf16[256,2048]{1,0:T(8,128)(2,1)S(1)} %copy-done, bf16[256,2048]{1,0:T(8,128)(2,1)S(1)} %copy-done.1, bf16[256,2048]{1,0:T(8,128)(2,1)S(1)} %copy-done.2, ...), custom_call_target="tpu_custom_call" | custom-call | bytes 1024 | tf_op jit(solution)/shard_map/grads/pallas_call | solution.py:279
  44.5 1.8 %collective-permute-start.14 = (bf16[3,128,512]{2,1,0:T(8,128)(2,1)S(1)}, bf16[3,128,512]{2,1,0:T(8,128)(2,1)S(1)}, u32[]{:S(2)}, u32[]{:S(2)}) collective-permute-start(bf16[3,128,512]{2,1,0:T(8,128)(2,1)S(1)} %get-tuple-element.68), channel_id=1, source_target_pairs={{0,1},{1,0},{2,3},{3,2},{4,5},{5,4},{6,7},{7,6},{8,9},{9,8},{10,11... | collective-permute-start | bytes 1179656 | tf_op jit(solution)/shard_map/ppermute | solution.py:298
  46.3 0.9 %place.4 = (bf16[128,4096]{1,0:T(8,128)(2,1)}, bf16[128,4096]{1,0:T(8,128)(2,1)}, bf16[128,4096]{1,0:T(8,128)(2,1)}) custom-call(bf16[3,128,512]{2,1,0:T(8,128)(2,1)S(1)} %get-tuple-element.53.rest_0_.refs_0_, bf16[3,128,512]{2,1,0:T(8,128)(2,1)S(1)} %collective-permute-done.9.rest_2_.refs_1_), custom_call_target="tpu_custom_call" | custom-call | bytes 1024 | tf_op jit(solution)/shard_map/place/pallas_call | solution.py:382
  47.2 0.9 %place.5 = (bf16[128,4096]{1,0:T(8,128)(2,1)}, bf16[128,4096]{1,0:T(8,128)(2,1)}, bf16[128,4096]{1,0:T(8,128)(2,1)}) custom-call(bf16[3,128,512]{2,1,0:T(8,128)(2,1)S(1)} %get-tuple-element.64.rest_0_.refs_0_, bf16[3,128,512]{2,1,0:T(8,128)(2,1)S(1)} %collective-permute-done.13.rest_1_.refs_1_, ...), custom_call_target="tpu_custom_call", output_to_operand_aliasing={{0}: (2, {}), {1}: (3, {}), {2}: (4, {})} | custom-call | bytes 1024 | tf_op jit(solution)/shard_map/place/pallas_call | solution.py:382
  48.2 4.0 %collective-permute-done.15.refs_1_ = bf16[3,128,512]{2,1,0:T(8,128)(2,1)S(1)} collective-permute-done((bf16[3,128,512]{2,1,0:T(8,128)(2,1)S(1)}, bf16[3,128,512]{2,1,0:T(8,128)(2,1)S(1)}, u32[]{:S(2)}, u32[]{:S(2)}) %collective-permute-start.15) | collective-permute-done | bytes 393248 | tf_op jit(solution)/shard_map/ppermute | solution.py:298
  52.2 0.9 %place.6 = (bf16[128,4096]{1,0:T(8,128)(2,1)}, bf16[128,4096]{1,0:T(8,128)(2,1)}, bf16[128,4096]{1,0:T(8,128)(2,1)}) custom-call(bf16[3,128,512]{2,1,0:T(8,128)(2,1)S(1)} %get-tuple-element.65.rest_0_.refs_0_, bf16[3,128,512]{2,1,0:T(8,128)(2,1)S(1)} %collective-permute-done.15.refs_1_, ...), custom_call_target="tpu_custom_call", output_to_operand_aliasing={{0}: (2, {}), {1}: (3, {}), {2}: (4, {})} | custom-call | bytes 1024 | tf_op jit(solution)/shard_map/place/pallas_call | solution.py:382
  53.1 6.7 %collective-permute-done.14.refs_1_ = bf16[3,128,512]{2,1,0:T(8,128)(2,1)S(1)} collective-permute-done((bf16[3,128,512]{2,1,0:T(8,128)(2,1)S(1)}, bf16[3,128,512]{2,1,0:T(8,128)(2,1)S(1)}, u32[]{:S(2)}, u32[]{:S(2)}) %collective-permute-start.14) | collective-permute-done | bytes 393248 | tf_op jit(solution)/shard_map/ppermute | solution.py:298
  59.8 0.9 %place.7 = (bf16[128,4096]{1,0:T(8,128)(2,1)}, bf16[128,4096]{1,0:T(8,128)(2,1)}, bf16[128,4096]{1,0:T(8,128)(2,1)}) custom-call(bf16[3,128,512]{2,1,0:T(8,128)(2,1)S(1)} %get-tuple-element.67.refs_0_, bf16[3,128,512]{2,1,0:T(8,128)(2,1)S(1)} %collective-permute-done.14.refs_1_, ...), custom_call_target="tpu_custom_call", output_to_operand_aliasing={{0}: (2, {}), {1}: (3, {}), {2}: (4, {})} | custom-call | bytes 1024 | tf_op jit(solution)/shard_map/place/pallas_call | solution.py:382
Async XLA Ops:
  0.6 0.7 %copy-start.4 = (s32[8]{0:T(128)S(1)}, s32[8]{0:T(128)}, u32[]{:S(2)}) copy-start(s32[8]{0:T(128)} %lengths.25) | copy-start | bytes 100
  2.9 2.5 %collective-permute-start.3 = (f32[8,128,128]{2,1,0:T(8,128)S(1)}, f32[8,128,128]{2,1,0:T(8,128)S(1)}, u32[]{:S(2)}, u32[]{:S(2)}) collective-permute-start(f32[8,128,128]{2,1,0:T(8,128)S(1)} %states.5), channel_id=1, source_target_pairs={{0,2},{2,0},{4,6},{6,4},{8,10},{10,8},{12,14},{14,12},{16,18},{18,... | collective-permute-start | bytes 1572872 | tf_op jit(solution)/shard_map/ppermute | solution.py:286
  3.5 10.6 %copy-start.1 = (bf16[256,2048]{1,0:T(8,128)(2,1)S(1)}, bf16[256,2048]{1,0:T(8,128)(2,1)}, u32[]{:S(2)}) copy-start(bf16[256,2048]{1,0:T(8,128)(2,1)} %v.17) | copy-start | bytes 3145732
  3.5 10.6 %copy-start.2 = (bf16[256,2048]{1,0:T(8,128)(2,1)S(1)}, bf16[256,2048]{1,0:T(8,128)(2,1)}, u32[]{:S(2)}) copy-start(bf16[256,2048]{1,0:T(8,128)(2,1)} %g.17) | copy-start | bytes 3145732
  3.5 10.6 %copy-start.3 = (bf16[256,2048]{1,0:T(8,128)(2,1)S(1)}, bf16[256,2048]{1,0:T(8,128)(2,1)}, u32[]{:S(2)}) copy-start(bf16[256,2048]{1,0:T(8,128)(2,1)} %q.13) | copy-start | bytes 3145732
  5.3 8.8 %copy-start = (bf16[256,2048]{1,0:T(8,128)(2,1)S(1)}, bf16[256,2048]{1,0:T(8,128)(2,1)}, u32[]{:S(2)}) copy-start(bf16[256,2048]{1,0:T(8,128)(2,1)} %k.17) | copy-start | bytes 3145732
  5.3 13.3 %collective-permute-start.2 = (f32[8,128,128]{2,1,0:T(8,128)S(1)}, f32[8,128,128]{2,1,0:T(8,128)S(1)}, u32[]{:S(2)}, u32[]{:S(2)}) collective-permute-start(f32[8,128,128]{2,1,0:T(8,128)S(1)} %get-tuple-element.47.kept), channel_id=1, source_target_pairs={{0,2},{2,0},{4,6},{6,4},{8,10},{10,8},{12,14},{14,12},{16,18},{18,... | collective-permute-start | bytes 1572872 | tf_op jit(solution)/shard_map/ppermute | solution.py:286
  6.0 13.0 %collective-permute-start.4 = (bf16[1040,128]{1,0:T(8,128)(2,1)S(1)}, bf16[1040,128]{1,0:T(8,128)(2,1)S(1)}, u32[]{:S(2)}, u32[]{:S(2)}) collective-permute-start(bf16[1040,128]{1,0:T(8,128)(2,1)S(1)} %get-tuple-element.48), channel_id=1, source_target_pairs={{0,6},{4,10},{8,14},{12,18},{16,22},{20,26},{24,30},{6,0},{10,4},{... | collective-permute-start | bytes 798728 | tf_op jit(solution)/shard_map/ppermute | solution.py:292
  10.6 8.4 %collective-permute-start.5 = (bf16[1024,128]{1,0:T(8,128)(2,1)S(1)}, bf16[1024,128]{1,0:T(8,128)(2,1)S(1)}, u32[]{:S(2)}, u32[]{:S(2)}) collective-permute-start(bf16[1024,128]{1,0:T(8,128)(2,1)S(1)} %get-tuple-element.49), channel_id=1, source_target_pairs={{0,10},{4,14},{8,18},{12,22},{16,26},{20,30},{10,0},{14,4},{18,8},... | collective-permute-start | bytes 786440 | tf_op jit(solution)/shard_map/ppermute | solution.py:292
  16.8 7.4 %collective-permute-start.1 = (f32[8,128,128]{2,1,0:T(8,128)S(1)}, f32[8,128,128]{2,1,0:T(8,128)S(1)}, u32[]{:S(2)}, u32[]{:S(2)}) collective-permute-start(f32[8,128,128]{2,1,0:T(8,128)S(1)} %get-tuple-element.45), channel_id=1, source_target_pairs={{0,2},{2,0},{4,6},{6,4},{8,10},{10,8},{12,14},{14,12},{16,18},{18,... | collective-permute-start | bytes 1572872 | tf_op jit(solution)/shard_map/ppermute | solution.py:286
  19.8 1.6 %collective-permute-start.6 = (f32[4,128,128]{2,1,0:T(8,128)S(1)}, f32[4,128,128]{2,1,0:T(8,128)S(1)}, u32[]{:S(2)}, u32[]{:S(2)}) collective-permute-start(f32[4,128,128]{2,1,0:T(8,128)S(1)} %get-tuple-element.52), channel_id=1, source_target_pairs={{0,2},{2,0},{4,6},{6,4},{8,10},{10,8},{12,14},{14,12},{16,18},{18,... | collective-permute-start | bytes 786440 | tf_op jit(solution)/shard_map/ppermute | solution.py:286
  19.9 12.7 %collective-permute-start = (f32[8,128,128]{2,1,0:T(8,128)S(1)}, f32[8,128,128]{2,1,0:T(8,128)S(1)}, u32[]{:S(2)}, u32[]{:S(2)}) collective-permute-start(f32[8,128,128]{2,1,0:T(8,128)S(1)} %get-tuple-element.44.kept), channel_id=1, source_target_pairs={{0,2},{2,0},{4,6},{6,4},{8,10},{10,8},{12,14},{14,12},{16,18},{18,... | collective-permute-start | bytes 1572872 | tf_op jit(solution)/shard_map/ppermute | solution.py:286
  22.7 13.0 %collective-permute-start.9 = (bf16[3,128,512]{2,1,0:T(8,128)(2,1)S(1)}, bf16[3,128,512]{2,1,0:T(8,128)(2,1)S(1)}, u32[]{:S(2)}, u32[]{:S(2)}) collective-permute-start(bf16[3,128,512]{2,1,0:T(8,128)(2,1)S(1)} %get-tuple-element.56), channel_id=1, source_target_pairs={{0,1},{1,0},{2,3},{3,2},{4,5},{5,4},{6,7},{7,6},{8,9},{9,8},{10,11... | collective-permute-start | bytes 1179656 | tf_op jit(solution)/shard_map/ppermute | solution.py:298
  24.2 6.4 %collective-permute-start.12 = (f32[4,128,128]{2,1,0:T(8,128)S(1)}, f32[4,128,128]{2,1,0:T(8,128)S(1)}, u32[]{:S(2)}, u32[]{:S(2)}) collective-permute-start(f32[4,128,128]{2,1,0:T(8,128)S(1)} %get-tuple-element.63), channel_id=1, source_target_pairs={{0,2},{2,0},{4,6},{6,4},{8,10},{10,8},{12,14},{14,12},{16,18},{18,... | collective-permute-start | bytes 786440 | tf_op jit(solution)/shard_map/ppermute | solution.py:286
  24.9 10.8 %collective-permute-start.7 = (bf16[1040,128]{1,0:T(8,128)(2,1)S(1)}, bf16[1040,128]{1,0:T(8,128)(2,1)S(1)}, u32[]{:S(2)}, u32[]{:S(2)}) collective-permute-start(bf16[1040,128]{1,0:T(8,128)(2,1)S(1)} %get-tuple-element.54), channel_id=1, source_target_pairs={{0,6},{4,10},{8,14},{12,18},{16,22},{20,26},{24,30},{6,0},{10,4},{... | collective-permute-start | bytes 798728 | tf_op jit(solution)/shard_map/ppermute | solution.py:292
  27.6 8.0 %collective-permute-start.8 = (bf16[1024,128]{1,0:T(8,128)(2,1)S(1)}, bf16[1024,128]{1,0:T(8,128)(2,1)S(1)}, u32[]{:S(2)}, u32[]{:S(2)}) collective-permute-start(bf16[1024,128]{1,0:T(8,128)(2,1)S(1)} %get-tuple-element.55), channel_id=1, source_target_pairs={{0,10},{4,14},{8,18},{12,22},{16,26},{20,30},{10,0},{14,4},{18,8},... | collective-permute-start | bytes 786440 | tf_op jit(solution)/shard_map/ppermute | solution.py:292
  31.9 10.4 %collective-permute-start.13 = (bf16[3,128,512]{2,1,0:T(8,128)(2,1)S(1)}, bf16[3,128,512]{2,1,0:T(8,128)(2,1)S(1)}, u32[]{:S(2)}, u32[]{:S(2)}) collective-permute-start(bf16[3,128,512]{2,1,0:T(8,128)(2,1)S(1)} %get-tuple-element.66), channel_id=1, source_target_pairs={{0,1},{1,0},{2,3},{3,2},{4,5},{5,4},{6,7},{7,6},{8,9},{9,8},{10,11... | collective-permute-start | bytes 1179656 | tf_op jit(solution)/shard_map/ppermute | solution.py:298
  36.4 1.6 %collective-permute-start.11 = (f32[4,128,128]{2,1,0:T(8,128)S(1)}, f32[4,128,128]{2,1,0:T(8,128)S(1)}, u32[]{:S(2)}, u32[]{:S(2)}) collective-permute-start(f32[4,128,128]{2,1,0:T(8,128)S(1)} %get-tuple-element.60), channel_id=1, source_target_pairs={{0,2},{2,0},{4,6},{6,4},{8,10},{10,8},{12,14},{14,12},{16,18},{18,... | collective-permute-start | bytes 786440 | tf_op jit(solution)/shard_map/ppermute | solution.py:286
  36.5 5.9 %collective-permute-start.10 = (f32[4,128,128]{2,1,0:T(8,128)S(1)}, f32[4,128,128]{2,1,0:T(8,128)S(1)}, u32[]{:S(2)}, u32[]{:S(2)}) collective-permute-start(f32[4,128,128]{2,1,0:T(8,128)S(1)} %get-tuple-element.58), channel_id=1, source_target_pairs={{0,2},{2,0},{4,6},{6,4},{8,10},{10,8},{12,14},{14,12},{16,18},{18,... | collective-permute-start | bytes 786440 | tf_op jit(solution)/shard_map/ppermute | solution.py:286
  40.1 12.0 %collective-permute-start.15 = (bf16[3,128,512]{2,1,0:T(8,128)(2,1)S(1)}, bf16[3,128,512]{2,1,0:T(8,128)(2,1)S(1)}, u32[]{:S(2)}, u32[]{:S(2)}) collective-permute-start(bf16[3,128,512]{2,1,0:T(8,128)(2,1)S(1)} %get-tuple-element.69), channel_id=1, source_target_pairs={{0,1},{1,0},{2,3},{3,2},{4,5},{5,4},{6,7},{7,6},{8,9},{9,8},{10,11... | collective-permute-start | bytes 1179656 | tf_op jit(solution)/shard_map/ppermute | solution.py:298
  44.5 15.3 %collective-permute-start.14 = (bf16[3,128,512]{2,1,0:T(8,128)(2,1)S(1)}, bf16[3,128,512]{2,1,0:T(8,128)(2,1)S(1)}, u32[]{:S(2)}, u32[]{:S(2)}) collective-permute-start(bf16[3,128,512]{2,1,0:T(8,128)(2,1)S(1)} %get-tuple-element.68), channel_id=1, source_target_pairs={{0,1},{1,0},{2,3},{3,2},{4,5},{5,4},{6,7},{7,6},{8,9},{9,8},{10,11... | collective-permute-start | bytes 1179656 | tf_op jit(solution)/shard_map/ppermute | solution.py:298

commit v4 on v3

--- a/solution.py
+++ b/solution.py
@@ -111,8 +111,8 @@
         sent[h] = jnp.where(first_core, head, tail)
 
 
-def pair_kernel(lengths, kept, got, *rest, ndocs, rows, hops):
-    sent = rest[-hops:]
+def pair_kernel(lengths, kept, got, *rest, ndocs, rows, hops, copies):
+    sent, again = rest[-hops - copies:len(rest) - copies], rest[len(rest) - copies:]
     place = lax.axis_index("seq")
     first_core = lax.rem(place, 2) == 0
     even = (place - lax.rem(place, 2)) * rows
@@ -126,10 +126,14 @@
         out[:size] = total
         if out.shape[0] > size:
             out[size:] = jnp.zeros((out.shape[0] - size, HEAD_DIM), LINK)
-
-
-def join_kernel(lengths, other, *rest, ndocs, rows, counts, hops):
-    came, mine, theirs = rest[:hops], rest[-2 * len(counts):-len(counts)], rest[-len(counts):]
+    for i, out in enumerate(again):
+        count = out.shape[0]
+        out[...] = kept[i * count:(i + 1) * count]
+
+
+def join_kernel(lengths, *rest, ndocs, rows, spans, hops):
+    others, came = rest[:len(spans)], rest[len(spans):len(spans) + hops]
+    mine, theirs = rest[-2 * len(spans):-len(spans)], rest[-len(spans):]
     place = lax.axis_index("seq")
     first_core = lax.rem(place, 2) == 0
     even = (place - lax.rem(place, 2)) * rows
@@ -146,15 +150,14 @@
         one(odd + rows + hop * 2 * rows < odd_e1, even - hop * 2 * rows > even_b0) for hop in range(hops)
     ]
     from_other, from_pair = one(odd < even_e1, odd > odd_b0), one(odd + rows < even_e1, even > odd_b0)
-    for c, count in enumerate(counts):
-        at = slice(sum(counts[:c]), sum(counts[:c + 1]))
-        lines = slice(at.start * HEAD_DIM, at.stop * HEAD_DIM)
+    for c, (other_at, came_at, count) in enumerate(spans):
+        lines = slice(came_at * HEAD_DIM, (came_at + count) * HEAD_DIM)
         total = weights[0] * came[0][lines].astype(jnp.float32)
         for hop in range(1, hops):
             total = total + weights[hop] * came[hop][lines].astype(jnp.float32)
         total = total.reshape(count, HEAD_DIM, HEAD_DIM)
         theirs[c][...] = total
-        mine[c][...] = from_other * other[at] + from_pair * total
+        mine[c][...] = from_other * others[c][other_at:other_at + count] + from_pair * total
 
 
 def split(a, axis):
@@ -236,14 +239,14 @@
     deal(done, outs, rows, groups)
 
 
-def place_kernel(*refs, groups, offset, cw, width):
-    parts, outs, sems = refs[:groups], refs[-4:-1], refs[-1]
+def place_kernel(*refs, groups, plan, width):
+    parts, outs, sems = refs[:len(plan)], refs[-4:-1], refs[-1]
     column = lax.axis_index("head")
     copies = []
-    for j in range(groups):
+    for ref, (j, offset, cw) in zip(parts, plan):
         start = pl.multiple_of(lax.rem(column + groups - j, groups) * width + offset, 128)
         for i in range(3):
-            copies.append(pltpu.make_async_copy(parts[j].at[i], outs[i].at[:, pl.ds(start, cw)], sems.at[len(copies)]))
+            copies.append(pltpu.make_async_copy(ref.at[i], outs[i].at[:, pl.ds(start, cw)], sems.at[len(copies)]))
             copies[-1].start()
     for copy in copies:
         copy.wait()
@@ -321,19 +324,21 @@
             [shape_of(heads, *square)] * 2, after=after, limit=GRAD_LIMIT,
         )
 
-    def pair_up(kept, got, after):
+    def pair_up(kept, got, copies, after):
         lines = kept.shape[0] * HEAD_DIM
-        outs = [shape_of(lines + PAD * (hops - hop), HEAD_DIM, dtype=LINK) for hop in range(1, hops + 1)]
-        totals = call("pair", functools.partial(pair_kernel, hops=hops, **sizes), (kept, got), outs, after=after)
-        return totals[-1], swap_pairs(totals)
-
-    def join(kept, came, chunks, after):
-        counts = [cw // HEAD_DIM for _, cw in chunks]
-        joined = call(
-            "join", functools.partial(join_kernel, counts=counts, hops=hops, **sizes), (swap_cores(kept), *came),
-            [shape_of(n, *square) for n in counts] * 2, after=after,
-        )
-        return [(mine, swap_cores(theirs)) for mine, theirs in zip(joined[:len(chunks)], joined[len(chunks):])]
+        outs = [shape_of(lines + PAD * (hops - hop + 1), HEAD_DIM, dtype=LINK) for hop in range(1, hops + 1)]
+        outs += [shape_of(kept.shape[0] // max(copies, 1), *square)] * copies
+        made = call(
+            "pair", functools.partial(pair_kernel, hops=hops, copies=copies, **sizes), (kept, got), outs, after=after
+        )
+        return made[hops - 1], swap_pairs(made[:hops]), [swap_cores(a) for a in made[hops:]]
+
+    def join(spans, others, came, after):
+        made = call(
+            "join", functools.partial(join_kernel, spans=spans, hops=hops, **sizes), (*others, *came),
+            [shape_of(count, *square) for _, _, count in spans] * 2, after=after,
+        )
+        return [(mine, swap_cores(theirs)) for mine, theirs in zip(made[:len(spans)], made[len(spans):])]
 
     def grads(masks, offset, cw, mine, theirs, after):
         return call(
@@ -362,11 +367,21 @@
             kept, *masks = states(True, start, half)
         else:
             kept, sent = late_states(start, half, [token])
-        total, came = pair_up(kept, swap_cores(sent), [made[0] for made in outs[:1]])
+        total, came, others = pair_up(
+            kept, swap_cores(sent), 0 if totals else len(chunks), [made[0] for made in outs[:1]]
+        )
         if not totals:
             near = [local(masks, *chunk) for chunk in chunks]
             token = near[0][1]
-        joined = join(kept, came, chunks, [parts[1] for parts in arrived[:1]] or [made[1] for made in near])
+        count = chunks[0][1] // HEAD_DIM
+        if totals:
+            spans = [(c * count, c * count, count) for c in range(len(chunks))]
+            joined = join(spans, [swap_cores(kept)] * len(chunks), came, [arrived[0][1]])
+        else:
+            joined, after = [], [made[1] for made in near]
+            for c in range(len(chunks)):
+                joined += join([(0, c * count, count)], others[c:c + 1], came, after)
+                after = [joined[-1][0]]
         for c, ((offset, cw), (mine, theirs)) in enumerate(zip(chunks, joined)):
             after = [made[0] for made in outs[-1:]] + [parts[1] for parts in arrived[1:-1]][-1:]
             if totals:
@@ -378,18 +393,22 @@
         cuts += chunks
 
     placed = []
-    for c, (offset, cw) in enumerate(cuts):
+    for c in range(len(cuts)):
+        own = [0, 1] if c == 0 else [c + 1]
+        plan = [(arrived[n][0], (0, *cuts[n])) for n in own if n < len(cuts)]
+        plan += [(arrived[c][j], (j, *cuts[c])) for j in range(1, groups)]
+        some = [array for array, _ in plan]
         placed = pl.pallas_call(
-            functools.partial(place_kernel, groups=groups, offset=offset, cw=cw, width=width),
+            functools.partial(place_kernel, groups=groups, plan=[where for _, where in plan], width=width),
             grid_spec=pl.GridSpec(
-                grid=(1,), in_specs=[anywhere] * (groups + len(placed)), out_specs=[anywhere] * 3,
-                scratch_shapes=[pltpu.SemaphoreType.DMA((3 * groups,))],
+                grid=(1,), in_specs=[anywhere] * (len(some) + len(placed)), out_specs=[anywhere] * 3,
+                scratch_shapes=[pltpu.SemaphoreType.DMA((3 * len(some),))],
             ),
             out_shape=[shape_of(part, width * groups, dtype=bf16)] * 3,
-            input_output_aliases={groups + i: i for i in range(len(placed))},
+            input_output_aliases={len(some) + i: i for i in range(len(placed))},
             cost_estimate=cheap,
             compiler_params=pltpu.CompilerParams(vmem_limit_bytes=VMEM_LIMIT), name="place",
-        )(*arrived[c], *placed)
+        )(*some, *placed)
     return tuple(placed)
 
 

time: 61 us -> 61.5 us (level)
    pallas_call x11 -> x12, Pallas kernels: 14 us -> 14.6 us  [call(): pl.pallas_call(kernel, in_specs=[in_smem] + [in_vmem] * len(args) + [anyw...]
    ppermute x8 -> x9, starting transfers between devices: 1.86 us -> 2.41 us  [swap_cores(): return lax.ppermute(a, 'seq', [(b, b ^ 1) for b in range(seq)])]
    ppermute x8 -> x9, waiting for transfers between devices: 2.07 us -> 1.99 us  [swap_cores(): return lax.ppermute(a, 'seq', [(b, b ^ 1) for b in range(seq)])]
  transfers between devices with their start and end apart: 16 -> 17, of which waited for: 7 -> 6; matrix products, arithmetic and copies ran while one was open for 0% -> 0% of each run, Pallas kernels for 31% -> 30%
where the time goes in v4:
time: 61.5 us; the launch traced here: 61.3 us
  Pallas kernels  21.7 us (35%)
  starting transfers between devices  20.4 us (33%)
  waiting for transfers between devices  17.6 us (29%)
  between operations  0.88 us (1%)
  local copies, waits for them, and re-layouts  0.67 us (1%)
    pallas_call x12, Pallas kernels, call(): pl.pallas_call(kernel, in_specs=[in_smem] + [in_vmem] * len(args) + [anyw...  14.6 us
    ppermute x4, starting transfers between devices, swap_pairs(): lax.ppermute(sent[hop - 1], 'seq', perm + [(b, a) for a, b in perm])  13.7 us
    ppermute x4, waiting for transfers between devices, send_rows(): lax.ppermute(outs[j], 'head', [(x, (x + j) % groups) for x in range(group...  12.4 us
    ppermute x4, starting transfers between devices, send_rows(): lax.ppermute(outs[j], 'head', [(x, (x + j) % groups) for x in range(group...  4.32 us
    pallas_call x4, Pallas kernels, shards(): pl.pallas_call(functools.partial(place_kernel, groups=groups, plan=[where...  3.7 us
    pallas_call x2, Pallas kernels, states(): pl.pallas_call(functools.partial(state_kernel, offset=offset, heads=heads...  3.44 us
    ppermute x4, waiting for transfers between devices, swap_pairs(): lax.ppermute(sent[hop - 1], 'seq', perm + [(b, a) for a, b in perm])  3.21 us
    ppermute x9, starting transfers between devices, swap_cores(): return lax.ppermute(a, 'seq', [(b, b ^ 1) for b in range(seq)])  2.41 us
  transfers between devices with their start and end apart: 17, of which 6 were waited for; matrix products, arithmetic and copies ran while one was open for 0% of the time, Pallas kernels for 30%

profile of v4, /device:TPU:0, one launch (start us, length us, event | category | flops | bytes accessed | tf_op | source)
XLA Modules:
  0.0 61.3 jit_solution(6228478034737375087)
XLA Ops:
  0.6 0.0 copy-start.4
  0.6 0.6 %copy-done.4 = s32[8]{0:T(128)S(1)} copy-done((s32[8]{0:T(128)S(1)}, s32[8]{0:T(128)}, u32[]{:S(2)}) %copy-start.4) | copy-done | bytes 56
  1.3 1.6 %states.5 = f32[8,128,128]{2,1,0:T(8,128)S(1)} custom-call(s32[8]{0:T(128)S(1)} %copy-done.4, bf16[256,2048]{1,0:T(8,128)(2,1)} %q.13, bf16[256,2048]{1,0:T(8,128)(2,1)} %k.17, bf16[256,2048]{1,0:T(8,128)(2,1)} %v.17, bf16[256,2048]{1,0:T(8,128)(2,1)} %g.17), custom_call_target="tpu_custom_call" | custom-call | bytes 1024 | tf_op jit(solution)/shard_map/states/pallas_call | solution.py:310
  2.9 0.5 collective-permute-start.2
  3.5 0.0 copy-start.1
  3.5 0.0 copy-start.2
  3.5 0.0 copy-start.3
  3.5 1.8 %states.3 = (f32[8,128,128]{2,1,0:T(8,128)S(1)}, bf16[256,256]{1,0:T(8,128)(2,1)S(1)}, bf16[256,256]{1,0:T(8,128)(2,1)S(1)}) custom-call(s32[8]{0:T(128)S(1)} %copy-done.4, bf16[256,2048]{1,0:T(8,128)(2,1)} %q.13, bf16[256,2048]{1,0:T(8,128)(2,1)} %k.17, bf16[256,2048]{1,0:T(8,128)(2,1)} %v.17, bf16[256,2048]{1,0:T(8,128)(2,1)} %g.17), custom_call_target="tpu_custom_call" | custom-call | bytes 1024 | tf_op jit(solution)/shard_map/states/pallas_call | solution.py:310
  5.3 0.0 copy-start
  5.3 0.0 collective-permute-done.2.got
  5.3 0.6 %pair.2 = (bf16[1056,128]{1,0:T(8,128)(2,1)S(1)}, bf16[1040,128]{1,0:T(8,128)(2,1)S(1)}, f32[4,128,128]{2,1,0:T(8,128)S(1)}, f32[4,128,128]{2,1,0:T(8,128)S(1)}) custom-call(s32[8]{0:T(128)S(1)} %copy-done.4, f32[8,128,128]{2,1,0:T(8,128)S(1)} %get-tuple-element.49.kept, f32[8,128,128]{2,1,0:T(8,128)S(1)} %collective-permute-done.2.got), custom_call_target="tpu_custom_call" | custom-call | bytes 1024 | tf_op jit(solution)/shard_map/pair/pallas_call | solution.py:282
  5.9 4.5 %collective-permute-start.4 = (bf16[1056,128]{1,0:T(8,128)(2,1)S(1)}, bf16[1056,128]{1,0:T(8,128)(2,1)S(1)}, u32[]{:S(2)}, u32[]{:S(2)}) collective-permute-start(bf16[1056,128]{1,0:T(8,128)(2,1)S(1)} %get-tuple-element.51), channel_id=1, source_target_pairs={{0,6},{4,10},{8,14},{12,18},{16,22},{20,26},{24,30},{6,0},{10,4},{... | collective-permute-start | bytes 811016 | tf_op jit(solution)/shard_map/ppermute | solution.py:295
  10.5 3.0 %collective-permute-start.5 = (bf16[1040,128]{1,0:T(8,128)(2,1)S(1)}, bf16[1040,128]{1,0:T(8,128)(2,1)S(1)}, u32[]{:S(2)}, u32[]{:S(2)}) collective-permute-start(bf16[1040,128]{1,0:T(8,128)(2,1)S(1)} %get-tuple-element.52), channel_id=1, source_target_pairs={{0,10},{4,14},{8,18},{12,22},{16,26},{20,30},{10,0},{14,4},{18,8},... | collective-permute-start | bytes 798728 | tf_op jit(solution)/shard_map/ppermute | solution.py:295
  13.5 0.1 collective-permute-start.3
  13.6 0.0 copy-done.1
  13.6 0.0 copy-done.2
  13.6 0.0 copy-done.3
  13.7 0.0 copy-done
  13.7 1.6 %local.2 = (f32[3,256,512]{2,1,0:T(8,128)S(1)}, f32[8,128]{1,0:T(8,128)S(1)}) custom-call(s32[8]{0:T(128)S(1)} %copy-done.4, bf16[256,2048]{1,0:T(8,128)(2,1)S(1)} %copy-done.3, bf16[256,2048]{1,0:T(8,128)(2,1)S(1)} %copy-done, bf16[256,2048]{1,0:T(8,128)(2,1)S(1)} %copy-done.1, bf16[256,2048]{1,0:T(8,128)(2,1)S(1)} %copy-done.2, ...), custom_call_target="tpu_custom_call" | custom-call | bytes 1024 | tf_op jit(solution)/shard_map/local/pallas_call | solution.py:282
  15.3 1.2 %states.4 = (f32[8,128,128]{2,1,0:T(8,128)S(1)}, f32[8,128,128]{2,1,0:T(8,128)S(1)}) custom-call(s32[8]{0:T(128)S(1)} %copy-done.4, bf16[256,2048]{1,0:T(8,128)(2,1)S(1)} %copy-done.3, bf16[256,2048]{1,0:T(8,128)(2,1)S(1)} %copy-done, bf16[256,2048]{1,0:T(8,128)(2,1)S(1)} %copy-done.1, bf16[256,2048]{1,0:T(8,128)(2,1)S(1)} %copy-done.2, ...), custom_call_target="tpu_custom_call" | custom-call | bytes 1024 | tf_op jit(solution)/shard_map/states/pallas_call | solution.py:282
  16.4 0.5 collective-permute-start.1
  17.0 1.6 %local.3 = (f32[3,256,512]{2,1,0:T(8,128)S(1)}, f32[8,128]{1,0:T(8,128)S(1)}) custom-call(s32[8]{0:T(128)S(1)} %copy-done.4, bf16[256,2048]{1,0:T(8,128)(2,1)S(1)} %copy-done.3, bf16[256,2048]{1,0:T(8,128)(2,1)S(1)} %copy-done, bf16[256,2048]{1,0:T(8,128)(2,1)S(1)} %copy-done.1, bf16[256,2048]{1,0:T(8,128)(2,1)S(1)} %copy-done.2, ...), custom_call_target="tpu_custom_call" | custom-call | bytes 1024 | tf_op jit(solution)/shard_map/local/pallas_call | solution.py:282
  18.6 0.0 collective-permute-done.3.rest_0_
  18.6 0.0 collective-permute-done.5.rest_2_
  18.6 0.0 collective-permute-done.4.rest_1_
  18.6 0.6 %join.3 = (f32[4,128,128]{2,1,0:T(8,128)S(1)}, f32[4,128,128]{2,1,0:T(8,128)S(1)}) custom-call(s32[8]{0:T(128)S(1)} %copy-done.4, f32[4,128,128]{2,1,0:T(8,128)S(1)} %collective-permute-done.3.rest_0_, bf16[1056,128]{1,0:T(8,128)(2,1)S(1)} %collective-permute-done.4.rest_1_, bf16[1040,128]{1,0:T(8,128)(2,1)S(1)} %collective-permute-done.5.rest_2_, ...), custom_call_target="tpu_custom_call" | custom-call | bytes 1024 | tf_op jit(solution)/shard_map/join/pallas_call | solution.py:282
  19.3 0.1 collective-permute-start.6
  19.4 0.5 collective-permute-start.12
  19.9 0.1 collective-permute-start
  20.0 0.9 %collective-permute-done.6.got = f32[4,128,128]{2,1,0:T(8,128)S(1)} collective-permute-done((f32[4,128,128]{2,1,0:T(8,128)S(1)}, f32[4,128,128]{2,1,0:T(8,128)S(1)}, u32[]{:S(2)}, u32[]{:S(2)}) %collective-permute-start.6) | collective-permute-done | bytes 262176 | tf_op jit(solution)/shard_map/ppermute | solution.py:289
  20.9 1.3 %carry.2 = (bf16[3,128,512]{2,1,0:T(8,128)(2,1)S(1)}, bf16[3,128,512]{2,1,0:T(8,128)(2,1)S(1)}) custom-call(s32[8]{0:T(128)S(1)} %copy-done.4, bf16[256,2048]{1,0:T(8,128)(2,1)S(1)} %copy-done, bf16[256,2048]{1,0:T(8,128)(2,1)S(1)} %copy-done.1, bf16[256,2048]{1,0:T(8,128)(2,1)S(1)} %copy-done.2, f32[3,256,512]{2,1,0:T(8,128)S(1)} %get-tuple-element.48.near, ...), custom_call_target="tpu_custom_call" | custom-call | bytes 1024 | tf_op jit(solution)/shard_map/carry/pallas_call | solution.py:282
  22.2 1.6 %collective-permute-start.9 = (bf16[3,128,512]{2,1,0:T(8,128)(2,1)S(1)}, bf16[3,128,512]{2,1,0:T(8,128)(2,1)S(1)}, u32[]{:S(2)}, u32[]{:S(2)}) collective-permute-start(bf16[3,128,512]{2,1,0:T(8,128)(2,1)S(1)} %get-tuple-element.59), channel_id=1, source_target_pairs={{0,1},{1,0},{2,3},{3,2},{4,5},{5,4},{6,7},{7,6},{8,9},{9,8},{10,11... | collective-permute-start | bytes 1179656 | tf_op jit(solution)/shard_map/ppermute | solution.py:301
  23.8 0.0 collective-permute-done.12.rest_0_
  23.8 0.6 %join.5 = (f32[4,128,128]{2,1,0:T(8,128)S(1)}, f32[4,128,128]{2,1,0:T(8,128)S(1)}) custom-call(s32[8]{0:T(128)S(1)} %copy-done.4, f32[4,128,128]{2,1,0:T(8,128)S(1)} %collective-permute-done.12.rest_0_, bf16[1056,128]{1,0:T(8,128)(2,1)S(1)} %collective-permute-done.4.rest_1_, bf16[1040,128]{1,0:T(8,128)(2,1)S(1)} %collective-permute-done.5.rest_2_, ...), custom_call_target="tpu_custom_call" | custom-call | bytes 1024 | tf_op jit(solution)/shard_map/join/pallas_call | solution.py:282
  24.4 0.1 collective-permute-start.13
  24.5 0.0 collective-permute-done.1.got
  24.5 0.6 %pair.3 = (bf16[1056,128]{1,0:T(8,128)(2,1)S(1)}, bf16[1040,128]{1,0:T(8,128)(2,1)S(1)}) custom-call(s32[8]{0:T(128)S(1)} %copy-done.4, f32[8,128,128]{2,1,0:T(8,128)S(1)} %get-tuple-element.46.kept, f32[8,128,128]{2,1,0:T(8,128)S(1)} %collective-permute-done.1.got, bf16[3,128,512]{2,1,0:T(8,128)(2,1)S(1)} %get-tuple-element.56.rest_0_.refs_0_), custom_call_target="tpu_custom_call" | custom-call | bytes 1024 | tf_op jit(solution)/shard_map/pair/pallas_call | solution.py:282
  25.1 3.1 %collective-permute-start.7 = (bf16[1056,128]{1,0:T(8,128)(2,1)S(1)}, bf16[1056,128]{1,0:T(8,128)(2,1)S(1)}, u32[]{:S(2)}, u32[]{:S(2)}) collective-permute-start(bf16[1056,128]{1,0:T(8,128)(2,1)S(1)} %get-tuple-element.57), channel_id=1, source_target_pairs={{0,6},{4,10},{8,14},{12,18},{16,22},{20,26},{24,30},{6,0},{10,4},{... | collective-permute-start | bytes 811016 | tf_op jit(solution)/shard_map/ppermute | solution.py:295
  28.2 3.0 %collective-permute-start.8 = (bf16[1040,128]{1,0:T(8,128)(2,1)S(1)}, bf16[1040,128]{1,0:T(8,128)(2,1)S(1)}, u32[]{:S(2)}, u32[]{:S(2)}) collective-permute-start(bf16[1040,128]{1,0:T(8,128)(2,1)S(1)} %get-tuple-element.58), channel_id=1, source_target_pairs={{0,10},{4,14},{8,18},{12,22},{16,26},{20,30},{10,0},{14,4},{18,8},... | collective-permute-start | bytes 798728 | tf_op jit(solution)/shard_map/ppermute | solution.py:295
  31.3 0.0 collective-permute-done.13.got
  31.3 1.3 %carry.3 = (bf16[3,128,512]{2,1,0:T(8,128)(2,1)S(1)}, bf16[3,128,512]{2,1,0:T(8,128)(2,1)S(1)}) custom-call(s32[8]{0:T(128)S(1)} %copy-done.4, bf16[256,2048]{1,0:T(8,128)(2,1)S(1)} %copy-done, bf16[256,2048]{1,0:T(8,128)(2,1)S(1)} %copy-done.1, bf16[256,2048]{1,0:T(8,128)(2,1)S(1)} %copy-done.2, f32[3,256,512]{2,1,0:T(8,128)S(1)} %get-tuple-element.64.near, ...), custom_call_target="tpu_custom_call" | custom-call | bytes 1024 | tf_op jit(solution)/shard_map/carry/pallas_call | solution.py:282
  32.6 0.6 collective-permute-start.14
  33.2 0.0 collective-permute-done.rest_0_.rest_1_
  33.2 3.2 %collective-permute-done.8.rest_3_ = bf16[1040,128]{1,0:T(8,128)(2,1)S(1)} collective-permute-done((bf16[1040,128]{1,0:T(8,128)(2,1)S(1)}, bf16[1040,128]{1,0:T(8,128)(2,1)S(1)}, u32[]{:S(2)}, u32[]{:S(2)}) %collective-permute-start.8) | collective-permute-done | bytes 266272 | tf_op jit(solution)/shard_map/ppermute | solution.py:295
  36.4 0.0 collective-permute-done.7.rest_2_
  36.4 0.0 collective-permute-done.9.rest_4_.refs_2_
  36.4 0.7 %join.4 = (f32[4,128,128]{2,1,0:T(8,128)S(1)}, f32[4,128,128]{2,1,0:T(8,128)S(1)}, f32[4,128,128]{2,1,0:T(8,128)S(1)}, f32[4,128,128]{2,1,0:T(8,128)S(1)}) custom-call(s32[8]{0:T(128)S(1)} %copy-done.4, f32[8,128,128]{2,1,0:T(8,128)S(1)} %collective-permute-done.rest_0_.rest_1_, f32[8,128,128]{2,1,0:T(8,128)S(1)} %collective-permute-done.rest_0_.rest_1_, ...), custom_call_target="tpu_custom_call" | custom-call | bytes 1024 | tf_op jit(solution)/shard_map/join/pallas_call | solution.py:282
  37.1 0.1 collective-permute-start.11
  37.2 0.5 collective-permute-start.10
  37.7 1.0 %collective-permute-done.11.got = f32[4,128,128]{2,1,0:T(8,128)S(1)} collective-permute-done((f32[4,128,128]{2,1,0:T(8,128)S(1)}, f32[4,128,128]{2,1,0:T(8,128)S(1)}, u32[]{:S(2)}, u32[]{:S(2)}) %collective-permute-start.11) | collective-permute-done | bytes 262176 | tf_op jit(solution)/shard_map/ppermute | solution.py:289
  38.7 2.2 %grads.2 = (bf16[3,128,512]{2,1,0:T(8,128)(2,1)S(1)}, bf16[3,128,512]{2,1,0:T(8,128)(2,1)S(1)}) custom-call(s32[8]{0:T(128)S(1)} %copy-done.4, bf16[256,2048]{1,0:T(8,128)(2,1)S(1)} %copy-done.3, bf16[256,2048]{1,0:T(8,128)(2,1)S(1)} %copy-done, bf16[256,2048]{1,0:T(8,128)(2,1)S(1)} %copy-done.1, bf16[256,2048]{1,0:T(8,128)(2,1)S(1)} %copy-done.2, ...), custom_call_target="tpu_custom_call" | custom-call | bytes 1024 | tf_op jit(solution)/shard_map/grads/pallas_call | solution.py:282
  40.8 0.6 collective-permute-start.16
  41.4 0.4 collective-permute-done.14.rest_1_.refs_1_
  41.8 0.0 collective-permute-done.10.got
  41.9 2.2 %grads.3 = (bf16[3,128,512]{2,1,0:T(8,128)(2,1)S(1)}, bf16[3,128,512]{2,1,0:T(8,128)(2,1)S(1)}) custom-call(s32[8]{0:T(128)S(1)} %copy-done.4, bf16[256,2048]{1,0:T(8,128)(2,1)S(1)} %copy-done.3, bf16[256,2048]{1,0:T(8,128)(2,1)S(1)} %copy-done, bf16[256,2048]{1,0:T(8,128)(2,1)S(1)} %copy-done.1, bf16[256,2048]{1,0:T(8,128)(2,1)S(1)} %copy-done.2, ...), custom_call_target="tpu_custom_call" | custom-call | bytes 1024 | tf_op jit(solution)/shard_map/grads/pallas_call | solution.py:282
  44.0 1.6 %collective-permute-start.15 = (bf16[3,128,512]{2,1,0:T(8,128)(2,1)S(1)}, bf16[3,128,512]{2,1,0:T(8,128)(2,1)S(1)}, u32[]{:S(2)}, u32[]{:S(2)}) collective-permute-start(bf16[3,128,512]{2,1,0:T(8,128)(2,1)S(1)} %get-tuple-element.71), channel_id=1, source_target_pairs={{0,1},{1,0},{2,3},{3,2},{4,5},{5,4},{6,7},{7,6},{8,9},{9,8},{10,11... | collective-permute-start | bytes 1179656 | tf_op jit(solution)/shard_map/ppermute | solution.py:301
  45.6 1.1 %place.4 = (bf16[128,4096]{1,0:T(8,128)(2,1)}, bf16[128,4096]{1,0:T(8,128)(2,1)}, bf16[128,4096]{1,0:T(8,128)(2,1)}) custom-call(bf16[3,128,512]{2,1,0:T(8,128)(2,1)S(1)} %get-tuple-element.56.rest_0_.refs_0_, bf16[3,128,512]{2,1,0:T(8,128)(2,1)S(1)} %get-tuple-element.68.rest_0_.refs_1_, bf16[3,128,512]{2,1,0:T(8,128)(2,1)S(1)} %collective-permute-done.9.rest_4_.refs_2_), custom_call_target="tpu_custom_call" | custom-call | bytes 1024 | tf_op jit(solution)/shard_map/place/pallas_call | solution.py:401
  46.7 0.9 %place.5 = (bf16[128,4096]{1,0:T(8,128)(2,1)}, bf16[128,4096]{1,0:T(8,128)(2,1)}, bf16[128,4096]{1,0:T(8,128)(2,1)}) custom-call(bf16[3,128,512]{2,1,0:T(8,128)(2,1)S(1)} %get-tuple-element.69.rest_0_.refs_0_, bf16[3,128,512]{2,1,0:T(8,128)(2,1)S(1)} %collective-permute-done.14.rest_1_.refs_1_, ...), custom_call_target="tpu_custom_call", output_to_operand_aliasing={{0}: (2, {}), {1}: (3, {}), {2}: (4, {})} | custom-call | bytes 1024 | tf_op jit(solution)/shard_map/place/pallas_call | solution.py:401
  47.6 5.3 %collective-permute-done.16.refs_1_ = bf16[3,128,512]{2,1,0:T(8,128)(2,1)S(1)} collective-permute-done((bf16[3,128,512]{2,1,0:T(8,128)(2,1)S(1)}, bf16[3,128,512]{2,1,0:T(8,128)(2,1)S(1)}, u32[]{:S(2)}, u32[]{:S(2)}) %collective-permute-start.16) | collective-permute-done | bytes 393248 | tf_op jit(solution)/shard_map/ppermute | solution.py:301
  52.9 0.9 %place.6 = (bf16[128,4096]{1,0:T(8,128)(2,1)}, bf16[128,4096]{1,0:T(8,128)(2,1)}, bf16[128,4096]{1,0:T(8,128)(2,1)}) custom-call(bf16[3,128,512]{2,1,0:T(8,128)(2,1)S(1)} %get-tuple-element.72.refs_0_, bf16[3,128,512]{2,1,0:T(8,128)(2,1)S(1)} %collective-permute-done.16.refs_1_, ...), custom_call_target="tpu_custom_call", output_to_operand_aliasing={{0}: (2, {}), {1}: (3, {}), {2}: (4, {})} | custom-call | bytes 1024 | tf_op jit(solution)/shard_map/place/pallas_call | solution.py:401
  53.8 6.7 %collective-permute-done.15.refs_0_ = bf16[3,128,512]{2,1,0:T(8,128)(2,1)S(1)} collective-permute-done((bf16[3,128,512]{2,1,0:T(8,128)(2,1)S(1)}, bf16[3,128,512]{2,1,0:T(8,128)(2,1)S(1)}, u32[]{:S(2)}, u32[]{:S(2)}) %collective-permute-start.15) | collective-permute-done | bytes 393248 | tf_op jit(solution)/shard_map/ppermute | solution.py:301
  60.5 0.8 %place.7 = (bf16[128,4096]{1,0:T(8,128)(2,1)}, bf16[128,4096]{1,0:T(8,128)(2,1)}, bf16[128,4096]{1,0:T(8,128)(2,1)}) custom-call(bf16[3,128,512]{2,1,0:T(8,128)(2,1)S(1)} %collective-permute-done.15.refs_0_, bf16[128,4096]{1,0:T(8,128)(2,1)} %get-tuple-element.80.refs_1_, ...), custom_call_target="tpu_custom_call", output_to_operand_aliasing={{0}: (1, {}), {1}: (2, {}), {2}: (3, {})} | custom-call | bytes 1024 | tf_op jit(solution)/shard_map/place/pallas_call | solution.py:401
Async XLA Ops:
  0.6 0.7 %copy-start.4 = (s32[8]{0:T(128)S(1)}, s32[8]{0:T(128)}, u32[]{:S(2)}) copy-start(s32[8]{0:T(128)} %lengths.27) | copy-start | bytes 100
  2.9 2.3 %collective-permute-start.2 = (f32[8,128,128]{2,1,0:T(8,128)S(1)}, f32[8,128,128]{2,1,0:T(8,128)S(1)}, u32[]{:S(2)}, u32[]{:S(2)}) collective-permute-start(f32[8,128,128]{2,1,0:T(8,128)S(1)} %states.5), channel_id=1, source_target_pairs={{0,2},{2,0},{4,6},{6,4},{8,10},{10,8},{12,14},{14,12},{16,18},{18,... | collective-permute-start | bytes 1572872 | tf_op jit(solution)/shard_map/ppermute | solution.py:289
  3.5 10.2 %copy-start.1 = (bf16[256,2048]{1,0:T(8,128)(2,1)S(1)}, bf16[256,2048]{1,0:T(8,128)(2,1)}, u32[]{:S(2)}) copy-start(bf16[256,2048]{1,0:T(8,128)(2,1)} %v.17) | copy-start | bytes 3145732
  3.5 10.2 %copy-start.2 = (bf16[256,2048]{1,0:T(8,128)(2,1)S(1)}, bf16[256,2048]{1,0:T(8,128)(2,1)}, u32[]{:S(2)}) copy-start(bf16[256,2048]{1,0:T(8,128)(2,1)} %g.17) | copy-start | bytes 3145732
  3.5 10.2 %copy-start.3 = (bf16[256,2048]{1,0:T(8,128)(2,1)S(1)}, bf16[256,2048]{1,0:T(8,128)(2,1)}, u32[]{:S(2)}) copy-start(bf16[256,2048]{1,0:T(8,128)(2,1)} %q.13) | copy-start | bytes 3145732
  5.3 8.4 %copy-start = (bf16[256,2048]{1,0:T(8,128)(2,1)S(1)}, bf16[256,2048]{1,0:T(8,128)(2,1)}, u32[]{:S(2)}) copy-start(bf16[256,2048]{1,0:T(8,128)(2,1)} %k.17) | copy-start | bytes 3145732
  5.9 12.7 %collective-permute-start.4 = (bf16[1056,128]{1,0:T(8,128)(2,1)S(1)}, bf16[1056,128]{1,0:T(8,128)(2,1)S(1)}, u32[]{:S(2)}, u32[]{:S(2)}) collective-permute-start(bf16[1056,128]{1,0:T(8,128)(2,1)S(1)} %get-tuple-element.51), channel_id=1, source_target_pairs={{0,6},{4,10},{8,14},{12,18},{16,22},{20,26},{24,30},{6,0},{10,4},{... | collective-permute-start | bytes 811016 | tf_op jit(solution)/shard_map/ppermute | solution.py:295
  10.5 8.2 %collective-permute-start.5 = (bf16[1040,128]{1,0:T(8,128)(2,1)S(1)}, bf16[1040,128]{1,0:T(8,128)(2,1)S(1)}, u32[]{:S(2)}, u32[]{:S(2)}) collective-permute-start(bf16[1040,128]{1,0:T(8,128)(2,1)S(1)} %get-tuple-element.52), channel_id=1, source_target_pairs={{0,10},{4,14},{8,18},{12,22},{16,26},{20,30},{10,0},{14,4},{18,8},... | collective-permute-start | bytes 798728 | tf_op jit(solution)/shard_map/ppermute | solution.py:295
  13.5 5.1 %collective-permute-start.3 = (f32[4,128,128]{2,1,0:T(8,128)S(1)}, f32[4,128,128]{2,1,0:T(8,128)S(1)}, u32[]{:S(2)}, u32[]{:S(2)}) collective-permute-start(f32[4,128,128]{2,1,0:T(8,128)S(1)} %get-tuple-element.50), channel_id=1, source_target_pairs={{0,2},{2,0},{4,6},{6,4},{8,10},{10,8},{12,14},{14,12},{16,18},{18,... | collective-permute-start | bytes 786440 | tf_op jit(solution)/shard_map/ppermute | solution.py:289
  16.4 8.1 %collective-permute-start.1 = (f32[8,128,128]{2,1,0:T(8,128)S(1)}, f32[8,128,128]{2,1,0:T(8,128)S(1)}, u32[]{:S(2)}, u32[]{:S(2)}) collective-permute-start(f32[8,128,128]{2,1,0:T(8,128)S(1)} %get-tuple-element.47), channel_id=1, source_target_pairs={{0,2},{2,0},{4,6},{6,4},{8,10},{10,8},{12,14},{14,12},{16,18},{18,... | collective-permute-start | bytes 1572872 | tf_op jit(solution)/shard_map/ppermute | solution.py:289
  19.3 1.6 %collective-permute-start.6 = (f32[4,128,128]{2,1,0:T(8,128)S(1)}, f32[4,128,128]{2,1,0:T(8,128)S(1)}, u32[]{:S(2)}, u32[]{:S(2)}) collective-permute-start(f32[4,128,128]{2,1,0:T(8,128)S(1)} %get-tuple-element.55), channel_id=1, source_target_pairs={{0,2},{2,0},{4,6},{6,4},{8,10},{10,8},{12,14},{14,12},{16,18},{18,... | collective-permute-start | bytes 786440 | tf_op jit(solution)/shard_map/ppermute | solution.py:289
  19.4 4.4 %collective-permute-start.12 = (f32[4,128,128]{2,1,0:T(8,128)S(1)}, f32[4,128,128]{2,1,0:T(8,128)S(1)}, u32[]{:S(2)}, u32[]{:S(2)}) collective-permute-start(f32[4,128,128]{2,1,0:T(8,128)S(1)} %get-tuple-element.65), channel_id=1, source_target_pairs={{0,2},{2,0},{4,6},{6,4},{8,10},{10,8},{12,14},{14,12},{16,18},{18,... | collective-permute-start | bytes 786440 | tf_op jit(solution)/shard_map/ppermute | solution.py:289
  19.9 13.3 %collective-permute-start = (f32[8,128,128]{2,1,0:T(8,128)S(1)}, f32[8,128,128]{2,1,0:T(8,128)S(1)}, u32[]{:S(2)}, u32[]{:S(2)}) collective-permute-start(f32[8,128,128]{2,1,0:T(8,128)S(1)} %get-tuple-element.46.kept), channel_id=1, source_target_pairs={{0,2},{2,0},{4,6},{6,4},{8,10},{10,8},{12,14},{14,12},{16,18},{18,... | collective-permute-start | bytes 1572872 | tf_op jit(solution)/shard_map/ppermute | solution.py:289
  22.2 14.2 %collective-permute-start.9 = (bf16[3,128,512]{2,1,0:T(8,128)(2,1)S(1)}, bf16[3,128,512]{2,1,0:T(8,128)(2,1)S(1)}, u32[]{:S(2)}, u32[]{:S(2)}) collective-permute-start(bf16[3,128,512]{2,1,0:T(8,128)(2,1)S(1)} %get-tuple-element.59), channel_id=1, source_target_pairs={{0,1},{1,0},{2,3},{3,2},{4,5},{5,4},{6,7},{7,6},{8,9},{9,8},{10,11... | collective-permute-start | bytes 1179656 | tf_op jit(solution)/shard_map/ppermute | solution.py:301
  24.4 6.8 %collective-permute-start.13 = (f32[4,128,128]{2,1,0:T(8,128)S(1)}, f32[4,128,128]{2,1,0:T(8,128)S(1)}, u32[]{:S(2)}, u32[]{:S(2)}) collective-permute-start(f32[4,128,128]{2,1,0:T(8,128)S(1)} %get-tuple-element.67), channel_id=1, source_target_pairs={{0,2},{2,0},{4,6},{6,4},{8,10},{10,8},{12,14},{14,12},{16,18},{18,... | collective-permute-start | bytes 786440 | tf_op jit(solution)/shard_map/ppermute | solution.py:289
  25.1 11.2 %collective-permute-start.7 = (bf16[1056,128]{1,0:T(8,128)(2,1)S(1)}, bf16[1056,128]{1,0:T(8,128)(2,1)S(1)}, u32[]{:S(2)}, u32[]{:S(2)}) collective-permute-start(bf16[1056,128]{1,0:T(8,128)(2,1)S(1)} %get-tuple-element.57), channel_id=1, source_target_pairs={{0,6},{4,10},{8,14},{12,18},{16,22},{20,26},{24,30},{6,0},{10,4},{... | collective-permute-start | bytes 811016 | tf_op jit(solution)/shard_map/ppermute | solution.py:295
  28.2 8.1 %collective-permute-start.8 = (bf16[1040,128]{1,0:T(8,128)(2,1)S(1)}, bf16[1040,128]{1,0:T(8,128)(2,1)S(1)}, u32[]{:S(2)}, u32[]{:S(2)}) collective-permute-start(bf16[1040,128]{1,0:T(8,128)(2,1)S(1)} %get-tuple-element.58), channel_id=1, source_target_pairs={{0,10},{4,14},{8,18},{12,22},{16,26},{20,30},{10,0},{14,4},{18,8},... | collective-permute-start | bytes 798728 | tf_op jit(solution)/shard_map/ppermute | solution.py:295
  32.6 9.3 %collective-permute-start.14 = (bf16[3,128,512]{2,1,0:T(8,128)(2,1)S(1)}, bf16[3,128,512]{2,1,0:T(8,128)(2,1)S(1)}, u32[]{:S(2)}, u32[]{:S(2)}) collective-permute-start(bf16[3,128,512]{2,1,0:T(8,128)(2,1)S(1)} %get-tuple-element.70), channel_id=1, source_target_pairs={{0,1},{1,0},{2,3},{3,2},{4,5},{5,4},{6,7},{7,6},{8,9},{9,8},{10,11... | collective-permute-start | bytes 1179656 | tf_op jit(solution)/shard_map/ppermute | solution.py:301
  37.1 1.6 %collective-permute-start.11 = (f32[4,128,128]{2,1,0:T(8,128)S(1)}, f32[4,128,128]{2,1,0:T(8,128)S(1)}, u32[]{:S(2)}, u32[]{:S(2)}) collective-permute-start(f32[4,128,128]{2,1,0:T(8,128)S(1)} %get-tuple-element.63), channel_id=1, source_target_pairs={{0,2},{2,0},{4,6},{6,4},{8,10},{10,8},{12,14},{14,12},{16,18},{18,... | collective-permute-start | bytes 786440 | tf_op jit(solution)/shard_map/ppermute | solution.py:289
  37.2 4.7 %collective-permute-start.10 = (f32[4,128,128]{2,1,0:T(8,128)S(1)}, f32[4,128,128]{2,1,0:T(8,128)S(1)}, u32[]{:S(2)}, u32[]{:S(2)}) collective-permute-start(f32[4,128,128]{2,1,0:T(8,128)S(1)} %get-tuple-element.61), channel_id=1, source_target_pairs={{0,2},{2,0},{4,6},{6,4},{8,10},{10,8},{12,14},{14,12},{16,18},{18,... | collective-permute-start | bytes 786440 | tf_op jit(solution)/shard_map/ppermute | solution.py:289
  40.8 12.0 %collective-permute-start.16 = (bf16[3,128,512]{2,1,0:T(8,128)(2,1)S(1)}, bf16[3,128,512]{2,1,0:T(8,128)(2,1)S(1)}, u32[]{:S(2)}, u32[]{:S(2)}) collective-permute-start(bf16[3,128,512]{2,1,0:T(8,128)(2,1)S(1)} %get-tuple-element.73), channel_id=1, source_target_pairs={{0,1},{1,0},{2,3},{3,2},{4,5},{5,4},{6,7},{7,6},{8,9},{9,8},{10,11... | collective-permute-start | bytes 1179656 | tf_op jit(solution)/shard_map/ppermute | solution.py:301
  44.0 16.5 %collective-permute-start.15 = (bf16[3,128,512]{2,1,0:T(8,128)(2,1)S(1)}, bf16[3,128,512]{2,1,0:T(8,128)(2,1)S(1)}, u32[]{:S(2)}, u32[]{:S(2)}) collective-permute-start(bf16[3,128,512]{2,1,0:T(8,128)(2,1)S(1)} %get-tuple-element.71), channel_id=1, source_target_pairs={{0,1},{1,0},{2,3},{3,2},{4,5},{5,4},{6,7},{7,6},{8,9},{9,8},{10,11... | collective-permute-start | bytes 1179656 | tf_op jit(solution)/shard_map/ppermute | solution.py:301

commit v5 on v4

--- a/solution.py
+++ b/solution.py
@@ -15,7 +15,7 @@
 LINK = jnp.bfloat16
 VMEM_LIMIT = 16 * 1024 * 1024
 GRAD_LIMIT = 32 * 1024 * 1024
-FIRST_LIMIT = 53 * 1024 * 1024
+FIRST_LIMIT = 56 * 1024 * 1024
 KEPT_LIMIT = 53 * 1024 * 1024
 NT = (((1,), (1,)), ((), ()))
 TN = (((0,), (0,)), ((), ()))
@@ -58,12 +58,13 @@
 
 
 def state_kernel(lengths, q, k, v, g, out, *rest, ndocs, rows, offset, heads, group, kept):
-    *masks, held, sems, known, got = rest
+    *masks, held, sems, known, got, made, leave = rest
     gw = group * HEAD_DIM
     place = lax.axis_index("seq")
     first_core = lax.rem(place, 2) == 0
 
     tails = first_core if kept else jnp.logical_not(first_core)
+    made = out if kept else made
 
     def copy(c, i, ref):
         src = ref.at[:, pl.ds(offset + c * gw, gw)]
@@ -96,7 +97,13 @@
             copy(h // group, 0, k).wait()
             copy(h // group, 1, v).wait()
         cols = slice(h * HEAD_DIM, (h + 1) * HEAD_DIM)
-        out[h] = dot(jnp.where(here, held[0, :, cols], zero), held[1, :, cols], TN)
+        made[h] = dot(jnp.where(here, held[0, :, cols], zero), held[1, :, cols], TN)
+        if not kept and h % group == group - 1:
+            some = pl.ds(h + 1 - group, group)
+            pltpu.make_async_copy(made.at[some], out.at[some], leave.at[h // group]).start()
+    for c in range(0 if kept else heads // group):
+        some = pl.ds(c * group, group)
+        pltpu.make_async_copy(made.at[some], out.at[some], leave.at[c]).wait()
 
 
 def late_state_kernel(lengths, q, k, v, g, *rest, ndocs, rows, offset, heads):
@@ -309,10 +316,11 @@
         outs = [shape_of(heads, *square)] + [shape_of(rows, rows, dtype=bf16)] * (2 * kept)
         return pl.pallas_call(
             functools.partial(state_kernel, offset=offset, heads=heads, group=group, kept=kept, **sizes),
-            in_specs=[anywhere] * 5, out_specs=[in_vmem] * len(outs), out_shape=outs,
+            in_specs=[anywhere] * 5, out_specs=[in_vmem] * len(outs) if kept else [anywhere], out_shape=outs,
             scratch_shapes=[
                 pltpu.VMEM((2, rows, half), bf16), pltpu.SemaphoreType.DMA((heads // group, 2)),
                 pltpu.SMEM((ndocs,), jnp.int32), pltpu.SemaphoreType.DMA,
+                pltpu.VMEM((heads if not kept else 1, *square), f32), pltpu.SemaphoreType.DMA((heads // group,)),
             ],
             cost_estimate=cheap, compiler_params=pltpu.CompilerParams(vmem_limit_bytes=KEPT_LIMIT if kept else FIRST_LIMIT), name="states",
         )(doc_lengths, *inputs)
@@ -378,10 +386,8 @@
             spans = [(c * count, c * count, count) for c in range(len(chunks))]
             joined = join(spans, [swap_cores(kept)] * len(chunks), came, [arrived[0][1]])
         else:
-            joined, after = [], [made[1] for made in near]
-            for c in range(len(chunks)):
-                joined += join([(0, c * count, count)], others[c:c + 1], came, after)
-                after = [joined[-1][0]]
+            spans = [(0, c * count, count) for c in range(len(chunks))]
+            joined = join(spans, others, came, [made[1] for made in near])
         for c, ((offset, cw), (mine, theirs)) in enumerate(zip(chunks, joined)):
             after = [made[0] for made in outs[-1:]] + [parts[1] for parts in arrived[1:-1]][-1:]
             if totals:

time: 61.5 us -> 61 us (level)
  local copies, waits for them, and re-layouts: 0.67 us -> 0.02 us
    pallas_call x2, Pallas kernels: 3.44 us -> 4.21 us  [states(): pl.pallas_call(functools.partial(state_kernel, offset=offset, heads=heads...]
    unnamed x10, local copies, waits for them, and re-layouts: 0.67 us -> 0.02 us
    pallas_call x12 -> x11, Pallas kernels: 14.6 us -> 14 us  [call(): pl.pallas_call(kernel, in_specs=[in_smem] + [in_vmem] * len(args) + [anyw...]
where the time goes in v5:
time: 61 us; the launch traced here: 60.7 us
  Pallas kernels  21.9 us (36%)
  starting transfers between devices  20.6 us (34%)
  waiting for transfers between devices  17.3 us (28%)
  between operations  0.86 us (1%)
    pallas_call x11, Pallas kernels, call(): pl.pallas_call(kernel, in_specs=[in_smem] + [in_vmem] * len(args) + [anyw...  14 us
    ppermute x4, starting transfers between devices, swap_pairs(): lax.ppermute(sent[hop - 1], 'seq', perm + [(b, a) for a, b in perm])  13.5 us
    ppermute x4, waiting for transfers between devices, send_rows(): lax.ppermute(outs[j], 'head', [(x, (x + j) % groups) for x in range(group...  12 us
    ppermute x4, starting transfers between devices, send_rows(): lax.ppermute(outs[j], 'head', [(x, (x + j) % groups) for x in range(group...  4.73 us
    pallas_call x2, Pallas kernels, states(): pl.pallas_call(functools.partial(state_kernel, offset=offset, heads=heads...  4.21 us
    pallas_call x4, Pallas kernels, shards(): pl.pallas_call(functools.partial(place_kernel, groups=groups, plan=[where...  3.7 us
    ppermute x4, waiting for transfers between devices, swap_pairs(): lax.ppermute(sent[hop - 1], 'seq', perm + [(b, a) for a, b in perm])  3.17 us
    ppermute x9, starting transfers between devices, swap_cores(): return lax.ppermute(a, 'seq', [(b, b ^ 1) for b in range(seq)])  2.45 us
  transfers between devices with their start and end apart: 17, of which 6 were waited for; matrix products, arithmetic and copies ran while one was open for 0% of the time, Pallas kernels for 30%

profile of v5, /device:TPU:0, one launch (start us, length us, event | category | flops | bytes accessed | tf_op | source)
XLA Modules:
  0.0 60.7 jit_solution(11456047543722402175)
XLA Ops:
  0.6 0.0 copy-start.4
  0.6 2.4 %states.5 = f32[8,128,128]{2,1,0:T(8,128)} custom-call(s32[8]{0:T(128)} %lengths.25, bf16[256,2048]{1,0:T(8,128)(2,1)} %q.13, bf16[256,2048]{1,0:T(8,128)(2,1)} %k.17, bf16[256,2048]{1,0:T(8,128)(2,1)} %v.17, bf16[256,2048]{1,0:T(8,128)(2,1)} %g.17), custom_call_target="tpu_custom_call" | custom-call | bytes 1024 | tf_op jit(solution)/shard_map/states/pallas_call | solution.py:317
  3.0 0.5 collective-permute-start.2
  3.5 0.0 copy-done.4
  3.5 0.0 copy-start.1
  3.5 0.0 copy-start.2
  3.5 0.0 copy-start.3
  3.6 1.8 %states.3 = (f32[8,128,128]{2,1,0:T(8,128)S(1)}, bf16[256,256]{1,0:T(8,128)(2,1)S(1)}, bf16[256,256]{1,0:T(8,128)(2,1)S(1)}) custom-call(s32[8]{0:T(128)S(1)} %copy-done.4, bf16[256,2048]{1,0:T(8,128)(2,1)} %q.13, bf16[256,2048]{1,0:T(8,128)(2,1)} %k.17, bf16[256,2048]{1,0:T(8,128)(2,1)} %v.17, bf16[256,2048]{1,0:T(8,128)(2,1)} %g.17), custom_call_target="tpu_custom_call" | custom-call | bytes 1024 | tf_op jit(solution)/shard_map/states/pallas_call | solution.py:317
  5.4 0.0 copy-start
  5.4 0.0 collective-permute-done.2.got
  5.4 0.6 %pair.2 = (bf16[1056,128]{1,0:T(8,128)(2,1)S(1)}, bf16[1040,128]{1,0:T(8,128)(2,1)S(1)}, f32[4,128,128]{2,1,0:T(8,128)S(1)}, f32[4,128,128]{2,1,0:T(8,128)S(1)}) custom-call(s32[8]{0:T(128)S(1)} %copy-done.4, f32[8,128,128]{2,1,0:T(8,128)S(1)} %get-tuple-element.49.kept, f32[8,128,128]{2,1,0:T(8,128)S(1)} %collective-permute-done.2.got), custom_call_target="tpu_custom_call" | custom-call | bytes 1024 | tf_op jit(solution)/shard_map/pair/pallas_call | solution.py:289
  6.1 4.5 %collective-permute-start.5 = (bf16[1056,128]{1,0:T(8,128)(2,1)S(1)}, bf16[1056,128]{1,0:T(8,128)(2,1)S(1)}, u32[]{:S(2)}, u32[]{:S(2)}) collective-permute-start(bf16[1056,128]{1,0:T(8,128)(2,1)S(1)} %get-tuple-element.52), channel_id=1, source_target_pairs={{0,6},{4,10},{8,14},{12,18},{16,22},{20,26},{24,30},{6,0},{10,4},{... | collective-permute-start | bytes 811016 | tf_op jit(solution)/shard_map/ppermute | solution.py:302
  10.6 3.2 %collective-permute-start.6 = (bf16[1040,128]{1,0:T(8,128)(2,1)S(1)}, bf16[1040,128]{1,0:T(8,128)(2,1)S(1)}, u32[]{:S(2)}, u32[]{:S(2)}) collective-permute-start(bf16[1040,128]{1,0:T(8,128)(2,1)S(1)} %get-tuple-element.53), channel_id=1, source_target_pairs={{0,10},{4,14},{8,18},{12,22},{16,26},{20,30},{10,0},{14,4},{18,8},... | collective-permute-start | bytes 798728 | tf_op jit(solution)/shard_map/ppermute | solution.py:302
  13.8 0.1 collective-permute-start.3
  13.9 0.5 collective-permute-start.4
  14.4 0.0 copy-done.1
  14.4 0.0 copy-done.2
  14.4 0.0 copy-done.3
  14.4 0.0 copy-done
  14.4 1.6 %local.2 = (f32[3,256,512]{2,1,0:T(8,128)S(1)}, f32[8,128]{1,0:T(8,128)S(1)}) custom-call(s32[8]{0:T(128)S(1)} %copy-done.4, bf16[256,2048]{1,0:T(8,128)(2,1)S(1)} %copy-done.3, bf16[256,2048]{1,0:T(8,128)(2,1)S(1)} %copy-done, bf16[256,2048]{1,0:T(8,128)(2,1)S(1)} %copy-done.1, bf16[256,2048]{1,0:T(8,128)(2,1)S(1)} %copy-done.2, ...), custom_call_target="tpu_custom_call" | custom-call | bytes 1024 | tf_op jit(solution)/shard_map/local/pallas_call | solution.py:289
  16.1 1.1 %states.4 = (f32[8,128,128]{2,1,0:T(8,128)S(1)}, f32[8,128,128]{2,1,0:T(8,128)S(1)}) custom-call(s32[8]{0:T(128)S(1)} %copy-done.4, bf16[256,2048]{1,0:T(8,128)(2,1)S(1)} %copy-done.3, bf16[256,2048]{1,0:T(8,128)(2,1)S(1)} %copy-done, bf16[256,2048]{1,0:T(8,128)(2,1)S(1)} %copy-done.1, bf16[256,2048]{1,0:T(8,128)(2,1)S(1)} %copy-done.2, ...), custom_call_target="tpu_custom_call" | custom-call | bytes 1024 | tf_op jit(solution)/shard_map/states/pallas_call | solution.py:289
  17.2 0.1 collective-permute-start.1
  17.4 1.6 %local.3 = (f32[3,256,512]{2,1,0:T(8,128)S(1)}, f32[8,128]{1,0:T(8,128)S(1)}) custom-call(s32[8]{0:T(128)S(1)} %copy-done.4, bf16[256,2048]{1,0:T(8,128)(2,1)S(1)} %copy-done.3, bf16[256,2048]{1,0:T(8,128)(2,1)S(1)} %copy-done, bf16[256,2048]{1,0:T(8,128)(2,1)S(1)} %copy-done.1, bf16[256,2048]{1,0:T(8,128)(2,1)S(1)} %copy-done.2, ...), custom_call_target="tpu_custom_call" | custom-call | bytes 1024 | tf_op jit(solution)/shard_map/local/pallas_call | solution.py:289
  19.0 0.0 collective-permute-done.3.rest_0_
  19.0 0.0 collective-permute-done.4.rest_1_
  19.0 0.0 collective-permute-done.6.rest_3_
  19.0 0.0 collective-permute-done.5.rest_2_
  19.0 0.7 %join.2 = (f32[4,128,128]{2,1,0:T(8,128)S(1)}, f32[4,128,128]{2,1,0:T(8,128)S(1)}, f32[4,128,128]{2,1,0:T(8,128)S(1)}, f32[4,128,128]{2,1,0:T(8,128)S(1)}) custom-call(s32[8]{0:T(128)S(1)} %copy-done.4, f32[4,128,128]{2,1,0:T(8,128)S(1)} %collective-permute-done.3.rest_0_, f32[4,128,128]{2,1,0:T(8,128)S(1)} %collective-permute-done.4.rest_1_, ...), custom_call_target="tpu_custom_call" | custom-call | bytes 1024 | tf_op jit(solution)/shard_map/join/pallas_call | solution.py:289
  19.7 0.5 collective-permute-start.7
  20.2 0.1 collective-permute-start
  20.3 1.1 %collective-permute-done.7.got = f32[4,128,128]{2,1,0:T(8,128)S(1)} collective-permute-done((f32[4,128,128]{2,1,0:T(8,128)S(1)}, f32[4,128,128]{2,1,0:T(8,128)S(1)}, u32[]{:S(2)}, u32[]{:S(2)}) %collective-permute-start.7) | collective-permute-done | bytes 262176 | tf_op jit(solution)/shard_map/ppermute | solution.py:296
  21.4 1.3 %carry.2 = (bf16[3,128,512]{2,1,0:T(8,128)(2,1)S(1)}, bf16[3,128,512]{2,1,0:T(8,128)(2,1)S(1)}) custom-call(s32[8]{0:T(128)S(1)} %copy-done.4, bf16[256,2048]{1,0:T(8,128)(2,1)S(1)} %copy-done, bf16[256,2048]{1,0:T(8,128)(2,1)S(1)} %copy-done.1, bf16[256,2048]{1,0:T(8,128)(2,1)S(1)} %copy-done.2, f32[3,256,512]{2,1,0:T(8,128)S(1)} %get-tuple-element.48.near, ...), custom_call_target="tpu_custom_call" | custom-call | bytes 1024 | tf_op jit(solution)/shard_map/carry/pallas_call | solution.py:289
  22.7 1.6 %collective-permute-start.10 = (bf16[3,128,512]{2,1,0:T(8,128)(2,1)S(1)}, bf16[3,128,512]{2,1,0:T(8,128)(2,1)S(1)}, u32[]{:S(2)}, u32[]{:S(2)}) collective-permute-start(bf16[3,128,512]{2,1,0:T(8,128)(2,1)S(1)} %get-tuple-element.60), channel_id=1, source_target_pairs={{0,1},{1,0},{2,3},{3,2},{4,5},{5,4},{6,7},{7,6},{8,9},{9,8},{10,11... | collective-permute-start | bytes 1179656 | tf_op jit(solution)/shard_map/ppermute | solution.py:308
  24.3 0.1 collective-permute-start.13
  24.4 0.0 collective-permute-done.1.got
  24.4 0.6 %pair.3 = (bf16[1056,128]{1,0:T(8,128)(2,1)S(1)}, bf16[1040,128]{1,0:T(8,128)(2,1)S(1)}) custom-call(s32[8]{0:T(128)S(1)} %copy-done.4, f32[8,128,128]{2,1,0:T(8,128)S(1)} %get-tuple-element.46.kept, f32[8,128,128]{2,1,0:T(8,128)S(1)} %collective-permute-done.1.got, bf16[3,128,512]{2,1,0:T(8,128)(2,1)S(1)} %get-tuple-element.57.rest_0_.refs_0_), custom_call_target="tpu_custom_call" | custom-call | bytes 1024 | tf_op jit(solution)/shard_map/pair/pallas_call | solution.py:289
  25.0 2.7 %collective-permute-start.8 = (bf16[1056,128]{1,0:T(8,128)(2,1)S(1)}, bf16[1056,128]{1,0:T(8,128)(2,1)S(1)}, u32[]{:S(2)}, u32[]{:S(2)}) collective-permute-start(bf16[1056,128]{1,0:T(8,128)(2,1)S(1)} %get-tuple-element.58), channel_id=1, source_target_pairs={{0,6},{4,10},{8,14},{12,18},{16,22},{20,26},{24,30},{6,0},{10,4},{... | collective-permute-start | bytes 811016 | tf_op jit(solution)/shard_map/ppermute | solution.py:302
  27.7 3.0 %collective-permute-start.9 = (bf16[1040,128]{1,0:T(8,128)(2,1)S(1)}, bf16[1040,128]{1,0:T(8,128)(2,1)S(1)}, u32[]{:S(2)}, u32[]{:S(2)}) collective-permute-start(bf16[1040,128]{1,0:T(8,128)(2,1)S(1)} %get-tuple-element.59), channel_id=1, source_target_pairs={{0,10},{4,14},{8,18},{12,22},{16,26},{20,30},{10,0},{14,4},{18,8},... | collective-permute-start | bytes 798728 | tf_op jit(solution)/shard_map/ppermute | solution.py:302
  30.7 0.0 collective-permute-done.13.got
  30.7 1.3 %carry.3 = (bf16[3,128,512]{2,1,0:T(8,128)(2,1)S(1)}, bf16[3,128,512]{2,1,0:T(8,128)(2,1)S(1)}) custom-call(s32[8]{0:T(128)S(1)} %copy-done.4, bf16[256,2048]{1,0:T(8,128)(2,1)S(1)} %copy-done, bf16[256,2048]{1,0:T(8,128)(2,1)S(1)} %copy-done.1, bf16[256,2048]{1,0:T(8,128)(2,1)S(1)} %copy-done.2, f32[3,256,512]{2,1,0:T(8,128)S(1)} %get-tuple-element.65.near, ...), custom_call_target="tpu_custom_call" | custom-call | bytes 1024 | tf_op jit(solution)/shard_map/carry/pallas_call | solution.py:289
  32.0 0.6 %collective-permute-start.14 = (bf16[3,128,512]{2,1,0:T(8,128)(2,1)S(1)}, bf16[3,128,512]{2,1,0:T(8,128)(2,1)S(1)}, u32[]{:S(2)}, u32[]{:S(2)}) collective-permute-start(bf16[3,128,512]{2,1,0:T(8,128)(2,1)S(1)} %get-tuple-element.70), channel_id=1, source_target_pairs={{0,1},{1,0},{2,3},{3,2},{4,5},{5,4},{6,7},{7,6},{8,9},{9,8},{10,11... | collective-permute-start | bytes 1179656 | tf_op jit(solution)/shard_map/ppermute | solution.py:308
  32.6 0.0 collective-permute-done.rest_0_.rest_1_
  32.6 3.2 %collective-permute-done.9.rest_3_ = bf16[1040,128]{1,0:T(8,128)(2,1)S(1)} collective-permute-done((bf16[1040,128]{1,0:T(8,128)(2,1)S(1)}, bf16[1040,128]{1,0:T(8,128)(2,1)S(1)}, u32[]{:S(2)}, u32[]{:S(2)}) %collective-permute-start.9) | collective-permute-done | bytes 266272 | tf_op jit(solution)/shard_map/ppermute | solution.py:302
  35.8 0.0 collective-permute-done.8.rest_2_
  35.8 0.0 collective-permute-done.10.rest_4_.refs_2_
  35.8 0.7 %join.3 = (f32[4,128,128]{2,1,0:T(8,128)S(1)}, f32[4,128,128]{2,1,0:T(8,128)S(1)}, f32[4,128,128]{2,1,0:T(8,128)S(1)}, f32[4,128,128]{2,1,0:T(8,128)S(1)}) custom-call(s32[8]{0:T(128)S(1)} %copy-done.4, f32[8,128,128]{2,1,0:T(8,128)S(1)} %collective-permute-done.rest_0_.rest_1_, f32[8,128,128]{2,1,0:T(8,128)S(1)} %collective-permute-done.rest_0_.rest_1_, ...), custom_call_target="tpu_custom_call" | custom-call | bytes 1024 | tf_op jit(solution)/shard_map/join/pallas_call | solution.py:289
  36.5 0.1 collective-permute-start.12
  36.6 0.5 collective-permute-start.11
  37.1 1.0 %collective-permute-done.12.got = f32[4,128,128]{2,1,0:T(8,128)S(1)} collective-permute-done((f32[4,128,128]{2,1,0:T(8,128)S(1)}, f32[4,128,128]{2,1,0:T(8,128)S(1)}, u32[]{:S(2)}, u32[]{:S(2)}) %collective-permute-start.12) | collective-permute-done | bytes 262176 | tf_op jit(solution)/shard_map/ppermute | solution.py:296
  38.1 2.2 %grads.2 = (bf16[3,128,512]{2,1,0:T(8,128)(2,1)S(1)}, bf16[3,128,512]{2,1,0:T(8,128)(2,1)S(1)}) custom-call(s32[8]{0:T(128)S(1)} %copy-done.4, bf16[256,2048]{1,0:T(8,128)(2,1)S(1)} %copy-done.3, bf16[256,2048]{1,0:T(8,128)(2,1)S(1)} %copy-done, bf16[256,2048]{1,0:T(8,128)(2,1)S(1)} %copy-done.1, bf16[256,2048]{1,0:T(8,128)(2,1)S(1)} %copy-done.2, ...), custom_call_target="tpu_custom_call" | custom-call | bytes 1024 | tf_op jit(solution)/shard_map/grads/pallas_call | solution.py:289
  40.3 0.6 %collective-permute-start.16 = (bf16[3,128,512]{2,1,0:T(8,128)(2,1)S(1)}, bf16[3,128,512]{2,1,0:T(8,128)(2,1)S(1)}, u32[]{:S(2)}, u32[]{:S(2)}) collective-permute-start(bf16[3,128,512]{2,1,0:T(8,128)(2,1)S(1)} %get-tuple-element.73), channel_id=1, source_target_pairs={{0,1},{1,0},{2,3},{3,2},{4,5},{5,4},{6,7},{7,6},{8,9},{9,8},{10,11... | collective-permute-start | bytes 1179656 | tf_op jit(solution)/shard_map/ppermute | solution.py:308
  40.9 1.7 %collective-permute-done.14.rest_1_.refs_1_ = bf16[3,128,512]{2,1,0:T(8,128)(2,1)S(1)} collective-permute-done((bf16[3,128,512]{2,1,0:T(8,128)(2,1)S(1)}, bf16[3,128,512]{2,1,0:T(8,128)(2,1)S(1)}, u32[]{:S(2)}, u32[]{:S(2)}) %collective-permute-start.14) | collective-permute-done | bytes 393248 | tf_op jit(solution)/shard_map/ppermute | solution.py:308
  42.6 0.0 collective-permute-done.11.got
  42.6 2.2 %grads.3 = (bf16[3,128,512]{2,1,0:T(8,128)(2,1)S(1)}, bf16[3,128,512]{2,1,0:T(8,128)(2,1)S(1)}) custom-call(s32[8]{0:T(128)S(1)} %copy-done.4, bf16[256,2048]{1,0:T(8,128)(2,1)S(1)} %copy-done.3, bf16[256,2048]{1,0:T(8,128)(2,1)S(1)} %copy-done, bf16[256,2048]{1,0:T(8,128)(2,1)S(1)} %copy-done.1, bf16[256,2048]{1,0:T(8,128)(2,1)S(1)} %copy-done.2, ...), custom_call_target="tpu_custom_call" | custom-call | bytes 1024 | tf_op jit(solution)/shard_map/grads/pallas_call | solution.py:289
  44.8 1.9 %collective-permute-start.15 = (bf16[3,128,512]{2,1,0:T(8,128)(2,1)S(1)}, bf16[3,128,512]{2,1,0:T(8,128)(2,1)S(1)}, u32[]{:S(2)}, u32[]{:S(2)}) collective-permute-start(bf16[3,128,512]{2,1,0:T(8,128)(2,1)S(1)} %get-tuple-element.71), channel_id=1, source_target_pairs={{0,1},{1,0},{2,3},{3,2},{4,5},{5,4},{6,7},{7,6},{8,9},{9,8},{10,11... | collective-permute-start | bytes 1179656 | tf_op jit(solution)/shard_map/ppermute | solution.py:308
  46.7 1.1 %place.4 = (bf16[128,4096]{1,0:T(8,128)(2,1)}, bf16[128,4096]{1,0:T(8,128)(2,1)}, bf16[128,4096]{1,0:T(8,128)(2,1)}) custom-call(bf16[3,128,512]{2,1,0:T(8,128)(2,1)S(1)} %get-tuple-element.57.rest_0_.refs_0_, bf16[3,128,512]{2,1,0:T(8,128)(2,1)S(1)} %get-tuple-element.68.rest_0_.refs_1_, bf16[3,128,512]{2,1,0:T(8,128)(2,1)S(1)} %collective-permute-done.10.rest_4_.refs_2_), custom_call_target="tpu_custom_call" | custom-call | bytes 1024 | tf_op jit(solution)/shard_map/place/pallas_call | solution.py:407
  47.8 0.9 %place.5 = (bf16[128,4096]{1,0:T(8,128)(2,1)}, bf16[128,4096]{1,0:T(8,128)(2,1)}, bf16[128,4096]{1,0:T(8,128)(2,1)}) custom-call(bf16[3,128,512]{2,1,0:T(8,128)(2,1)S(1)} %get-tuple-element.69.rest_0_.refs_0_, bf16[3,128,512]{2,1,0:T(8,128)(2,1)S(1)} %collective-permute-done.14.rest_1_.refs_1_, ...), custom_call_target="tpu_custom_call", output_to_operand_aliasing={{0}: (2, {}), {1}: (3, {}), {2}: (4, {})} | custom-call | bytes 1024 | tf_op jit(solution)/shard_map/place/pallas_call | solution.py:407
  48.7 3.6 %collective-permute-done.16.refs_1_ = bf16[3,128,512]{2,1,0:T(8,128)(2,1)S(1)} collective-permute-done((bf16[3,128,512]{2,1,0:T(8,128)(2,1)S(1)}, bf16[3,128,512]{2,1,0:T(8,128)(2,1)S(1)}, u32[]{:S(2)}, u32[]{:S(2)}) %collective-permute-start.16) | collective-permute-done | bytes 393248 | tf_op jit(solution)/shard_map/ppermute | solution.py:308
  52.3 0.9 %place.6 = (bf16[128,4096]{1,0:T(8,128)(2,1)}, bf16[128,4096]{1,0:T(8,128)(2,1)}, bf16[128,4096]{1,0:T(8,128)(2,1)}) custom-call(bf16[3,128,512]{2,1,0:T(8,128)(2,1)S(1)} %get-tuple-element.72.refs_0_, bf16[3,128,512]{2,1,0:T(8,128)(2,1)S(1)} %collective-permute-done.16.refs_1_, ...), custom_call_target="tpu_custom_call", output_to_operand_aliasing={{0}: (2, {}), {1}: (3, {}), {2}: (4, {})} | custom-call | bytes 1024 | tf_op jit(solution)/shard_map/place/pallas_call | solution.py:407
  53.3 6.7 %collective-permute-done.15.refs_0_ = bf16[3,128,512]{2,1,0:T(8,128)(2,1)S(1)} collective-permute-done((bf16[3,128,512]{2,1,0:T(8,128)(2,1)S(1)}, bf16[3,128,512]{2,1,0:T(8,128)(2,1)S(1)}, u32[]{:S(2)}, u32[]{:S(2)}) %collective-permute-start.15) | collective-permute-done | bytes 393248 | tf_op jit(solution)/shard_map/ppermute | solution.py:308
  60.0 0.8 %place.7 = (bf16[128,4096]{1,0:T(8,128)(2,1)}, bf16[128,4096]{1,0:T(8,128)(2,1)}, bf16[128,4096]{1,0:T(8,128)(2,1)}) custom-call(bf16[3,128,512]{2,1,0:T(8,128)(2,1)S(1)} %collective-permute-done.15.refs_0_, bf16[128,4096]{1,0:T(8,128)(2,1)} %get-tuple-element.80.refs_1_, ...), custom_call_target="tpu_custom_call", output_to_operand_aliasing={{0}: (1, {}), {1}: (2, {}), {2}: (3, {})} | custom-call | bytes 1024 | tf_op jit(solution)/shard_map/place/pallas_call | solution.py:407
Async XLA Ops:
  0.6 2.9 %copy-start.4 = (s32[8]{0:T(128)S(1)}, s32[8]{0:T(128)}, u32[]{:S(2)}) copy-start(s32[8]{0:T(128)} %lengths.25) | copy-start | bytes 100
  3.0 2.4 %collective-permute-start.2 = (f32[8,128,128]{2,1,0:T(8,128)}, f32[8,128,128]{2,1,0:T(8,128)S(1)}, u32[]{:S(2)}, u32[]{:S(2)}) collective-permute-start(f32[8,128,128]{2,1,0:T(8,128)} %states.5), channel_id=1, source_target_pairs={{0,2},{2,0},{4,6},{6,4},{8,10},{10,8},{12,14},{14,12},{16,18},{18,... | collective-permute-start | bytes 1572872 | tf_op jit(solution)/shard_map/ppermute | solution.py:296
  3.5 10.9 %copy-start.1 = (bf16[256,2048]{1,0:T(8,128)(2,1)S(1)}, bf16[256,2048]{1,0:T(8,128)(2,1)}, u32[]{:S(2)}) copy-start(bf16[256,2048]{1,0:T(8,128)(2,1)} %v.17) | copy-start | bytes 3145732
  3.5 10.9 %copy-start.2 = (bf16[256,2048]{1,0:T(8,128)(2,1)S(1)}, bf16[256,2048]{1,0:T(8,128)(2,1)}, u32[]{:S(2)}) copy-start(bf16[256,2048]{1,0:T(8,128)(2,1)} %g.17) | copy-start | bytes 3145732
  3.5 10.9 %copy-start.3 = (bf16[256,2048]{1,0:T(8,128)(2,1)S(1)}, bf16[256,2048]{1,0:T(8,128)(2,1)}, u32[]{:S(2)}) copy-start(bf16[256,2048]{1,0:T(8,128)(2,1)} %q.13) | copy-start | bytes 3145732
  5.4 9.0 %copy-start = (bf16[256,2048]{1,0:T(8,128)(2,1)S(1)}, bf16[256,2048]{1,0:T(8,128)(2,1)}, u32[]{:S(2)}) copy-start(bf16[256,2048]{1,0:T(8,128)(2,1)} %k.17) | copy-start | bytes 3145732
  6.1 12.9 %collective-permute-start.5 = (bf16[1056,128]{1,0:T(8,128)(2,1)S(1)}, bf16[1056,128]{1,0:T(8,128)(2,1)S(1)}, u32[]{:S(2)}, u32[]{:S(2)}) collective-permute-start(bf16[1056,128]{1,0:T(8,128)(2,1)S(1)} %get-tuple-element.52), channel_id=1, source_target_pairs={{0,6},{4,10},{8,14},{12,18},{16,22},{20,26},{24,30},{6,0},{10,4},{... | collective-permute-start | bytes 811016 | tf_op jit(solution)/shard_map/ppermute | solution.py:302
  10.6 8.4 %collective-permute-start.6 = (bf16[1040,128]{1,0:T(8,128)(2,1)S(1)}, bf16[1040,128]{1,0:T(8,128)(2,1)S(1)}, u32[]{:S(2)}, u32[]{:S(2)}) collective-permute-start(bf16[1040,128]{1,0:T(8,128)(2,1)S(1)} %get-tuple-element.53), channel_id=1, source_target_pairs={{0,10},{4,14},{8,18},{12,22},{16,26},{20,30},{10,0},{14,4},{18,8},... | collective-permute-start | bytes 798728 | tf_op jit(solution)/shard_map/ppermute | solution.py:302
  13.8 5.1 %collective-permute-start.3 = (f32[4,128,128]{2,1,0:T(8,128)S(1)}, f32[4,128,128]{2,1,0:T(8,128)S(1)}, u32[]{:S(2)}, u32[]{:S(2)}) collective-permute-start(f32[4,128,128]{2,1,0:T(8,128)S(1)} %get-tuple-element.50), channel_id=1, source_target_pairs={{0,2},{2,0},{4,6},{6,4},{8,10},{10,8},{12,14},{14,12},{16,18},{18,... | collective-permute-start | bytes 786440 | tf_op jit(solution)/shard_map/ppermute | solution.py:296
  13.9 5.1 %collective-permute-start.4 = (f32[4,128,128]{2,1,0:T(8,128)S(1)}, f32[4,128,128]{2,1,0:T(8,128)S(1)}, u32[]{:S(2)}, u32[]{:S(2)}) collective-permute-start(f32[4,128,128]{2,1,0:T(8,128)S(1)} %get-tuple-element.51), channel_id=1, source_target_pairs={{0,2},{2,0},{4,6},{6,4},{8,10},{10,8},{12,14},{14,12},{16,18},{18,... | collective-permute-start | bytes 786440 | tf_op jit(solution)/shard_map/ppermute | solution.py:296
  17.2 7.2 %collective-permute-start.1 = (f32[8,128,128]{2,1,0:T(8,128)S(1)}, f32[8,128,128]{2,1,0:T(8,128)S(1)}, u32[]{:S(2)}, u32[]{:S(2)}) collective-permute-start(f32[8,128,128]{2,1,0:T(8,128)S(1)} %get-tuple-element.47), channel_id=1, source_target_pairs={{0,2},{2,0},{4,6},{6,4},{8,10},{10,8},{12,14},{14,12},{16,18},{18,... | collective-permute-start | bytes 1572872 | tf_op jit(solution)/shard_map/ppermute | solution.py:296
  19.7 1.7 %collective-permute-start.7 = (f32[4,128,128]{2,1,0:T(8,128)S(1)}, f32[4,128,128]{2,1,0:T(8,128)S(1)}, u32[]{:S(2)}, u32[]{:S(2)}) collective-permute-start(f32[4,128,128]{2,1,0:T(8,128)S(1)} %get-tuple-element.56), channel_id=1, source_target_pairs={{0,2},{2,0},{4,6},{6,4},{8,10},{10,8},{12,14},{14,12},{16,18},{18,... | collective-permute-start | bytes 786440 | tf_op jit(solution)/shard_map/ppermute | solution.py:296
  20.2 12.4 %collective-permute-start = (f32[8,128,128]{2,1,0:T(8,128)S(1)}, f32[8,128,128]{2,1,0:T(8,128)S(1)}, u32[]{:S(2)}, u32[]{:S(2)}) collective-permute-start(f32[8,128,128]{2,1,0:T(8,128)S(1)} %get-tuple-element.46.kept), channel_id=1, source_target_pairs={{0,2},{2,0},{4,6},{6,4},{8,10},{10,8},{12,14},{14,12},{16,18},{18,... | collective-permute-start | bytes 1572872 | tf_op jit(solution)/shard_map/ppermute | solution.py:296
  22.7 13.1 %collective-permute-start.10 = (bf16[3,128,512]{2,1,0:T(8,128)(2,1)S(1)}, bf16[3,128,512]{2,1,0:T(8,128)(2,1)S(1)}, u32[]{:S(2)}, u32[]{:S(2)}) collective-permute-start(bf16[3,128,512]{2,1,0:T(8,128)(2,1)S(1)} %get-tuple-element.60), channel_id=1, source_target_pairs={{0,1},{1,0},{2,3},{3,2},{4,5},{5,4},{6,7},{7,6},{8,9},{9,8},{10,11... | collective-permute-start | bytes 1179656 | tf_op jit(solution)/shard_map/ppermute | solution.py:308
  24.3 6.4 %collective-permute-start.13 = (f32[4,128,128]{2,1,0:T(8,128)S(1)}, f32[4,128,128]{2,1,0:T(8,128)S(1)}, u32[]{:S(2)}, u32[]{:S(2)}) collective-permute-start(f32[4,128,128]{2,1,0:T(8,128)S(1)} %get-tuple-element.67), channel_id=1, source_target_pairs={{0,2},{2,0},{4,6},{6,4},{8,10},{10,8},{12,14},{14,12},{16,18},{18,... | collective-permute-start | bytes 786440 | tf_op jit(solution)/shard_map/ppermute | solution.py:296
  25.0 10.8 %collective-permute-start.8 = (bf16[1056,128]{1,0:T(8,128)(2,1)S(1)}, bf16[1056,128]{1,0:T(8,128)(2,1)S(1)}, u32[]{:S(2)}, u32[]{:S(2)}) collective-permute-start(bf16[1056,128]{1,0:T(8,128)(2,1)S(1)} %get-tuple-element.58), channel_id=1, source_target_pairs={{0,6},{4,10},{8,14},{12,18},{16,22},{20,26},{24,30},{6,0},{10,4},{... | collective-permute-start | bytes 811016 | tf_op jit(solution)/shard_map/ppermute | solution.py:302
  27.7 8.1 %collective-permute-start.9 = (bf16[1040,128]{1,0:T(8,128)(2,1)S(1)}, bf16[1040,128]{1,0:T(8,128)(2,1)S(1)}, u32[]{:S(2)}, u32[]{:S(2)}) collective-permute-start(bf16[1040,128]{1,0:T(8,128)(2,1)S(1)} %get-tuple-element.59), channel_id=1, source_target_pairs={{0,10},{4,14},{8,18},{12,22},{16,26},{20,30},{10,0},{14,4},{18,8},... | collective-permute-start | bytes 798728 | tf_op jit(solution)/shard_map/ppermute | solution.py:302
  32.0 10.6 %collective-permute-start.14 = (bf16[3,128,512]{2,1,0:T(8,128)(2,1)S(1)}, bf16[3,128,512]{2,1,0:T(8,128)(2,1)S(1)}, u32[]{:S(2)}, u32[]{:S(2)}) collective-permute-start(bf16[3,128,512]{2,1,0:T(8,128)(2,1)S(1)} %get-tuple-element.70), channel_id=1, source_target_pairs={{0,1},{1,0},{2,3},{3,2},{4,5},{5,4},{6,7},{7,6},{8,9},{9,8},{10,11... | collective-permute-start | bytes 1179656 | tf_op jit(solution)/shard_map/ppermute | solution.py:308
  36.5 1.6 %collective-permute-start.12 = (f32[4,128,128]{2,1,0:T(8,128)S(1)}, f32[4,128,128]{2,1,0:T(8,128)S(1)}, u32[]{:S(2)}, u32[]{:S(2)}) collective-permute-start(f32[4,128,128]{2,1,0:T(8,128)S(1)} %get-tuple-element.64), channel_id=1, source_target_pairs={{0,2},{2,0},{4,6},{6,4},{8,10},{10,8},{12,14},{14,12},{16,18},{18,... | collective-permute-start | bytes 786440 | tf_op jit(solution)/shard_map/ppermute | solution.py:296
  36.6 6.0 %collective-permute-start.11 = (f32[4,128,128]{2,1,0:T(8,128)S(1)}, f32[4,128,128]{2,1,0:T(8,128)S(1)}, u32[]{:S(2)}, u32[]{:S(2)}) collective-permute-start(f32[4,128,128]{2,1,0:T(8,128)S(1)} %get-tuple-element.62), channel_id=1, source_target_pairs={{0,2},{2,0},{4,6},{6,4},{8,10},{10,8},{12,14},{14,12},{16,18},{18,... | collective-permute-start | bytes 786440 | tf_op jit(solution)/shard_map/ppermute | solution.py:296
  40.3 12.0 %collective-permute-start.16 = (bf16[3,128,512]{2,1,0:T(8,128)(2,1)S(1)}, bf16[3,128,512]{2,1,0:T(8,128)(2,1)S(1)}, u32[]{:S(2)}, u32[]{:S(2)}) collective-permute-start(bf16[3,128,512]{2,1,0:T(8,128)(2,1)S(1)} %get-tuple-element.73), channel_id=1, source_target_pairs={{0,1},{1,0},{2,3},{3,2},{4,5},{5,4},{6,7},{7,6},{8,9},{9,8},{10,11... | collective-permute-start | bytes 1179656 | tf_op jit(solution)/shard_map/ppermute | solution.py:308
  44.8 15.2 %collective-permute-start.15 = (bf16[3,128,512]{2,1,0:T(8,128)(2,1)S(1)}, bf16[3,128,512]{2,1,0:T(8,128)(2,1)S(1)}, u32[]{:S(2)}, u32[]{:S(2)}) collective-permute-start(bf16[3,128,512]{2,1,0:T(8,128)(2,1)S(1)} %get-tuple-element.71), channel_id=1, source_target_pairs={{0,1},{1,0},{2,3},{3,2},{4,5},{5,4},{6,7},{7,6},{8,9},{9,8},{10,11... | collective-permute-start | bytes 1179656 | tf_op jit(solution)/shard_map/ppermute | solution.py:308

commit v6 on v5

--- a/solution.py
+++ b/solution.py
@@ -98,11 +98,11 @@
             copy(h // group, 1, v).wait()
         cols = slice(h * HEAD_DIM, (h + 1) * HEAD_DIM)
         made[h] = dot(jnp.where(here, held[0, :, cols], zero), held[1, :, cols], TN)
-        if not kept and h % group == group - 1:
-            some = pl.ds(h + 1 - group, group)
-            pltpu.make_async_copy(made.at[some], out.at[some], leave.at[h // group]).start()
-    for c in range(0 if kept else heads // group):
-        some = pl.ds(c * group, group)
+        if not kept and h % 2 == 1:
+            some = pl.ds(h - 1, 2)
+            pltpu.make_async_copy(made.at[some], out.at[some], leave.at[h // 2]).start()
+    for c in range(0 if kept else heads // 2):
+        some = pl.ds(2 * c, 2)
         pltpu.make_async_copy(made.at[some], out.at[some], leave.at[c]).wait()
 
 
@@ -246,6 +246,54 @@
     deal(done, outs, rows, groups)
 
 
+def add_mine_kernel(lengths, k, v, g, near, mine, *rest, ndocs, rows, offset, heads):
+    out = rest[-1]
+    first_core, first_rows, last_rows = own_range(lengths, ndocs, rows)
+
+    @pl.when(first_core)
+    def _():
+        for h in range(heads):
+            cols = slice(h * HEAD_DIM, (h + 1) * HEAD_DIM)
+            at = slice(offset + h * HEAD_DIM, offset + (h + 1) * HEAD_DIM)
+            out[0, :, cols] = near[0, :, cols]
+            for i, value in enumerate(carries_of_grad(k, v, mine[h], last_rows, at)):
+                out[1 + i, :, cols] = near[1 + i, :, cols] + value
+
+    @pl.when(jnp.logical_not(first_core))
+    def _():
+        for h in range(heads):
+            cols = slice(h * HEAD_DIM, (h + 1) * HEAD_DIM)
+            at = slice(offset + h * HEAD_DIM, offset + (h + 1) * HEAD_DIM)
+            out[0, :, cols] = near[0, :, cols] + carry_of_state(g, mine[h], first_rows, at)
+            for i in range(1, 3):
+                out[i, :, cols] = near[i, :, cols]
+
+
+def add_got_kernel(lengths, k, v, g, near, got, *rest, ndocs, rows, offset, heads, groups):
+    outs, done = rest[-1 - groups:-1], rest[-1]
+    first_core, first_rows, last_rows = own_range(lengths, ndocs, rows)
+
+    @pl.when(first_core)
+    def _():
+        for h in range(heads):
+            cols = slice(h * HEAD_DIM, (h + 1) * HEAD_DIM)
+            at = slice(offset + h * HEAD_DIM, offset + (h + 1) * HEAD_DIM)
+            done[0, :, cols] = (near[0, :, cols] + carry_of_state(g, got[h], first_rows, at)).astype(jnp.bfloat16)
+            for i in range(1, 3):
+                done[i, :, cols] = near[i, :, cols].astype(jnp.bfloat16)
+
+    @pl.when(jnp.logical_not(first_core))
+    def _():
+        for h in range(heads):
+            cols = slice(h * HEAD_DIM, (h + 1) * HEAD_DIM)
+            at = slice(offset + h * HEAD_DIM, offset + (h + 1) * HEAD_DIM)
+            done[0, :, cols] = near[0, :, cols].astype(jnp.bfloat16)
+            for i, value in enumerate(carries_of_grad(k, v, got[h], last_rows, at)):
+                done[1 + i, :, cols] = (near[1 + i, :, cols] + value).astype(jnp.bfloat16)
+
+    deal(done, outs, rows, groups)
+
+
 def place_kernel(*refs, groups, plan, width):
     parts, outs, sems = refs[:len(plan)], refs[-4:-1], refs[-1]
     column = lax.axis_index("head")
@@ -285,11 +333,11 @@
     def shape_of(*dims, dtype=f32):
         return jax.ShapeDtypeStruct(dims, dtype)
 
-    def call(name, kernel, args, outs, scratch=(), after=(), limit=VMEM_LIMIT):
+    def call(name, kernel, args, outs, scratch=(), after=(), limit=VMEM_LIMIT, same={}):
         return pl.pallas_call(
             kernel, in_specs=[in_smem] + [in_vmem] * len(args) + [anywhere] * len(after), out_specs=[in_vmem] * len(outs), out_shape=outs,
             scratch_shapes=list(scratch), cost_estimate=cheap,
-            compiler_params=pltpu.CompilerParams(vmem_limit_bytes=limit), name=name,
+            compiler_params=pltpu.CompilerParams(vmem_limit_bytes=limit), name=name, input_output_aliases=same,
         )(doc_lengths, *args, *after)
 
     def swap_cores(a):
@@ -320,7 +368,7 @@
             scratch_shapes=[
                 pltpu.VMEM((2, rows, half), bf16), pltpu.SemaphoreType.DMA((heads // group, 2)),
                 pltpu.SMEM((ndocs,), jnp.int32), pltpu.SemaphoreType.DMA,
-                pltpu.VMEM((heads if not kept else 1, *square), f32), pltpu.SemaphoreType.DMA((heads // group,)),
+                pltpu.VMEM((heads if not kept else 1, *square), f32), pltpu.SemaphoreType.DMA((heads // 2,)),
             ],
             cost_estimate=cheap, compiler_params=pltpu.CompilerParams(vmem_limit_bytes=KEPT_LIMIT if kept else FIRST_LIMIT), name="states",
         )(doc_lengths, *inputs)
@@ -359,6 +407,17 @@
         kernel = functools.partial(local_kernel, offset=offset, heads=cw // HEAD_DIM)
         return call(
             "local", kernel, (*inputs, *masks), [shape_of(3, rows, cw), shape_of(8, HEAD_DIM)], limit=GRAD_LIMIT,
+        )
+
+    def first_carry(near, offset, cw, mine, theirs):
+        more = dict(offset=offset, heads=cw // HEAD_DIM, **sizes)
+        near = call(
+            "add_mine", functools.partial(add_mine_kernel, **more), (*inputs[1:], near, mine), [shape_of(3, rows, cw)],
+            limit=GRAD_LIMIT, same={4: 0},
+        )[0]
+        return call(
+            "add_got", functools.partial(add_got_kernel, groups=groups, **more), (*inputs[1:], near, theirs),
+            [shape_of(3, part, cw, dtype=bf16)] * groups, [pltpu.VMEM((3, rows, cw), bf16)], limit=GRAD_LIMIT,
         )
 
     def carry(near, offset, cw, mine, theirs, after):
@@ -392,6 +451,8 @@
             after = [made[0] for made in outs[-1:]] + [parts[1] for parts in arrived[1:-1]][-1:]
             if totals:
                 outs.append(grads(masks, offset, cw, mine, theirs, after))
+            elif c == 0:
+                outs.append(first_carry(near[c][0], offset, cw, mine, theirs))
             else:
                 outs.append(carry(near[c][0], offset, cw, mine, theirs, after))
             arrived.append(send_rows(outs[-1]))

time: 61 us -> 60.9 us (level)
  waiting for transfers between devices: 17.3 us -> 16.2 us
  Pallas kernels: 21.9 us -> 22.9 us
    ppermute x9, waiting for transfers between devices: 2.13 us -> 1.05 us  [swap_cores(): return lax.ppermute(a, 'seq', [(b, b ^ 1) for b in range(seq)])]
    pallas_call x11 -> x12, Pallas kernels: 14 us -> 15 us  [call(): pl.pallas_call(kernel, in_specs=[in_smem] + [in_vmem] * len(args) + [anyw...]
  transfers between devices with their start and end apart: 17 -> 17, of which waited for: 6 -> 5; matrix products, arithmetic and copies ran while one was open for 0% -> 0% of each run, Pallas kernels for 30% -> 31%
where the time goes in v6:
time: 60.9 us; the launch traced here: 60.6 us
  Pallas kernels  22.9 us (38%)
  starting transfers between devices  20.7 us (34%)
  waiting for transfers between devices  16.2 us (27%)
  between operations  0.87 us (1%)
    pallas_call x12, Pallas kernels, call(): pl.pallas_call(kernel, in_specs=[in_smem] + [in_vmem] * len(args) + [anyw...  15 us
    ppermute x4, starting transfers between devices, swap_pairs(): lax.ppermute(sent[hop - 1], 'seq', perm + [(b, a) for a, b in perm])  13.4 us
    ppermute x4, waiting for transfers between devices, send_rows(): lax.ppermute(outs[j], 'head', [(x, (x + j) % groups) for x in range(group...  12 us
    ppermute x4, starting transfers between devices, send_rows(): lax.ppermute(outs[j], 'head', [(x, (x + j) % groups) for x in range(group...  4.71 us
    pallas_call x2, Pallas kernels, states(): pl.pallas_call(functools.partial(state_kernel, offset=offset, heads=heads...  4.19 us
    pallas_call x4, Pallas kernels, shards(): pl.pallas_call(functools.partial(place_kernel, groups=groups, plan=[where...  3.7 us
    ppermute x4, waiting for transfers between devices, swap_pairs(): lax.ppermute(sent[hop - 1], 'seq', perm + [(b, a) for a, b in perm])  3.18 us
    ppermute x9, starting transfers between devices, swap_cores(): return lax.ppermute(a, 'seq', [(b, b ^ 1) for b in range(seq)])  2.54 us
  transfers between devices with their start and end apart: 17, of which 5 were waited for; matrix products, arithmetic and copies ran while one was open for 0% of the time, Pallas kernels for 31%

profile of v6, /device:TPU:0, one launch (start us, length us, event | category | flops | bytes accessed | tf_op | source)
XLA Modules:
  0.0 60.6 jit_solution(10488634319860177461)
XLA Ops:
  0.6 0.0 copy-start.4
  0.6 2.3 %states.5 = f32[8,128,128]{2,1,0:T(8,128)} custom-call(s32[8]{0:T(128)} %lengths.27, bf16[256,2048]{1,0:T(8,128)(2,1)} %q.13, bf16[256,2048]{1,0:T(8,128)(2,1)} %k.19, bf16[256,2048]{1,0:T(8,128)(2,1)} %v.19, bf16[256,2048]{1,0:T(8,128)(2,1)} %g.19), custom_call_target="tpu_custom_call" | custom-call | bytes 1024 | tf_op jit(solution)/shard_map/states/pallas_call | solution.py:365
  3.0 0.5 collective-permute-start.2
  3.5 0.0 copy-done.4
  3.5 0.0 copy-start.1
  3.5 0.0 copy-start.2
  3.5 0.0 copy-start.3
  3.5 1.8 %states.3 = (f32[8,128,128]{2,1,0:T(8,128)S(1)}, bf16[256,256]{1,0:T(8,128)(2,1)S(1)}, bf16[256,256]{1,0:T(8,128)(2,1)S(1)}) custom-call(s32[8]{0:T(128)S(1)} %copy-done.4, bf16[256,2048]{1,0:T(8,128)(2,1)} %q.13, bf16[256,2048]{1,0:T(8,128)(2,1)} %k.19, bf16[256,2048]{1,0:T(8,128)(2,1)} %v.19, bf16[256,2048]{1,0:T(8,128)(2,1)} %g.19), custom_call_target="tpu_custom_call" | custom-call | bytes 1024 | tf_op jit(solution)/shard_map/states/pallas_call | solution.py:365
  5.4 0.0 copy-start
  5.4 0.0 collective-permute-done.2.got
  5.4 0.7 %pair.2 = (bf16[1056,128]{1,0:T(8,128)(2,1)S(1)}, bf16[1040,128]{1,0:T(8,128)(2,1)S(1)}, f32[4,128,128]{2,1,0:T(8,128)S(1)}, f32[4,128,128]{2,1,0:T(8,128)S(1)}) custom-call(s32[8]{0:T(128)S(1)} %copy-done.4, f32[8,128,128]{2,1,0:T(8,128)S(1)} %get-tuple-element.49.kept, f32[8,128,128]{2,1,0:T(8,128)S(1)} %collective-permute-done.2.got), custom_call_target="tpu_custom_call" | custom-call | bytes 1024 | tf_op jit(solution)/shard_map/pair/pallas_call | solution.py:337
  6.1 4.5 %collective-permute-start.5 = (bf16[1056,128]{1,0:T(8,128)(2,1)S(1)}, bf16[1056,128]{1,0:T(8,128)(2,1)S(1)}, u32[]{:S(2)}, u32[]{:S(2)}) collective-permute-start(bf16[1056,128]{1,0:T(8,128)(2,1)S(1)} %get-tuple-element.52), channel_id=1, source_target_pairs={{0,6},{4,10},{8,14},{12,18},{16,22},{20,26},{24,30},{6,0},{10,4},{... | collective-permute-start | bytes 811016 | tf_op jit(solution)/shard_map/ppermute | solution.py:350
  10.6 3.2 %collective-permute-start.6 = (bf16[1040,128]{1,0:T(8,128)(2,1)S(1)}, bf16[1040,128]{1,0:T(8,128)(2,1)S(1)}, u32[]{:S(2)}, u32[]{:S(2)}) collective-permute-start(bf16[1040,128]{1,0:T(8,128)(2,1)S(1)} %get-tuple-element.53), channel_id=1, source_target_pairs={{0,10},{4,14},{8,18},{12,22},{16,26},{20,30},{10,0},{14,4},{18,8},... | collective-permute-start | bytes 798728 | tf_op jit(solution)/shard_map/ppermute | solution.py:350
  13.8 0.1 collective-permute-start.3
  13.9 0.5 collective-permute-start.4
  14.4 0.0 copy-done.1
  14.4 0.0 copy-done.2
  14.4 0.0 copy-done.3
  14.4 0.0 copy-done
  14.4 1.6 %local.2 = (f32[3,256,512]{2,1,0:T(8,128)S(1)}, f32[8,128]{1,0:T(8,128)S(1)}) custom-call(s32[8]{0:T(128)S(1)} %copy-done.4, bf16[256,2048]{1,0:T(8,128)(2,1)S(1)} %copy-done.3, bf16[256,2048]{1,0:T(8,128)(2,1)S(1)} %copy-done, bf16[256,2048]{1,0:T(8,128)(2,1)S(1)} %copy-done.1, bf16[256,2048]{1,0:T(8,128)(2,1)S(1)} %copy-done.2, ...), custom_call_target="tpu_custom_call" | custom-call | bytes 1024 | tf_op jit(solution)/shard_map/local/pallas_call | solution.py:337
  16.0 1.1 %states.4 = (f32[8,128,128]{2,1,0:T(8,128)S(1)}, f32[8,128,128]{2,1,0:T(8,128)S(1)}) custom-call(s32[8]{0:T(128)S(1)} %copy-done.4, bf16[256,2048]{1,0:T(8,128)(2,1)S(1)} %copy-done.3, bf16[256,2048]{1,0:T(8,128)(2,1)S(1)} %copy-done, bf16[256,2048]{1,0:T(8,128)(2,1)S(1)} %copy-done.1, bf16[256,2048]{1,0:T(8,128)(2,1)S(1)} %copy-done.2, ...), custom_call_target="tpu_custom_call" | custom-call | bytes 1024 | tf_op jit(solution)/shard_map/states/pallas_call | solution.py:337
  17.2 0.1 collective-permute-start.1
  17.3 1.6 %local.3 = (f32[3,256,512]{2,1,0:T(8,128)S(1)}, f32[8,128]{1,0:T(8,128)S(1)}) custom-call(s32[8]{0:T(128)S(1)} %copy-done.4, bf16[256,2048]{1,0:T(8,128)(2,1)S(1)} %copy-done.3, bf16[256,2048]{1,0:T(8,128)(2,1)S(1)} %copy-done, bf16[256,2048]{1,0:T(8,128)(2,1)S(1)} %copy-done.1, bf16[256,2048]{1,0:T(8,128)(2,1)S(1)} %copy-done.2, ...), custom_call_target="tpu_custom_call" | custom-call | bytes 1024 | tf_op jit(solution)/shard_map/local/pallas_call | solution.py:337
  19.0 0.0 collective-permute-done.3.rest_0_
  19.0 0.0 collective-permute-done.4.rest_1_
  19.0 0.0 collective-permute-done.6.rest_3_
  19.0 0.0 collective-permute-done.5.rest_2_
  19.0 0.7 %join.2 = (f32[4,128,128]{2,1,0:T(8,128)S(1)}, f32[4,128,128]{2,1,0:T(8,128)S(1)}, f32[4,128,128]{2,1,0:T(8,128)S(1)}, f32[4,128,128]{2,1,0:T(8,128)S(1)}) custom-call(s32[8]{0:T(128)S(1)} %copy-done.4, f32[4,128,128]{2,1,0:T(8,128)S(1)} %collective-permute-done.3.rest_0_, f32[4,128,128]{2,1,0:T(8,128)S(1)} %collective-permute-done.4.rest_1_, ...), custom_call_target="tpu_custom_call" | custom-call | bytes 1024 | tf_op jit(solution)/shard_map/join/pallas_call | solution.py:337
  19.7 0.5 collective-permute-start.7
  20.2 0.1 collective-permute-start
  20.3 1.2 %add_mine.1.near = f32[3,256,512]{2,1,0:T(8,128)S(1)} custom-call(s32[8]{0:T(128)S(1)} %copy-done.4, bf16[256,2048]{1,0:T(8,128)(2,1)S(1)} %copy-done, bf16[256,2048]{1,0:T(8,128)(2,1)S(1)} %copy-done.1, bf16[256,2048]{1,0:T(8,128)(2,1)S(1)} %copy-done.2, f32[3,256,512]{2,1,0:T(8,128)S(1)} %get-tuple-element.48.near, ...), custom_call_target="tpu_custom_call", output_to_operand_aliasing={{}: (4, {})} | custom-call | bytes 1024 | tf_op jit(solution)/shard_map/add_mine/pallas_call | solution.py:337
  21.5 0.0 collective-permute-done.7.got
  21.6 1.0 %add_got.1 = (bf16[3,128,512]{2,1,0:T(8,128)(2,1)S(1)}, bf16[3,128,512]{2,1,0:T(8,128)(2,1)S(1)}) custom-call(s32[8]{0:T(128)S(1)} %copy-done.4, bf16[256,2048]{1,0:T(8,128)(2,1)S(1)} %copy-done, bf16[256,2048]{1,0:T(8,128)(2,1)S(1)} %copy-done.1, bf16[256,2048]{1,0:T(8,128)(2,1)S(1)} %copy-done.2, f32[3,256,512]{2,1,0:T(8,128)S(1)} %add_mine.1.near, ...), custom_call_target="tpu_custom_call" | custom-call | bytes 1024 | tf_op jit(solution)/shard_map/add_got/pallas_call | solution.py:337
  22.6 1.6 %collective-permute-start.10 = (bf16[3,128,512]{2,1,0:T(8,128)(2,1)S(1)}, bf16[3,128,512]{2,1,0:T(8,128)(2,1)S(1)}, u32[]{:S(2)}, u32[]{:S(2)}) collective-permute-start(bf16[3,128,512]{2,1,0:T(8,128)(2,1)S(1)} %get-tuple-element.60), channel_id=1, source_target_pairs={{0,1},{1,0},{2,3},{3,2},{4,5},{5,4},{6,7},{7,6},{8,9},{9,8},{10,11... | collective-permute-start | bytes 1179656 | tf_op jit(solution)/shard_map/ppermute | solution.py:356
  24.1 0.2 collective-permute-start.13
  24.3 0.0 collective-permute-done.1.got
  24.3 0.6 %pair.3 = (bf16[1056,128]{1,0:T(8,128)(2,1)S(1)}, bf16[1040,128]{1,0:T(8,128)(2,1)S(1)}) custom-call(s32[8]{0:T(128)S(1)} %copy-done.4, f32[8,128,128]{2,1,0:T(8,128)S(1)} %get-tuple-element.46.kept, f32[8,128,128]{2,1,0:T(8,128)S(1)} %collective-permute-done.1.got, bf16[3,128,512]{2,1,0:T(8,128)(2,1)S(1)} %get-tuple-element.57.rest_0_.refs_0_), custom_call_target="tpu_custom_call" | custom-call | bytes 1024 | tf_op jit(solution)/shard_map/pair/pallas_call | solution.py:337
  24.9 2.7 %collective-permute-start.8 = (bf16[1056,128]{1,0:T(8,128)(2,1)S(1)}, bf16[1056,128]{1,0:T(8,128)(2,1)S(1)}, u32[]{:S(2)}, u32[]{:S(2)}) collective-permute-start(bf16[1056,128]{1,0:T(8,128)(2,1)S(1)} %get-tuple-element.58), channel_id=1, source_target_pairs={{0,6},{4,10},{8,14},{12,18},{16,22},{20,26},{24,30},{6,0},{10,4},{... | collective-permute-start | bytes 811016 | tf_op jit(solution)/shard_map/ppermute | solution.py:350
  27.6 3.0 %collective-permute-start.9 = (bf16[1040,128]{1,0:T(8,128)(2,1)S(1)}, bf16[1040,128]{1,0:T(8,128)(2,1)S(1)}, u32[]{:S(2)}, u32[]{:S(2)}) collective-permute-start(bf16[1040,128]{1,0:T(8,128)(2,1)S(1)} %get-tuple-element.59), channel_id=1, source_target_pairs={{0,10},{4,14},{8,18},{12,22},{16,26},{20,30},{10,0},{14,4},{18,8},... | collective-permute-start | bytes 798728 | tf_op jit(solution)/shard_map/ppermute | solution.py:350
  30.6 0.0 collective-permute-done.13.got
  30.6 1.3 %carry.1 = (bf16[3,128,512]{2,1,0:T(8,128)(2,1)S(1)}, bf16[3,128,512]{2,1,0:T(8,128)(2,1)S(1)}) custom-call(s32[8]{0:T(128)S(1)} %copy-done.4, bf16[256,2048]{1,0:T(8,128)(2,1)S(1)} %copy-done, bf16[256,2048]{1,0:T(8,128)(2,1)S(1)} %copy-done.1, bf16[256,2048]{1,0:T(8,128)(2,1)S(1)} %copy-done.2, f32[3,256,512]{2,1,0:T(8,128)S(1)} %get-tuple-element.65.near, ...), custom_call_target="tpu_custom_call" | custom-call | bytes 1024 | tf_op jit(solution)/shard_map/carry/pallas_call | solution.py:337
  32.0 0.6 collective-permute-start.14
  32.6 0.0 collective-permute-done.rest_0_.rest_1_
  32.6 3.2 %collective-permute-done.9.rest_3_ = bf16[1040,128]{1,0:T(8,128)(2,1)S(1)} collective-permute-done((bf16[1040,128]{1,0:T(8,128)(2,1)S(1)}, bf16[1040,128]{1,0:T(8,128)(2,1)S(1)}, u32[]{:S(2)}, u32[]{:S(2)}) %collective-permute-start.9) | collective-permute-done | bytes 266272 | tf_op jit(solution)/shard_map/ppermute | solution.py:350
  35.7 0.0 collective-permute-done.8.rest_2_
  35.7 0.0 collective-permute-done.10.rest_4_.refs_2_
  35.7 0.7 %join.3 = (f32[4,128,128]{2,1,0:T(8,128)S(1)}, f32[4,128,128]{2,1,0:T(8,128)S(1)}, f32[4,128,128]{2,1,0:T(8,128)S(1)}, f32[4,128,128]{2,1,0:T(8,128)S(1)}) custom-call(s32[8]{0:T(128)S(1)} %copy-done.4, f32[8,128,128]{2,1,0:T(8,128)S(1)} %collective-permute-done.rest_0_.rest_1_, f32[8,128,128]{2,1,0:T(8,128)S(1)} %collective-permute-done.rest_0_.rest_1_, ...), custom_call_target="tpu_custom_call" | custom-call | bytes 1024 | tf_op jit(solution)/shard_map/join/pallas_call | solution.py:337
  36.5 0.1 collective-permute-start.12
  36.5 0.5 collective-permute-start.11
  37.0 1.0 %collective-permute-done.12.got = f32[4,128,128]{2,1,0:T(8,128)S(1)} collective-permute-done((f32[4,128,128]{2,1,0:T(8,128)S(1)}, f32[4,128,128]{2,1,0:T(8,128)S(1)}, u32[]{:S(2)}, u32[]{:S(2)}) %collective-permute-start.12) | collective-permute-done | bytes 262176 | tf_op jit(solution)/shard_map/ppermute | solution.py:344
  38.1 2.2 %grads.2 = (bf16[3,128,512]{2,1,0:T(8,128)(2,1)S(1)}, bf16[3,128,512]{2,1,0:T(8,128)(2,1)S(1)}) custom-call(s32[8]{0:T(128)S(1)} %copy-done.4, bf16[256,2048]{1,0:T(8,128)(2,1)S(1)} %copy-done.3, bf16[256,2048]{1,0:T(8,128)(2,1)S(1)} %copy-done, bf16[256,2048]{1,0:T(8,128)(2,1)S(1)} %copy-done.1, bf16[256,2048]{1,0:T(8,128)(2,1)S(1)} %copy-done.2, ...), custom_call_target="tpu_custom_call" | custom-call | bytes 1024 | tf_op jit(solution)/shard_map/grads/pallas_call | solution.py:337
  40.2 0.6 collective-permute-start.16
  40.8 1.7 %collective-permute-done.14.rest_1_.refs_1_ = bf16[3,128,512]{2,1,0:T(8,128)(2,1)S(1)} collective-permute-done((bf16[3,128,512]{2,1,0:T(8,128)(2,1)S(1)}, bf16[3,128,512]{2,1,0:T(8,128)(2,1)S(1)}, u32[]{:S(2)}, u32[]{:S(2)}) %collective-permute-start.14) | collective-permute-done | bytes 393248 | tf_op jit(solution)/shard_map/ppermute | solution.py:356
  42.5 0.0 collective-permute-done.11.got
  42.5 2.2 %grads.3 = (bf16[3,128,512]{2,1,0:T(8,128)(2,1)S(1)}, bf16[3,128,512]{2,1,0:T(8,128)(2,1)S(1)}) custom-call(s32[8]{0:T(128)S(1)} %copy-done.4, bf16[256,2048]{1,0:T(8,128)(2,1)S(1)} %copy-done.3, bf16[256,2048]{1,0:T(8,128)(2,1)S(1)} %copy-done, bf16[256,2048]{1,0:T(8,128)(2,1)S(1)} %copy-done.1, bf16[256,2048]{1,0:T(8,128)(2,1)S(1)} %copy-done.2, ...), custom_call_target="tpu_custom_call" | custom-call | bytes 1024 | tf_op jit(solution)/shard_map/grads/pallas_call | solution.py:337
  44.7 2.0 %collective-permute-start.15 = (bf16[3,128,512]{2,1,0:T(8,128)(2,1)S(1)}, bf16[3,128,512]{2,1,0:T(8,128)(2,1)S(1)}, u32[]{:S(2)}, u32[]{:S(2)}) collective-permute-start(bf16[3,128,512]{2,1,0:T(8,128)(2,1)S(1)} %get-tuple-element.71), channel_id=1, source_target_pairs={{0,1},{1,0},{2,3},{3,2},{4,5},{5,4},{6,7},{7,6},{8,9},{9,8},{10,11... | collective-permute-start | bytes 1179656 | tf_op jit(solution)/shard_map/ppermute | solution.py:356
  46.6 1.1 %place.4 = (bf16[128,4096]{1,0:T(8,128)(2,1)}, bf16[128,4096]{1,0:T(8,128)(2,1)}, bf16[128,4096]{1,0:T(8,128)(2,1)}) custom-call(bf16[3,128,512]{2,1,0:T(8,128)(2,1)S(1)} %get-tuple-element.57.rest_0_.refs_0_, bf16[3,128,512]{2,1,0:T(8,128)(2,1)S(1)} %get-tuple-element.68.rest_0_.refs_1_, bf16[3,128,512]{2,1,0:T(8,128)(2,1)S(1)} %collective-permute-done.10.rest_4_.refs_2_), custom_call_target="tpu_custom_call" | custom-call | bytes 1024 | tf_op jit(solution)/shard_map/place/pallas_call | solution.py:468
  47.7 0.9 %place.5 = (bf16[128,4096]{1,0:T(8,128)(2,1)}, bf16[128,4096]{1,0:T(8,128)(2,1)}, bf16[128,4096]{1,0:T(8,128)(2,1)}) custom-call(bf16[3,128,512]{2,1,0:T(8,128)(2,1)S(1)} %get-tuple-element.69.rest_0_.refs_0_, bf16[3,128,512]{2,1,0:T(8,128)(2,1)S(1)} %collective-permute-done.14.rest_1_.refs_1_, ...), custom_call_target="tpu_custom_call", output_to_operand_aliasing={{0}: (2, {}), {1}: (3, {}), {2}: (4, {})} | custom-call | bytes 1024 | tf_op jit(solution)/shard_map/place/pallas_call | solution.py:468
  48.6 3.6 %collective-permute-done.16.refs_1_ = bf16[3,128,512]{2,1,0:T(8,128)(2,1)S(1)} collective-permute-done((bf16[3,128,512]{2,1,0:T(8,128)(2,1)S(1)}, bf16[3,128,512]{2,1,0:T(8,128)(2,1)S(1)}, u32[]{:S(2)}, u32[]{:S(2)}) %collective-permute-start.16) | collective-permute-done | bytes 393248 | tf_op jit(solution)/shard_map/ppermute | solution.py:356
  52.3 0.9 %place.6 = (bf16[128,4096]{1,0:T(8,128)(2,1)}, bf16[128,4096]{1,0:T(8,128)(2,1)}, bf16[128,4096]{1,0:T(8,128)(2,1)}) custom-call(bf16[3,128,512]{2,1,0:T(8,128)(2,1)S(1)} %get-tuple-element.72.refs_0_, bf16[3,128,512]{2,1,0:T(8,128)(2,1)S(1)} %collective-permute-done.16.refs_1_, ...), custom_call_target="tpu_custom_call", output_to_operand_aliasing={{0}: (2, {}), {1}: (3, {}), {2}: (4, {})} | custom-call | bytes 1024 | tf_op jit(solution)/shard_map/place/pallas_call | solution.py:468
  53.2 6.7 %collective-permute-done.15.refs_0_ = bf16[3,128,512]{2,1,0:T(8,128)(2,1)S(1)} collective-permute-done((bf16[3,128,512]{2,1,0:T(8,128)(2,1)S(1)}, bf16[3,128,512]{2,1,0:T(8,128)(2,1)S(1)}, u32[]{:S(2)}, u32[]{:S(2)}) %collective-permute-start.15) | collective-permute-done | bytes 393248 | tf_op jit(solution)/shard_map/ppermute | solution.py:356
  59.9 0.8 %place.7 = (bf16[128,4096]{1,0:T(8,128)(2,1)}, bf16[128,4096]{1,0:T(8,128)(2,1)}, bf16[128,4096]{1,0:T(8,128)(2,1)}) custom-call(bf16[3,128,512]{2,1,0:T(8,128)(2,1)S(1)} %collective-permute-done.15.refs_0_, bf16[128,4096]{1,0:T(8,128)(2,1)} %get-tuple-element.80.refs_1_, ...), custom_call_target="tpu_custom_call", output_to_operand_aliasing={{0}: (1, {}), {1}: (2, {}), {2}: (3, {})} | custom-call | bytes 1024 | tf_op jit(solution)/shard_map/place/pallas_call | solution.py:468
Async XLA Ops:
  0.6 2.9 %copy-start.4 = (s32[8]{0:T(128)S(1)}, s32[8]{0:T(128)}, u32[]{:S(2)}) copy-start(s32[8]{0:T(128)} %lengths.27) | copy-start | bytes 100
  3.0 2.4 %collective-permute-start.2 = (f32[8,128,128]{2,1,0:T(8,128)}, f32[8,128,128]{2,1,0:T(8,128)S(1)}, u32[]{:S(2)}, u32[]{:S(2)}) collective-permute-start(f32[8,128,128]{2,1,0:T(8,128)} %states.5), channel_id=1, source_target_pairs={{0,2},{2,0},{4,6},{6,4},{8,10},{10,8},{12,14},{14,12},{16,18},{18,... | collective-permute-start | bytes 1572872 | tf_op jit(solution)/shard_map/ppermute | solution.py:344
  3.5 10.9 %copy-start.1 = (bf16[256,2048]{1,0:T(8,128)(2,1)S(1)}, bf16[256,2048]{1,0:T(8,128)(2,1)}, u32[]{:S(2)}) copy-start(bf16[256,2048]{1,0:T(8,128)(2,1)} %v.19) | copy-start | bytes 3145732
  3.5 10.9 %copy-start.2 = (bf16[256,2048]{1,0:T(8,128)(2,1)S(1)}, bf16[256,2048]{1,0:T(8,128)(2,1)}, u32[]{:S(2)}) copy-start(bf16[256,2048]{1,0:T(8,128)(2,1)} %g.19) | copy-start | bytes 3145732
  3.5 10.9 %copy-start.3 = (bf16[256,2048]{1,0:T(8,128)(2,1)S(1)}, bf16[256,2048]{1,0:T(8,128)(2,1)}, u32[]{:S(2)}) copy-start(bf16[256,2048]{1,0:T(8,128)(2,1)} %q.13) | copy-start | bytes 3145732
  5.4 9.0 %copy-start = (bf16[256,2048]{1,0:T(8,128)(2,1)S(1)}, bf16[256,2048]{1,0:T(8,128)(2,1)}, u32[]{:S(2)}) copy-start(bf16[256,2048]{1,0:T(8,128)(2,1)} %k.19) | copy-start | bytes 3145732
  6.1 12.9 %collective-permute-start.5 = (bf16[1056,128]{1,0:T(8,128)(2,1)S(1)}, bf16[1056,128]{1,0:T(8,128)(2,1)S(1)}, u32[]{:S(2)}, u32[]{:S(2)}) collective-permute-start(bf16[1056,128]{1,0:T(8,128)(2,1)S(1)} %get-tuple-element.52), channel_id=1, source_target_pairs={{0,6},{4,10},{8,14},{12,18},{16,22},{20,26},{24,30},{6,0},{10,4},{... | collective-permute-start | bytes 811016 | tf_op jit(solution)/shard_map/ppermute | solution.py:350
  10.6 8.4 %collective-permute-start.6 = (bf16[1040,128]{1,0:T(8,128)(2,1)S(1)}, bf16[1040,128]{1,0:T(8,128)(2,1)S(1)}, u32[]{:S(2)}, u32[]{:S(2)}) collective-permute-start(bf16[1040,128]{1,0:T(8,128)(2,1)S(1)} %get-tuple-element.53), channel_id=1, source_target_pairs={{0,10},{4,14},{8,18},{12,22},{16,26},{20,30},{10,0},{14,4},{18,8},... | collective-permute-start | bytes 798728 | tf_op jit(solution)/shard_map/ppermute | solution.py:350
  13.8 5.1 %collective-permute-start.3 = (f32[4,128,128]{2,1,0:T(8,128)S(1)}, f32[4,128,128]{2,1,0:T(8,128)S(1)}, u32[]{:S(2)}, u32[]{:S(2)}) collective-permute-start(f32[4,128,128]{2,1,0:T(8,128)S(1)} %get-tuple-element.50), channel_id=1, source_target_pairs={{0,2},{2,0},{4,6},{6,4},{8,10},{10,8},{12,14},{14,12},{16,18},{18,... | collective-permute-start | bytes 786440 | tf_op jit(solution)/shard_map/ppermute | solution.py:344
  13.9 5.1 %collective-permute-start.4 = (f32[4,128,128]{2,1,0:T(8,128)S(1)}, f32[4,128,128]{2,1,0:T(8,128)S(1)}, u32[]{:S(2)}, u32[]{:S(2)}) collective-permute-start(f32[4,128,128]{2,1,0:T(8,128)S(1)} %get-tuple-element.51), channel_id=1, source_target_pairs={{0,2},{2,0},{4,6},{6,4},{8,10},{10,8},{12,14},{14,12},{16,18},{18,... | collective-permute-start | bytes 786440 | tf_op jit(solution)/shard_map/ppermute | solution.py:344
  17.2 7.1 %collective-permute-start.1 = (f32[8,128,128]{2,1,0:T(8,128)S(1)}, f32[8,128,128]{2,1,0:T(8,128)S(1)}, u32[]{:S(2)}, u32[]{:S(2)}) collective-permute-start(f32[8,128,128]{2,1,0:T(8,128)S(1)} %get-tuple-element.47), channel_id=1, source_target_pairs={{0,2},{2,0},{4,6},{6,4},{8,10},{10,8},{12,14},{14,12},{16,18},{18,... | collective-permute-start | bytes 1572872 | tf_op jit(solution)/shard_map/ppermute | solution.py:344
  19.7 1.8 %collective-permute-start.7 = (f32[4,128,128]{2,1,0:T(8,128)S(1)}, f32[4,128,128]{2,1,0:T(8,128)S(1)}, u32[]{:S(2)}, u32[]{:S(2)}) collective-permute-start(f32[4,128,128]{2,1,0:T(8,128)S(1)} %get-tuple-element.56), channel_id=1, source_target_pairs={{0,2},{2,0},{4,6},{6,4},{8,10},{10,8},{12,14},{14,12},{16,18},{18,... | collective-permute-start | bytes 786440 | tf_op jit(solution)/shard_map/ppermute | solution.py:344
  20.2 12.3 %collective-permute-start = (f32[8,128,128]{2,1,0:T(8,128)S(1)}, f32[8,128,128]{2,1,0:T(8,128)S(1)}, u32[]{:S(2)}, u32[]{:S(2)}) collective-permute-start(f32[8,128,128]{2,1,0:T(8,128)S(1)} %get-tuple-element.46.kept), channel_id=1, source_target_pairs={{0,2},{2,0},{4,6},{6,4},{8,10},{10,8},{12,14},{14,12},{16,18},{18,... | collective-permute-start | bytes 1572872 | tf_op jit(solution)/shard_map/ppermute | solution.py:344
  22.6 13.2 %collective-permute-start.10 = (bf16[3,128,512]{2,1,0:T(8,128)(2,1)S(1)}, bf16[3,128,512]{2,1,0:T(8,128)(2,1)S(1)}, u32[]{:S(2)}, u32[]{:S(2)}) collective-permute-start(bf16[3,128,512]{2,1,0:T(8,128)(2,1)S(1)} %get-tuple-element.60), channel_id=1, source_target_pairs={{0,1},{1,0},{2,3},{3,2},{4,5},{5,4},{6,7},{7,6},{8,9},{9,8},{10,11... | collective-permute-start | bytes 1179656 | tf_op jit(solution)/shard_map/ppermute | solution.py:356
  24.1 6.5 %collective-permute-start.13 = (f32[4,128,128]{2,1,0:T(8,128)S(1)}, f32[4,128,128]{2,1,0:T(8,128)S(1)}, u32[]{:S(2)}, u32[]{:S(2)}) collective-permute-start(f32[4,128,128]{2,1,0:T(8,128)S(1)} %get-tuple-element.67), channel_id=1, source_target_pairs={{0,2},{2,0},{4,6},{6,4},{8,10},{10,8},{12,14},{14,12},{16,18},{18,... | collective-permute-start | bytes 786440 | tf_op jit(solution)/shard_map/ppermute | solution.py:344
  24.9 10.8 %collective-permute-start.8 = (bf16[1056,128]{1,0:T(8,128)(2,1)S(1)}, bf16[1056,128]{1,0:T(8,128)(2,1)S(1)}, u32[]{:S(2)}, u32[]{:S(2)}) collective-permute-start(bf16[1056,128]{1,0:T(8,128)(2,1)S(1)} %get-tuple-element.58), channel_id=1, source_target_pairs={{0,6},{4,10},{8,14},{12,18},{16,22},{20,26},{24,30},{6,0},{10,4},{... | collective-permute-start | bytes 811016 | tf_op jit(solution)/shard_map/ppermute | solution.py:350
  27.6 8.1 %collective-permute-start.9 = (bf16[1040,128]{1,0:T(8,128)(2,1)S(1)}, bf16[1040,128]{1,0:T(8,128)(2,1)S(1)}, u32[]{:S(2)}, u32[]{:S(2)}) collective-permute-start(bf16[1040,128]{1,0:T(8,128)(2,1)S(1)} %get-tuple-element.59), channel_id=1, source_target_pairs={{0,10},{4,14},{8,18},{12,22},{16,26},{20,30},{10,0},{14,4},{18,8},... | collective-permute-start | bytes 798728 | tf_op jit(solution)/shard_map/ppermute | solution.py:350
  32.0 10.5 %collective-permute-start.14 = (bf16[3,128,512]{2,1,0:T(8,128)(2,1)S(1)}, bf16[3,128,512]{2,1,0:T(8,128)(2,1)S(1)}, u32[]{:S(2)}, u32[]{:S(2)}) collective-permute-start(bf16[3,128,512]{2,1,0:T(8,128)(2,1)S(1)} %get-tuple-element.70), channel_id=1, source_target_pairs={{0,1},{1,0},{2,3},{3,2},{4,5},{5,4},{6,7},{7,6},{8,9},{9,8},{10,11... | collective-permute-start | bytes 1179656 | tf_op jit(solution)/shard_map/ppermute | solution.py:356
  36.5 1.6 %collective-permute-start.12 = (f32[4,128,128]{2,1,0:T(8,128)S(1)}, f32[4,128,128]{2,1,0:T(8,128)S(1)}, u32[]{:S(2)}, u32[]{:S(2)}) collective-permute-start(f32[4,128,128]{2,1,0:T(8,128)S(1)} %get-tuple-element.64), channel_id=1, source_target_pairs={{0,2},{2,0},{4,6},{6,4},{8,10},{10,8},{12,14},{14,12},{16,18},{18,... | collective-permute-start | bytes 786440 | tf_op jit(solution)/shard_map/ppermute | solution.py:344
  36.5 6.0 %collective-permute-start.11 = (f32[4,128,128]{2,1,0:T(8,128)S(1)}, f32[4,128,128]{2,1,0:T(8,128)S(1)}, u32[]{:S(2)}, u32[]{:S(2)}) collective-permute-start(f32[4,128,128]{2,1,0:T(8,128)S(1)} %get-tuple-element.62), channel_id=1, source_target_pairs={{0,2},{2,0},{4,6},{6,4},{8,10},{10,8},{12,14},{14,12},{16,18},{18,... | collective-permute-start | bytes 786440 | tf_op jit(solution)/shard_map/ppermute | solution.py:344
  40.2 12.0 %collective-permute-start.16 = (bf16[3,128,512]{2,1,0:T(8,128)(2,1)S(1)}, bf16[3,128,512]{2,1,0:T(8,128)(2,1)S(1)}, u32[]{:S(2)}, u32[]{:S(2)}) collective-permute-start(bf16[3,128,512]{2,1,0:T(8,128)(2,1)S(1)} %get-tuple-element.73), channel_id=1, source_target_pairs={{0,1},{1,0},{2,3},{3,2},{4,5},{5,4},{6,7},{7,6},{8,9},{9,8},{10,11... | collective-permute-start | bytes 1179656 | tf_op jit(solution)/shard_map/ppermute | solution.py:356
  44.7 15.2 %collective-permute-start.15 = (bf16[3,128,512]{2,1,0:T(8,128)(2,1)S(1)}, bf16[3,128,512]{2,1,0:T(8,128)(2,1)S(1)}, u32[]{:S(2)}, u32[]{:S(2)}) collective-permute-start(bf16[3,128,512]{2,1,0:T(8,128)(2,1)S(1)} %get-tuple-element.71), channel_id=1, source_target_pairs={{0,1},{1,0},{2,3},{3,2},{4,5},{5,4},{6,7},{7,6},{8,9},{9,8},{10,11... | collective-permute-start | bytes 1179656 | tf_op jit(solution)/shard_map/ppermute | solution.py:356

commit v7 on v4

--- a/solution.py
+++ b/solution.py
@@ -387,7 +387,7 @@
             if totals:
                 outs.append(grads(masks, offset, cw, mine, theirs, after))
             else:
-                outs.append(carry(near[c][0], offset, cw, mine, theirs, after))
+                outs.append(carry(near[c][0], offset, cw, mine, theirs, after or [made for made, _ in joined[1:]]))
             arrived.append(send_rows(outs[-1]))
         totals = [total]
         cuts += chunks

time: 61.5 us -> 60.8 us (0.989)
  waiting for transfers between devices: 17.6 us -> 16.8 us
  transfers between devices with their start and end apart: 17 -> 17, of which waited for: 6 -> 7; matrix products, arithmetic and copies ran while one was open for 0% -> 0% of each run, Pallas kernels for 30% -> 31%
where the time goes in v7:
time: 60.8 us; the launch traced here: 60.5 us
  Pallas kernels  21.8 us (36%)
  starting transfers between devices  20.5 us (34%)
  waiting for transfers between devices  16.8 us (28%)
  between operations  0.86 us (1%)
  local copies, waits for them, and re-layouts  0.67 us (1%)
    pallas_call x12, Pallas kernels, call(): pl.pallas_call(kernel, in_specs=[in_smem] + [in_vmem] * len(args) + [anyw...  14.6 us
    ppermute x4, starting transfers between devices, swap_pairs(): lax.ppermute(sent[hop - 1], 'seq', perm + [(b, a) for a, b in perm])  13.4 us
    ppermute x4, waiting for transfers between devices, send_rows(): lax.ppermute(outs[j], 'head', [(x, (x + j) % groups) for x in range(group...  12.1 us
    ppermute x4, starting transfers between devices, send_rows(): lax.ppermute(outs[j], 'head', [(x, (x + j) % groups) for x in range(group...  4.57 us
    pallas_call x4, Pallas kernels, shards(): pl.pallas_call(functools.partial(place_kernel, groups=groups, plan=[where...  3.7 us
    pallas_call x2, Pallas kernels, states(): pl.pallas_call(functools.partial(state_kernel, offset=offset, heads=heads...  3.44 us
    ppermute x4, waiting for transfers between devices, swap_pairs(): lax.ppermute(sent[hop - 1], 'seq', perm + [(b, a) for a, b in perm])  3.18 us
    ppermute x9, starting transfers between devices, swap_cores(): return lax.ppermute(a, 'seq', [(b, b ^ 1) for b in range(seq)])  2.49 us
  transfers between devices with their start and end apart: 17, of which 7 were waited for; matrix products, arithmetic and copies ran while one was open for 0% of the time, Pallas kernels for 31%

profile of v7, /device:TPU:0, one launch (start us, length us, event | category | flops | bytes accessed | tf_op | source)
XLA Modules:
  0.0 60.5 jit_solution(14612459683904036181)
XLA Ops:
  0.6 0.0 copy-start.4
  0.6 0.6 %copy-done.4 = s32[8]{0:T(128)S(1)} copy-done((s32[8]{0:T(128)S(1)}, s32[8]{0:T(128)}, u32[]{:S(2)}) %copy-start.4) | copy-done | bytes 56
  1.3 1.6 %states.5 = f32[8,128,128]{2,1,0:T(8,128)S(1)} custom-call(s32[8]{0:T(128)S(1)} %copy-done.4, bf16[256,2048]{1,0:T(8,128)(2,1)} %q.13, bf16[256,2048]{1,0:T(8,128)(2,1)} %k.17, bf16[256,2048]{1,0:T(8,128)(2,1)} %v.17, bf16[256,2048]{1,0:T(8,128)(2,1)} %g.17), custom_call_target="tpu_custom_call" | custom-call | bytes 1024 | tf_op jit(solution)/shard_map/states/pallas_call | solution.py:310
  2.9 0.5 collective-permute-start.2
  3.5 0.0 copy-start.1
  3.5 0.0 copy-start.2
  3.5 0.0 copy-start.3
  3.5 1.8 %states.3 = (f32[8,128,128]{2,1,0:T(8,128)S(1)}, bf16[256,256]{1,0:T(8,128)(2,1)S(1)}, bf16[256,256]{1,0:T(8,128)(2,1)S(1)}) custom-call(s32[8]{0:T(128)S(1)} %copy-done.4, bf16[256,2048]{1,0:T(8,128)(2,1)} %q.13, bf16[256,2048]{1,0:T(8,128)(2,1)} %k.17, bf16[256,2048]{1,0:T(8,128)(2,1)} %v.17, bf16[256,2048]{1,0:T(8,128)(2,1)} %g.17), custom_call_target="tpu_custom_call" | custom-call | bytes 1024 | tf_op jit(solution)/shard_map/states/pallas_call | solution.py:310
  5.3 0.0 copy-start
  5.3 0.0 collective-permute-done.2.got
  5.3 0.6 %pair.2 = (bf16[1056,128]{1,0:T(8,128)(2,1)S(1)}, bf16[1040,128]{1,0:T(8,128)(2,1)S(1)}, f32[4,128,128]{2,1,0:T(8,128)S(1)}, f32[4,128,128]{2,1,0:T(8,128)S(1)}) custom-call(s32[8]{0:T(128)S(1)} %copy-done.4, f32[8,128,128]{2,1,0:T(8,128)S(1)} %get-tuple-element.49.kept, f32[8,128,128]{2,1,0:T(8,128)S(1)} %collective-permute-done.2.got), custom_call_target="tpu_custom_call" | custom-call | bytes 1024 | tf_op jit(solution)/shard_map/pair/pallas_call | solution.py:282
  5.9 4.5 %collective-permute-start.4 = (bf16[1056,128]{1,0:T(8,128)(2,1)S(1)}, bf16[1056,128]{1,0:T(8,128)(2,1)S(1)}, u32[]{:S(2)}, u32[]{:S(2)}) collective-permute-start(bf16[1056,128]{1,0:T(8,128)(2,1)S(1)} %get-tuple-element.51), channel_id=1, source_target_pairs={{0,6},{4,10},{8,14},{12,18},{16,22},{20,26},{24,30},{6,0},{10,4},{... | collective-permute-start | bytes 811016 | tf_op jit(solution)/shard_map/ppermute | solution.py:295
  10.5 3.0 %collective-permute-start.5 = (bf16[1040,128]{1,0:T(8,128)(2,1)S(1)}, bf16[1040,128]{1,0:T(8,128)(2,1)S(1)}, u32[]{:S(2)}, u32[]{:S(2)}) collective-permute-start(bf16[1040,128]{1,0:T(8,128)(2,1)S(1)} %get-tuple-element.52), channel_id=1, source_target_pairs={{0,10},{4,14},{8,18},{12,22},{16,26},{20,30},{10,0},{14,4},{18,8},... | collective-permute-start | bytes 798728 | tf_op jit(solution)/shard_map/ppermute | solution.py:295
  13.5 0.1 collective-permute-start.3
  13.6 0.0 copy-done.1
  13.6 0.0 copy-done.2
  13.6 0.0 copy-done.3
  13.7 0.0 copy-done
  13.7 1.6 %local.2 = (f32[3,256,512]{2,1,0:T(8,128)S(1)}, f32[8,128]{1,0:T(8,128)S(1)}) custom-call(s32[8]{0:T(128)S(1)} %copy-done.4, bf16[256,2048]{1,0:T(8,128)(2,1)S(1)} %copy-done.3, bf16[256,2048]{1,0:T(8,128)(2,1)S(1)} %copy-done, bf16[256,2048]{1,0:T(8,128)(2,1)S(1)} %copy-done.1, bf16[256,2048]{1,0:T(8,128)(2,1)S(1)} %copy-done.2, ...), custom_call_target="tpu_custom_call" | custom-call | bytes 1024 | tf_op jit(solution)/shard_map/local/pallas_call | solution.py:282
  15.3 1.2 %states.4 = (f32[8,128,128]{2,1,0:T(8,128)S(1)}, f32[8,128,128]{2,1,0:T(8,128)S(1)}) custom-call(s32[8]{0:T(128)S(1)} %copy-done.4, bf16[256,2048]{1,0:T(8,128)(2,1)S(1)} %copy-done.3, bf16[256,2048]{1,0:T(8,128)(2,1)S(1)} %copy-done, bf16[256,2048]{1,0:T(8,128)(2,1)S(1)} %copy-done.1, bf16[256,2048]{1,0:T(8,128)(2,1)S(1)} %copy-done.2, ...), custom_call_target="tpu_custom_call" | custom-call | bytes 1024 | tf_op jit(solution)/shard_map/states/pallas_call | solution.py:282
  16.4 0.5 collective-permute-start.1
  17.0 1.6 %local.3 = (f32[3,256,512]{2,1,0:T(8,128)S(1)}, f32[8,128]{1,0:T(8,128)S(1)}) custom-call(s32[8]{0:T(128)S(1)} %copy-done.4, bf16[256,2048]{1,0:T(8,128)(2,1)S(1)} %copy-done.3, bf16[256,2048]{1,0:T(8,128)(2,1)S(1)} %copy-done, bf16[256,2048]{1,0:T(8,128)(2,1)S(1)} %copy-done.1, bf16[256,2048]{1,0:T(8,128)(2,1)S(1)} %copy-done.2, ...), custom_call_target="tpu_custom_call" | custom-call | bytes 1024 | tf_op jit(solution)/shard_map/local/pallas_call | solution.py:282
  18.6 0.1 collective-permute-start.7
  18.7 0.0 collective-permute-done.3.rest_0_
  18.7 0.0 collective-permute-done.5.rest_2_
  18.7 0.0 collective-permute-done.4.rest_1_
  18.7 0.7 %join.3 = (f32[4,128,128]{2,1,0:T(8,128)S(1)}, f32[4,128,128]{2,1,0:T(8,128)S(1)}) custom-call(s32[8]{0:T(128)S(1)} %copy-done.4, f32[4,128,128]{2,1,0:T(8,128)S(1)} %collective-permute-done.3.rest_0_, bf16[1056,128]{1,0:T(8,128)(2,1)S(1)} %collective-permute-done.4.rest_1_, bf16[1040,128]{1,0:T(8,128)(2,1)S(1)} %collective-permute-done.5.rest_2_, ...), custom_call_target="tpu_custom_call" | custom-call | bytes 1024 | tf_op jit(solution)/shard_map/join/pallas_call | solution.py:282
  19.4 0.5 collective-permute-start.6
  19.9 0.1 collective-permute-start
  20.0 0.2 collective-permute-done.7.rest_0_
  20.2 0.6 %join.4 = (f32[4,128,128]{2,1,0:T(8,128)S(1)}, f32[4,128,128]{2,1,0:T(8,128)S(1)}) custom-call(s32[8]{0:T(128)S(1)} %copy-done.4, f32[4,128,128]{2,1,0:T(8,128)S(1)} %collective-permute-done.7.rest_0_, bf16[1056,128]{1,0:T(8,128)(2,1)S(1)} %collective-permute-done.4.rest_1_, bf16[1040,128]{1,0:T(8,128)(2,1)S(1)} %collective-permute-done.5.rest_2_, ...), custom_call_target="tpu_custom_call" | custom-call | bytes 1024 | tf_op jit(solution)/shard_map/join/pallas_call | solution.py:282
  20.9 0.2 collective-permute-done.6.got
  21.1 1.3 %carry.2 = (bf16[3,128,512]{2,1,0:T(8,128)(2,1)S(1)}, bf16[3,128,512]{2,1,0:T(8,128)(2,1)S(1)}) custom-call(s32[8]{0:T(128)S(1)} %copy-done.4, bf16[256,2048]{1,0:T(8,128)(2,1)S(1)} %copy-done, bf16[256,2048]{1,0:T(8,128)(2,1)S(1)} %copy-done.1, bf16[256,2048]{1,0:T(8,128)(2,1)S(1)} %copy-done.2, f32[3,256,512]{2,1,0:T(8,128)S(1)} %get-tuple-element.48.near, ...), custom_call_target="tpu_custom_call" | custom-call | bytes 1024 | tf_op jit(solution)/shard_map/carry/pallas_call | solution.py:282
  22.4 1.6 %collective-permute-start.10 = (bf16[3,128,512]{2,1,0:T(8,128)(2,1)S(1)}, bf16[3,128,512]{2,1,0:T(8,128)(2,1)S(1)}, u32[]{:S(2)}, u32[]{:S(2)}) collective-permute-start(bf16[3,128,512]{2,1,0:T(8,128)(2,1)S(1)} %get-tuple-element.61), channel_id=1, source_target_pairs={{0,1},{1,0},{2,3},{3,2},{4,5},{5,4},{6,7},{7,6},{8,9},{9,8},{10,11... | collective-permute-start | bytes 1179656 | tf_op jit(solution)/shard_map/ppermute | solution.py:301
  23.9 0.1 collective-permute-start.13
  24.0 0.0 collective-permute-done.1.got
  24.0 0.6 %pair.3 = (bf16[1056,128]{1,0:T(8,128)(2,1)S(1)}, bf16[1040,128]{1,0:T(8,128)(2,1)S(1)}) custom-call(s32[8]{0:T(128)S(1)} %copy-done.4, f32[8,128,128]{2,1,0:T(8,128)S(1)} %get-tuple-element.46.kept, f32[8,128,128]{2,1,0:T(8,128)S(1)} %collective-permute-done.1.got, bf16[3,128,512]{2,1,0:T(8,128)(2,1)S(1)} %get-tuple-element.58.rest_0_.refs_0_), custom_call_target="tpu_custom_call" | custom-call | bytes 1024 | tf_op jit(solution)/shard_map/pair/pallas_call | solution.py:282
  24.7 2.9 %collective-permute-start.8 = (bf16[1056,128]{1,0:T(8,128)(2,1)S(1)}, bf16[1056,128]{1,0:T(8,128)(2,1)S(1)}, u32[]{:S(2)}, u32[]{:S(2)}) collective-permute-start(bf16[1056,128]{1,0:T(8,128)(2,1)S(1)} %get-tuple-element.59), channel_id=1, source_target_pairs={{0,6},{4,10},{8,14},{12,18},{16,22},{20,26},{24,30},{6,0},{10,4},{... | collective-permute-start | bytes 811016 | tf_op jit(solution)/shard_map/ppermute | solution.py:295
  27.5 3.0 %collective-permute-start.9 = (bf16[1040,128]{1,0:T(8,128)(2,1)S(1)}, bf16[1040,128]{1,0:T(8,128)(2,1)S(1)}, u32[]{:S(2)}, u32[]{:S(2)}) collective-permute-start(bf16[1040,128]{1,0:T(8,128)(2,1)S(1)} %get-tuple-element.60), channel_id=1, source_target_pairs={{0,10},{4,14},{8,18},{12,22},{16,26},{20,30},{10,0},{14,4},{18,8},... | collective-permute-start | bytes 798728 | tf_op jit(solution)/shard_map/ppermute | solution.py:295
  30.5 0.0 collective-permute-done.13.got
  30.5 1.3 %carry.3 = (bf16[3,128,512]{2,1,0:T(8,128)(2,1)S(1)}, bf16[3,128,512]{2,1,0:T(8,128)(2,1)S(1)}) custom-call(s32[8]{0:T(128)S(1)} %copy-done.4, bf16[256,2048]{1,0:T(8,128)(2,1)S(1)} %copy-done, bf16[256,2048]{1,0:T(8,128)(2,1)S(1)} %copy-done.1, bf16[256,2048]{1,0:T(8,128)(2,1)S(1)} %copy-done.2, f32[3,256,512]{2,1,0:T(8,128)S(1)} %get-tuple-element.66.near, ...), custom_call_target="tpu_custom_call" | custom-call | bytes 1024 | tf_op jit(solution)/shard_map/carry/pallas_call | solution.py:282
  31.8 0.6 collective-permute-start.14
  32.4 0.0 collective-permute-done.rest_0_.rest_1_
  32.4 3.2 %collective-permute-done.9.rest_3_ = bf16[1040,128]{1,0:T(8,128)(2,1)S(1)} collective-permute-done((bf16[1040,128]{1,0:T(8,128)(2,1)S(1)}, bf16[1040,128]{1,0:T(8,128)(2,1)S(1)}, u32[]{:S(2)}, u32[]{:S(2)}) %collective-permute-start.9) | collective-permute-done | bytes 266272 | tf_op jit(solution)/shard_map/ppermute | solution.py:295
  35.6 0.0 collective-permute-done.8.rest_2_
  35.6 0.0 collective-permute-done.10.rest_4_.refs_2_
  35.6 0.7 %join.5 = (f32[4,128,128]{2,1,0:T(8,128)S(1)}, f32[4,128,128]{2,1,0:T(8,128)S(1)}, f32[4,128,128]{2,1,0:T(8,128)S(1)}, f32[4,128,128]{2,1,0:T(8,128)S(1)}) custom-call(s32[8]{0:T(128)S(1)} %copy-done.4, f32[8,128,128]{2,1,0:T(8,128)S(1)} %collective-permute-done.rest_0_.rest_1_, f32[8,128,128]{2,1,0:T(8,128)S(1)} %collective-permute-done.rest_0_.rest_1_, ...), custom_call_target="tpu_custom_call" | custom-call | bytes 1024 | tf_op jit(solution)/shard_map/join/pallas_call | solution.py:282
  36.4 0.1 collective-permute-start.12
  36.4 0.5 collective-permute-start.11
  36.9 1.0 %collective-permute-done.12.got = f32[4,128,128]{2,1,0:T(8,128)S(1)} collective-permute-done((f32[4,128,128]{2,1,0:T(8,128)S(1)}, f32[4,128,128]{2,1,0:T(8,128)S(1)}, u32[]{:S(2)}, u32[]{:S(2)}) %collective-permute-start.12) | collective-permute-done | bytes 262176 | tf_op jit(solution)/shard_map/ppermute | solution.py:289
  38.0 2.2 %grads.2 = (bf16[3,128,512]{2,1,0:T(8,128)(2,1)S(1)}, bf16[3,128,512]{2,1,0:T(8,128)(2,1)S(1)}) custom-call(s32[8]{0:T(128)S(1)} %copy-done.4, bf16[256,2048]{1,0:T(8,128)(2,1)S(1)} %copy-done.3, bf16[256,2048]{1,0:T(8,128)(2,1)S(1)} %copy-done, bf16[256,2048]{1,0:T(8,128)(2,1)S(1)} %copy-done.1, bf16[256,2048]{1,0:T(8,128)(2,1)S(1)} %copy-done.2, ...), custom_call_target="tpu_custom_call" | custom-call | bytes 1024 | tf_op jit(solution)/shard_map/grads/pallas_call | solution.py:282
  40.1 0.6 collective-permute-start.16
  40.7 1.5 %collective-permute-done.14.rest_1_.refs_1_ = bf16[3,128,512]{2,1,0:T(8,128)(2,1)S(1)} collective-permute-done((bf16[3,128,512]{2,1,0:T(8,128)(2,1)S(1)}, bf16[3,128,512]{2,1,0:T(8,128)(2,1)S(1)}, u32[]{:S(2)}, u32[]{:S(2)}) %collective-permute-start.14) | collective-permute-done | bytes 393248 | tf_op jit(solution)/shard_map/ppermute | solution.py:301
  42.3 0.0 collective-permute-done.11.got
  42.3 2.2 %grads.3 = (bf16[3,128,512]{2,1,0:T(8,128)(2,1)S(1)}, bf16[3,128,512]{2,1,0:T(8,128)(2,1)S(1)}) custom-call(s32[8]{0:T(128)S(1)} %copy-done.4, bf16[256,2048]{1,0:T(8,128)(2,1)S(1)} %copy-done.3, bf16[256,2048]{1,0:T(8,128)(2,1)S(1)} %copy-done, bf16[256,2048]{1,0:T(8,128)(2,1)S(1)} %copy-done.1, bf16[256,2048]{1,0:T(8,128)(2,1)S(1)} %copy-done.2, ...), custom_call_target="tpu_custom_call" | custom-call | bytes 1024 | tf_op jit(solution)/shard_map/grads/pallas_call | solution.py:282
  44.4 1.8 %collective-permute-start.15 = (bf16[3,128,512]{2,1,0:T(8,128)(2,1)S(1)}, bf16[3,128,512]{2,1,0:T(8,128)(2,1)S(1)}, u32[]{:S(2)}, u32[]{:S(2)}) collective-permute-start(bf16[3,128,512]{2,1,0:T(8,128)(2,1)S(1)} %get-tuple-element.71), channel_id=1, source_target_pairs={{0,1},{1,0},{2,3},{3,2},{4,5},{5,4},{6,7},{7,6},{8,9},{9,8},{10,11... | collective-permute-start | bytes 1179656 | tf_op jit(solution)/shard_map/ppermute | solution.py:301
  46.2 1.1 %place.4 = (bf16[128,4096]{1,0:T(8,128)(2,1)}, bf16[128,4096]{1,0:T(8,128)(2,1)}, bf16[128,4096]{1,0:T(8,128)(2,1)}) custom-call(bf16[3,128,512]{2,1,0:T(8,128)(2,1)S(1)} %get-tuple-element.58.rest_0_.refs_0_, bf16[3,128,512]{2,1,0:T(8,128)(2,1)S(1)} %get-tuple-element.68.rest_0_.refs_1_, bf16[3,128,512]{2,1,0:T(8,128)(2,1)S(1)} %collective-permute-done.10.rest_4_.refs_2_), custom_call_target="tpu_custom_call" | custom-call | bytes 1024 | tf_op jit(solution)/shard_map/place/pallas_call | solution.py:401
  47.3 0.9 %place.5 = (bf16[128,4096]{1,0:T(8,128)(2,1)}, bf16[128,4096]{1,0:T(8,128)(2,1)}, bf16[128,4096]{1,0:T(8,128)(2,1)}) custom-call(bf16[3,128,512]{2,1,0:T(8,128)(2,1)S(1)} %get-tuple-element.69.rest_0_.refs_0_, bf16[3,128,512]{2,1,0:T(8,128)(2,1)S(1)} %collective-permute-done.14.rest_1_.refs_1_, ...), custom_call_target="tpu_custom_call", output_to_operand_aliasing={{0}: (2, {}), {1}: (3, {}), {2}: (4, {})} | custom-call | bytes 1024 | tf_op jit(solution)/shard_map/place/pallas_call | solution.py:401
  48.2 3.9 %collective-permute-done.16.refs_1_ = bf16[3,128,512]{2,1,0:T(8,128)(2,1)S(1)} collective-permute-done((bf16[3,128,512]{2,1,0:T(8,128)(2,1)S(1)}, bf16[3,128,512]{2,1,0:T(8,128)(2,1)S(1)}, u32[]{:S(2)}, u32[]{:S(2)}) %collective-permute-start.16) | collective-permute-done | bytes 393248 | tf_op jit(solution)/shard_map/ppermute | solution.py:301
  52.2 0.9 %place.6 = (bf16[128,4096]{1,0:T(8,128)(2,1)}, bf16[128,4096]{1,0:T(8,128)(2,1)}, bf16[128,4096]{1,0:T(8,128)(2,1)}) custom-call(bf16[3,128,512]{2,1,0:T(8,128)(2,1)S(1)} %get-tuple-element.72.refs_0_, bf16[3,128,512]{2,1,0:T(8,128)(2,1)S(1)} %collective-permute-done.16.refs_1_, ...), custom_call_target="tpu_custom_call", output_to_operand_aliasing={{0}: (2, {}), {1}: (3, {}), {2}: (4, {})} | custom-call | bytes 1024 | tf_op jit(solution)/shard_map/place/pallas_call | solution.py:401
  53.1 6.7 %collective-permute-done.15.refs_0_ = bf16[3,128,512]{2,1,0:T(8,128)(2,1)S(1)} collective-permute-done((bf16[3,128,512]{2,1,0:T(8,128)(2,1)S(1)}, bf16[3,128,512]{2,1,0:T(8,128)(2,1)S(1)}, u32[]{:S(2)}, u32[]{:S(2)}) %collective-permute-start.15) | collective-permute-done | bytes 393248 | tf_op jit(solution)/shard_map/ppermute | solution.py:301
  59.8 0.8 %place.7 = (bf16[128,4096]{1,0:T(8,128)(2,1)}, bf16[128,4096]{1,0:T(8,128)(2,1)}, bf16[128,4096]{1,0:T(8,128)(2,1)}) custom-call(bf16[3,128,512]{2,1,0:T(8,128)(2,1)S(1)} %collective-permute-done.15.refs_0_, bf16[128,4096]{1,0:T(8,128)(2,1)} %get-tuple-element.80.refs_1_, ...), custom_call_target="tpu_custom_call", output_to_operand_aliasing={{0}: (1, {}), {1}: (2, {}), {2}: (3, {})} | custom-call | bytes 1024 | tf_op jit(solution)/shard_map/place/pallas_call | solution.py:401
Async XLA Ops:
  0.6 0.7 %copy-start.4 = (s32[8]{0:T(128)S(1)}, s32[8]{0:T(128)}, u32[]{:S(2)}) copy-start(s32[8]{0:T(128)} %lengths.27) | copy-start | bytes 100
  2.9 2.3 %collective-permute-start.2 = (f32[8,128,128]{2,1,0:T(8,128)S(1)}, f32[8,128,128]{2,1,0:T(8,128)S(1)}, u32[]{:S(2)}, u32[]{:S(2)}) collective-permute-start(f32[8,128,128]{2,1,0:T(8,128)S(1)} %states.5), channel_id=1, source_target_pairs={{0,2},{2,0},{4,6},{6,4},{8,10},{10,8},{12,14},{14,12},{16,18},{18,... | collective-permute-start | bytes 1572872 | tf_op jit(solution)/shard_map/ppermute | solution.py:289
  3.5 10.2 %copy-start.1 = (bf16[256,2048]{1,0:T(8,128)(2,1)S(1)}, bf16[256,2048]{1,0:T(8,128)(2,1)}, u32[]{:S(2)}) copy-start(bf16[256,2048]{1,0:T(8,128)(2,1)} %v.17) | copy-start | bytes 3145732
  3.5 10.2 %copy-start.2 = (bf16[256,2048]{1,0:T(8,128)(2,1)S(1)}, bf16[256,2048]{1,0:T(8,128)(2,1)}, u32[]{:S(2)}) copy-start(bf16[256,2048]{1,0:T(8,128)(2,1)} %g.17) | copy-start | bytes 3145732
  3.5 10.2 %copy-start.3 = (bf16[256,2048]{1,0:T(8,128)(2,1)S(1)}, bf16[256,2048]{1,0:T(8,128)(2,1)}, u32[]{:S(2)}) copy-start(bf16[256,2048]{1,0:T(8,128)(2,1)} %q.13) | copy-start | bytes 3145732
  5.3 8.4 %copy-start = (bf16[256,2048]{1,0:T(8,128)(2,1)S(1)}, bf16[256,2048]{1,0:T(8,128)(2,1)}, u32[]{:S(2)}) copy-start(bf16[256,2048]{1,0:T(8,128)(2,1)} %k.17) | copy-start | bytes 3145732
  5.9 12.8 %collective-permute-start.4 = (bf16[1056,128]{1,0:T(8,128)(2,1)S(1)}, bf16[1056,128]{1,0:T(8,128)(2,1)S(1)}, u32[]{:S(2)}, u32[]{:S(2)}) collective-permute-start(bf16[1056,128]{1,0:T(8,128)(2,1)S(1)} %get-tuple-element.51), channel_id=1, source_target_pairs={{0,6},{4,10},{8,14},{12,18},{16,22},{20,26},{24,30},{6,0},{10,4},{... | collective-permute-start | bytes 811016 | tf_op jit(solution)/shard_map/ppermute | solution.py:295
  10.5 8.2 %collective-permute-start.5 = (bf16[1040,128]{1,0:T(8,128)(2,1)S(1)}, bf16[1040,128]{1,0:T(8,128)(2,1)S(1)}, u32[]{:S(2)}, u32[]{:S(2)}) collective-permute-start(bf16[1040,128]{1,0:T(8,128)(2,1)S(1)} %get-tuple-element.52), channel_id=1, source_target_pairs={{0,10},{4,14},{8,18},{12,22},{16,26},{20,30},{10,0},{14,4},{18,8},... | collective-permute-start | bytes 798728 | tf_op jit(solution)/shard_map/ppermute | solution.py:295
  13.5 5.2 %collective-permute-start.3 = (f32[4,128,128]{2,1,0:T(8,128)S(1)}, f32[4,128,128]{2,1,0:T(8,128)S(1)}, u32[]{:S(2)}, u32[]{:S(2)}) collective-permute-start(f32[4,128,128]{2,1,0:T(8,128)S(1)} %get-tuple-element.50), channel_id=1, source_target_pairs={{0,2},{2,0},{4,6},{6,4},{8,10},{10,8},{12,14},{14,12},{16,18},{18,... | collective-permute-start | bytes 786440 | tf_op jit(solution)/shard_map/ppermute | solution.py:289
  16.4 7.6 %collective-permute-start.1 = (f32[8,128,128]{2,1,0:T(8,128)S(1)}, f32[8,128,128]{2,1,0:T(8,128)S(1)}, u32[]{:S(2)}, u32[]{:S(2)}) collective-permute-start(f32[8,128,128]{2,1,0:T(8,128)S(1)} %get-tuple-element.47), channel_id=1, source_target_pairs={{0,2},{2,0},{4,6},{6,4},{8,10},{10,8},{12,14},{14,12},{16,18},{18,... | collective-permute-start | bytes 1572872 | tf_op jit(solution)/shard_map/ppermute | solution.py:289
  18.6 1.6 %collective-permute-start.7 = (f32[4,128,128]{2,1,0:T(8,128)S(1)}, f32[4,128,128]{2,1,0:T(8,128)S(1)}, u32[]{:S(2)}, u32[]{:S(2)}) collective-permute-start(f32[4,128,128]{2,1,0:T(8,128)S(1)} %get-tuple-element.56), channel_id=1, source_target_pairs={{0,2},{2,0},{4,6},{6,4},{8,10},{10,8},{12,14},{14,12},{16,18},{18,... | collective-permute-start | bytes 786440 | tf_op jit(solution)/shard_map/ppermute | solution.py:289
  19.4 1.7 %collective-permute-start.6 = (f32[4,128,128]{2,1,0:T(8,128)S(1)}, f32[4,128,128]{2,1,0:T(8,128)S(1)}, u32[]{:S(2)}, u32[]{:S(2)}) collective-permute-start(f32[4,128,128]{2,1,0:T(8,128)S(1)} %get-tuple-element.55), channel_id=1, source_target_pairs={{0,2},{2,0},{4,6},{6,4},{8,10},{10,8},{12,14},{14,12},{16,18},{18,... | collective-permute-start | bytes 786440 | tf_op jit(solution)/shard_map/ppermute | solution.py:289
  19.9 12.5 %collective-permute-start = (f32[8,128,128]{2,1,0:T(8,128)S(1)}, f32[8,128,128]{2,1,0:T(8,128)S(1)}, u32[]{:S(2)}, u32[]{:S(2)}) collective-permute-start(f32[8,128,128]{2,1,0:T(8,128)S(1)} %get-tuple-element.46.kept), channel_id=1, source_target_pairs={{0,2},{2,0},{4,6},{6,4},{8,10},{10,8},{12,14},{14,12},{16,18},{18,... | collective-permute-start | bytes 1572872 | tf_op jit(solution)/shard_map/ppermute | solution.py:289
  22.4 13.3 %collective-permute-start.10 = (bf16[3,128,512]{2,1,0:T(8,128)(2,1)S(1)}, bf16[3,128,512]{2,1,0:T(8,128)(2,1)S(1)}, u32[]{:S(2)}, u32[]{:S(2)}) collective-permute-start(bf16[3,128,512]{2,1,0:T(8,128)(2,1)S(1)} %get-tuple-element.61), channel_id=1, source_target_pairs={{0,1},{1,0},{2,3},{3,2},{4,5},{5,4},{6,7},{7,6},{8,9},{9,8},{10,11... | collective-permute-start | bytes 1179656 | tf_op jit(solution)/shard_map/ppermute | solution.py:301
  23.9 6.6 %collective-permute-start.13 = (f32[4,128,128]{2,1,0:T(8,128)S(1)}, f32[4,128,128]{2,1,0:T(8,128)S(1)}, u32[]{:S(2)}, u32[]{:S(2)}) collective-permute-start(f32[4,128,128]{2,1,0:T(8,128)S(1)} %get-tuple-element.67), channel_id=1, source_target_pairs={{0,2},{2,0},{4,6},{6,4},{8,10},{10,8},{12,14},{14,12},{16,18},{18,... | collective-permute-start | bytes 786440 | tf_op jit(solution)/shard_map/ppermute | solution.py:289
  24.7 11.0 %collective-permute-start.8 = (bf16[1056,128]{1,0:T(8,128)(2,1)S(1)}, bf16[1056,128]{1,0:T(8,128)(2,1)S(1)}, u32[]{:S(2)}, u32[]{:S(2)}) collective-permute-start(bf16[1056,128]{1,0:T(8,128)(2,1)S(1)} %get-tuple-element.59), channel_id=1, source_target_pairs={{0,6},{4,10},{8,14},{12,18},{16,22},{20,26},{24,30},{6,0},{10,4},{... | collective-permute-start | bytes 811016 | tf_op jit(solution)/shard_map/ppermute | solution.py:295
  27.5 8.1 %collective-permute-start.9 = (bf16[1040,128]{1,0:T(8,128)(2,1)S(1)}, bf16[1040,128]{1,0:T(8,128)(2,1)S(1)}, u32[]{:S(2)}, u32[]{:S(2)}) collective-permute-start(bf16[1040,128]{1,0:T(8,128)(2,1)S(1)} %get-tuple-element.60), channel_id=1, source_target_pairs={{0,10},{4,14},{8,18},{12,22},{16,26},{20,30},{10,0},{14,4},{18,8},... | collective-permute-start | bytes 798728 | tf_op jit(solution)/shard_map/ppermute | solution.py:295
  31.8 10.4 %collective-permute-start.14 = (bf16[3,128,512]{2,1,0:T(8,128)(2,1)S(1)}, bf16[3,128,512]{2,1,0:T(8,128)(2,1)S(1)}, u32[]{:S(2)}, u32[]{:S(2)}) collective-permute-start(bf16[3,128,512]{2,1,0:T(8,128)(2,1)S(1)} %get-tuple-element.70), channel_id=1, source_target_pairs={{0,1},{1,0},{2,3},{3,2},{4,5},{5,4},{6,7},{7,6},{8,9},{9,8},{10,11... | collective-permute-start | bytes 1179656 | tf_op jit(solution)/shard_map/ppermute | solution.py:301
  36.4 1.6 %collective-permute-start.12 = (f32[4,128,128]{2,1,0:T(8,128)S(1)}, f32[4,128,128]{2,1,0:T(8,128)S(1)}, u32[]{:S(2)}, u32[]{:S(2)}) collective-permute-start(f32[4,128,128]{2,1,0:T(8,128)S(1)} %get-tuple-element.65), channel_id=1, source_target_pairs={{0,2},{2,0},{4,6},{6,4},{8,10},{10,8},{12,14},{14,12},{16,18},{18,... | collective-permute-start | bytes 786440 | tf_op jit(solution)/shard_map/ppermute | solution.py:289
  36.4 5.8 %collective-permute-start.11 = (f32[4,128,128]{2,1,0:T(8,128)S(1)}, f32[4,128,128]{2,1,0:T(8,128)S(1)}, u32[]{:S(2)}, u32[]{:S(2)}) collective-permute-start(f32[4,128,128]{2,1,0:T(8,128)S(1)} %get-tuple-element.63), channel_id=1, source_target_pairs={{0,2},{2,0},{4,6},{6,4},{8,10},{10,8},{12,14},{14,12},{16,18},{18,... | collective-permute-start | bytes 786440 | tf_op jit(solution)/shard_map/ppermute | solution.py:289
  40.1 12.0 %collective-permute-start.16 = (bf16[3,128,512]{2,1,0:T(8,128)(2,1)S(1)}, bf16[3,128,512]{2,1,0:T(8,128)(2,1)S(1)}, u32[]{:S(2)}, u32[]{:S(2)}) collective-permute-start(bf16[3,128,512]{2,1,0:T(8,128)(2,1)S(1)} %get-tuple-element.73), channel_id=1, source_target_pairs={{0,1},{1,0},{2,3},{3,2},{4,5},{5,4},{6,7},{7,6},{8,9},{9,8},{10,11... | collective-permute-start | bytes 1179656 | tf_op jit(solution)/shard_map/ppermute | solution.py:301
  44.4 15.3 %collective-permute-start.15 = (bf16[3,128,512]{2,1,0:T(8,128)(2,1)S(1)}, bf16[3,128,512]{2,1,0:T(8,128)(2,1)S(1)}, u32[]{:S(2)}, u32[]{:S(2)}) collective-permute-start(bf16[3,128,512]{2,1,0:T(8,128)(2,1)S(1)} %get-tuple-element.71), channel_id=1, source_target_pairs={{0,1},{1,0},{2,3},{3,2},{4,5},{5,4},{6,7},{7,6},{8,9},{9,8},{10,11... | collective-permute-start | bytes 1179656 | tf_op jit(solution)/shard_map/ppermute | solution.py:301

commit v8 on v4

--- a/solution.py
+++ b/solution.py
@@ -239,6 +239,29 @@
     deal(done, outs, rows, groups)
 
 
+def carry_rows_kernel(lengths, k, v, g, near, mine, got, *rest, ndocs, rows, offset, heads, groups, shifts):
+    outs = rest[-len(shifts):]
+    place, column, part = lax.axis_index("seq"), lax.axis_index("head"), rows // groups
+    first_core = lax.rem(place, 2) == 0
+    _, _, _, _, first, last = block_range(lengths, ndocs, place * rows, rows)
+    order = lax.broadcasted_iota(jnp.int32, (part, HEAD_DIM), 0)
+    for j, out in zip(shifts, outs):
+        start = pl.multiple_of(lax.rem(column + j, groups) * part, part)
+        lines = pl.ds(start, part)
+        first_rows, last_rows = order + start < first, order + start >= last
+        for h in range(heads):
+            cols = slice(h * HEAD_DIM, (h + 1) * HEAD_DIM)
+            at = slice(offset + h * HEAD_DIM, offset + (h + 1) * HEAD_DIM)
+            state = split(jnp.where(first_core, got[h], mine[h]), 1)
+            grad = jnp.where(first_core, mine[h], got[h])
+            k2, v2, g2 = (jnp.concatenate([ref[lines, at]] * 2, axis=1) for ref in (k, v, g))
+            carry_q = jnp.where(first_rows, dot(g2, state, NT), 0.0)
+            carry_k = jnp.where(last_rows, dot(v2, split(grad, 1), NT), 0.0)
+            carry_v = jnp.where(last_rows, dot(k2, split(grad, 0), NN), 0.0)
+            for i, value in enumerate((carry_q, carry_k, carry_v)):
+                out[i, :, cols] = (near[i, lines, cols] + value).astype(jnp.bfloat16)
+
+
 def place_kernel(*refs, groups, plan, width):
     parts, outs, sems = refs[:len(plan)], refs[-4:-1], refs[-1]
     column = lax.axis_index("head")
@@ -360,6 +383,13 @@
             [pltpu.VMEM((3, rows, cw), bf16)], after, GRAD_LIMIT,
         )
 
+    def carry_rows(shifts, near, offset, cw, mine, theirs, after):
+        kernel = functools.partial(
+            carry_rows_kernel, offset=offset, heads=cw // HEAD_DIM, groups=groups, shifts=shifts, **sizes
+        )
+        outs = [shape_of(3, part, cw, dtype=bf16)] * len(shifts)
+        return call("carry", kernel, (*inputs[1:], near, mine, theirs), outs, after=after, limit=GRAD_LIMIT)
+
     cuts, outs, arrived, totals, masks = [], [], [], [], None
     for start, half, chunks in halves:
         if not totals:
@@ -368,7 +398,7 @@
         else:
             kept, sent = late_states(start, half, [token])
         total, came, others = pair_up(
-            kept, swap_cores(sent), 0 if totals else len(chunks), [made[0] for made in outs[:1]]
+            kept, swap_cores(sent), 0 if totals else len(chunks), [made[-1] for made in outs[:1]]
         )
         if not totals:
             near = [local(masks, *chunk) for chunk in chunks]
@@ -383,12 +413,17 @@
                 joined += join([(0, c * count, count)], others[c:c + 1], came, after)
                 after = [joined[-1][0]]
         for c, ((offset, cw), (mine, theirs)) in enumerate(zip(chunks, joined)):
-            after = [made[0] for made in outs[-1:]] + [parts[1] for parts in arrived[1:-1]][-1:]
+            after = [made[-1] for made in outs[-1:]] + [parts[1] for parts in arrived[1:-1]][-1:]
             if totals:
                 outs.append(grads(masks, offset, cw, mine, theirs, after))
+            elif c == 0:
+                first = (near[0][0], offset, cw, mine, theirs)
+                outs.append([None, *carry_rows(range(1, groups), *first, [made for made, _ in joined[1:]])])
             else:
                 outs.append(carry(near[c][0], offset, cw, mine, theirs, after))
             arrived.append(send_rows(outs[-1]))
+        if not totals:
+            arrived[0][0] = carry_rows([0], *first, [outs[-1][-1]])[0]
         totals = [total]
         cuts += chunks
 

time: 61.5 us -> 60.4 us (0.982)
  waiting for transfers between devices: 17.6 us -> 15.8 us
    ppermute x4, waiting for transfers between devices: 12.4 us -> 11.2 us  [send_rows(): lax.ppermute(outs[j], 'head', [(x, (x + j) % groups) for x in range(group...]
    pallas_call x12 -> x13, Pallas kernels: 14.6 us -> 15.2 us  [call(): pl.pallas_call(kernel, in_specs=[in_smem] + [in_vmem] * len(args) + [anyw...]
  transfers between devices with their start and end apart: 17 -> 17, of which waited for: 6 -> 7; matrix products, arithmetic and copies ran while one was open for 0% -> 0% of each run, Pallas kernels for 30% -> 32%
where the time goes in v8:
time: 60.4 us; the launch traced here: 60.2 us
  Pallas kernels  22.3 us (37%)
  starting transfers between devices  20.5 us (34%)
  waiting for transfers between devices  15.8 us (26%)
  between operations  0.87 us (1%)
  local copies, waits for them, and re-layouts  0.67 us (1%)
    pallas_call x13, Pallas kernels, call(): pl.pallas_call(kernel, in_specs=[in_smem] + [in_vmem] * len(args) + [anyw...  15.2 us
    ppermute x4, starting transfers between devices, swap_pairs(): lax.ppermute(sent[hop - 1], 'seq', perm + [(b, a) for a, b in perm])  13.4 us
    ppermute x4, waiting for transfers between devices, send_rows(): lax.ppermute(outs[j], 'head', [(x, (x + j) % groups) for x in range(group...  11.2 us
    ppermute x4, starting transfers between devices, send_rows(): lax.ppermute(outs[j], 'head', [(x, (x + j) % groups) for x in range(group...  4.58 us
    pallas_call x4, Pallas kernels, shards(): pl.pallas_call(functools.partial(place_kernel, groups=groups, plan=[where...  3.71 us
    pallas_call x2, Pallas kernels, states(): pl.pallas_call(functools.partial(state_kernel, offset=offset, heads=heads...  3.44 us
    ppermute x4, waiting for transfers between devices, swap_pairs(): lax.ppermute(sent[hop - 1], 'seq', perm + [(b, a) for a, b in perm])  3.19 us
    ppermute x9, starting transfers between devices, swap_cores(): return lax.ppermute(a, 'seq', [(b, b ^ 1) for b in range(seq)])  2.49 us
  transfers between devices with their start and end apart: 17, of which 7 were waited for; matrix products, arithmetic and copies ran while one was open for 0% of the time, Pallas kernels for 32%

profile of v8, /device:TPU:0, one launch (start us, length us, event | category | flops | bytes accessed | tf_op | source)
XLA Modules:
  0.0 60.2 jit_solution(8685886849965534738)
XLA Ops:
  0.6 0.0 copy-start.4
  0.6 0.6 %copy-done.4 = s32[8]{0:T(128)S(1)} copy-done((s32[8]{0:T(128)S(1)}, s32[8]{0:T(128)}, u32[]{:S(2)}) %copy-start.4) | copy-done | bytes 56
  1.3 1.6 %states.5 = f32[8,128,128]{2,1,0:T(8,128)S(1)} custom-call(s32[8]{0:T(128)S(1)} %copy-done.4, bf16[256,2048]{1,0:T(8,128)(2,1)} %q.13, bf16[256,2048]{1,0:T(8,128)(2,1)} %k.19, bf16[256,2048]{1,0:T(8,128)(2,1)} %v.19, bf16[256,2048]{1,0:T(8,128)(2,1)} %g.19), custom_call_target="tpu_custom_call" | custom-call | bytes 1024 | tf_op jit(solution)/shard_map/states/pallas_call | solution.py:333
  2.9 0.5 collective-permute-start.2
  3.5 0.0 copy-start.1
  3.5 0.0 copy-start.2
  3.5 0.0 copy-start.3
  3.5 1.8 %states.3 = (f32[8,128,128]{2,1,0:T(8,128)S(1)}, bf16[256,256]{1,0:T(8,128)(2,1)S(1)}, bf16[256,256]{1,0:T(8,128)(2,1)S(1)}) custom-call(s32[8]{0:T(128)S(1)} %copy-done.4, bf16[256,2048]{1,0:T(8,128)(2,1)} %q.13, bf16[256,2048]{1,0:T(8,128)(2,1)} %k.19, bf16[256,2048]{1,0:T(8,128)(2,1)} %v.19, bf16[256,2048]{1,0:T(8,128)(2,1)} %g.19), custom_call_target="tpu_custom_call" | custom-call | bytes 1024 | tf_op jit(solution)/shard_map/states/pallas_call | solution.py:333
  5.3 0.0 copy-start
  5.3 0.0 collective-permute-done.2.got
  5.3 0.6 %pair.2 = (bf16[1056,128]{1,0:T(8,128)(2,1)S(1)}, bf16[1040,128]{1,0:T(8,128)(2,1)S(1)}, f32[4,128,128]{2,1,0:T(8,128)S(1)}, f32[4,128,128]{2,1,0:T(8,128)S(1)}) custom-call(s32[8]{0:T(128)S(1)} %copy-done.4, f32[8,128,128]{2,1,0:T(8,128)S(1)} %get-tuple-element.47.kept, f32[8,128,128]{2,1,0:T(8,128)S(1)} %collective-permute-done.2.got), custom_call_target="tpu_custom_call" | custom-call | bytes 1024 | tf_op jit(solution)/shard_map/pair/pallas_call | solution.py:305
  5.9 4.5 %collective-permute-start.4 = (bf16[1056,128]{1,0:T(8,128)(2,1)S(1)}, bf16[1056,128]{1,0:T(8,128)(2,1)S(1)}, u32[]{:S(2)}, u32[]{:S(2)}) collective-permute-start(bf16[1056,128]{1,0:T(8,128)(2,1)S(1)} %get-tuple-element.49), channel_id=1, source_target_pairs={{0,6},{4,10},{8,14},{12,18},{16,22},{20,26},{24,30},{6,0},{10,4},{... | collective-permute-start | bytes 811016 | tf_op jit(solution)/shard_map/ppermute | solution.py:318
  10.5 3.0 %collective-permute-start.5 = (bf16[1040,128]{1,0:T(8,128)(2,1)S(1)}, bf16[1040,128]{1,0:T(8,128)(2,1)S(1)}, u32[]{:S(2)}, u32[]{:S(2)}) collective-permute-start(bf16[1040,128]{1,0:T(8,128)(2,1)S(1)} %get-tuple-element.50), channel_id=1, source_target_pairs={{0,10},{4,14},{8,18},{12,22},{16,26},{20,30},{10,0},{14,4},{18,8},... | collective-permute-start | bytes 798728 | tf_op jit(solution)/shard_map/ppermute | solution.py:318
  13.5 0.1 collective-permute-start.3
  13.6 0.0 copy-done.1
  13.6 0.0 copy-done.2
  13.6 0.0 copy-done.3
  13.7 0.0 copy-done
  13.7 1.6 %local.2 = (f32[3,256,512]{2,1,0:T(8,128)S(1)}, f32[8,128]{1,0:T(8,128)S(1)}) custom-call(s32[8]{0:T(128)S(1)} %copy-done.4, bf16[256,2048]{1,0:T(8,128)(2,1)S(1)} %copy-done.3, bf16[256,2048]{1,0:T(8,128)(2,1)S(1)} %copy-done, bf16[256,2048]{1,0:T(8,128)(2,1)S(1)} %copy-done.1, bf16[256,2048]{1,0:T(8,128)(2,1)S(1)} %copy-done.2, ...), custom_call_target="tpu_custom_call" | custom-call | bytes 1024 | tf_op jit(solution)/shard_map/local/pallas_call | solution.py:305
  15.3 1.2 %states.4 = (f32[8,128,128]{2,1,0:T(8,128)S(1)}, f32[8,128,128]{2,1,0:T(8,128)S(1)}) custom-call(s32[8]{0:T(128)S(1)} %copy-done.4, bf16[256,2048]{1,0:T(8,128)(2,1)S(1)} %copy-done.3, bf16[256,2048]{1,0:T(8,128)(2,1)S(1)} %copy-done, bf16[256,2048]{1,0:T(8,128)(2,1)S(1)} %copy-done.1, bf16[256,2048]{1,0:T(8,128)(2,1)S(1)} %copy-done.2, ...), custom_call_target="tpu_custom_call" | custom-call | bytes 1024 | tf_op jit(solution)/shard_map/states/pallas_call | solution.py:305
  16.4 0.5 collective-permute-start.1
  17.0 1.6 %local.3 = (f32[3,256,512]{2,1,0:T(8,128)S(1)}, f32[8,128]{1,0:T(8,128)S(1)}) custom-call(s32[8]{0:T(128)S(1)} %copy-done.4, bf16[256,2048]{1,0:T(8,128)(2,1)S(1)} %copy-done.3, bf16[256,2048]{1,0:T(8,128)(2,1)S(1)} %copy-done, bf16[256,2048]{1,0:T(8,128)(2,1)S(1)} %copy-done.1, bf16[256,2048]{1,0:T(8,128)(2,1)S(1)} %copy-done.2, ...), custom_call_target="tpu_custom_call" | custom-call | bytes 1024 | tf_op jit(solution)/shard_map/local/pallas_call | solution.py:305
  18.6 0.1 collective-permute-start.7
  18.7 0.0 collective-permute-done.3.rest_0_
  18.7 0.0 collective-permute-done.5.rest_2_
  18.7 0.0 collective-permute-done.4.rest_1_
  18.7 0.7 %join.3 = (f32[4,128,128]{2,1,0:T(8,128)S(1)}, f32[4,128,128]{2,1,0:T(8,128)S(1)}) custom-call(s32[8]{0:T(128)S(1)} %copy-done.4, f32[4,128,128]{2,1,0:T(8,128)S(1)} %collective-permute-done.3.rest_0_, bf16[1056,128]{1,0:T(8,128)(2,1)S(1)} %collective-permute-done.4.rest_1_, bf16[1040,128]{1,0:T(8,128)(2,1)S(1)} %collective-permute-done.5.rest_2_, ...), custom_call_target="tpu_custom_call" | custom-call | bytes 1024 | tf_op jit(solution)/shard_map/join/pallas_call | solution.py:305
  19.4 0.5 collective-permute-start.6
  19.9 0.1 collective-permute-start
  20.0 0.2 collective-permute-done.7.rest_0_
  20.2 0.6 %join.4 = (f32[4,128,128]{2,1,0:T(8,128)S(1)}, f32[4,128,128]{2,1,0:T(8,128)S(1)}) custom-call(s32[8]{0:T(128)S(1)} %copy-done.4, f32[4,128,128]{2,1,0:T(8,128)S(1)} %collective-permute-done.7.rest_0_, bf16[1056,128]{1,0:T(8,128)(2,1)S(1)} %collective-permute-done.4.rest_1_, bf16[1040,128]{1,0:T(8,128)(2,1)S(1)} %collective-permute-done.5.rest_2_, ...), custom_call_target="tpu_custom_call" | custom-call | bytes 1024 | tf_op jit(solution)/shard_map/join/pallas_call | solution.py:305
  20.9 0.2 collective-permute-done.6.got
  21.1 0.9 %carry.3.rest_0_ = bf16[3,128,512]{2,1,0:T(8,128)(2,1)S(1)} custom-call(s32[8]{0:T(128)S(1)} %copy-done.4, bf16[256,2048]{1,0:T(8,128)(2,1)S(1)} %copy-done, bf16[256,2048]{1,0:T(8,128)(2,1)S(1)} %copy-done.1, bf16[256,2048]{1,0:T(8,128)(2,1)S(1)} %copy-done.2, f32[3,256,512]{2,1,0:T(8,128)S(1)} %get-tuple-element.46.near, ...), custom_call_target="tpu_custom_call" | custom-call | bytes 1024 | tf_op jit(solution)/shard_map/carry/pallas_call | solution.py:305
  22.0 1.6 %collective-permute-start.10 = (bf16[3,128,512]{2,1,0:T(8,128)(2,1)S(1)}, bf16[3,128,512]{2,1,0:T(8,128)(2,1)S(1)}, u32[]{:S(2)}, u32[]{:S(2)}) collective-permute-start(bf16[3,128,512]{2,1,0:T(8,128)(2,1)S(1)} %carry.3.rest_0_), channel_id=1, source_target_pairs={{0,1},{1,0},{2,3},{3,2},{4,5},{5,4},{6,7},{7,6},{8,9},{9,8},{10,11... | collective-permute-start | bytes 1179656 | tf_op jit(solution)/shard_map/ppermute | solution.py:324
  23.6 0.1 collective-permute-start.13
  23.7 0.0 collective-permute-done.1.got
  23.7 0.6 %pair.3 = (bf16[1056,128]{1,0:T(8,128)(2,1)S(1)}, bf16[1040,128]{1,0:T(8,128)(2,1)S(1)}) custom-call(s32[8]{0:T(128)S(1)} %copy-done.4, f32[8,128,128]{2,1,0:T(8,128)S(1)} %get-tuple-element.44.kept, f32[8,128,128]{2,1,0:T(8,128)S(1)} %collective-permute-done.1.got, bf16[3,128,512]{2,1,0:T(8,128)(2,1)S(1)} %carry.3.rest_0_), custom_call_target="tpu_custom_call" | custom-call | bytes 1024 | tf_op jit(solution)/shard_map/pair/pallas_call | solution.py:305
  24.3 2.9 %collective-permute-start.8 = (bf16[1056,128]{1,0:T(8,128)(2,1)S(1)}, bf16[1056,128]{1,0:T(8,128)(2,1)S(1)}, u32[]{:S(2)}, u32[]{:S(2)}) collective-permute-start(bf16[1056,128]{1,0:T(8,128)(2,1)S(1)} %get-tuple-element.56), channel_id=1, source_target_pairs={{0,6},{4,10},{8,14},{12,18},{16,22},{20,26},{24,30},{6,0},{10,4},{... | collective-permute-start | bytes 811016 | tf_op jit(solution)/shard_map/ppermute | solution.py:318
  27.2 3.0 %collective-permute-start.9 = (bf16[1040,128]{1,0:T(8,128)(2,1)S(1)}, bf16[1040,128]{1,0:T(8,128)(2,1)S(1)}, u32[]{:S(2)}, u32[]{:S(2)}) collective-permute-start(bf16[1040,128]{1,0:T(8,128)(2,1)S(1)} %get-tuple-element.57), channel_id=1, source_target_pairs={{0,10},{4,14},{8,18},{12,22},{16,26},{20,30},{10,0},{14,4},{18,8},... | collective-permute-start | bytes 798728 | tf_op jit(solution)/shard_map/ppermute | solution.py:318
  30.2 0.0 collective-permute-done.13.got
  30.2 1.3 %carry.4 = (bf16[3,128,512]{2,1,0:T(8,128)(2,1)S(1)}, bf16[3,128,512]{2,1,0:T(8,128)(2,1)S(1)}) custom-call(s32[8]{0:T(128)S(1)} %copy-done.4, bf16[256,2048]{1,0:T(8,128)(2,1)S(1)} %copy-done, bf16[256,2048]{1,0:T(8,128)(2,1)S(1)} %copy-done.1, bf16[256,2048]{1,0:T(8,128)(2,1)S(1)} %copy-done.2, f32[3,256,512]{2,1,0:T(8,128)S(1)} %get-tuple-element.62.near, ...), custom_call_target="tpu_custom_call" | custom-call | bytes 1024 | tf_op jit(solution)/shard_map/carry/pallas_call | solution.py:305
  31.5 0.6 %collective-permute-start.14 = (bf16[3,128,512]{2,1,0:T(8,128)(2,1)S(1)}, bf16[3,128,512]{2,1,0:T(8,128)(2,1)S(1)}, u32[]{:S(2)}, u32[]{:S(2)}) collective-permute-start(bf16[3,128,512]{2,1,0:T(8,128)(2,1)S(1)} %get-tuple-element.64.rest_0_), channel_id=1, source_target_pairs={{0,1},{1,0},{2,3},{3,2},{4,5},{5,4},{6,7},{7,6},{8,9},{9,8},{10,11... | collective-permute-start | bytes 1179656 | tf_op jit(solution)/shard_map/ppermute | solution.py:324
  32.1 0.0 collective-permute-done.rest_0_.rest_1_
  32.1 3.2 %collective-permute-done.9.rest_3_ = bf16[1040,128]{1,0:T(8,128)(2,1)S(1)} collective-permute-done((bf16[1040,128]{1,0:T(8,128)(2,1)S(1)}, bf16[1040,128]{1,0:T(8,128)(2,1)S(1)}, u32[]{:S(2)}, u32[]{:S(2)}) %collective-permute-start.9) | collective-permute-done | bytes 266272 | tf_op jit(solution)/shard_map/ppermute | solution.py:318
  35.3 0.0 collective-permute-done.8.rest_2_
  35.3 0.0 collective-permute-done.10.rest_4_.refs_2_
  35.3 0.7 %join.5 = (f32[4,128,128]{2,1,0:T(8,128)S(1)}, f32[4,128,128]{2,1,0:T(8,128)S(1)}, f32[4,128,128]{2,1,0:T(8,128)S(1)}, f32[4,128,128]{2,1,0:T(8,128)S(1)}) custom-call(s32[8]{0:T(128)S(1)} %copy-done.4, f32[8,128,128]{2,1,0:T(8,128)S(1)} %collective-permute-done.rest_0_.rest_1_, f32[8,128,128]{2,1,0:T(8,128)S(1)} %collective-permute-done.rest_0_.rest_1_, ...), custom_call_target="tpu_custom_call" | custom-call | bytes 1024 | tf_op jit(solution)/shard_map/join/pallas_call | solution.py:305
  36.0 0.1 collective-permute-start.12
  36.1 0.5 collective-permute-start.11
  36.6 1.0 %collective-permute-done.12.got = f32[4,128,128]{2,1,0:T(8,128)S(1)} collective-permute-done((f32[4,128,128]{2,1,0:T(8,128)S(1)}, f32[4,128,128]{2,1,0:T(8,128)S(1)}, u32[]{:S(2)}, u32[]{:S(2)}) %collective-permute-start.12) | collective-permute-done | bytes 262176 | tf_op jit(solution)/shard_map/ppermute | solution.py:312
  37.6 2.2 %grads.2 = (bf16[3,128,512]{2,1,0:T(8,128)(2,1)S(1)}, bf16[3,128,512]{2,1,0:T(8,128)(2,1)S(1)}) custom-call(s32[8]{0:T(128)S(1)} %copy-done.4, bf16[256,2048]{1,0:T(8,128)(2,1)S(1)} %copy-done.3, bf16[256,2048]{1,0:T(8,128)(2,1)S(1)} %copy-done, bf16[256,2048]{1,0:T(8,128)(2,1)S(1)} %copy-done.1, bf16[256,2048]{1,0:T(8,128)(2,1)S(1)} %copy-done.2, ...), custom_call_target="tpu_custom_call" | custom-call | bytes 1024 | tf_op jit(solution)/shard_map/grads/pallas_call | solution.py:305
  39.7 0.6 %collective-permute-start.16 = (bf16[3,128,512]{2,1,0:T(8,128)(2,1)S(1)}, bf16[3,128,512]{2,1,0:T(8,128)(2,1)S(1)}, u32[]{:S(2)}, u32[]{:S(2)}) collective-permute-start(bf16[3,128,512]{2,1,0:T(8,128)(2,1)S(1)} %get-tuple-element.65.rest_0_), channel_id=1, source_target_pairs={{0,1},{1,0},{2,3},{3,2},{4,5},{5,4},{6,7},{7,6},{8,9},{9,8},{10,11... | collective-permute-start | bytes 1179656 | tf_op jit(solution)/shard_map/ppermute | solution.py:324
  40.4 1.6 %collective-permute-done.14.rest_1_.refs_1_ = bf16[3,128,512]{2,1,0:T(8,128)(2,1)S(1)} collective-permute-done((bf16[3,128,512]{2,1,0:T(8,128)(2,1)S(1)}, bf16[3,128,512]{2,1,0:T(8,128)(2,1)S(1)}, u32[]{:S(2)}, u32[]{:S(2)}) %collective-permute-start.14) | collective-permute-done | bytes 393248 | tf_op jit(solution)/shard_map/ppermute | solution.py:324
  41.9 0.0 collective-permute-done.11.got
  41.9 2.2 %grads.3 = (bf16[3,128,512]{2,1,0:T(8,128)(2,1)S(1)}, bf16[3,128,512]{2,1,0:T(8,128)(2,1)S(1)}) custom-call(s32[8]{0:T(128)S(1)} %copy-done.4, bf16[256,2048]{1,0:T(8,128)(2,1)S(1)} %copy-done.3, bf16[256,2048]{1,0:T(8,128)(2,1)S(1)} %copy-done, bf16[256,2048]{1,0:T(8,128)(2,1)S(1)} %copy-done.1, bf16[256,2048]{1,0:T(8,128)(2,1)S(1)} %copy-done.2, ...), custom_call_target="tpu_custom_call" | custom-call | bytes 1024 | tf_op jit(solution)/shard_map/grads/pallas_call | solution.py:305
  44.1 1.8 %collective-permute-start.15 = (bf16[3,128,512]{2,1,0:T(8,128)(2,1)S(1)}, bf16[3,128,512]{2,1,0:T(8,128)(2,1)S(1)}, u32[]{:S(2)}, u32[]{:S(2)}) collective-permute-start(bf16[3,128,512]{2,1,0:T(8,128)(2,1)S(1)} %get-tuple-element.66), channel_id=1, source_target_pairs={{0,1},{1,0},{2,3},{3,2},{4,5},{5,4},{6,7},{7,6},{8,9},{9,8},{10,11... | collective-permute-start | bytes 1179656 | tf_op jit(solution)/shard_map/ppermute | solution.py:324
  45.9 0.9 %carry.5.refs_0_ = bf16[3,128,512]{2,1,0:T(8,128)(2,1)S(1)} custom-call(s32[8]{0:T(128)S(1)} %copy-done.4, bf16[256,2048]{1,0:T(8,128)(2,1)S(1)} %copy-done, bf16[256,2048]{1,0:T(8,128)(2,1)S(1)} %copy-done.1, bf16[256,2048]{1,0:T(8,128)(2,1)S(1)} %copy-done.2, f32[3,256,512]{2,1,0:T(8,128)S(1)} %get-tuple-element.46.near, ...), custom_call_target="tpu_custom_call" | custom-call | bytes 1024 | tf_op jit(solution)/shard_map/carry/pallas_call | solution.py:305
  46.8 1.1 %place.4 = (bf16[128,4096]{1,0:T(8,128)(2,1)}, bf16[128,4096]{1,0:T(8,128)(2,1)}, bf16[128,4096]{1,0:T(8,128)(2,1)}) custom-call(bf16[3,128,512]{2,1,0:T(8,128)(2,1)S(1)} %carry.5.refs_0_, bf16[3,128,512]{2,1,0:T(8,128)(2,1)S(1)} %get-tuple-element.69.refs_1_, bf16[3,128,512]{2,1,0:T(8,128)(2,1)S(1)} %collective-permute-done.10.rest_4_.refs_2_), custom_call_target="tpu_custom_call" | custom-call | bytes 1024 | tf_op jit(solution)/shard_map/place/pallas_call | solution.py:436
  47.9 0.9 %place.5 = (bf16[128,4096]{1,0:T(8,128)(2,1)}, bf16[128,4096]{1,0:T(8,128)(2,1)}, bf16[128,4096]{1,0:T(8,128)(2,1)}) custom-call(bf16[3,128,512]{2,1,0:T(8,128)(2,1)S(1)} %get-tuple-element.68.refs_0_, bf16[3,128,512]{2,1,0:T(8,128)(2,1)S(1)} %collective-permute-done.14.rest_1_.refs_1_, ...), custom_call_target="tpu_custom_call", output_to_operand_aliasing={{0}: (2, {}), {1}: (3, {}), {2}: (4, {})} | custom-call | bytes 1024 | tf_op jit(solution)/shard_map/place/pallas_call | solution.py:436
  48.9 2.9 %collective-permute-done.16.refs_1_ = bf16[3,128,512]{2,1,0:T(8,128)(2,1)S(1)} collective-permute-done((bf16[3,128,512]{2,1,0:T(8,128)(2,1)S(1)}, bf16[3,128,512]{2,1,0:T(8,128)(2,1)S(1)}, u32[]{:S(2)}, u32[]{:S(2)}) %collective-permute-start.16) | collective-permute-done | bytes 393248 | tf_op jit(solution)/shard_map/ppermute | solution.py:324
  51.8 0.9 %place.6 = (bf16[128,4096]{1,0:T(8,128)(2,1)}, bf16[128,4096]{1,0:T(8,128)(2,1)}, bf16[128,4096]{1,0:T(8,128)(2,1)}) custom-call(bf16[3,128,512]{2,1,0:T(8,128)(2,1)S(1)} %get-tuple-element.67.refs_0_, bf16[3,128,512]{2,1,0:T(8,128)(2,1)S(1)} %collective-permute-done.16.refs_1_, ...), custom_call_target="tpu_custom_call", output_to_operand_aliasing={{0}: (2, {}), {1}: (3, {}), {2}: (4, {})} | custom-call | bytes 1024 | tf_op jit(solution)/shard_map/place/pallas_call | solution.py:436
  52.7 6.7 %collective-permute-done.15.refs_0_ = bf16[3,128,512]{2,1,0:T(8,128)(2,1)S(1)} collective-permute-done((bf16[3,128,512]{2,1,0:T(8,128)(2,1)S(1)}, bf16[3,128,512]{2,1,0:T(8,128)(2,1)S(1)}, u32[]{:S(2)}, u32[]{:S(2)}) %collective-permute-start.15) | collective-permute-done | bytes 393248 | tf_op jit(solution)/shard_map/ppermute | solution.py:324
  59.4 0.8 %place.7 = (bf16[128,4096]{1,0:T(8,128)(2,1)}, bf16[128,4096]{1,0:T(8,128)(2,1)}, bf16[128,4096]{1,0:T(8,128)(2,1)}) custom-call(bf16[3,128,512]{2,1,0:T(8,128)(2,1)S(1)} %collective-permute-done.15.refs_0_, bf16[128,4096]{1,0:T(8,128)(2,1)} %get-tuple-element.76.refs_1_, ...), custom_call_target="tpu_custom_call", output_to_operand_aliasing={{0}: (1, {}), {1}: (2, {}), {2}: (3, {})} | custom-call | bytes 1024 | tf_op jit(solution)/shard_map/place/pallas_call | solution.py:436
Async XLA Ops:
  0.6 0.7 %copy-start.4 = (s32[8]{0:T(128)S(1)}, s32[8]{0:T(128)}, u32[]{:S(2)}) copy-start(s32[8]{0:T(128)} %lengths.29) | copy-start | bytes 100
  2.9 2.3 %collective-permute-start.2 = (f32[8,128,128]{2,1,0:T(8,128)S(1)}, f32[8,128,128]{2,1,0:T(8,128)S(1)}, u32[]{:S(2)}, u32[]{:S(2)}) collective-permute-start(f32[8,128,128]{2,1,0:T(8,128)S(1)} %states.5), channel_id=1, source_target_pairs={{0,2},{2,0},{4,6},{6,4},{8,10},{10,8},{12,14},{14,12},{16,18},{18,... | collective-permute-start | bytes 1572872 | tf_op jit(solution)/shard_map/ppermute | solution.py:312
  3.5 10.2 %copy-start.1 = (bf16[256,2048]{1,0:T(8,128)(2,1)S(1)}, bf16[256,2048]{1,0:T(8,128)(2,1)}, u32[]{:S(2)}) copy-start(bf16[256,2048]{1,0:T(8,128)(2,1)} %v.19) | copy-start | bytes 3145732
  3.5 10.2 %copy-start.2 = (bf16[256,2048]{1,0:T(8,128)(2,1)S(1)}, bf16[256,2048]{1,0:T(8,128)(2,1)}, u32[]{:S(2)}) copy-start(bf16[256,2048]{1,0:T(8,128)(2,1)} %g.19) | copy-start | bytes 3145732
  3.5 10.2 %copy-start.3 = (bf16[256,2048]{1,0:T(8,128)(2,1)S(1)}, bf16[256,2048]{1,0:T(8,128)(2,1)}, u32[]{:S(2)}) copy-start(bf16[256,2048]{1,0:T(8,128)(2,1)} %q.13) | copy-start | bytes 3145732
  5.3 8.4 %copy-start = (bf16[256,2048]{1,0:T(8,128)(2,1)S(1)}, bf16[256,2048]{1,0:T(8,128)(2,1)}, u32[]{:S(2)}) copy-start(bf16[256,2048]{1,0:T(8,128)(2,1)} %k.19) | copy-start | bytes 3145732
  5.9 12.8 %collective-permute-start.4 = (bf16[1056,128]{1,0:T(8,128)(2,1)S(1)}, bf16[1056,128]{1,0:T(8,128)(2,1)S(1)}, u32[]{:S(2)}, u32[]{:S(2)}) collective-permute-start(bf16[1056,128]{1,0:T(8,128)(2,1)S(1)} %get-tuple-element.49), channel_id=1, source_target_pairs={{0,6},{4,10},{8,14},{12,18},{16,22},{20,26},{24,30},{6,0},{10,4},{... | collective-permute-start | bytes 811016 | tf_op jit(solution)/shard_map/ppermute | solution.py:318
  10.5 8.2 %collective-permute-start.5 = (bf16[1040,128]{1,0:T(8,128)(2,1)S(1)}, bf16[1040,128]{1,0:T(8,128)(2,1)S(1)}, u32[]{:S(2)}, u32[]{:S(2)}) collective-permute-start(bf16[1040,128]{1,0:T(8,128)(2,1)S(1)} %get-tuple-element.50), channel_id=1, source_target_pairs={{0,10},{4,14},{8,18},{12,22},{16,26},{20,30},{10,0},{14,4},{18,8},... | collective-permute-start | bytes 798728 | tf_op jit(solution)/shard_map/ppermute | solution.py:318
  13.5 5.2 %collective-permute-start.3 = (f32[4,128,128]{2,1,0:T(8,128)S(1)}, f32[4,128,128]{2,1,0:T(8,128)S(1)}, u32[]{:S(2)}, u32[]{:S(2)}) collective-permute-start(f32[4,128,128]{2,1,0:T(8,128)S(1)} %get-tuple-element.48), channel_id=1, source_target_pairs={{0,2},{2,0},{4,6},{6,4},{8,10},{10,8},{12,14},{14,12},{16,18},{18,... | collective-permute-start | bytes 786440 | tf_op jit(solution)/shard_map/ppermute | solution.py:312
  16.4 7.2 %collective-permute-start.1 = (f32[8,128,128]{2,1,0:T(8,128)S(1)}, f32[8,128,128]{2,1,0:T(8,128)S(1)}, u32[]{:S(2)}, u32[]{:S(2)}) collective-permute-start(f32[8,128,128]{2,1,0:T(8,128)S(1)} %get-tuple-element.45), channel_id=1, source_target_pairs={{0,2},{2,0},{4,6},{6,4},{8,10},{10,8},{12,14},{14,12},{16,18},{18,... | collective-permute-start | bytes 1572872 | tf_op jit(solution)/shard_map/ppermute | solution.py:312
  18.6 1.6 %collective-permute-start.7 = (f32[4,128,128]{2,1,0:T(8,128)S(1)}, f32[4,128,128]{2,1,0:T(8,128)S(1)}, u32[]{:S(2)}, u32[]{:S(2)}) collective-permute-start(f32[4,128,128]{2,1,0:T(8,128)S(1)} %get-tuple-element.54), channel_id=1, source_target_pairs={{0,2},{2,0},{4,6},{6,4},{8,10},{10,8},{12,14},{14,12},{16,18},{18,... | collective-permute-start | bytes 786440 | tf_op jit(solution)/shard_map/ppermute | solution.py:312
  19.4 1.7 %collective-permute-start.6 = (f32[4,128,128]{2,1,0:T(8,128)S(1)}, f32[4,128,128]{2,1,0:T(8,128)S(1)}, u32[]{:S(2)}, u32[]{:S(2)}) collective-permute-start(f32[4,128,128]{2,1,0:T(8,128)S(1)} %get-tuple-element.53), channel_id=1, source_target_pairs={{0,2},{2,0},{4,6},{6,4},{8,10},{10,8},{12,14},{14,12},{16,18},{18,... | collective-permute-start | bytes 786440 | tf_op jit(solution)/shard_map/ppermute | solution.py:312
  19.9 12.2 %collective-permute-start = (f32[8,128,128]{2,1,0:T(8,128)S(1)}, f32[8,128,128]{2,1,0:T(8,128)S(1)}, u32[]{:S(2)}, u32[]{:S(2)}) collective-permute-start(f32[8,128,128]{2,1,0:T(8,128)S(1)} %get-tuple-element.44.kept), channel_id=1, source_target_pairs={{0,2},{2,0},{4,6},{6,4},{8,10},{10,8},{12,14},{14,12},{16,18},{18,... | collective-permute-start | bytes 1572872 | tf_op jit(solution)/shard_map/ppermute | solution.py:312
  22.0 13.2 %collective-permute-start.10 = (bf16[3,128,512]{2,1,0:T(8,128)(2,1)S(1)}, bf16[3,128,512]{2,1,0:T(8,128)(2,1)S(1)}, u32[]{:S(2)}, u32[]{:S(2)}) collective-permute-start(bf16[3,128,512]{2,1,0:T(8,128)(2,1)S(1)} %carry.3.rest_0_), channel_id=1, source_target_pairs={{0,1},{1,0},{2,3},{3,2},{4,5},{5,4},{6,7},{7,6},{8,9},{9,8},{10,11... | collective-permute-start | bytes 1179656 | tf_op jit(solution)/shard_map/ppermute | solution.py:324
  23.6 6.6 %collective-permute-start.13 = (f32[4,128,128]{2,1,0:T(8,128)S(1)}, f32[4,128,128]{2,1,0:T(8,128)S(1)}, u32[]{:S(2)}, u32[]{:S(2)}) collective-permute-start(f32[4,128,128]{2,1,0:T(8,128)S(1)} %get-tuple-element.63), channel_id=1, source_target_pairs={{0,2},{2,0},{4,6},{6,4},{8,10},{10,8},{12,14},{14,12},{16,18},{18,... | collective-permute-start | bytes 786440 | tf_op jit(solution)/shard_map/ppermute | solution.py:312
  24.3 11.0 %collective-permute-start.8 = (bf16[1056,128]{1,0:T(8,128)(2,1)S(1)}, bf16[1056,128]{1,0:T(8,128)(2,1)S(1)}, u32[]{:S(2)}, u32[]{:S(2)}) collective-permute-start(bf16[1056,128]{1,0:T(8,128)(2,1)S(1)} %get-tuple-element.56), channel_id=1, source_target_pairs={{0,6},{4,10},{8,14},{12,18},{16,22},{20,26},{24,30},{6,0},{10,4},{... | collective-permute-start | bytes 811016 | tf_op jit(solution)/shard_map/ppermute | solution.py:318
  27.2 8.1 %collective-permute-start.9 = (bf16[1040,128]{1,0:T(8,128)(2,1)S(1)}, bf16[1040,128]{1,0:T(8,128)(2,1)S(1)}, u32[]{:S(2)}, u32[]{:S(2)}) collective-permute-start(bf16[1040,128]{1,0:T(8,128)(2,1)S(1)} %get-tuple-element.57), channel_id=1, source_target_pairs={{0,10},{4,14},{8,18},{12,22},{16,26},{20,30},{10,0},{14,4},{18,8},... | collective-permute-start | bytes 798728 | tf_op jit(solution)/shard_map/ppermute | solution.py:318
  31.5 10.4 %collective-permute-start.14 = (bf16[3,128,512]{2,1,0:T(8,128)(2,1)S(1)}, bf16[3,128,512]{2,1,0:T(8,128)(2,1)S(1)}, u32[]{:S(2)}, u32[]{:S(2)}) collective-permute-start(bf16[3,128,512]{2,1,0:T(8,128)(2,1)S(1)} %get-tuple-element.64.rest_0_), channel_id=1, source_target_pairs={{0,1},{1,0},{2,3},{3,2},{4,5},{5,4},{6,7},{7,6},{8,9},{9,8},{10,11... | collective-permute-start | bytes 1179656 | tf_op jit(solution)/shard_map/ppermute | solution.py:324
  36.0 1.6 %collective-permute-start.12 = (f32[4,128,128]{2,1,0:T(8,128)S(1)}, f32[4,128,128]{2,1,0:T(8,128)S(1)}, u32[]{:S(2)}, u32[]{:S(2)}) collective-permute-start(f32[4,128,128]{2,1,0:T(8,128)S(1)} %get-tuple-element.61), channel_id=1, source_target_pairs={{0,2},{2,0},{4,6},{6,4},{8,10},{10,8},{12,14},{14,12},{16,18},{18,... | collective-permute-start | bytes 786440 | tf_op jit(solution)/shard_map/ppermute | solution.py:312
  36.1 5.8 %collective-permute-start.11 = (f32[4,128,128]{2,1,0:T(8,128)S(1)}, f32[4,128,128]{2,1,0:T(8,128)S(1)}, u32[]{:S(2)}, u32[]{:S(2)}) collective-permute-start(f32[4,128,128]{2,1,0:T(8,128)S(1)} %get-tuple-element.59), channel_id=1, source_target_pairs={{0,2},{2,0},{4,6},{6,4},{8,10},{10,8},{12,14},{14,12},{16,18},{18,... | collective-permute-start | bytes 786440 | tf_op jit(solution)/shard_map/ppermute | solution.py:312
  39.7 12.0 %collective-permute-start.16 = (bf16[3,128,512]{2,1,0:T(8,128)(2,1)S(1)}, bf16[3,128,512]{2,1,0:T(8,128)(2,1)S(1)}, u32[]{:S(2)}, u32[]{:S(2)}) collective-permute-start(bf16[3,128,512]{2,1,0:T(8,128)(2,1)S(1)} %get-tuple-element.65.rest_0_), channel_id=1, source_target_pairs={{0,1},{1,0},{2,3},{3,2},{4,5},{5,4},{6,7},{7,6},{8,9},{9,8},{10,11... | collective-permute-start | bytes 1179656 | tf_op jit(solution)/shard_map/ppermute | solution.py:324
  44.1 15.3 %collective-permute-start.15 = (bf16[3,128,512]{2,1,0:T(8,128)(2,1)S(1)}, bf16[3,128,512]{2,1,0:T(8,128)(2,1)S(1)}, u32[]{:S(2)}, u32[]{:S(2)}) collective-permute-start(bf16[3,128,512]{2,1,0:T(8,128)(2,1)S(1)} %get-tuple-element.66), channel_id=1, source_target_pairs={{0,1},{1,0},{2,3},{3,2},{4,5},{5,4},{6,7},{7,6},{8,9},{9,8},{10,11... | collective-permute-start | bytes 1179656 | tf_op jit(solution)/shard_map/ppermute | solution.py:324

commit v9 on v8

--- a/solution.py
+++ b/solution.py
@@ -223,20 +223,6 @@
         at = slice(offset + h * HEAD_DIM, offset + (h + 1) * HEAD_DIM)
         for i, value in enumerate(local_part(q, k, v, g, lower, upper, at)):
             near[i, :, cols] = value
-
-
-def carry_kernel(lengths, k, v, g, near, mine, got, *rest, ndocs, rows, offset, heads, groups):
-    outs, done = rest[-1 - groups:-1], rest[-1]
-    first_core, first_rows, last_rows = own_range(lengths, ndocs, rows)
-    for h in range(heads):
-        cols = slice(h * HEAD_DIM, (h + 1) * HEAD_DIM)
-        at = slice(offset + h * HEAD_DIM, offset + (h + 1) * HEAD_DIM)
-        state = jnp.where(first_core, got[h], mine[h])
-        grad = jnp.where(first_core, mine[h], got[h])
-        carries = (carry_of_state(g, state, first_rows, at), *carries_of_grad(k, v, grad, last_rows, at))
-        for i in range(3):
-            done[i, :, cols] = (near[i, :, cols] + carries[i]).astype(jnp.bfloat16)
-    deal(done, outs, rows, groups)
 
 
 def carry_rows_kernel(lengths, k, v, g, near, mine, got, *rest, ndocs, rows, offset, heads, groups, shifts):
@@ -376,13 +362,6 @@
             "local", kernel, (*inputs, *masks), [shape_of(3, rows, cw), shape_of(8, HEAD_DIM)], limit=GRAD_LIMIT,
         )
 
-    def carry(near, offset, cw, mine, theirs, after):
-        kernel = functools.partial(carry_kernel, offset=offset, heads=cw // HEAD_DIM, groups=groups, **sizes)
-        return call(
-            "carry", kernel, (*inputs[1:], near, mine, theirs), [shape_of(3, part, cw, dtype=bf16)] * groups,
-            [pltpu.VMEM((3, rows, cw), bf16)], after, GRAD_LIMIT,
-        )
-
     def carry_rows(shifts, near, offset, cw, mine, theirs, after):
         kernel = functools.partial(
             carry_rows_kernel, offset=offset, heads=cw // HEAD_DIM, groups=groups, shifts=shifts, **sizes
@@ -390,7 +369,7 @@
         outs = [shape_of(3, part, cw, dtype=bf16)] * len(shifts)
         return call("carry", kernel, (*inputs[1:], near, mine, theirs), outs, after=after, limit=GRAD_LIMIT)
 
-    cuts, outs, arrived, totals, masks = [], [], [], [], None
+    cuts, outs, arrived, totals, masks, early = [], [], [], [], None, []
     for start, half, chunks in halves:
         if not totals:
             (sent,) = states(False, start, half)
@@ -416,14 +395,14 @@
             after = [made[-1] for made in outs[-1:]] + [parts[1] for parts in arrived[1:-1]][-1:]
             if totals:
                 outs.append(grads(masks, offset, cw, mine, theirs, after))
-            elif c == 0:
-                first = (near[0][0], offset, cw, mine, theirs)
-                outs.append([None, *carry_rows(range(1, groups), *first, [made for made, _ in joined[1:]])])
             else:
-                outs.append(carry(near[c][0], offset, cw, mine, theirs, after))
+                after = after or [made for made, _ in joined[1:]]
+                early.append((near[c][0], offset, cw, mine, theirs))
+                outs.append([None, *carry_rows(range(1, groups), *early[-1], after)])
             arrived.append(send_rows(outs[-1]))
         if not totals:
-            arrived[0][0] = carry_rows([0], *first, [outs[-1][-1]])[0]
+            for c, parts in enumerate(early):
+                arrived[c][0] = carry_rows([0], *parts, [outs[-1][-1]])[0]
         totals = [total]
         cuts += chunks
 

time: 60.4 us -> 60.4 us (level)
    ppermute x4, waiting for transfers between devices: 11.2 us -> 10.2 us  [send_rows(): lax.ppermute(outs[j], 'head', [(x, (x + j) % groups) for x in range(group...]
    pallas_call x13 -> x14, Pallas kernels: 15.2 us -> 15.8 us  [call(): pl.pallas_call(kernel, in_specs=[in_smem] + [in_vmem] * len(args) + [anyw...]
  transfers between devices with their start and end apart: 17 -> 17, of which waited for: 7 -> 7; matrix products, arithmetic and copies ran while one was open for 0% -> 0% of each run, Pallas kernels for 32% -> 33%
where the time goes in v9:
time: 60.4 us; the launch traced here: 60.2 us
  Pallas kernels  22.9 us (38%)
  starting transfers between devices  20.5 us (34%)
  waiting for transfers between devices  15.2 us (25%)
  between operations  0.87 us (1%)
  local copies, waits for them, and re-layouts  0.67 us (1%)
    pallas_call x14, Pallas kernels, call(): pl.pallas_call(kernel, in_specs=[in_smem] + [in_vmem] * len(args) + [anyw...  15.8 us
    ppermute x4, starting transfers between devices, swap_pairs(): lax.ppermute(sent[hop - 1], 'seq', perm + [(b, a) for a, b in perm])  13.4 us
    ppermute x4, waiting for transfers between devices, send_rows(): lax.ppermute(outs[j], 'head', [(x, (x + j) % groups) for x in range(group...  10.2 us
    ppermute x4, starting transfers between devices, send_rows(): lax.ppermute(outs[j], 'head', [(x, (x + j) % groups) for x in range(group...  4.57 us
    pallas_call x4, Pallas kernels, shards(): pl.pallas_call(functools.partial(place_kernel, groups=groups, plan=[where...  3.71 us
    ppermute x4, waiting for transfers between devices, swap_pairs(): lax.ppermute(sent[hop - 1], 'seq', perm + [(b, a) for a, b in perm])  3.54 us
    pallas_call x2, Pallas kernels, states(): pl.pallas_call(functools.partial(state_kernel, offset=offset, heads=heads...  3.44 us
    ppermute x9, starting transfers between devices, swap_cores(): return lax.ppermute(a, 'seq', [(b, b ^ 1) for b in range(seq)])  2.49 us
  transfers between devices with their start and end apart: 17, of which 7 were waited for; matrix products, arithmetic and copies ran while one was open for 0% of the time, Pallas kernels for 33%

profile of v9, /device:TPU:0, one launch (start us, length us, event | category | flops | bytes accessed | tf_op | source)
XLA Modules:
  0.0 60.2 jit_solution(9456792818688401802)
XLA Ops:
  0.6 0.0 copy-start.4
  0.6 0.6 %copy-done.4 = s32[8]{0:T(128)S(1)} copy-done((s32[8]{0:T(128)S(1)}, s32[8]{0:T(128)}, u32[]{:S(2)}) %copy-start.4) | copy-done | bytes 56
  1.3 1.6 %states.5 = f32[8,128,128]{2,1,0:T(8,128)S(1)} custom-call(s32[8]{0:T(128)S(1)} %copy-done.4, bf16[256,2048]{1,0:T(8,128)(2,1)} %q.13, bf16[256,2048]{1,0:T(8,128)(2,1)} %k.21, bf16[256,2048]{1,0:T(8,128)(2,1)} %v.21, bf16[256,2048]{1,0:T(8,128)(2,1)} %g.21), custom_call_target="tpu_custom_call" | custom-call | bytes 1024 | tf_op jit(solution)/shard_map/states/pallas_call | solution.py:319
  2.9 0.5 collective-permute-start.2
  3.5 0.0 copy-start.1
  3.5 0.0 copy-start.2
  3.5 0.0 copy-start.3
  3.5 1.8 %states.3 = (f32[8,128,128]{2,1,0:T(8,128)S(1)}, bf16[256,256]{1,0:T(8,128)(2,1)S(1)}, bf16[256,256]{1,0:T(8,128)(2,1)S(1)}) custom-call(s32[8]{0:T(128)S(1)} %copy-done.4, bf16[256,2048]{1,0:T(8,128)(2,1)} %q.13, bf16[256,2048]{1,0:T(8,128)(2,1)} %k.21, bf16[256,2048]{1,0:T(8,128)(2,1)} %v.21, bf16[256,2048]{1,0:T(8,128)(2,1)} %g.21), custom_call_target="tpu_custom_call" | custom-call | bytes 1024 | tf_op jit(solution)/shard_map/states/pallas_call | solution.py:319
  5.3 0.0 copy-start
  5.3 0.0 collective-permute-done.2.got
  5.3 0.7 %pair.2 = (bf16[1056,128]{1,0:T(8,128)(2,1)S(1)}, bf16[1040,128]{1,0:T(8,128)(2,1)S(1)}, f32[4,128,128]{2,1,0:T(8,128)S(1)}, f32[4,128,128]{2,1,0:T(8,128)S(1)}) custom-call(s32[8]{0:T(128)S(1)} %copy-done.4, f32[8,128,128]{2,1,0:T(8,128)S(1)} %get-tuple-element.45.kept, f32[8,128,128]{2,1,0:T(8,128)S(1)} %collective-permute-done.2.got), custom_call_target="tpu_custom_call" | custom-call | bytes 1024 | tf_op jit(solution)/shard_map/pair/pallas_call | solution.py:291
  5.9 4.5 %collective-permute-start.4 = (bf16[1056,128]{1,0:T(8,128)(2,1)S(1)}, bf16[1056,128]{1,0:T(8,128)(2,1)S(1)}, u32[]{:S(2)}, u32[]{:S(2)}) collective-permute-start(bf16[1056,128]{1,0:T(8,128)(2,1)S(1)} %get-tuple-element.47), channel_id=1, source_target_pairs={{0,6},{4,10},{8,14},{12,18},{16,22},{20,26},{24,30},{6,0},{10,4},{... | collective-permute-start | bytes 811016 | tf_op jit(solution)/shard_map/ppermute | solution.py:304
  10.5 3.0 %collective-permute-start.5 = (bf16[1040,128]{1,0:T(8,128)(2,1)S(1)}, bf16[1040,128]{1,0:T(8,128)(2,1)S(1)}, u32[]{:S(2)}, u32[]{:S(2)}) collective-permute-start(bf16[1040,128]{1,0:T(8,128)(2,1)S(1)} %get-tuple-element.48), channel_id=1, source_target_pairs={{0,10},{4,14},{8,18},{12,22},{16,26},{20,30},{10,0},{14,4},{18,8},... | collective-permute-start | bytes 798728 | tf_op jit(solution)/shard_map/ppermute | solution.py:304
  13.6 0.1 collective-permute-start.3
  13.6 0.0 copy-done.1
  13.6 0.0 copy-done.2
  13.6 0.0 copy-done.3
  13.7 0.0 copy-done
  13.7 1.6 %local.2 = (f32[3,256,512]{2,1,0:T(8,128)S(1)}, f32[8,128]{1,0:T(8,128)S(1)}) custom-call(s32[8]{0:T(128)S(1)} %copy-done.4, bf16[256,2048]{1,0:T(8,128)(2,1)S(1)} %copy-done.3, bf16[256,2048]{1,0:T(8,128)(2,1)S(1)} %copy-done, bf16[256,2048]{1,0:T(8,128)(2,1)S(1)} %copy-done.1, bf16[256,2048]{1,0:T(8,128)(2,1)S(1)} %copy-done.2, ...), custom_call_target="tpu_custom_call" | custom-call | bytes 1024 | tf_op jit(solution)/shard_map/local/pallas_call | solution.py:291
  15.3 1.2 %states.4 = (f32[8,128,128]{2,1,0:T(8,128)S(1)}, f32[8,128,128]{2,1,0:T(8,128)S(1)}) custom-call(s32[8]{0:T(128)S(1)} %copy-done.4, bf16[256,2048]{1,0:T(8,128)(2,1)S(1)} %copy-done.3, bf16[256,2048]{1,0:T(8,128)(2,1)S(1)} %copy-done, bf16[256,2048]{1,0:T(8,128)(2,1)S(1)} %copy-done.1, bf16[256,2048]{1,0:T(8,128)(2,1)S(1)} %copy-done.2, ...), custom_call_target="tpu_custom_call" | custom-call | bytes 1024 | tf_op jit(solution)/shard_map/states/pallas_call | solution.py:291
  16.5 0.5 collective-permute-start.1
  17.0 1.6 %local.3 = (f32[3,256,512]{2,1,0:T(8,128)S(1)}, f32[8,128]{1,0:T(8,128)S(1)}) custom-call(s32[8]{0:T(128)S(1)} %copy-done.4, bf16[256,2048]{1,0:T(8,128)(2,1)S(1)} %copy-done.3, bf16[256,2048]{1,0:T(8,128)(2,1)S(1)} %copy-done, bf16[256,2048]{1,0:T(8,128)(2,1)S(1)} %copy-done.1, bf16[256,2048]{1,0:T(8,128)(2,1)S(1)} %copy-done.2, ...), custom_call_target="tpu_custom_call" | custom-call | bytes 1024 | tf_op jit(solution)/shard_map/local/pallas_call | solution.py:291
  18.6 0.1 collective-permute-start.7
  18.7 0.0 collective-permute-done.3.rest_0_
  18.7 0.0 collective-permute-done.5.rest_2_
  18.7 0.0 collective-permute-done.4.rest_1_
  18.7 0.7 %join.3 = (f32[4,128,128]{2,1,0:T(8,128)S(1)}, f32[4,128,128]{2,1,0:T(8,128)S(1)}) custom-call(s32[8]{0:T(128)S(1)} %copy-done.4, f32[4,128,128]{2,1,0:T(8,128)S(1)} %collective-permute-done.3.rest_0_, bf16[1056,128]{1,0:T(8,128)(2,1)S(1)} %collective-permute-done.4.rest_1_, bf16[1040,128]{1,0:T(8,128)(2,1)S(1)} %collective-permute-done.5.rest_2_, ...), custom_call_target="tpu_custom_call" | custom-call | bytes 1024 | tf_op jit(solution)/shard_map/join/pallas_call | solution.py:291
  19.4 0.5 collective-permute-start.6
  19.9 0.1 collective-permute-start
  20.0 0.2 collective-permute-done.7.rest_0_
  20.2 0.6 %join.4 = (f32[4,128,128]{2,1,0:T(8,128)S(1)}, f32[4,128,128]{2,1,0:T(8,128)S(1)}) custom-call(s32[8]{0:T(128)S(1)} %copy-done.4, f32[4,128,128]{2,1,0:T(8,128)S(1)} %collective-permute-done.7.rest_0_, bf16[1056,128]{1,0:T(8,128)(2,1)S(1)} %collective-permute-done.4.rest_1_, bf16[1040,128]{1,0:T(8,128)(2,1)S(1)} %collective-permute-done.5.rest_2_, ...), custom_call_target="tpu_custom_call" | custom-call | bytes 1024 | tf_op jit(solution)/shard_map/join/pallas_call | solution.py:291
  20.9 0.2 collective-permute-done.6.got
  21.1 0.9 %carry.4.rest_0_ = bf16[3,128,512]{2,1,0:T(8,128)(2,1)S(1)} custom-call(s32[8]{0:T(128)S(1)} %copy-done.4, bf16[256,2048]{1,0:T(8,128)(2,1)S(1)} %copy-done, bf16[256,2048]{1,0:T(8,128)(2,1)S(1)} %copy-done.1, bf16[256,2048]{1,0:T(8,128)(2,1)S(1)} %copy-done.2, f32[3,256,512]{2,1,0:T(8,128)S(1)} %get-tuple-element.44.near, ...), custom_call_target="tpu_custom_call" | custom-call | bytes 1024 | tf_op jit(solution)/shard_map/carry/pallas_call | solution.py:291
  22.0 1.6 %collective-permute-start.10 = (bf16[3,128,512]{2,1,0:T(8,128)(2,1)S(1)}, bf16[3,128,512]{2,1,0:T(8,128)(2,1)S(1)}, u32[]{:S(2)}, u32[]{:S(2)}) collective-permute-start(bf16[3,128,512]{2,1,0:T(8,128)(2,1)S(1)} %carry.4.rest_0_), channel_id=1, source_target_pairs={{0,1},{1,0},{2,3},{3,2},{4,5},{5,4},{6,7},{7,6},{8,9},{9,8},{10,11... | collective-permute-start | bytes 1179656 | tf_op jit(solution)/shard_map/ppermute | solution.py:310
  23.6 0.1 collective-permute-start.13
  23.7 0.0 collective-permute-done.1.got
  23.7 0.6 %pair.3 = (bf16[1056,128]{1,0:T(8,128)(2,1)S(1)}, bf16[1040,128]{1,0:T(8,128)(2,1)S(1)}) custom-call(s32[8]{0:T(128)S(1)} %copy-done.4, f32[8,128,128]{2,1,0:T(8,128)S(1)} %get-tuple-element.42.kept, f32[8,128,128]{2,1,0:T(8,128)S(1)} %collective-permute-done.1.got, bf16[3,128,512]{2,1,0:T(8,128)(2,1)S(1)} %carry.4.rest_0_), custom_call_target="tpu_custom_call" | custom-call | bytes 1024 | tf_op jit(solution)/shard_map/pair/pallas_call | solution.py:291
  24.3 2.9 %collective-permute-start.8 = (bf16[1056,128]{1,0:T(8,128)(2,1)S(1)}, bf16[1056,128]{1,0:T(8,128)(2,1)S(1)}, u32[]{:S(2)}, u32[]{:S(2)}) collective-permute-start(bf16[1056,128]{1,0:T(8,128)(2,1)S(1)} %get-tuple-element.54), channel_id=1, source_target_pairs={{0,6},{4,10},{8,14},{12,18},{16,22},{20,26},{24,30},{6,0},{10,4},{... | collective-permute-start | bytes 811016 | tf_op jit(solution)/shard_map/ppermute | solution.py:304
  27.2 3.0 %collective-permute-start.9 = (bf16[1040,128]{1,0:T(8,128)(2,1)S(1)}, bf16[1040,128]{1,0:T(8,128)(2,1)S(1)}, u32[]{:S(2)}, u32[]{:S(2)}) collective-permute-start(bf16[1040,128]{1,0:T(8,128)(2,1)S(1)} %get-tuple-element.55), channel_id=1, source_target_pairs={{0,10},{4,14},{8,18},{12,22},{16,26},{20,30},{10,0},{14,4},{18,8},... | collective-permute-start | bytes 798728 | tf_op jit(solution)/shard_map/ppermute | solution.py:304
  30.2 0.0 collective-permute-done.13.got
  30.2 1.0 %carry.5.rest_0_ = bf16[3,128,512]{2,1,0:T(8,128)(2,1)S(1)} custom-call(s32[8]{0:T(128)S(1)} %copy-done.4, bf16[256,2048]{1,0:T(8,128)(2,1)S(1)} %copy-done, bf16[256,2048]{1,0:T(8,128)(2,1)S(1)} %copy-done.1, bf16[256,2048]{1,0:T(8,128)(2,1)S(1)} %copy-done.2, f32[3,256,512]{2,1,0:T(8,128)S(1)} %get-tuple-element.60.near, ...), custom_call_target="tpu_custom_call" | custom-call | bytes 1024 | tf_op jit(solution)/shard_map/carry/pallas_call | solution.py:291
  31.1 0.6 collective-permute-start.14
  31.7 0.0 collective-permute-done.rest_0_.rest_1_
  31.7 3.5 %collective-permute-done.9.rest_3_ = bf16[1040,128]{1,0:T(8,128)(2,1)S(1)} collective-permute-done((bf16[1040,128]{1,0:T(8,128)(2,1)S(1)}, bf16[1040,128]{1,0:T(8,128)(2,1)S(1)}, u32[]{:S(2)}, u32[]{:S(2)}) %collective-permute-start.9) | collective-permute-done | bytes 266272 | tf_op jit(solution)/shard_map/ppermute | solution.py:304
  35.3 0.0 collective-permute-done.8.rest_2_
  35.3 0.0 collective-permute-done.10.rest_4_.refs_2_
  35.3 0.7 %join.5 = (f32[4,128,128]{2,1,0:T(8,128)S(1)}, f32[4,128,128]{2,1,0:T(8,128)S(1)}, f32[4,128,128]{2,1,0:T(8,128)S(1)}, f32[4,128,128]{2,1,0:T(8,128)S(1)}) custom-call(s32[8]{0:T(128)S(1)} %copy-done.4, f32[8,128,128]{2,1,0:T(8,128)S(1)} %collective-permute-done.rest_0_.rest_1_, f32[8,128,128]{2,1,0:T(8,128)S(1)} %collective-permute-done.rest_0_.rest_1_, ...), custom_call_target="tpu_custom_call" | custom-call | bytes 1024 | tf_op jit(solution)/shard_map/join/pallas_call | solution.py:291
  36.0 0.1 collective-permute-start.12
  36.1 0.5 collective-permute-start.11
  36.6 1.0 %collective-permute-done.12.got = f32[4,128,128]{2,1,0:T(8,128)S(1)} collective-permute-done((f32[4,128,128]{2,1,0:T(8,128)S(1)}, f32[4,128,128]{2,1,0:T(8,128)S(1)}, u32[]{:S(2)}, u32[]{:S(2)}) %collective-permute-start.12) | collective-permute-done | bytes 262176 | tf_op jit(solution)/shard_map/ppermute | solution.py:298
  37.6 2.2 %grads.2 = (bf16[3,128,512]{2,1,0:T(8,128)(2,1)S(1)}, bf16[3,128,512]{2,1,0:T(8,128)(2,1)S(1)}) custom-call(s32[8]{0:T(128)S(1)} %copy-done.4, bf16[256,2048]{1,0:T(8,128)(2,1)S(1)} %copy-done.3, bf16[256,2048]{1,0:T(8,128)(2,1)S(1)} %copy-done, bf16[256,2048]{1,0:T(8,128)(2,1)S(1)} %copy-done.1, bf16[256,2048]{1,0:T(8,128)(2,1)S(1)} %copy-done.2, ...), custom_call_target="tpu_custom_call" | custom-call | bytes 1024 | tf_op jit(solution)/shard_map/grads/pallas_call | solution.py:291
  39.8 0.6 %collective-permute-start.16 = (bf16[3,128,512]{2,1,0:T(8,128)(2,1)S(1)}, bf16[3,128,512]{2,1,0:T(8,128)(2,1)S(1)}, u32[]{:S(2)}, u32[]{:S(2)}) collective-permute-start(bf16[3,128,512]{2,1,0:T(8,128)(2,1)S(1)} %get-tuple-element.62.rest_0_), channel_id=1, source_target_pairs={{0,1},{1,0},{2,3},{3,2},{4,5},{5,4},{6,7},{7,6},{8,9},{9,8},{10,11... | collective-permute-start | bytes 1179656 | tf_op jit(solution)/shard_map/ppermute | solution.py:310
  40.4 1.6 %collective-permute-done.14.rest_1_.refs_1_ = bf16[3,128,512]{2,1,0:T(8,128)(2,1)S(1)} collective-permute-done((bf16[3,128,512]{2,1,0:T(8,128)(2,1)S(1)}, bf16[3,128,512]{2,1,0:T(8,128)(2,1)S(1)}, u32[]{:S(2)}, u32[]{:S(2)}) %collective-permute-start.14) | collective-permute-done | bytes 393248 | tf_op jit(solution)/shard_map/ppermute | solution.py:310
  41.9 0.0 collective-permute-done.11.got
  41.9 2.2 %grads.3 = (bf16[3,128,512]{2,1,0:T(8,128)(2,1)S(1)}, bf16[3,128,512]{2,1,0:T(8,128)(2,1)S(1)}) custom-call(s32[8]{0:T(128)S(1)} %copy-done.4, bf16[256,2048]{1,0:T(8,128)(2,1)S(1)} %copy-done.3, bf16[256,2048]{1,0:T(8,128)(2,1)S(1)} %copy-done, bf16[256,2048]{1,0:T(8,128)(2,1)S(1)} %copy-done.1, bf16[256,2048]{1,0:T(8,128)(2,1)S(1)} %copy-done.2, ...), custom_call_target="tpu_custom_call" | custom-call | bytes 1024 | tf_op jit(solution)/shard_map/grads/pallas_call | solution.py:291
  44.1 1.8 %collective-permute-start.15 = (bf16[3,128,512]{2,1,0:T(8,128)(2,1)S(1)}, bf16[3,128,512]{2,1,0:T(8,128)(2,1)S(1)}, u32[]{:S(2)}, u32[]{:S(2)}) collective-permute-start(bf16[3,128,512]{2,1,0:T(8,128)(2,1)S(1)} %get-tuple-element.63), channel_id=1, source_target_pairs={{0,1},{1,0},{2,3},{3,2},{4,5},{5,4},{6,7},{7,6},{8,9},{9,8},{10,11... | collective-permute-start | bytes 1179656 | tf_op jit(solution)/shard_map/ppermute | solution.py:310
  45.9 0.9 %carry.7.refs_1_ = bf16[3,128,512]{2,1,0:T(8,128)(2,1)S(1)} custom-call(s32[8]{0:T(128)S(1)} %copy-done.4, bf16[256,2048]{1,0:T(8,128)(2,1)S(1)} %copy-done, bf16[256,2048]{1,0:T(8,128)(2,1)S(1)} %copy-done.1, bf16[256,2048]{1,0:T(8,128)(2,1)S(1)} %copy-done.2, f32[3,256,512]{2,1,0:T(8,128)S(1)} %get-tuple-element.60.near, ...), custom_call_target="tpu_custom_call" | custom-call | bytes 1024 | tf_op jit(solution)/shard_map/carry/pallas_call | solution.py:291
  46.8 0.9 %carry.6.refs_0_ = bf16[3,128,512]{2,1,0:T(8,128)(2,1)S(1)} custom-call(s32[8]{0:T(128)S(1)} %copy-done.4, bf16[256,2048]{1,0:T(8,128)(2,1)S(1)} %copy-done, bf16[256,2048]{1,0:T(8,128)(2,1)S(1)} %copy-done.1, bf16[256,2048]{1,0:T(8,128)(2,1)S(1)} %copy-done.2, f32[3,256,512]{2,1,0:T(8,128)S(1)} %get-tuple-element.44.near, ...), custom_call_target="tpu_custom_call" | custom-call | bytes 1024 | tf_op jit(solution)/shard_map/carry/pallas_call | solution.py:291
  47.8 1.1 %place.4 = (bf16[128,4096]{1,0:T(8,128)(2,1)}, bf16[128,4096]{1,0:T(8,128)(2,1)}, bf16[128,4096]{1,0:T(8,128)(2,1)}) custom-call(bf16[3,128,512]{2,1,0:T(8,128)(2,1)S(1)} %carry.6.refs_0_, bf16[3,128,512]{2,1,0:T(8,128)(2,1)S(1)} %carry.7.refs_1_, bf16[3,128,512]{2,1,0:T(8,128)(2,1)S(1)} %collective-permute-done.10.rest_4_.refs_2_), custom_call_target="tpu_custom_call" | custom-call | bytes 1024 | tf_op jit(solution)/shard_map/place/pallas_call | solution.py:415
  48.9 0.9 %place.5 = (bf16[128,4096]{1,0:T(8,128)(2,1)}, bf16[128,4096]{1,0:T(8,128)(2,1)}, bf16[128,4096]{1,0:T(8,128)(2,1)}) custom-call(bf16[3,128,512]{2,1,0:T(8,128)(2,1)S(1)} %get-tuple-element.65.refs_0_, bf16[3,128,512]{2,1,0:T(8,128)(2,1)S(1)} %collective-permute-done.14.rest_1_.refs_1_, ...), custom_call_target="tpu_custom_call", output_to_operand_aliasing={{0}: (2, {}), {1}: (3, {}), {2}: (4, {})} | custom-call | bytes 1024 | tf_op jit(solution)/shard_map/place/pallas_call | solution.py:415
  49.8 1.9 %collective-permute-done.16.refs_1_ = bf16[3,128,512]{2,1,0:T(8,128)(2,1)S(1)} collective-permute-done((bf16[3,128,512]{2,1,0:T(8,128)(2,1)S(1)}, bf16[3,128,512]{2,1,0:T(8,128)(2,1)S(1)}, u32[]{:S(2)}, u32[]{:S(2)}) %collective-permute-start.16) | collective-permute-done | bytes 393248 | tf_op jit(solution)/shard_map/ppermute | solution.py:310
  51.8 0.9 %place.6 = (bf16[128,4096]{1,0:T(8,128)(2,1)}, bf16[128,4096]{1,0:T(8,128)(2,1)}, bf16[128,4096]{1,0:T(8,128)(2,1)}) custom-call(bf16[3,128,512]{2,1,0:T(8,128)(2,1)S(1)} %get-tuple-element.64.refs_0_, bf16[3,128,512]{2,1,0:T(8,128)(2,1)S(1)} %collective-permute-done.16.refs_1_, ...), custom_call_target="tpu_custom_call", output_to_operand_aliasing={{0}: (2, {}), {1}: (3, {}), {2}: (4, {})} | custom-call | bytes 1024 | tf_op jit(solution)/shard_map/place/pallas_call | solution.py:415
  52.7 6.7 %collective-permute-done.15.refs_0_ = bf16[3,128,512]{2,1,0:T(8,128)(2,1)S(1)} collective-permute-done((bf16[3,128,512]{2,1,0:T(8,128)(2,1)S(1)}, bf16[3,128,512]{2,1,0:T(8,128)(2,1)S(1)}, u32[]{:S(2)}, u32[]{:S(2)}) %collective-permute-start.15) | collective-permute-done | bytes 393248 | tf_op jit(solution)/shard_map/ppermute | solution.py:310
  59.4 0.8 %place.7 = (bf16[128,4096]{1,0:T(8,128)(2,1)}, bf16[128,4096]{1,0:T(8,128)(2,1)}, bf16[128,4096]{1,0:T(8,128)(2,1)}) custom-call(bf16[3,128,512]{2,1,0:T(8,128)(2,1)S(1)} %collective-permute-done.15.refs_0_, bf16[128,4096]{1,0:T(8,128)(2,1)} %get-tuple-element.72.refs_1_, ...), custom_call_target="tpu_custom_call", output_to_operand_aliasing={{0}: (1, {}), {1}: (2, {}), {2}: (3, {})} | custom-call | bytes 1024 | tf_op jit(solution)/shard_map/place/pallas_call | solution.py:415
Async XLA Ops:
  0.6 0.7 %copy-start.4 = (s32[8]{0:T(128)S(1)}, s32[8]{0:T(128)}, u32[]{:S(2)}) copy-start(s32[8]{0:T(128)} %lengths.31) | copy-start | bytes 100
  2.9 2.3 %collective-permute-start.2 = (f32[8,128,128]{2,1,0:T(8,128)S(1)}, f32[8,128,128]{2,1,0:T(8,128)S(1)}, u32[]{:S(2)}, u32[]{:S(2)}) collective-permute-start(f32[8,128,128]{2,1,0:T(8,128)S(1)} %states.5), channel_id=1, source_target_pairs={{0,2},{2,0},{4,6},{6,4},{8,10},{10,8},{12,14},{14,12},{16,18},{18,... | collective-permute-start | bytes 1572872 | tf_op jit(solution)/shard_map/ppermute | solution.py:298
  3.5 10.2 %copy-start.1 = (bf16[256,2048]{1,0:T(8,128)(2,1)S(1)}, bf16[256,2048]{1,0:T(8,128)(2,1)}, u32[]{:S(2)}) copy-start(bf16[256,2048]{1,0:T(8,128)(2,1)} %v.21) | copy-start | bytes 3145732
  3.5 10.2 %copy-start.2 = (bf16[256,2048]{1,0:T(8,128)(2,1)S(1)}, bf16[256,2048]{1,0:T(8,128)(2,1)}, u32[]{:S(2)}) copy-start(bf16[256,2048]{1,0:T(8,128)(2,1)} %g.21) | copy-start | bytes 3145732
  3.5 10.2 %copy-start.3 = (bf16[256,2048]{1,0:T(8,128)(2,1)S(1)}, bf16[256,2048]{1,0:T(8,128)(2,1)}, u32[]{:S(2)}) copy-start(bf16[256,2048]{1,0:T(8,128)(2,1)} %q.13) | copy-start | bytes 3145732
  5.3 8.4 %copy-start = (bf16[256,2048]{1,0:T(8,128)(2,1)S(1)}, bf16[256,2048]{1,0:T(8,128)(2,1)}, u32[]{:S(2)}) copy-start(bf16[256,2048]{1,0:T(8,128)(2,1)} %k.21) | copy-start | bytes 3145732
  5.9 12.8 %collective-permute-start.4 = (bf16[1056,128]{1,0:T(8,128)(2,1)S(1)}, bf16[1056,128]{1,0:T(8,128)(2,1)S(1)}, u32[]{:S(2)}, u32[]{:S(2)}) collective-permute-start(bf16[1056,128]{1,0:T(8,128)(2,1)S(1)} %get-tuple-element.47), channel_id=1, source_target_pairs={{0,6},{4,10},{8,14},{12,18},{16,22},{20,26},{24,30},{6,0},{10,4},{... | collective-permute-start | bytes 811016 | tf_op jit(solution)/shard_map/ppermute | solution.py:304
  10.5 8.2 %collective-permute-start.5 = (bf16[1040,128]{1,0:T(8,128)(2,1)S(1)}, bf16[1040,128]{1,0:T(8,128)(2,1)S(1)}, u32[]{:S(2)}, u32[]{:S(2)}) collective-permute-start(bf16[1040,128]{1,0:T(8,128)(2,1)S(1)} %get-tuple-element.48), channel_id=1, source_target_pairs={{0,10},{4,14},{8,18},{12,22},{16,26},{20,30},{10,0},{14,4},{18,8},... | collective-permute-start | bytes 798728 | tf_op jit(solution)/shard_map/ppermute | solution.py:304
  13.6 5.2 %collective-permute-start.3 = (f32[4,128,128]{2,1,0:T(8,128)S(1)}, f32[4,128,128]{2,1,0:T(8,128)S(1)}, u32[]{:S(2)}, u32[]{:S(2)}) collective-permute-start(f32[4,128,128]{2,1,0:T(8,128)S(1)} %get-tuple-element.46), channel_id=1, source_target_pairs={{0,2},{2,0},{4,6},{6,4},{8,10},{10,8},{12,14},{14,12},{16,18},{18,... | collective-permute-start | bytes 786440 | tf_op jit(solution)/shard_map/ppermute | solution.py:298
  16.5 7.2 %collective-permute-start.1 = (f32[8,128,128]{2,1,0:T(8,128)S(1)}, f32[8,128,128]{2,1,0:T(8,128)S(1)}, u32[]{:S(2)}, u32[]{:S(2)}) collective-permute-start(f32[8,128,128]{2,1,0:T(8,128)S(1)} %get-tuple-element.43), channel_id=1, source_target_pairs={{0,2},{2,0},{4,6},{6,4},{8,10},{10,8},{12,14},{14,12},{16,18},{18,... | collective-permute-start | bytes 1572872 | tf_op jit(solution)/shard_map/ppermute | solution.py:298
  18.6 1.6 %collective-permute-start.7 = (f32[4,128,128]{2,1,0:T(8,128)S(1)}, f32[4,128,128]{2,1,0:T(8,128)S(1)}, u32[]{:S(2)}, u32[]{:S(2)}) collective-permute-start(f32[4,128,128]{2,1,0:T(8,128)S(1)} %get-tuple-element.52), channel_id=1, source_target_pairs={{0,2},{2,0},{4,6},{6,4},{8,10},{10,8},{12,14},{14,12},{16,18},{18,... | collective-permute-start | bytes 786440 | tf_op jit(solution)/shard_map/ppermute | solution.py:298
  19.4 1.7 %collective-permute-start.6 = (f32[4,128,128]{2,1,0:T(8,128)S(1)}, f32[4,128,128]{2,1,0:T(8,128)S(1)}, u32[]{:S(2)}, u32[]{:S(2)}) collective-permute-start(f32[4,128,128]{2,1,0:T(8,128)S(1)} %get-tuple-element.51), channel_id=1, source_target_pairs={{0,2},{2,0},{4,6},{6,4},{8,10},{10,8},{12,14},{14,12},{16,18},{18,... | collective-permute-start | bytes 786440 | tf_op jit(solution)/shard_map/ppermute | solution.py:298
  19.9 11.8 %collective-permute-start = (f32[8,128,128]{2,1,0:T(8,128)S(1)}, f32[8,128,128]{2,1,0:T(8,128)S(1)}, u32[]{:S(2)}, u32[]{:S(2)}) collective-permute-start(f32[8,128,128]{2,1,0:T(8,128)S(1)} %get-tuple-element.42.kept), channel_id=1, source_target_pairs={{0,2},{2,0},{4,6},{6,4},{8,10},{10,8},{12,14},{14,12},{16,18},{18,... | collective-permute-start | bytes 1572872 | tf_op jit(solution)/shard_map/ppermute | solution.py:298
  22.0 13.2 %collective-permute-start.10 = (bf16[3,128,512]{2,1,0:T(8,128)(2,1)S(1)}, bf16[3,128,512]{2,1,0:T(8,128)(2,1)S(1)}, u32[]{:S(2)}, u32[]{:S(2)}) collective-permute-start(bf16[3,128,512]{2,1,0:T(8,128)(2,1)S(1)} %carry.4.rest_0_), channel_id=1, source_target_pairs={{0,1},{1,0},{2,3},{3,2},{4,5},{5,4},{6,7},{7,6},{8,9},{9,8},{10,11... | collective-permute-start | bytes 1179656 | tf_op jit(solution)/shard_map/ppermute | solution.py:310
  23.6 6.6 %collective-permute-start.13 = (f32[4,128,128]{2,1,0:T(8,128)S(1)}, f32[4,128,128]{2,1,0:T(8,128)S(1)}, u32[]{:S(2)}, u32[]{:S(2)}) collective-permute-start(f32[4,128,128]{2,1,0:T(8,128)S(1)} %get-tuple-element.61), channel_id=1, source_target_pairs={{0,2},{2,0},{4,6},{6,4},{8,10},{10,8},{12,14},{14,12},{16,18},{18,... | collective-permute-start | bytes 786440 | tf_op jit(solution)/shard_map/ppermute | solution.py:298
  24.3 11.0 %collective-permute-start.8 = (bf16[1056,128]{1,0:T(8,128)(2,1)S(1)}, bf16[1056,128]{1,0:T(8,128)(2,1)S(1)}, u32[]{:S(2)}, u32[]{:S(2)}) collective-permute-start(bf16[1056,128]{1,0:T(8,128)(2,1)S(1)} %get-tuple-element.54), channel_id=1, source_target_pairs={{0,6},{4,10},{8,14},{12,18},{16,22},{20,26},{24,30},{6,0},{10,4},{... | collective-permute-start | bytes 811016 | tf_op jit(solution)/shard_map/ppermute | solution.py:304
  27.2 8.1 %collective-permute-start.9 = (bf16[1040,128]{1,0:T(8,128)(2,1)S(1)}, bf16[1040,128]{1,0:T(8,128)(2,1)S(1)}, u32[]{:S(2)}, u32[]{:S(2)}) collective-permute-start(bf16[1040,128]{1,0:T(8,128)(2,1)S(1)} %get-tuple-element.55), channel_id=1, source_target_pairs={{0,10},{4,14},{8,18},{12,22},{16,26},{20,30},{10,0},{14,4},{18,8},... | collective-permute-start | bytes 798728 | tf_op jit(solution)/shard_map/ppermute | solution.py:304
  31.1 10.8 %collective-permute-start.14 = (bf16[3,128,512]{2,1,0:T(8,128)(2,1)S(1)}, bf16[3,128,512]{2,1,0:T(8,128)(2,1)S(1)}, u32[]{:S(2)}, u32[]{:S(2)}) collective-permute-start(bf16[3,128,512]{2,1,0:T(8,128)(2,1)S(1)} %carry.5.rest_0_), channel_id=1, source_target_pairs={{0,1},{1,0},{2,3},{3,2},{4,5},{5,4},{6,7},{7,6},{8,9},{9,8},{10,11... | collective-permute-start | bytes 1179656 | tf_op jit(solution)/shard_map/ppermute | solution.py:310
  36.0 1.6 %collective-permute-start.12 = (f32[4,128,128]{2,1,0:T(8,128)S(1)}, f32[4,128,128]{2,1,0:T(8,128)S(1)}, u32[]{:S(2)}, u32[]{:S(2)}) collective-permute-start(f32[4,128,128]{2,1,0:T(8,128)S(1)} %get-tuple-element.59), channel_id=1, source_target_pairs={{0,2},{2,0},{4,6},{6,4},{8,10},{10,8},{12,14},{14,12},{16,18},{18,... | collective-permute-start | bytes 786440 | tf_op jit(solution)/shard_map/ppermute | solution.py:298
  36.1 5.8 %collective-permute-start.11 = (f32[4,128,128]{2,1,0:T(8,128)S(1)}, f32[4,128,128]{2,1,0:T(8,128)S(1)}, u32[]{:S(2)}, u32[]{:S(2)}) collective-permute-start(f32[4,128,128]{2,1,0:T(8,128)S(1)} %get-tuple-element.57), channel_id=1, source_target_pairs={{0,2},{2,0},{4,6},{6,4},{8,10},{10,8},{12,14},{14,12},{16,18},{18,... | collective-permute-start | bytes 786440 | tf_op jit(solution)/shard_map/ppermute | solution.py:298
  39.8 12.0 %collective-permute-start.16 = (bf16[3,128,512]{2,1,0:T(8,128)(2,1)S(1)}, bf16[3,128,512]{2,1,0:T(8,128)(2,1)S(1)}, u32[]{:S(2)}, u32[]{:S(2)}) collective-permute-start(bf16[3,128,512]{2,1,0:T(8,128)(2,1)S(1)} %get-tuple-element.62.rest_0_), channel_id=1, source_target_pairs={{0,1},{1,0},{2,3},{3,2},{4,5},{5,4},{6,7},{7,6},{8,9},{9,8},{10,11... | collective-permute-start | bytes 1179656 | tf_op jit(solution)/shard_map/ppermute | solution.py:310
  44.1 15.3 %collective-permute-start.15 = (bf16[3,128,512]{2,1,0:T(8,128)(2,1)S(1)}, bf16[3,128,512]{2,1,0:T(8,128)(2,1)S(1)}, u32[]{:S(2)}, u32[]{:S(2)}) collective-permute-start(bf16[3,128,512]{2,1,0:T(8,128)(2,1)S(1)} %get-tuple-element.63), channel_id=1, source_target_pairs={{0,1},{1,0},{2,3},{3,2},{4,5},{5,4},{6,7},{7,6},{8,9},{9,8},{10,11... | collective-permute-start | bytes 1179656 | tf_op jit(solution)/shard_map/ppermute | solution.py:310

commit v10 on v9

--- a/solution.py
+++ b/solution.py
@@ -377,15 +377,15 @@
         else:
             kept, sent = late_states(start, half, [token])
         total, came, others = pair_up(
-            kept, swap_cores(sent), 0 if totals else len(chunks), [made[-1] for made in outs[:1]]
+            kept, swap_cores(sent), len(chunks), [made[-1] for made in outs[:1]]
         )
         if not totals:
             near = [local(masks, *chunk) for chunk in chunks]
             token = near[0][1]
         count = chunks[0][1] // HEAD_DIM
         if totals:
-            spans = [(c * count, c * count, count) for c in range(len(chunks))]
-            joined = join(spans, [swap_cores(kept)] * len(chunks), came, [arrived[0][1]])
+            spans = [(0, c * count, count) for c in range(len(chunks))]
+            joined = join(spans, others, came, [arrived[0][1]])
         else:
             joined, after = [], [made[1] for made in near]
             for c in range(len(chunks)):

time: 60.4 us -> 60.8 us (level)
  waiting for transfers between devices: 15.2 us -> 16.5 us
  starting transfers between devices: 20.5 us -> 19.5 us
    ppermute x4, waiting for transfers between devices: 10.2 us -> 11.6 us  [send_rows(): lax.ppermute(outs[j], 'head', [(x, (x + j) % groups) for x in range(group...]
    ppermute x4, starting transfers between devices: 4.57 us -> 3.38 us  [send_rows(): lax.ppermute(outs[j], 'head', [(x, (x + j) % groups) for x in range(group...]
    ppermute x9 -> x10, starting transfers between devices: 2.49 us -> 2.62 us  [swap_cores(): return lax.ppermute(a, 'seq', [(b, b ^ 1) for b in range(seq)])]
    ppermute x9 -> x10, waiting for transfers between devices: 1.47 us -> 1.41 us  [swap_cores(): return lax.ppermute(a, 'seq', [(b, b ^ 1) for b in range(seq)])]
  transfers between devices with their start and end apart: 17 -> 18, of which waited for: 7 -> 6; matrix products, arithmetic and copies ran while one was open for 0% -> 0% of each run, Pallas kernels for 33% -> 33%
where the time goes in v10:
time: 60.8 us; the launch traced here: 60.5 us
  Pallas kernels  23 us (38%)
  starting transfers between devices  19.5 us (32%)
  waiting for transfers between devices  16.5 us (27%)
  between operations  0.92 us (2%)
  local copies, waits for them, and re-layouts  0.67 us (1%)
    pallas_call x14, Pallas kernels, call(): pl.pallas_call(kernel, in_specs=[in_smem] + [in_vmem] * len(args) + [anyw...  15.8 us
    ppermute x4, starting transfers between devices, swap_pairs(): lax.ppermute(sent[hop - 1], 'seq', perm + [(b, a) for a, b in perm])  13.5 us
    ppermute x4, waiting for transfers between devices, send_rows(): lax.ppermute(outs[j], 'head', [(x, (x + j) % groups) for x in range(group...  11.6 us
    pallas_call x4, Pallas kernels, shards(): pl.pallas_call(functools.partial(place_kernel, groups=groups, plan=[where...  3.71 us
    ppermute x4, waiting for transfers between devices, swap_pairs(): lax.ppermute(sent[hop - 1], 'seq', perm + [(b, a) for a, b in perm])  3.45 us
    pallas_call x2, Pallas kernels, states(): pl.pallas_call(functools.partial(state_kernel, offset=offset, heads=heads...  3.44 us
    ppermute x4, starting transfers between devices, send_rows(): lax.ppermute(outs[j], 'head', [(x, (x + j) % groups) for x in range(group...  3.38 us
    ppermute x10, starting transfers between devices, swap_cores(): return lax.ppermute(a, 'seq', [(b, b ^ 1) for b in range(seq)])  2.62 us
  transfers between devices with their start and end apart: 18, of which 6 were waited for; matrix products, arithmetic and copies ran while one was open for 0% of the time, Pallas kernels for 33%

profile of v10, /device:TPU:0, one launch (start us, length us, event | category | flops | bytes accessed | tf_op | source)
XLA Modules:
  0.0 60.5 jit_solution(699754660466797997)
XLA Ops:
  0.6 0.0 copy-start.4
  0.6 0.6 %copy-done.4 = s32[8]{0:T(128)S(1)} copy-done((s32[8]{0:T(128)S(1)}, s32[8]{0:T(128)}, u32[]{:S(2)}) %copy-start.4) | copy-done | bytes 56
  1.3 1.6 %states.5 = f32[8,128,128]{2,1,0:T(8,128)S(1)} custom-call(s32[8]{0:T(128)S(1)} %copy-done.4, bf16[256,2048]{1,0:T(8,128)(2,1)} %q.13, bf16[256,2048]{1,0:T(8,128)(2,1)} %k.21, bf16[256,2048]{1,0:T(8,128)(2,1)} %v.21, bf16[256,2048]{1,0:T(8,128)(2,1)} %g.21), custom_call_target="tpu_custom_call" | custom-call | bytes 1024 | tf_op jit(solution)/shard_map/states/pallas_call | solution.py:319
  2.9 0.5 collective-permute-start.1
  3.5 0.0 copy-start.1
  3.5 1.8 %states.3 = (f32[8,128,128]{2,1,0:T(8,128)S(1)}, bf16[256,256]{1,0:T(8,128)(2,1)S(1)}, bf16[256,256]{1,0:T(8,128)(2,1)S(1)}) custom-call(s32[8]{0:T(128)S(1)} %copy-done.4, bf16[256,2048]{1,0:T(8,128)(2,1)} %q.13, bf16[256,2048]{1,0:T(8,128)(2,1)} %k.21, bf16[256,2048]{1,0:T(8,128)(2,1)} %v.21, bf16[256,2048]{1,0:T(8,128)(2,1)} %g.21), custom_call_target="tpu_custom_call" | custom-call | bytes 1024 | tf_op jit(solution)/shard_map/states/pallas_call | solution.py:319
  5.3 0.0 copy-start
  5.3 0.0 collective-permute-done.1.got
  5.3 0.6 %pair.2 = (bf16[1056,128]{1,0:T(8,128)(2,1)S(1)}, bf16[1040,128]{1,0:T(8,128)(2,1)S(1)}, f32[4,128,128]{2,1,0:T(8,128)S(1)}, f32[4,128,128]{2,1,0:T(8,128)S(1)}) custom-call(s32[8]{0:T(128)S(1)} %copy-done.4, f32[8,128,128]{2,1,0:T(8,128)S(1)} %get-tuple-element.47.kept, f32[8,128,128]{2,1,0:T(8,128)S(1)} %collective-permute-done.1.got), custom_call_target="tpu_custom_call" | custom-call | bytes 1024 | tf_op jit(solution)/shard_map/pair/pallas_call | solution.py:291
  5.9 4.5 %collective-permute-start.3 = (bf16[1056,128]{1,0:T(8,128)(2,1)S(1)}, bf16[1056,128]{1,0:T(8,128)(2,1)S(1)}, u32[]{:S(2)}, u32[]{:S(2)}) collective-permute-start(bf16[1056,128]{1,0:T(8,128)(2,1)S(1)} %get-tuple-element.49), channel_id=1, source_target_pairs={{0,6},{4,10},{8,14},{12,18},{16,22},{20,26},{24,30},{6,0},{10,4},{... | collective-permute-start | bytes 811016 | tf_op jit(solution)/shard_map/ppermute | solution.py:304
  10.5 3.0 %collective-permute-start.4 = (bf16[1040,128]{1,0:T(8,128)(2,1)S(1)}, bf16[1040,128]{1,0:T(8,128)(2,1)S(1)}, u32[]{:S(2)}, u32[]{:S(2)}) collective-permute-start(bf16[1040,128]{1,0:T(8,128)(2,1)S(1)} %get-tuple-element.50), channel_id=1, source_target_pairs={{0,10},{4,14},{8,18},{12,22},{16,26},{20,30},{10,0},{14,4},{18,8},... | collective-permute-start | bytes 798728 | tf_op jit(solution)/shard_map/ppermute | solution.py:304
  13.5 0.1 collective-permute-start.2
  13.6 0.0 copy-done.1
  13.6 0.0 copy-done.2
  13.6 0.0 copy-done.3
  13.7 0.0 copy-done
  13.7 1.6 %local.2 = (f32[3,256,512]{2,1,0:T(8,128)S(1)}, f32[8,128]{1,0:T(8,128)S(1)}) custom-call(s32[8]{0:T(128)S(1)} %copy-done.4, bf16[256,2048]{1,0:T(8,128)(2,1)S(1)} %copy-done.3, bf16[256,2048]{1,0:T(8,128)(2,1)S(1)} %copy-done, bf16[256,2048]{1,0:T(8,128)(2,1)S(1)} %copy-done.1, bf16[256,2048]{1,0:T(8,128)(2,1)S(1)} %copy-done.2, ...), custom_call_target="tpu_custom_call" | custom-call | bytes 1024 | tf_op jit(solution)/shard_map/local/pallas_call | solution.py:291
  15.3 1.2 %states.4 = (f32[8,128,128]{2,1,0:T(8,128)S(1)}, f32[8,128,128]{2,1,0:T(8,128)S(1)}) custom-call(s32[8]{0:T(128)S(1)} %copy-done.4, bf16[256,2048]{1,0:T(8,128)(2,1)S(1)} %copy-done.3, bf16[256,2048]{1,0:T(8,128)(2,1)S(1)} %copy-done, bf16[256,2048]{1,0:T(8,128)(2,1)S(1)} %copy-done.1, bf16[256,2048]{1,0:T(8,128)(2,1)S(1)} %copy-done.2, ...), custom_call_target="tpu_custom_call" | custom-call | bytes 1024 | tf_op jit(solution)/shard_map/states/pallas_call | solution.py:291
  16.4 0.5 collective-permute-start
  17.0 0.1 collective-permute-start.6
  17.1 1.6 %local.3 = (f32[3,256,512]{2,1,0:T(8,128)S(1)}, f32[8,128]{1,0:T(8,128)S(1)}) custom-call(s32[8]{0:T(128)S(1)} %copy-done.4, bf16[256,2048]{1,0:T(8,128)(2,1)S(1)} %copy-done.3, bf16[256,2048]{1,0:T(8,128)(2,1)S(1)} %copy-done, bf16[256,2048]{1,0:T(8,128)(2,1)S(1)} %copy-done.1, bf16[256,2048]{1,0:T(8,128)(2,1)S(1)} %copy-done.2, ...), custom_call_target="tpu_custom_call" | custom-call | bytes 1024 | tf_op jit(solution)/shard_map/local/pallas_call | solution.py:291
  18.7 0.0 collective-permute-done.2.rest_0_
  18.7 0.0 collective-permute-done.4.rest_2_
  18.7 0.0 collective-permute-done.3.rest_1_
  18.7 0.7 %join.3 = (f32[4,128,128]{2,1,0:T(8,128)S(1)}, f32[4,128,128]{2,1,0:T(8,128)S(1)}) custom-call(s32[8]{0:T(128)S(1)} %copy-done.4, f32[4,128,128]{2,1,0:T(8,128)S(1)} %collective-permute-done.2.rest_0_, bf16[1056,128]{1,0:T(8,128)(2,1)S(1)} %collective-permute-done.3.rest_1_, bf16[1040,128]{1,0:T(8,128)(2,1)S(1)} %collective-permute-done.4.rest_2_, ...), custom_call_target="tpu_custom_call" | custom-call | bytes 1024 | tf_op jit(solution)/shard_map/join/pallas_call | solution.py:291
  19.4 0.5 collective-permute-start.5
  19.9 0.0 collective-permute-done.6.rest_0_
  19.9 0.6 %join.4 = (f32[4,128,128]{2,1,0:T(8,128)S(1)}, f32[4,128,128]{2,1,0:T(8,128)S(1)}) custom-call(s32[8]{0:T(128)S(1)} %copy-done.4, f32[4,128,128]{2,1,0:T(8,128)S(1)} %collective-permute-done.6.rest_0_, bf16[1056,128]{1,0:T(8,128)(2,1)S(1)} %collective-permute-done.3.rest_1_, bf16[1040,128]{1,0:T(8,128)(2,1)S(1)} %collective-permute-done.4.rest_2_, ...), custom_call_target="tpu_custom_call" | custom-call | bytes 1024 | tf_op jit(solution)/shard_map/join/pallas_call | solution.py:291
  20.5 0.1 collective-permute-start.14
  20.7 0.4 collective-permute-done.5.got
  21.0 1.0 %carry.4.rest_0_ = bf16[3,128,512]{2,1,0:T(8,128)(2,1)S(1)} custom-call(s32[8]{0:T(128)S(1)} %copy-done.4, bf16[256,2048]{1,0:T(8,128)(2,1)S(1)} %copy-done, bf16[256,2048]{1,0:T(8,128)(2,1)S(1)} %copy-done.1, bf16[256,2048]{1,0:T(8,128)(2,1)S(1)} %copy-done.2, f32[3,256,512]{2,1,0:T(8,128)S(1)} %get-tuple-element.46.near, ...), custom_call_target="tpu_custom_call" | custom-call | bytes 1024 | tf_op jit(solution)/shard_map/carry/pallas_call | solution.py:291
  22.0 1.6 %collective-permute-start.11 = (bf16[3,128,512]{2,1,0:T(8,128)(2,1)S(1)}, bf16[3,128,512]{2,1,0:T(8,128)(2,1)S(1)}, u32[]{:S(2)}, u32[]{:S(2)}) collective-permute-start(bf16[3,128,512]{2,1,0:T(8,128)(2,1)S(1)} %carry.4.rest_0_), channel_id=1, source_target_pairs={{0,1},{1,0},{2,3},{3,2},{4,5},{5,4},{6,7},{7,6},{8,9},{9,8},{10,11... | collective-permute-start | bytes 1179656 | tf_op jit(solution)/shard_map/ppermute | solution.py:310
  23.6 0.0 collective-permute-done.got
  23.6 0.6 %pair.3 = (bf16[1056,128]{1,0:T(8,128)(2,1)S(1)}, bf16[1040,128]{1,0:T(8,128)(2,1)S(1)}, f32[4,128,128]{2,1,0:T(8,128)S(1)}, f32[4,128,128]{2,1,0:T(8,128)S(1)}) custom-call(s32[8]{0:T(128)S(1)} %copy-done.4, f32[8,128,128]{2,1,0:T(8,128)S(1)} %get-tuple-element.44.kept, f32[8,128,128]{2,1,0:T(8,128)S(1)} %collective-permute-done.got, ...), custom_call_target="tpu_custom_call" | custom-call | bytes 1024 | tf_op jit(solution)/shard_map/pair/pallas_call | solution.py:291
  24.2 0.1 collective-permute-start.7
  24.4 2.9 %collective-permute-start.9 = (bf16[1056,128]{1,0:T(8,128)(2,1)S(1)}, bf16[1056,128]{1,0:T(8,128)(2,1)S(1)}, u32[]{:S(2)}, u32[]{:S(2)}) collective-permute-start(bf16[1056,128]{1,0:T(8,128)(2,1)S(1)} %get-tuple-element.58), channel_id=1, source_target_pairs={{0,6},{4,10},{8,14},{12,18},{16,22},{20,26},{24,30},{6,0},{10,4},{... | collective-permute-start | bytes 811016 | tf_op jit(solution)/shard_map/ppermute | solution.py:304
  27.2 3.0 %collective-permute-start.10 = (bf16[1040,128]{1,0:T(8,128)(2,1)S(1)}, bf16[1040,128]{1,0:T(8,128)(2,1)S(1)}, u32[]{:S(2)}, u32[]{:S(2)}) collective-permute-start(bf16[1040,128]{1,0:T(8,128)(2,1)S(1)} %get-tuple-element.59), channel_id=1, source_target_pairs={{0,10},{4,14},{8,18},{12,22},{16,26},{20,30},{10,0},{14,4},{18,8},... | collective-permute-start | bytes 798728 | tf_op jit(solution)/shard_map/ppermute | solution.py:304
  30.3 0.0 collective-permute-done.14.got
  30.3 0.1 collective-permute-start.8
  30.3 0.9 %carry.5.rest_0_ = bf16[3,128,512]{2,1,0:T(8,128)(2,1)S(1)} custom-call(s32[8]{0:T(128)S(1)} %copy-done.4, bf16[256,2048]{1,0:T(8,128)(2,1)S(1)} %copy-done, bf16[256,2048]{1,0:T(8,128)(2,1)S(1)} %copy-done.1, bf16[256,2048]{1,0:T(8,128)(2,1)S(1)} %copy-done.2, f32[3,256,512]{2,1,0:T(8,128)S(1)} %get-tuple-element.64.near, ...), custom_call_target="tpu_custom_call" | custom-call | bytes 1024 | tf_op jit(solution)/shard_map/carry/pallas_call | solution.py:291
  31.3 0.0 collective-permute-done.7.rest_0_
  31.3 0.6 collective-permute-start.15
  31.9 0.0 collective-permute-done.8.rest_1_
  31.9 3.4 %collective-permute-done.10.rest_3_ = bf16[1040,128]{1,0:T(8,128)(2,1)S(1)} collective-permute-done((bf16[1040,128]{1,0:T(8,128)(2,1)S(1)}, bf16[1040,128]{1,0:T(8,128)(2,1)S(1)}, u32[]{:S(2)}, u32[]{:S(2)}) %collective-permute-start.10) | collective-permute-done | bytes 266272 | tf_op jit(solution)/shard_map/ppermute | solution.py:304
  35.4 0.0 collective-permute-done.9.rest_2_
  35.4 0.0 collective-permute-done.11.rest_4_.refs_2_
  35.4 0.7 %join.5 = (f32[4,128,128]{2,1,0:T(8,128)S(1)}, f32[4,128,128]{2,1,0:T(8,128)S(1)}, f32[4,128,128]{2,1,0:T(8,128)S(1)}, f32[4,128,128]{2,1,0:T(8,128)S(1)}) custom-call(s32[8]{0:T(128)S(1)} %copy-done.4, f32[4,128,128]{2,1,0:T(8,128)S(1)} %collective-permute-done.7.rest_0_, f32[4,128,128]{2,1,0:T(8,128)S(1)} %collective-permute-done.8.rest_1_, ...), custom_call_target="tpu_custom_call" | custom-call | bytes 1024 | tf_op jit(solution)/shard_map/join/pallas_call | solution.py:291
  36.1 0.1 collective-permute-start.13
  36.2 0.5 collective-permute-start.12
  36.7 1.0 %collective-permute-done.13.got = f32[4,128,128]{2,1,0:T(8,128)S(1)} collective-permute-done((f32[4,128,128]{2,1,0:T(8,128)S(1)}, f32[4,128,128]{2,1,0:T(8,128)S(1)}, u32[]{:S(2)}, u32[]{:S(2)}) %collective-permute-start.13) | collective-permute-done | bytes 262176 | tf_op jit(solution)/shard_map/ppermute | solution.py:298
  37.7 2.2 %grads.2 = (bf16[3,128,512]{2,1,0:T(8,128)(2,1)S(1)}, bf16[3,128,512]{2,1,0:T(8,128)(2,1)S(1)}) custom-call(s32[8]{0:T(128)S(1)} %copy-done.4, bf16[256,2048]{1,0:T(8,128)(2,1)S(1)} %copy-done.3, bf16[256,2048]{1,0:T(8,128)(2,1)S(1)} %copy-done, bf16[256,2048]{1,0:T(8,128)(2,1)S(1)} %copy-done.1, bf16[256,2048]{1,0:T(8,128)(2,1)S(1)} %copy-done.2, ...), custom_call_target="tpu_custom_call" | custom-call | bytes 1024 | tf_op jit(solution)/shard_map/grads/pallas_call | solution.py:291
  39.9 0.6 %collective-permute-start.17 = (bf16[3,128,512]{2,1,0:T(8,128)(2,1)S(1)}, bf16[3,128,512]{2,1,0:T(8,128)(2,1)S(1)}, u32[]{:S(2)}, u32[]{:S(2)}) collective-permute-start(bf16[3,128,512]{2,1,0:T(8,128)(2,1)S(1)} %get-tuple-element.66.rest_0_), channel_id=1, source_target_pairs={{0,1},{1,0},{2,3},{3,2},{4,5},{5,4},{6,7},{7,6},{8,9},{9,8},{10,11... | collective-permute-start | bytes 1179656 | tf_op jit(solution)/shard_map/ppermute | solution.py:310
  40.5 2.6 %collective-permute-done.15.rest_1_.refs_1_ = bf16[3,128,512]{2,1,0:T(8,128)(2,1)S(1)} collective-permute-done((bf16[3,128,512]{2,1,0:T(8,128)(2,1)S(1)}, bf16[3,128,512]{2,1,0:T(8,128)(2,1)S(1)}, u32[]{:S(2)}, u32[]{:S(2)}) %collective-permute-start.15) | collective-permute-done | bytes 393248 | tf_op jit(solution)/shard_map/ppermute | solution.py:310
  43.1 0.0 collective-permute-done.12.got
  43.1 2.2 %grads.3 = (bf16[3,128,512]{2,1,0:T(8,128)(2,1)S(1)}, bf16[3,128,512]{2,1,0:T(8,128)(2,1)S(1)}) custom-call(s32[8]{0:T(128)S(1)} %copy-done.4, bf16[256,2048]{1,0:T(8,128)(2,1)S(1)} %copy-done.3, bf16[256,2048]{1,0:T(8,128)(2,1)S(1)} %copy-done, bf16[256,2048]{1,0:T(8,128)(2,1)S(1)} %copy-done.1, bf16[256,2048]{1,0:T(8,128)(2,1)S(1)} %copy-done.2, ...), custom_call_target="tpu_custom_call" | custom-call | bytes 1024 | tf_op jit(solution)/shard_map/grads/pallas_call | solution.py:291
  45.2 0.6 collective-permute-start.16
  45.8 0.9 %carry.7.refs_1_ = bf16[3,128,512]{2,1,0:T(8,128)(2,1)S(1)} custom-call(s32[8]{0:T(128)S(1)} %copy-done.4, bf16[256,2048]{1,0:T(8,128)(2,1)S(1)} %copy-done, bf16[256,2048]{1,0:T(8,128)(2,1)S(1)} %copy-done.1, bf16[256,2048]{1,0:T(8,128)(2,1)S(1)} %copy-done.2, f32[3,256,512]{2,1,0:T(8,128)S(1)} %get-tuple-element.64.near, ...), custom_call_target="tpu_custom_call" | custom-call | bytes 1024 | tf_op jit(solution)/shard_map/carry/pallas_call | solution.py:291
  46.8 1.0 %carry.6.refs_0_ = bf16[3,128,512]{2,1,0:T(8,128)(2,1)S(1)} custom-call(s32[8]{0:T(128)S(1)} %copy-done.4, bf16[256,2048]{1,0:T(8,128)(2,1)S(1)} %copy-done, bf16[256,2048]{1,0:T(8,128)(2,1)S(1)} %copy-done.1, bf16[256,2048]{1,0:T(8,128)(2,1)S(1)} %copy-done.2, f32[3,256,512]{2,1,0:T(8,128)S(1)} %get-tuple-element.46.near, ...), custom_call_target="tpu_custom_call" | custom-call | bytes 1024 | tf_op jit(solution)/shard_map/carry/pallas_call | solution.py:291
  47.7 1.1 %place.4 = (bf16[128,4096]{1,0:T(8,128)(2,1)}, bf16[128,4096]{1,0:T(8,128)(2,1)}, bf16[128,4096]{1,0:T(8,128)(2,1)}) custom-call(bf16[3,128,512]{2,1,0:T(8,128)(2,1)S(1)} %carry.6.refs_0_, bf16[3,128,512]{2,1,0:T(8,128)(2,1)S(1)} %carry.7.refs_1_, bf16[3,128,512]{2,1,0:T(8,128)(2,1)S(1)} %collective-permute-done.11.rest_4_.refs_2_), custom_call_target="tpu_custom_call" | custom-call | bytes 1024 | tf_op jit(solution)/shard_map/place/pallas_call | solution.py:415
  48.8 0.9 %place.5 = (bf16[128,4096]{1,0:T(8,128)(2,1)}, bf16[128,4096]{1,0:T(8,128)(2,1)}, bf16[128,4096]{1,0:T(8,128)(2,1)}) custom-call(bf16[3,128,512]{2,1,0:T(8,128)(2,1)S(1)} %get-tuple-element.69.refs_0_, bf16[3,128,512]{2,1,0:T(8,128)(2,1)S(1)} %collective-permute-done.15.rest_1_.refs_1_, ...), custom_call_target="tpu_custom_call", output_to_operand_aliasing={{0}: (2, {}), {1}: (3, {}), {2}: (4, {})} | custom-call | bytes 1024 | tf_op jit(solution)/shard_map/place/pallas_call | solution.py:415
  49.8 2.1 %collective-permute-done.17.refs_1_ = bf16[3,128,512]{2,1,0:T(8,128)(2,1)S(1)} collective-permute-done((bf16[3,128,512]{2,1,0:T(8,128)(2,1)S(1)}, bf16[3,128,512]{2,1,0:T(8,128)(2,1)S(1)}, u32[]{:S(2)}, u32[]{:S(2)}) %collective-permute-start.17) | collective-permute-done | bytes 393248 | tf_op jit(solution)/shard_map/ppermute | solution.py:310
  51.9 0.9 %place.6 = (bf16[128,4096]{1,0:T(8,128)(2,1)}, bf16[128,4096]{1,0:T(8,128)(2,1)}, bf16[128,4096]{1,0:T(8,128)(2,1)}) custom-call(bf16[3,128,512]{2,1,0:T(8,128)(2,1)S(1)} %get-tuple-element.68.refs_0_, bf16[3,128,512]{2,1,0:T(8,128)(2,1)S(1)} %collective-permute-done.17.refs_1_, ...), custom_call_target="tpu_custom_call", output_to_operand_aliasing={{0}: (2, {}), {1}: (3, {}), {2}: (4, {})} | custom-call | bytes 1024 | tf_op jit(solution)/shard_map/place/pallas_call | solution.py:415
  52.8 6.9 %collective-permute-done.16.refs_0_ = bf16[3,128,512]{2,1,0:T(8,128)(2,1)S(1)} collective-permute-done((bf16[3,128,512]{2,1,0:T(8,128)(2,1)S(1)}, bf16[3,128,512]{2,1,0:T(8,128)(2,1)S(1)}, u32[]{:S(2)}, u32[]{:S(2)}) %collective-permute-start.16) | collective-permute-done | bytes 393248 | tf_op jit(solution)/shard_map/ppermute | solution.py:310
  59.7 0.8 %place.7 = (bf16[128,4096]{1,0:T(8,128)(2,1)}, bf16[128,4096]{1,0:T(8,128)(2,1)}, bf16[128,4096]{1,0:T(8,128)(2,1)}) custom-call(bf16[3,128,512]{2,1,0:T(8,128)(2,1)S(1)} %collective-permute-done.16.refs_0_, bf16[128,4096]{1,0:T(8,128)(2,1)} %get-tuple-element.76.refs_1_, ...), custom_call_target="tpu_custom_call", output_to_operand_aliasing={{0}: (1, {}), {1}: (2, {}), {2}: (3, {})} | custom-call | bytes 1024 | tf_op jit(solution)/shard_map/place/pallas_call | solution.py:415
  (2 shorter events, 0.0 us)
Async XLA Ops:
  0.6 0.7 %copy-start.4 = (s32[8]{0:T(128)S(1)}, s32[8]{0:T(128)}, u32[]{:S(2)}) copy-start(s32[8]{0:T(128)} %lengths.31) | copy-start | bytes 100
  2.9 2.3 %collective-permute-start.1 = (f32[8,128,128]{2,1,0:T(8,128)S(1)}, f32[8,128,128]{2,1,0:T(8,128)S(1)}, u32[]{:S(2)}, u32[]{:S(2)}) collective-permute-start(f32[8,128,128]{2,1,0:T(8,128)S(1)} %states.5), channel_id=1, source_target_pairs={{0,2},{2,0},{4,6},{6,4},{8,10},{10,8},{12,14},{14,12},{16,18},{18,... | collective-permute-start | bytes 1572872 | tf_op jit(solution)/shard_map/ppermute | solution.py:298
  3.5 10.2 %copy-start.1 = (bf16[256,2048]{1,0:T(8,128)(2,1)S(1)}, bf16[256,2048]{1,0:T(8,128)(2,1)}, u32[]{:S(2)}) copy-start(bf16[256,2048]{1,0:T(8,128)(2,1)} %v.21) | copy-start | bytes 3145732
  3.5 10.2 %copy-start.2 = (bf16[256,2048]{1,0:T(8,128)(2,1)S(1)}, bf16[256,2048]{1,0:T(8,128)(2,1)}, u32[]{:S(2)}) copy-start(bf16[256,2048]{1,0:T(8,128)(2,1)} %g.21) | copy-start | bytes 3145732
  3.5 10.2 %copy-start.3 = (bf16[256,2048]{1,0:T(8,128)(2,1)S(1)}, bf16[256,2048]{1,0:T(8,128)(2,1)}, u32[]{:S(2)}) copy-start(bf16[256,2048]{1,0:T(8,128)(2,1)} %q.13) | copy-start | bytes 3145732
  5.3 8.4 %copy-start = (bf16[256,2048]{1,0:T(8,128)(2,1)S(1)}, bf16[256,2048]{1,0:T(8,128)(2,1)}, u32[]{:S(2)}) copy-start(bf16[256,2048]{1,0:T(8,128)(2,1)} %k.21) | copy-start | bytes 3145732
  5.9 12.8 %collective-permute-start.3 = (bf16[1056,128]{1,0:T(8,128)(2,1)S(1)}, bf16[1056,128]{1,0:T(8,128)(2,1)S(1)}, u32[]{:S(2)}, u32[]{:S(2)}) collective-permute-start(bf16[1056,128]{1,0:T(8,128)(2,1)S(1)} %get-tuple-element.49), channel_id=1, source_target_pairs={{0,6},{4,10},{8,14},{12,18},{16,22},{20,26},{24,30},{6,0},{10,4},{... | collective-permute-start | bytes 811016 | tf_op jit(solution)/shard_map/ppermute | solution.py:304
  10.5 8.2 %collective-permute-start.4 = (bf16[1040,128]{1,0:T(8,128)(2,1)S(1)}, bf16[1040,128]{1,0:T(8,128)(2,1)S(1)}, u32[]{:S(2)}, u32[]{:S(2)}) collective-permute-start(bf16[1040,128]{1,0:T(8,128)(2,1)S(1)} %get-tuple-element.50), channel_id=1, source_target_pairs={{0,10},{4,14},{8,18},{12,22},{16,26},{20,30},{10,0},{14,4},{18,8},... | collective-permute-start | bytes 798728 | tf_op jit(solution)/shard_map/ppermute | solution.py:304
  13.5 5.1 %collective-permute-start.2 = (f32[4,128,128]{2,1,0:T(8,128)S(1)}, f32[4,128,128]{2,1,0:T(8,128)S(1)}, u32[]{:S(2)}, u32[]{:S(2)}) collective-permute-start(f32[4,128,128]{2,1,0:T(8,128)S(1)} %get-tuple-element.48), channel_id=1, source_target_pairs={{0,2},{2,0},{4,6},{6,4},{8,10},{10,8},{12,14},{14,12},{16,18},{18,... | collective-permute-start | bytes 786440 | tf_op jit(solution)/shard_map/ppermute | solution.py:298
  16.4 7.1 %collective-permute-start = (f32[8,128,128]{2,1,0:T(8,128)S(1)}, f32[8,128,128]{2,1,0:T(8,128)S(1)}, u32[]{:S(2)}, u32[]{:S(2)}) collective-permute-start(f32[8,128,128]{2,1,0:T(8,128)S(1)} %get-tuple-element.45), channel_id=1, source_target_pairs={{0,2},{2,0},{4,6},{6,4},{8,10},{10,8},{12,14},{14,12},{16,18},{18,... | collective-permute-start | bytes 1572872 | tf_op jit(solution)/shard_map/ppermute | solution.py:298
  17.0 2.9 %collective-permute-start.6 = (f32[4,128,128]{2,1,0:T(8,128)S(1)}, f32[4,128,128]{2,1,0:T(8,128)S(1)}, u32[]{:S(2)}, u32[]{:S(2)}) collective-permute-start(f32[4,128,128]{2,1,0:T(8,128)S(1)} %get-tuple-element.54), channel_id=1, source_target_pairs={{0,2},{2,0},{4,6},{6,4},{8,10},{10,8},{12,14},{14,12},{16,18},{18,... | collective-permute-start | bytes 786440 | tf_op jit(solution)/shard_map/ppermute | solution.py:298
  19.4 1.7 %collective-permute-start.5 = (f32[4,128,128]{2,1,0:T(8,128)S(1)}, f32[4,128,128]{2,1,0:T(8,128)S(1)}, u32[]{:S(2)}, u32[]{:S(2)}) collective-permute-start(f32[4,128,128]{2,1,0:T(8,128)S(1)} %get-tuple-element.53), channel_id=1, source_target_pairs={{0,2},{2,0},{4,6},{6,4},{8,10},{10,8},{12,14},{14,12},{16,18},{18,... | collective-permute-start | bytes 786440 | tf_op jit(solution)/shard_map/ppermute | solution.py:298
  20.5 9.7 %collective-permute-start.14 = (f32[4,128,128]{2,1,0:T(8,128)S(1)}, f32[4,128,128]{2,1,0:T(8,128)S(1)}, u32[]{:S(2)}, u32[]{:S(2)}) collective-permute-start(f32[4,128,128]{2,1,0:T(8,128)S(1)} %get-tuple-element.65), channel_id=1, source_target_pairs={{0,2},{2,0},{4,6},{6,4},{8,10},{10,8},{12,14},{14,12},{16,18},{18,... | collective-permute-start | bytes 786440 | tf_op jit(solution)/shard_map/ppermute | solution.py:298
  22.0 13.4 %collective-permute-start.11 = (bf16[3,128,512]{2,1,0:T(8,128)(2,1)S(1)}, bf16[3,128,512]{2,1,0:T(8,128)(2,1)S(1)}, u32[]{:S(2)}, u32[]{:S(2)}) collective-permute-start(bf16[3,128,512]{2,1,0:T(8,128)(2,1)S(1)} %carry.4.rest_0_), channel_id=1, source_target_pairs={{0,1},{1,0},{2,3},{3,2},{4,5},{5,4},{6,7},{7,6},{8,9},{9,8},{10,11... | collective-permute-start | bytes 1179656 | tf_op jit(solution)/shard_map/ppermute | solution.py:310
  24.2 7.1 %collective-permute-start.7 = (f32[4,128,128]{2,1,0:T(8,128)S(1)}, f32[4,128,128]{2,1,0:T(8,128)S(1)}, u32[]{:S(2)}, u32[]{:S(2)}) collective-permute-start(f32[4,128,128]{2,1,0:T(8,128)S(1)} %get-tuple-element.56), channel_id=1, source_target_pairs={{0,2},{2,0},{4,6},{6,4},{8,10},{10,8},{12,14},{14,12},{16,18},{18,... | collective-permute-start | bytes 786440 | tf_op jit(solution)/shard_map/ppermute | solution.py:298
  24.4 11.0 %collective-permute-start.9 = (bf16[1056,128]{1,0:T(8,128)(2,1)S(1)}, bf16[1056,128]{1,0:T(8,128)(2,1)S(1)}, u32[]{:S(2)}, u32[]{:S(2)}) collective-permute-start(bf16[1056,128]{1,0:T(8,128)(2,1)S(1)} %get-tuple-element.58), channel_id=1, source_target_pairs={{0,6},{4,10},{8,14},{12,18},{16,22},{20,26},{24,30},{6,0},{10,4},{... | collective-permute-start | bytes 811016 | tf_op jit(solution)/shard_map/ppermute | solution.py:304
  27.2 8.1 %collective-permute-start.10 = (bf16[1040,128]{1,0:T(8,128)(2,1)S(1)}, bf16[1040,128]{1,0:T(8,128)(2,1)S(1)}, u32[]{:S(2)}, u32[]{:S(2)}) collective-permute-start(bf16[1040,128]{1,0:T(8,128)(2,1)S(1)} %get-tuple-element.59), channel_id=1, source_target_pairs={{0,10},{4,14},{8,18},{12,22},{16,26},{20,30},{10,0},{14,4},{18,8},... | collective-permute-start | bytes 798728 | tf_op jit(solution)/shard_map/ppermute | solution.py:304
  30.3 1.6 %collective-permute-start.8 = (f32[4,128,128]{2,1,0:T(8,128)S(1)}, f32[4,128,128]{2,1,0:T(8,128)S(1)}, u32[]{:S(2)}, u32[]{:S(2)}) collective-permute-start(f32[4,128,128]{2,1,0:T(8,128)S(1)} %get-tuple-element.57), channel_id=1, source_target_pairs={{0,2},{2,0},{4,6},{6,4},{8,10},{10,8},{12,14},{14,12},{16,18},{18,... | collective-permute-start | bytes 786440 | tf_op jit(solution)/shard_map/ppermute | solution.py:298
  31.3 11.8 %collective-permute-start.15 = (bf16[3,128,512]{2,1,0:T(8,128)(2,1)S(1)}, bf16[3,128,512]{2,1,0:T(8,128)(2,1)S(1)}, u32[]{:S(2)}, u32[]{:S(2)}) collective-permute-start(bf16[3,128,512]{2,1,0:T(8,128)(2,1)S(1)} %carry.5.rest_0_), channel_id=1, source_target_pairs={{0,1},{1,0},{2,3},{3,2},{4,5},{5,4},{6,7},{7,6},{8,9},{9,8},{10,11... | collective-permute-start | bytes 1179656 | tf_op jit(solution)/shard_map/ppermute | solution.py:310
  36.1 1.6 %collective-permute-start.13 = (f32[4,128,128]{2,1,0:T(8,128)S(1)}, f32[4,128,128]{2,1,0:T(8,128)S(1)}, u32[]{:S(2)}, u32[]{:S(2)}) collective-permute-start(f32[4,128,128]{2,1,0:T(8,128)S(1)} %get-tuple-element.63), channel_id=1, source_target_pairs={{0,2},{2,0},{4,6},{6,4},{8,10},{10,8},{12,14},{14,12},{16,18},{18,... | collective-permute-start | bytes 786440 | tf_op jit(solution)/shard_map/ppermute | solution.py:298
  36.2 6.9 %collective-permute-start.12 = (f32[4,128,128]{2,1,0:T(8,128)S(1)}, f32[4,128,128]{2,1,0:T(8,128)S(1)}, u32[]{:S(2)}, u32[]{:S(2)}) collective-permute-start(f32[4,128,128]{2,1,0:T(8,128)S(1)} %get-tuple-element.61), channel_id=1, source_target_pairs={{0,2},{2,0},{4,6},{6,4},{8,10},{10,8},{12,14},{14,12},{16,18},{18,... | collective-permute-start | bytes 786440 | tf_op jit(solution)/shard_map/ppermute | solution.py:298
  39.9 12.0 %collective-permute-start.17 = (bf16[3,128,512]{2,1,0:T(8,128)(2,1)S(1)}, bf16[3,128,512]{2,1,0:T(8,128)(2,1)S(1)}, u32[]{:S(2)}, u32[]{:S(2)}) collective-permute-start(bf16[3,128,512]{2,1,0:T(8,128)(2,1)S(1)} %get-tuple-element.66.rest_0_), channel_id=1, source_target_pairs={{0,1},{1,0},{2,3},{3,2},{4,5},{5,4},{6,7},{7,6},{8,9},{9,8},{10,11... | collective-permute-start | bytes 1179656 | tf_op jit(solution)/shard_map/ppermute | solution.py:310
  45.2 14.5 %collective-permute-start.16 = (bf16[3,128,512]{2,1,0:T(8,128)(2,1)S(1)}, bf16[3,128,512]{2,1,0:T(8,128)(2,1)S(1)}, u32[]{:S(2)}, u32[]{:S(2)}) collective-permute-start(bf16[3,128,512]{2,1,0:T(8,128)(2,1)S(1)} %get-tuple-element.67), channel_id=1, source_target_pairs={{0,1},{1,0},{2,3},{3,2},{4,5},{5,4},{6,7},{7,6},{8,9},{9,8},{10,11... | collective-permute-start | bytes 1179656 | tf_op jit(solution)/shard_map/ppermute | solution.py:310

commit v11 on v8

--- a/solution.py
+++ b/solution.py
@@ -57,7 +57,24 @@
     upper[...] = jnp.where((line <= across) & (line >= begin_across), 1.0, 0.0).astype(upper.dtype)
 
 
-def state_kernel(lengths, q, k, v, g, out, *rest, ndocs, rows, offset, heads, group, kept):
+def fill_table(lengths, table, ndocs, rows, hops):
+    place = lax.axis_index("seq")
+    first_core = lax.rem(place, 2) == 0
+    even = (place - lax.rem(place, 2)) * rows
+    odd = even + rows
+    even_b0, even_e0 = doc_at(lengths, ndocs, even)
+    _, even_e1 = doc_at(lengths, ndocs, odd - 1)
+    odd_b0, _ = doc_at(lengths, ndocs, odd)
+    odd_b1, odd_e1 = doc_at(lengths, ndocs, odd + rows - 1)
+    flags = [(odd_b1 < odd, even_e0 > odd)]
+    flags += [(odd + rows + hop * 2 * rows < odd_e1, even - hop * 2 * rows > even_b0) for hop in range(hops)]
+    flags += [(odd < even_e1, odd > odd_b0), (odd + rows < even_e1, even > odd_b0)]
+    for row, (if_first, if_second) in enumerate(flags):
+        value = jnp.where(jnp.where(first_core, if_first, if_second), 1.0, 0.0)
+        table[row:row + 1] = jnp.full((1, HEAD_DIM), value, jnp.float32)
+
+
+def state_kernel(lengths, q, k, v, g, out, *rest, ndocs, rows, offset, heads, group, kept, hops):
     *masks, held, sems, known, got = rest
     gw = group * HEAD_DIM
     place = lax.axis_index("seq")
@@ -85,7 +102,8 @@
 
     fetch.wait()
     if masks:
-        make_masks(known, *masks, ndocs, rows)
+        make_masks(known, *masks[:2], ndocs, rows)
+        fill_table(known, masks[2], ndocs, rows, hops)
     _, _, _, _, first, last = block_range(known, ndocs, place * rows, rows)
     order = lax.broadcasted_iota(jnp.int32, (rows, HEAD_DIM), 0)
     zero = jnp.zeros((), held.dtype)
@@ -111,15 +129,9 @@
         sent[h] = jnp.where(first_core, head, tail)
 
 
-def pair_kernel(lengths, kept, got, *rest, ndocs, rows, hops, copies):
+def pair_kernel(table, kept, got, *rest, hops, copies):
     sent, again = rest[-hops - copies:len(rest) - copies], rest[len(rest) - copies:]
-    place = lax.axis_index("seq")
-    first_core = lax.rem(place, 2) == 0
-    even = (place - lax.rem(place, 2)) * rows
-    odd = even + rows
-    _, even_e0 = doc_at(lengths, ndocs, even)
-    odd_b1, _ = doc_at(lengths, ndocs, odd + rows - 1)
-    joins = jnp.where(jnp.where(first_core, odd_b1 < odd, even_e0 > odd), 1.0, 0.0)
+    joins = table[0:1]
     size = kept.shape[0] * HEAD_DIM
     total = (got[...] + joins * kept[...]).astype(LINK).reshape(size, HEAD_DIM)
     for out in sent:
@@ -131,25 +143,11 @@
         out[...] = kept[i * count:(i + 1) * count]
 
 
-def join_kernel(lengths, *rest, ndocs, rows, spans, hops):
+def join_kernel(table, *rest, spans, hops):
     others, came = rest[:len(spans)], rest[len(spans):len(spans) + hops]
     mine, theirs = rest[-2 * len(spans):-len(spans)], rest[-len(spans):]
-    place = lax.axis_index("seq")
-    first_core = lax.rem(place, 2) == 0
-    even = (place - lax.rem(place, 2)) * rows
-    odd = even + rows
-    even_b0, _ = doc_at(lengths, ndocs, even)
-    _, even_e1 = doc_at(lengths, ndocs, odd - 1)
-    odd_b0, _ = doc_at(lengths, ndocs, odd)
-    _, odd_e1 = doc_at(lengths, ndocs, odd + rows - 1)
-
-    def one(if_first, if_second):
-        return jnp.where(jnp.where(first_core, if_first, if_second), 1.0, 0.0)
-
-    weights = [
-        one(odd + rows + hop * 2 * rows < odd_e1, even - hop * 2 * rows > even_b0) for hop in range(hops)
-    ]
-    from_other, from_pair = one(odd < even_e1, odd > odd_b0), one(odd + rows < even_e1, even > odd_b0)
+    weights = [table[1 + hop:2 + hop] for hop in range(hops)]
+    from_other, from_pair = table[1 + hops:2 + hops], table[2 + hops:3 + hops]
     for c, (other_at, came_at, count) in enumerate(spans):
         lines = slice(came_at * HEAD_DIM, (came_at + count) * HEAD_DIM)
         total = weights[0] * came[0][lines].astype(jnp.float32)
@@ -301,12 +299,13 @@
     def shape_of(*dims, dtype=f32):
         return jax.ShapeDtypeStruct(dims, dtype)
 
-    def call(name, kernel, args, outs, scratch=(), after=(), limit=VMEM_LIMIT):
+    def call(name, kernel, args, outs, scratch=(), after=(), limit=VMEM_LIMIT, known=None):
+        known = doc_lengths if known is None else known
         return pl.pallas_call(
-            kernel, in_specs=[in_smem] + [in_vmem] * len(args) + [anywhere] * len(after), out_specs=[in_vmem] * len(outs), out_shape=outs,
+            kernel, in_specs=[in_smem if known is doc_lengths else in_vmem] + [in_vmem] * len(args) + [anywhere] * len(after), out_specs=[in_vmem] * len(outs), out_shape=outs,
             scratch_shapes=list(scratch), cost_estimate=cheap,
             compiler_params=pltpu.CompilerParams(vmem_limit_bytes=limit), name=name,
-        )(doc_lengths, *args, *after)
+        )(known, *args, *after)
 
     def swap_cores(a):
         return lax.ppermute(a, "seq", [(b, b ^ 1) for b in range(seq)])
@@ -329,9 +328,9 @@
     def states(kept, offset, half):
         heads = half // HEAD_DIM
         group = GROUP if heads % GROUP == 0 else 2
-        outs = [shape_of(heads, *square)] + [shape_of(rows, rows, dtype=bf16)] * (2 * kept)
+        outs = [shape_of(heads, *square)] + ([shape_of(rows, rows, dtype=bf16)] * 2 + [shape_of(16, HEAD_DIM)]) * kept
         return pl.pallas_call(
-            functools.partial(state_kernel, offset=offset, heads=heads, group=group, kept=kept, **sizes),
+            functools.partial(state_kernel, offset=offset, heads=heads, group=group, kept=kept, hops=hops, **sizes),
             in_specs=[anywhere] * 5, out_specs=[in_vmem] * len(outs), out_shape=outs,
             scratch_shapes=[
                 pltpu.VMEM((2, rows, half), bf16), pltpu.SemaphoreType.DMA((heads // group, 2)),
@@ -347,19 +346,19 @@
             [shape_of(heads, *square)] * 2, after=after, limit=GRAD_LIMIT,
         )
 
-    def pair_up(kept, got, copies, after):
+    def pair_up(table, kept, got, copies, after):
         lines = kept.shape[0] * HEAD_DIM
         outs = [shape_of(lines + PAD * (hops - hop + 1), HEAD_DIM, dtype=LINK) for hop in range(1, hops + 1)]
         outs += [shape_of(kept.shape[0] // max(copies, 1), *square)] * copies
         made = call(
-            "pair", functools.partial(pair_kernel, hops=hops, copies=copies, **sizes), (kept, got), outs, after=after
+            "pair", functools.partial(pair_kernel, hops=hops, copies=copies), (kept, got), outs, after=after, known=table
         )
         return made[hops - 1], swap_pairs(made[:hops]), [swap_cores(a) for a in made[hops:]]
 
-    def join(spans, others, came, after):
+    def join(table, spans, others, came, after):
         made = call(
-            "join", functools.partial(join_kernel, spans=spans, hops=hops, **sizes), (*others, *came),
-            [shape_of(count, *square) for _, _, count in spans] * 2, after=after,
+            "join", functools.partial(join_kernel, spans=spans, hops=hops), (*others, *came),
+            [shape_of(count, *square) for _, _, count in spans] * 2, after=after, known=table,
         )
         return [(mine, swap_cores(theirs)) for mine, theirs in zip(made[:len(spans)], made[len(spans):])]
 
@@ -394,11 +393,11 @@
     for start, half, chunks in halves:
         if not totals:
             (sent,) = states(False, start, half)
-            kept, *masks = states(True, start, half)
+            kept, *masks, table = states(True, start, half)
         else:
             kept, sent = late_states(start, half, [token])
         total, came, others = pair_up(
-            kept, swap_cores(sent), 0 if totals else len(chunks), [made[-1] for made in outs[:1]]
+            table, kept, swap_cores(sent), 0 if totals else len(chunks), [made[-1] for made in outs[:1]]
         )
         if not totals:
             near = [local(masks, *chunk) for chunk in chunks]
@@ -406,11 +405,11 @@
         count = chunks[0][1] // HEAD_DIM
         if totals:
             spans = [(c * count, c * count, count) for c in range(len(chunks))]
-            joined = join(spans, [swap_cores(kept)] * len(chunks), came, [arrived[0][1]])
+            joined = join(table, spans, [swap_cores(kept)] * len(chunks), came, [arrived[0][1]])
         else:
             joined, after = [], [made[1] for made in near]
             for c in range(len(chunks)):
-                joined += join([(0, c * count, count)], others[c:c + 1], came, after)
+                joined += join(table, [(0, c * count, count)], others[c:c + 1], came, after)
                 after = [joined[-1][0]]
         for c, ((offset, cw), (mine, theirs)) in enumerate(zip(chunks, joined)):
             after = [made[-1] for made in outs[-1:]] + [parts[1] for parts in arrived[1:-1]][-1:]

time: 60.4 us -> 58.8 us (0.974)
  Pallas kernels: 22.3 us -> 19.6 us
  waiting for transfers between devices: 15.8 us -> 16.6 us
    pallas_call x13, Pallas kernels: 15.2 us -> 12.4 us  [call(): pl.pallas_call(kernel, in_specs=[in_smem if known is doc_lengths else in_...]
    ppermute x9, waiting for transfers between devices: 1.47 us -> 2.12 us  [swap_cores(): return lax.ppermute(a, 'seq', [(b, b ^ 1) for b in range(seq)])]
  transfers between devices with their start and end apart: 17 -> 17, of which waited for: 7 -> 7; matrix products, arithmetic and copies ran while one was open for 0% -> 0% of each run, Pallas kernels for 32% -> 29%
where the time goes in v11:
time: 58.8 us; the launch traced here: 58.6 us
  starting transfers between devices  20.8 us (35%)
  Pallas kernels  19.6 us (33%)
  waiting for transfers between devices  16.6 us (28%)
  between operations  0.86 us (1%)
  local copies, waits for them, and re-layouts  0.67 us (1%)
    ppermute x4, starting transfers between devices, swap_pairs(): lax.ppermute(sent[hop - 1], 'seq', perm + [(b, a) for a, b in perm])  13.6 us
    pallas_call x13, Pallas kernels, call(): pl.pallas_call(kernel, in_specs=[in_smem if known is doc_lengths else in_...  12.4 us
    ppermute x4, waiting for transfers between devices, send_rows(): lax.ppermute(outs[j], 'head', [(x, (x + j) % groups) for x in range(group...  11.4 us
    ppermute x4, starting transfers between devices, send_rows(): lax.ppermute(outs[j], 'head', [(x, (x + j) % groups) for x in range(group...  4.85 us
    pallas_call x4, Pallas kernels, shards(): pl.pallas_call(functools.partial(place_kernel, groups=groups, plan=[where...  3.71 us
    pallas_call x2, Pallas kernels, states(): pl.pallas_call(functools.partial(state_kernel, offset=offset, heads=heads...  3.44 us
    ppermute x4, waiting for transfers between devices, swap_pairs(): lax.ppermute(sent[hop - 1], 'seq', perm + [(b, a) for a, b in perm])  3.16 us
    ppermute x9, starting transfers between devices, swap_cores(): return lax.ppermute(a, 'seq', [(b, b ^ 1) for b in range(seq)])  2.43 us
  transfers between devices with their start and end apart: 17, of which 7 were waited for; matrix products, arithmetic and copies ran while one was open for 0% of the time, Pallas kernels for 29%

profile of v11, /device:TPU:0, one launch (start us, length us, event | category | flops | bytes accessed | tf_op | source)
XLA Modules:
  0.0 58.6 jit_solution(10416916032743709668)
XLA Ops:
  0.6 0.0 copy-start.4
  0.6 0.6 %copy-done.4 = s32[8]{0:T(128)S(1)} copy-done((s32[8]{0:T(128)S(1)}, s32[8]{0:T(128)}, u32[]{:S(2)}) %copy-start.4) | copy-done | bytes 56
  1.3 1.6 %states.5 = f32[8,128,128]{2,1,0:T(8,128)S(1)} custom-call(s32[8]{0:T(128)S(1)} %copy-done.4, bf16[256,2048]{1,0:T(8,128)(2,1)} %q.13, bf16[256,2048]{1,0:T(8,128)(2,1)} %k.19, bf16[256,2048]{1,0:T(8,128)(2,1)} %v.19, bf16[256,2048]{1,0:T(8,128)(2,1)} %g.19), custom_call_target="tpu_custom_call" | custom-call | bytes 1024 | tf_op jit(solution)/shard_map/states/pallas_call | solution.py:332
  2.9 0.5 collective-permute-start.2
  3.5 0.0 copy-start.1
  3.5 0.0 copy-start.2
  3.5 0.0 copy-start.3
  3.5 1.8 %states.3 = (f32[8,128,128]{2,1,0:T(8,128)S(1)}, bf16[256,256]{1,0:T(8,128)(2,1)S(1)}, bf16[256,256]{1,0:T(8,128)(2,1)S(1)}, f32[16,128]{1,0:T(8,128)S(1)}) custom-call(s32[8]{0:T(128)S(1)} %copy-done.4, bf16[256,2048]{1,0:T(8,128)(2,1)} %q.13, bf16[256,2048]{1,0:T(8,128)(2,1)} %k.19, bf16[256,2048]{1,0:T(8,128)(2,1)} %v.19, bf16[256,2048]{1,0:T(8,128)(2,1)} %g.19), custom_call_target="tpu_custom_call" | custom-call | bytes 1024 | tf_op jit(solution)/shard_map/states/pallas_call | solution.py:332
  5.3 0.0 copy-start
  5.3 0.0 collective-permute-done.2.got
  5.3 0.1 pair.2
  5.4 4.7 %collective-permute-start.4 = (bf16[1056,128]{1,0:T(8,128)(2,1)S(1)}, bf16[1056,128]{1,0:T(8,128)(2,1)S(1)}, u32[]{:S(2)}, u32[]{:S(2)}) collective-permute-start(bf16[1056,128]{1,0:T(8,128)(2,1)S(1)} %get-tuple-element.51), channel_id=1, source_target_pairs={{0,6},{4,10},{8,14},{12,18},{16,22},{20,26},{24,30},{6,0},{10,4},{... | collective-permute-start | bytes 811016 | tf_op jit(solution)/shard_map/ppermute | solution.py:317
  10.1 3.1 %collective-permute-start.5 = (bf16[1040,128]{1,0:T(8,128)(2,1)S(1)}, bf16[1040,128]{1,0:T(8,128)(2,1)S(1)}, u32[]{:S(2)}, u32[]{:S(2)}) collective-permute-start(bf16[1040,128]{1,0:T(8,128)(2,1)S(1)} %get-tuple-element.52), channel_id=1, source_target_pairs={{0,10},{4,14},{8,18},{12,22},{16,26},{20,30},{10,0},{14,4},{18,8},... | collective-permute-start | bytes 798728 | tf_op jit(solution)/shard_map/ppermute | solution.py:317
  13.1 0.1 collective-permute-start.3
  13.2 0.0 copy-done.1
  13.2 0.0 copy-done.2
  13.2 0.0 copy-done.3
  13.2 0.0 copy-done
  13.3 1.6 %local.2 = (f32[3,256,512]{2,1,0:T(8,128)S(1)}, f32[8,128]{1,0:T(8,128)S(1)}) custom-call(s32[8]{0:T(128)S(1)} %copy-done.4, bf16[256,2048]{1,0:T(8,128)(2,1)S(1)} %copy-done.3, bf16[256,2048]{1,0:T(8,128)(2,1)S(1)} %copy-done, bf16[256,2048]{1,0:T(8,128)(2,1)S(1)} %copy-done.1, bf16[256,2048]{1,0:T(8,128)(2,1)S(1)} %copy-done.2, ...), custom_call_target="tpu_custom_call" | custom-call | bytes 1024 | tf_op jit(solution)/shard_map/local/pallas_call | solution.py:304
  14.9 1.2 %states.4 = (f32[8,128,128]{2,1,0:T(8,128)S(1)}, f32[8,128,128]{2,1,0:T(8,128)S(1)}) custom-call(s32[8]{0:T(128)S(1)} %copy-done.4, bf16[256,2048]{1,0:T(8,128)(2,1)S(1)} %copy-done.3, bf16[256,2048]{1,0:T(8,128)(2,1)S(1)} %copy-done, bf16[256,2048]{1,0:T(8,128)(2,1)S(1)} %copy-done.1, bf16[256,2048]{1,0:T(8,128)(2,1)S(1)} %copy-done.2, ...), custom_call_target="tpu_custom_call" | custom-call | bytes 1024 | tf_op jit(solution)/shard_map/states/pallas_call | solution.py:304
  16.0 0.5 collective-permute-start.1
  16.6 1.6 %local.3 = (f32[3,256,512]{2,1,0:T(8,128)S(1)}, f32[8,128]{1,0:T(8,128)S(1)}) custom-call(s32[8]{0:T(128)S(1)} %copy-done.4, bf16[256,2048]{1,0:T(8,128)(2,1)S(1)} %copy-done.3, bf16[256,2048]{1,0:T(8,128)(2,1)S(1)} %copy-done, bf16[256,2048]{1,0:T(8,128)(2,1)S(1)} %copy-done.1, bf16[256,2048]{1,0:T(8,128)(2,1)S(1)} %copy-done.2, ...), custom_call_target="tpu_custom_call" | custom-call | bytes 1024 | tf_op jit(solution)/shard_map/local/pallas_call | solution.py:304
  18.2 0.1 collective-permute-start.7
  18.3 0.0 collective-permute-done.3.rest_0_
  18.3 0.0 collective-permute-done.5.rest_2_
  18.3 0.0 collective-permute-done.4.rest_1_
  18.3 0.1 join.3
  18.4 0.5 collective-permute-start.6
  18.9 0.1 collective-permute-start
  19.0 0.8 %collective-permute-done.7.rest_0_ = f32[4,128,128]{2,1,0:T(8,128)S(1)} collective-permute-done((f32[4,128,128]{2,1,0:T(8,128)S(1)}, f32[4,128,128]{2,1,0:T(8,128)S(1)}, u32[]{:S(2)}, u32[]{:S(2)}) %collective-permute-start.7) | collective-permute-done | bytes 262176 | tf_op jit(solution)/shard_map/ppermute | solution.py:311
  19.8 0.1 join.4
  19.9 0.3 collective-permute-done.6.got
  20.2 0.9 %carry.3.rest_0_ = bf16[3,128,512]{2,1,0:T(8,128)(2,1)S(1)} custom-call(s32[8]{0:T(128)S(1)} %copy-done.4, bf16[256,2048]{1,0:T(8,128)(2,1)S(1)} %copy-done, bf16[256,2048]{1,0:T(8,128)(2,1)S(1)} %copy-done.1, bf16[256,2048]{1,0:T(8,128)(2,1)S(1)} %copy-done.2, f32[3,256,512]{2,1,0:T(8,128)S(1)} %get-tuple-element.48.near, ...), custom_call_target="tpu_custom_call" | custom-call | bytes 1024 | tf_op jit(solution)/shard_map/carry/pallas_call | solution.py:304
  21.1 1.6 %collective-permute-start.10 = (bf16[3,128,512]{2,1,0:T(8,128)(2,1)S(1)}, bf16[3,128,512]{2,1,0:T(8,128)(2,1)S(1)}, u32[]{:S(2)}, u32[]{:S(2)}) collective-permute-start(bf16[3,128,512]{2,1,0:T(8,128)(2,1)S(1)} %carry.3.rest_0_), channel_id=1, source_target_pairs={{0,1},{1,0},{2,3},{3,2},{4,5},{5,4},{6,7},{7,6},{8,9},{9,8},{10,11... | collective-permute-start | bytes 1179656 | tf_op jit(solution)/shard_map/ppermute | solution.py:323
  22.7 0.0 collective-permute-start.13
  22.7 0.0 collective-permute-done.1.got
  22.7 0.1 pair.3
  22.8 2.9 %collective-permute-start.8 = (bf16[1056,128]{1,0:T(8,128)(2,1)S(1)}, bf16[1056,128]{1,0:T(8,128)(2,1)S(1)}, u32[]{:S(2)}, u32[]{:S(2)}) collective-permute-start(bf16[1056,128]{1,0:T(8,128)(2,1)S(1)} %get-tuple-element.58), channel_id=1, source_target_pairs={{0,6},{4,10},{8,14},{12,18},{16,22},{20,26},{24,30},{6,0},{10,4},{... | collective-permute-start | bytes 811016 | tf_op jit(solution)/shard_map/ppermute | solution.py:317
  25.6 3.0 %collective-permute-start.9 = (bf16[1040,128]{1,0:T(8,128)(2,1)S(1)}, bf16[1040,128]{1,0:T(8,128)(2,1)S(1)}, u32[]{:S(2)}, u32[]{:S(2)}) collective-permute-start(bf16[1040,128]{1,0:T(8,128)(2,1)S(1)} %get-tuple-element.59), channel_id=1, source_target_pairs={{0,10},{4,14},{8,18},{12,22},{16,26},{20,30},{10,0},{14,4},{18,8},... | collective-permute-start | bytes 798728 | tf_op jit(solution)/shard_map/ppermute | solution.py:317
  28.6 0.0 collective-permute-done.13.got
  28.6 1.3 %carry.4 = (bf16[3,128,512]{2,1,0:T(8,128)(2,1)S(1)}, bf16[3,128,512]{2,1,0:T(8,128)(2,1)S(1)}) custom-call(s32[8]{0:T(128)S(1)} %copy-done.4, bf16[256,2048]{1,0:T(8,128)(2,1)S(1)} %copy-done, bf16[256,2048]{1,0:T(8,128)(2,1)S(1)} %copy-done.1, bf16[256,2048]{1,0:T(8,128)(2,1)S(1)} %copy-done.2, f32[3,256,512]{2,1,0:T(8,128)S(1)} %get-tuple-element.64.near, ...), custom_call_target="tpu_custom_call" | custom-call | bytes 1024 | tf_op jit(solution)/shard_map/carry/pallas_call | solution.py:304
  29.9 0.6 %collective-permute-start.14 = (bf16[3,128,512]{2,1,0:T(8,128)(2,1)S(1)}, bf16[3,128,512]{2,1,0:T(8,128)(2,1)S(1)}, u32[]{:S(2)}, u32[]{:S(2)}) collective-permute-start(bf16[3,128,512]{2,1,0:T(8,128)(2,1)S(1)} %get-tuple-element.66.rest_0_), channel_id=1, source_target_pairs={{0,1},{1,0},{2,3},{3,2},{4,5},{5,4},{6,7},{7,6},{8,9},{9,8},{10,11... | collective-permute-start | bytes 1179656 | tf_op jit(solution)/shard_map/ppermute | solution.py:323
  30.5 0.0 collective-permute-done.rest_0_.rest_1_
  30.5 3.2 %collective-permute-done.9.rest_3_ = bf16[1040,128]{1,0:T(8,128)(2,1)S(1)} collective-permute-done((bf16[1040,128]{1,0:T(8,128)(2,1)S(1)}, bf16[1040,128]{1,0:T(8,128)(2,1)S(1)}, u32[]{:S(2)}, u32[]{:S(2)}) %collective-permute-start.9) | collective-permute-done | bytes 266272 | tf_op jit(solution)/shard_map/ppermute | solution.py:317
  33.7 0.0 collective-permute-done.8.rest_2_
  33.7 0.0 collective-permute-done.10.rest_4_.refs_2_
  33.7 0.1 join.5
  33.9 0.1 collective-permute-start.12
  33.9 0.5 collective-permute-start.11
  34.4 1.0 %collective-permute-done.12.got = f32[4,128,128]{2,1,0:T(8,128)S(1)} collective-permute-done((f32[4,128,128]{2,1,0:T(8,128)S(1)}, f32[4,128,128]{2,1,0:T(8,128)S(1)}, u32[]{:S(2)}, u32[]{:S(2)}) %collective-permute-start.12) | collective-permute-done | bytes 262176 | tf_op jit(solution)/shard_map/ppermute | solution.py:311
  35.5 2.2 %grads.2 = (bf16[3,128,512]{2,1,0:T(8,128)(2,1)S(1)}, bf16[3,128,512]{2,1,0:T(8,128)(2,1)S(1)}) custom-call(s32[8]{0:T(128)S(1)} %copy-done.4, bf16[256,2048]{1,0:T(8,128)(2,1)S(1)} %copy-done.3, bf16[256,2048]{1,0:T(8,128)(2,1)S(1)} %copy-done, bf16[256,2048]{1,0:T(8,128)(2,1)S(1)} %copy-done.1, bf16[256,2048]{1,0:T(8,128)(2,1)S(1)} %copy-done.2, ...), custom_call_target="tpu_custom_call" | custom-call | bytes 1024 | tf_op jit(solution)/shard_map/grads/pallas_call | solution.py:304
  37.6 1.0 %collective-permute-start.16 = (bf16[3,128,512]{2,1,0:T(8,128)(2,1)S(1)}, bf16[3,128,512]{2,1,0:T(8,128)(2,1)S(1)}, u32[]{:S(2)}, u32[]{:S(2)}) collective-permute-start(bf16[3,128,512]{2,1,0:T(8,128)(2,1)S(1)} %get-tuple-element.67.rest_0_), channel_id=1, source_target_pairs={{0,1},{1,0},{2,3},{3,2},{4,5},{5,4},{6,7},{7,6},{8,9},{9,8},{10,11... | collective-permute-start | bytes 1179656 | tf_op jit(solution)/shard_map/ppermute | solution.py:323
  38.6 2.8 %collective-permute-done.14.rest_1_.refs_1_ = bf16[3,128,512]{2,1,0:T(8,128)(2,1)S(1)} collective-permute-done((bf16[3,128,512]{2,1,0:T(8,128)(2,1)S(1)}, bf16[3,128,512]{2,1,0:T(8,128)(2,1)S(1)}, u32[]{:S(2)}, u32[]{:S(2)}) %collective-permute-start.14) | collective-permute-done | bytes 393248 | tf_op jit(solution)/shard_map/ppermute | solution.py:323
  41.4 0.0 collective-permute-done.11.got
  41.4 2.2 %grads.3 = (bf16[3,128,512]{2,1,0:T(8,128)(2,1)S(1)}, bf16[3,128,512]{2,1,0:T(8,128)(2,1)S(1)}) custom-call(s32[8]{0:T(128)S(1)} %copy-done.4, bf16[256,2048]{1,0:T(8,128)(2,1)S(1)} %copy-done.3, bf16[256,2048]{1,0:T(8,128)(2,1)S(1)} %copy-done, bf16[256,2048]{1,0:T(8,128)(2,1)S(1)} %copy-done.1, bf16[256,2048]{1,0:T(8,128)(2,1)S(1)} %copy-done.2, ...), custom_call_target="tpu_custom_call" | custom-call | bytes 1024 | tf_op jit(solution)/shard_map/grads/pallas_call | solution.py:304
  43.5 1.7 %collective-permute-start.15 = (bf16[3,128,512]{2,1,0:T(8,128)(2,1)S(1)}, bf16[3,128,512]{2,1,0:T(8,128)(2,1)S(1)}, u32[]{:S(2)}, u32[]{:S(2)}) collective-permute-start(bf16[3,128,512]{2,1,0:T(8,128)(2,1)S(1)} %get-tuple-element.68), channel_id=1, source_target_pairs={{0,1},{1,0},{2,3},{3,2},{4,5},{5,4},{6,7},{7,6},{8,9},{9,8},{10,11... | collective-permute-start | bytes 1179656 | tf_op jit(solution)/shard_map/ppermute | solution.py:323
  45.3 0.9 %carry.5.refs_0_ = bf16[3,128,512]{2,1,0:T(8,128)(2,1)S(1)} custom-call(s32[8]{0:T(128)S(1)} %copy-done.4, bf16[256,2048]{1,0:T(8,128)(2,1)S(1)} %copy-done, bf16[256,2048]{1,0:T(8,128)(2,1)S(1)} %copy-done.1, bf16[256,2048]{1,0:T(8,128)(2,1)S(1)} %copy-done.2, f32[3,256,512]{2,1,0:T(8,128)S(1)} %get-tuple-element.48.near, ...), custom_call_target="tpu_custom_call" | custom-call | bytes 1024 | tf_op jit(solution)/shard_map/carry/pallas_call | solution.py:304
  46.2 1.1 %place.4 = (bf16[128,4096]{1,0:T(8,128)(2,1)}, bf16[128,4096]{1,0:T(8,128)(2,1)}, bf16[128,4096]{1,0:T(8,128)(2,1)}) custom-call(bf16[3,128,512]{2,1,0:T(8,128)(2,1)S(1)} %carry.5.refs_0_, bf16[3,128,512]{2,1,0:T(8,128)(2,1)S(1)} %get-tuple-element.71.refs_1_, bf16[3,128,512]{2,1,0:T(8,128)(2,1)S(1)} %collective-permute-done.10.rest_4_.refs_2_), custom_call_target="tpu_custom_call" | custom-call | bytes 1024 | tf_op jit(solution)/shard_map/place/pallas_call | solution.py:435
  47.3 0.9 %place.5 = (bf16[128,4096]{1,0:T(8,128)(2,1)}, bf16[128,4096]{1,0:T(8,128)(2,1)}, bf16[128,4096]{1,0:T(8,128)(2,1)}) custom-call(bf16[3,128,512]{2,1,0:T(8,128)(2,1)S(1)} %get-tuple-element.70.refs_0_, bf16[3,128,512]{2,1,0:T(8,128)(2,1)S(1)} %collective-permute-done.14.rest_1_.refs_1_, ...), custom_call_target="tpu_custom_call", output_to_operand_aliasing={{0}: (2, {}), {1}: (3, {}), {2}: (4, {})} | custom-call | bytes 1024 | tf_op jit(solution)/shard_map/place/pallas_call | solution.py:435
  48.3 1.5 %collective-permute-done.16.refs_1_ = bf16[3,128,512]{2,1,0:T(8,128)(2,1)S(1)} collective-permute-done((bf16[3,128,512]{2,1,0:T(8,128)(2,1)S(1)}, bf16[3,128,512]{2,1,0:T(8,128)(2,1)S(1)}, u32[]{:S(2)}, u32[]{:S(2)}) %collective-permute-start.16) | collective-permute-done | bytes 393248 | tf_op jit(solution)/shard_map/ppermute | solution.py:323
  49.8 0.9 %place.6 = (bf16[128,4096]{1,0:T(8,128)(2,1)}, bf16[128,4096]{1,0:T(8,128)(2,1)}, bf16[128,4096]{1,0:T(8,128)(2,1)}) custom-call(bf16[3,128,512]{2,1,0:T(8,128)(2,1)S(1)} %get-tuple-element.69.refs_0_, bf16[3,128,512]{2,1,0:T(8,128)(2,1)S(1)} %collective-permute-done.16.refs_1_, ...), custom_call_target="tpu_custom_call", output_to_operand_aliasing={{0}: (2, {}), {1}: (3, {}), {2}: (4, {})} | custom-call | bytes 1024 | tf_op jit(solution)/shard_map/place/pallas_call | solution.py:435
  50.7 7.1 %collective-permute-done.15.refs_0_ = bf16[3,128,512]{2,1,0:T(8,128)(2,1)S(1)} collective-permute-done((bf16[3,128,512]{2,1,0:T(8,128)(2,1)S(1)}, bf16[3,128,512]{2,1,0:T(8,128)(2,1)S(1)}, u32[]{:S(2)}, u32[]{:S(2)}) %collective-permute-start.15) | collective-permute-done | bytes 393248 | tf_op jit(solution)/shard_map/ppermute | solution.py:323
  57.8 0.8 %place.7 = (bf16[128,4096]{1,0:T(8,128)(2,1)}, bf16[128,4096]{1,0:T(8,128)(2,1)}, bf16[128,4096]{1,0:T(8,128)(2,1)}) custom-call(bf16[3,128,512]{2,1,0:T(8,128)(2,1)S(1)} %collective-permute-done.15.refs_0_, bf16[128,4096]{1,0:T(8,128)(2,1)} %get-tuple-element.78.refs_1_, ...), custom_call_target="tpu_custom_call", output_to_operand_aliasing={{0}: (1, {}), {1}: (2, {}), {2}: (3, {})} | custom-call | bytes 1024 | tf_op jit(solution)/shard_map/place/pallas_call | solution.py:435
Async XLA Ops:
  0.6 0.7 %copy-start.4 = (s32[8]{0:T(128)S(1)}, s32[8]{0:T(128)}, u32[]{:S(2)}) copy-start(s32[8]{0:T(128)} %lengths.19) | copy-start | bytes 100
  2.9 2.3 %collective-permute-start.2 = (f32[8,128,128]{2,1,0:T(8,128)S(1)}, f32[8,128,128]{2,1,0:T(8,128)S(1)}, u32[]{:S(2)}, u32[]{:S(2)}) collective-permute-start(f32[8,128,128]{2,1,0:T(8,128)S(1)} %states.5), channel_id=1, source_target_pairs={{0,2},{2,0},{4,6},{6,4},{8,10},{10,8},{12,14},{14,12},{16,18},{18,... | collective-permute-start | bytes 1572872 | tf_op jit(solution)/shard_map/ppermute | solution.py:311
  3.5 9.8 %copy-start.1 = (bf16[256,2048]{1,0:T(8,128)(2,1)S(1)}, bf16[256,2048]{1,0:T(8,128)(2,1)}, u32[]{:S(2)}) copy-start(bf16[256,2048]{1,0:T(8,128)(2,1)} %v.19) | copy-start | bytes 3145732
  3.5 9.8 %copy-start.2 = (bf16[256,2048]{1,0:T(8,128)(2,1)S(1)}, bf16[256,2048]{1,0:T(8,128)(2,1)}, u32[]{:S(2)}) copy-start(bf16[256,2048]{1,0:T(8,128)(2,1)} %g.19) | copy-start | bytes 3145732
  3.5 9.8 %copy-start.3 = (bf16[256,2048]{1,0:T(8,128)(2,1)S(1)}, bf16[256,2048]{1,0:T(8,128)(2,1)}, u32[]{:S(2)}) copy-start(bf16[256,2048]{1,0:T(8,128)(2,1)} %q.13) | copy-start | bytes 3145732
  5.3 8.0 %copy-start = (bf16[256,2048]{1,0:T(8,128)(2,1)S(1)}, bf16[256,2048]{1,0:T(8,128)(2,1)}, u32[]{:S(2)}) copy-start(bf16[256,2048]{1,0:T(8,128)(2,1)} %k.19) | copy-start | bytes 3145732
  5.4 12.9 %collective-permute-start.4 = (bf16[1056,128]{1,0:T(8,128)(2,1)S(1)}, bf16[1056,128]{1,0:T(8,128)(2,1)S(1)}, u32[]{:S(2)}, u32[]{:S(2)}) collective-permute-start(bf16[1056,128]{1,0:T(8,128)(2,1)S(1)} %get-tuple-element.51), channel_id=1, source_target_pairs={{0,6},{4,10},{8,14},{12,18},{16,22},{20,26},{24,30},{6,0},{10,4},{... | collective-permute-start | bytes 811016 | tf_op jit(solution)/shard_map/ppermute | solution.py:317
  10.1 8.2 %collective-permute-start.5 = (bf16[1040,128]{1,0:T(8,128)(2,1)S(1)}, bf16[1040,128]{1,0:T(8,128)(2,1)S(1)}, u32[]{:S(2)}, u32[]{:S(2)}) collective-permute-start(bf16[1040,128]{1,0:T(8,128)(2,1)S(1)} %get-tuple-element.52), channel_id=1, source_target_pairs={{0,10},{4,14},{8,18},{12,22},{16,26},{20,30},{10,0},{14,4},{18,8},... | collective-permute-start | bytes 798728 | tf_op jit(solution)/shard_map/ppermute | solution.py:317
  13.1 5.2 %collective-permute-start.3 = (f32[4,128,128]{2,1,0:T(8,128)S(1)}, f32[4,128,128]{2,1,0:T(8,128)S(1)}, u32[]{:S(2)}, u32[]{:S(2)}) collective-permute-start(f32[4,128,128]{2,1,0:T(8,128)S(1)} %get-tuple-element.50), channel_id=1, source_target_pairs={{0,2},{2,0},{4,6},{6,4},{8,10},{10,8},{12,14},{14,12},{16,18},{18,... | collective-permute-start | bytes 786440 | tf_op jit(solution)/shard_map/ppermute | solution.py:311
  16.0 6.7 %collective-permute-start.1 = (f32[8,128,128]{2,1,0:T(8,128)S(1)}, f32[8,128,128]{2,1,0:T(8,128)S(1)}, u32[]{:S(2)}, u32[]{:S(2)}) collective-permute-start(f32[8,128,128]{2,1,0:T(8,128)S(1)} %get-tuple-element.47), channel_id=1, source_target_pairs={{0,2},{2,0},{4,6},{6,4},{8,10},{10,8},{12,14},{14,12},{16,18},{18,... | collective-permute-start | bytes 1572872 | tf_op jit(solution)/shard_map/ppermute | solution.py:311
  18.2 1.6 %collective-permute-start.7 = (f32[4,128,128]{2,1,0:T(8,128)S(1)}, f32[4,128,128]{2,1,0:T(8,128)S(1)}, u32[]{:S(2)}, u32[]{:S(2)}) collective-permute-start(f32[4,128,128]{2,1,0:T(8,128)S(1)} %get-tuple-element.56), channel_id=1, source_target_pairs={{0,2},{2,0},{4,6},{6,4},{8,10},{10,8},{12,14},{14,12},{16,18},{18,... | collective-permute-start | bytes 786440 | tf_op jit(solution)/shard_map/ppermute | solution.py:311
  18.4 1.8 %collective-permute-start.6 = (f32[4,128,128]{2,1,0:T(8,128)S(1)}, f32[4,128,128]{2,1,0:T(8,128)S(1)}, u32[]{:S(2)}, u32[]{:S(2)}) collective-permute-start(f32[4,128,128]{2,1,0:T(8,128)S(1)} %get-tuple-element.55), channel_id=1, source_target_pairs={{0,2},{2,0},{4,6},{6,4},{8,10},{10,8},{12,14},{14,12},{16,18},{18,... | collective-permute-start | bytes 786440 | tf_op jit(solution)/shard_map/ppermute | solution.py:311
  18.9 11.6 %collective-permute-start = (f32[8,128,128]{2,1,0:T(8,128)S(1)}, f32[8,128,128]{2,1,0:T(8,128)S(1)}, u32[]{:S(2)}, u32[]{:S(2)}) collective-permute-start(f32[8,128,128]{2,1,0:T(8,128)S(1)} %get-tuple-element.46.kept), channel_id=1, source_target_pairs={{0,2},{2,0},{4,6},{6,4},{8,10},{10,8},{12,14},{14,12},{16,18},{18,... | collective-permute-start | bytes 1572872 | tf_op jit(solution)/shard_map/ppermute | solution.py:311
  21.1 12.6 %collective-permute-start.10 = (bf16[3,128,512]{2,1,0:T(8,128)(2,1)S(1)}, bf16[3,128,512]{2,1,0:T(8,128)(2,1)S(1)}, u32[]{:S(2)}, u32[]{:S(2)}) collective-permute-start(bf16[3,128,512]{2,1,0:T(8,128)(2,1)S(1)} %carry.3.rest_0_), channel_id=1, source_target_pairs={{0,1},{1,0},{2,3},{3,2},{4,5},{5,4},{6,7},{7,6},{8,9},{9,8},{10,11... | collective-permute-start | bytes 1179656 | tf_op jit(solution)/shard_map/ppermute | solution.py:323
  22.7 5.9 %collective-permute-start.13 = (f32[4,128,128]{2,1,0:T(8,128)S(1)}, f32[4,128,128]{2,1,0:T(8,128)S(1)}, u32[]{:S(2)}, u32[]{:S(2)}) collective-permute-start(f32[4,128,128]{2,1,0:T(8,128)S(1)} %get-tuple-element.65), channel_id=1, source_target_pairs={{0,2},{2,0},{4,6},{6,4},{8,10},{10,8},{12,14},{14,12},{16,18},{18,... | collective-permute-start | bytes 786440 | tf_op jit(solution)/shard_map/ppermute | solution.py:311
  22.8 11.0 %collective-permute-start.8 = (bf16[1056,128]{1,0:T(8,128)(2,1)S(1)}, bf16[1056,128]{1,0:T(8,128)(2,1)S(1)}, u32[]{:S(2)}, u32[]{:S(2)}) collective-permute-start(bf16[1056,128]{1,0:T(8,128)(2,1)S(1)} %get-tuple-element.58), channel_id=1, source_target_pairs={{0,6},{4,10},{8,14},{12,18},{16,22},{20,26},{24,30},{6,0},{10,4},{... | collective-permute-start | bytes 811016 | tf_op jit(solution)/shard_map/ppermute | solution.py:317
  25.6 8.1 %collective-permute-start.9 = (bf16[1040,128]{1,0:T(8,128)(2,1)S(1)}, bf16[1040,128]{1,0:T(8,128)(2,1)S(1)}, u32[]{:S(2)}, u32[]{:S(2)}) collective-permute-start(bf16[1040,128]{1,0:T(8,128)(2,1)S(1)} %get-tuple-element.59), channel_id=1, source_target_pairs={{0,10},{4,14},{8,18},{12,22},{16,26},{20,30},{10,0},{14,4},{18,8},... | collective-permute-start | bytes 798728 | tf_op jit(solution)/shard_map/ppermute | solution.py:317
  29.9 11.4 %collective-permute-start.14 = (bf16[3,128,512]{2,1,0:T(8,128)(2,1)S(1)}, bf16[3,128,512]{2,1,0:T(8,128)(2,1)S(1)}, u32[]{:S(2)}, u32[]{:S(2)}) collective-permute-start(bf16[3,128,512]{2,1,0:T(8,128)(2,1)S(1)} %get-tuple-element.66.rest_0_), channel_id=1, source_target_pairs={{0,1},{1,0},{2,3},{3,2},{4,5},{5,4},{6,7},{7,6},{8,9},{9,8},{10,11... | collective-permute-start | bytes 1179656 | tf_op jit(solution)/shard_map/ppermute | solution.py:323
  33.9 1.6 %collective-permute-start.12 = (f32[4,128,128]{2,1,0:T(8,128)S(1)}, f32[4,128,128]{2,1,0:T(8,128)S(1)}, u32[]{:S(2)}, u32[]{:S(2)}) collective-permute-start(f32[4,128,128]{2,1,0:T(8,128)S(1)} %get-tuple-element.63), channel_id=1, source_target_pairs={{0,2},{2,0},{4,6},{6,4},{8,10},{10,8},{12,14},{14,12},{16,18},{18,... | collective-permute-start | bytes 786440 | tf_op jit(solution)/shard_map/ppermute | solution.py:311
  33.9 7.4 %collective-permute-start.11 = (f32[4,128,128]{2,1,0:T(8,128)S(1)}, f32[4,128,128]{2,1,0:T(8,128)S(1)}, u32[]{:S(2)}, u32[]{:S(2)}) collective-permute-start(f32[4,128,128]{2,1,0:T(8,128)S(1)} %get-tuple-element.61), channel_id=1, source_target_pairs={{0,2},{2,0},{4,6},{6,4},{8,10},{10,8},{12,14},{14,12},{16,18},{18,... | collective-permute-start | bytes 786440 | tf_op jit(solution)/shard_map/ppermute | solution.py:311
  37.6 12.1 %collective-permute-start.16 = (bf16[3,128,512]{2,1,0:T(8,128)(2,1)S(1)}, bf16[3,128,512]{2,1,0:T(8,128)(2,1)S(1)}, u32[]{:S(2)}, u32[]{:S(2)}) collective-permute-start(bf16[3,128,512]{2,1,0:T(8,128)(2,1)S(1)} %get-tuple-element.67.rest_0_), channel_id=1, source_target_pairs={{0,1},{1,0},{2,3},{3,2},{4,5},{5,4},{6,7},{7,6},{8,9},{9,8},{10,11... | collective-permute-start | bytes 1179656 | tf_op jit(solution)/shard_map/ppermute | solution.py:323
  43.5 14.2 %collective-permute-start.15 = (bf16[3,128,512]{2,1,0:T(8,128)(2,1)S(1)}, bf16[3,128,512]{2,1,0:T(8,128)(2,1)S(1)}, u32[]{:S(2)}, u32[]{:S(2)}) collective-permute-start(bf16[3,128,512]{2,1,0:T(8,128)(2,1)S(1)} %get-tuple-element.68), channel_id=1, source_target_pairs={{0,1},{1,0},{2,3},{3,2},{4,5},{5,4},{6,7},{7,6},{8,9},{9,8},{10,11... | collective-permute-start | bytes 1179656 | tf_op jit(solution)/shard_map/ppermute | solution.py:323

commit v12 on v11

--- a/solution.py
+++ b/solution.py
@@ -12,6 +12,7 @@
 GROUP = 4
 CHUNK = 4
 PAD = 16
+FIRST, LAST = 14, 15
 LINK = jnp.bfloat16
 VMEM_LIMIT = 16 * 1024 * 1024
 GRAD_LIMIT = 32 * 1024 * 1024
@@ -72,6 +73,9 @@
     for row, (if_first, if_second) in enumerate(flags):
         value = jnp.where(jnp.where(first_core, if_first, if_second), 1.0, 0.0)
         table[row:row + 1] = jnp.full((1, HEAD_DIM), value, jnp.float32)
+    _, _, _, _, first, last = block_range(lengths, ndocs, place * rows, rows)
+    for row, value in ((FIRST, first), (LAST, last)):
+        table[row:row + 1] = jnp.full((1, HEAD_DIM), value, jnp.int32).astype(jnp.float32)
 
 
 def state_kernel(lengths, q, k, v, g, out, *rest, ndocs, rows, offset, heads, group, kept, hops):
@@ -117,9 +121,9 @@
         out[h] = dot(jnp.where(here, held[0, :, cols], zero), held[1, :, cols], TN)
 
 
-def late_state_kernel(lengths, q, k, v, g, *rest, ndocs, rows, offset, heads):
+def late_state_kernel(table, q, k, v, g, *rest, ndocs, rows, offset, heads):
     kept, sent = rest[-2:]
-    first_core, first_rows, last_rows = own_range(lengths, ndocs, rows)
+    first_core, first_rows, last_rows = own_range(table, rows)
     zero = jnp.zeros((), q.dtype)
     for h in range(heads):
         at = slice(offset + h * HEAD_DIM, offset + (h + 1) * HEAD_DIM)
@@ -163,11 +167,9 @@
     return jnp.concatenate([high, (a - high.astype(jnp.float32)).astype(jnp.bfloat16)], axis=axis)
 
 
-def own_range(lengths, ndocs, rows):
-    place = lax.axis_index("seq")
-    _, _, _, _, first, last = block_range(lengths, ndocs, place * rows, rows)
-    order = lax.broadcasted_iota(jnp.int32, (rows, HEAD_DIM), 0)
-    return lax.rem(place, 2) == 0, order < first, order >= last
+def own_range(table, rows, start=0):
+    order = (lax.broadcasted_iota(jnp.int32, (rows, HEAD_DIM), 0) + start).astype(jnp.float32)
+    return lax.rem(lax.axis_index("seq"), 2) == 0, order < table[FIRST:FIRST + 1], order >= table[LAST:LAST + 1]
 
 
 def local_part(q, k, v, g, lower, upper, at):
@@ -199,9 +201,9 @@
             outs[j][i] = done[i, at, :]
 
 
-def grad_kernel(lengths, q, k, v, g, lower, upper, mine, got, *rest, ndocs, rows, offset, heads, groups):
+def grad_kernel(table, q, k, v, g, lower, upper, mine, got, *rest, ndocs, rows, offset, heads, groups):
     outs, done = rest[-1 - groups:-1], rest[-1]
-    first_core, first_rows, last_rows = own_range(lengths, ndocs, rows)
+    first_core, first_rows, last_rows = own_range(table, rows)
     for h in range(heads):
         cols = slice(h * HEAD_DIM, (h + 1) * HEAD_DIM)
         at = slice(offset + h * HEAD_DIM, offset + (h + 1) * HEAD_DIM)
@@ -214,7 +216,7 @@
     deal(done, outs, rows, groups)
 
 
-def local_kernel(lengths, q, k, v, g, lower, upper, near, token, *, offset, heads):
+def local_kernel(table, q, k, v, g, lower, upper, near, token, *, offset, heads):
     token[...] = jnp.zeros_like(token)
     for h in range(heads):
         cols = slice(h * HEAD_DIM, (h + 1) * HEAD_DIM)
@@ -223,9 +225,9 @@
             near[i, :, cols] = value
 
 
-def carry_kernel(lengths, k, v, g, near, mine, got, *rest, ndocs, rows, offset, heads, groups):
+def carry_kernel(table, k, v, g, near, mine, got, *rest, ndocs, rows, offset, heads, groups):
     outs, done = rest[-1 - groups:-1], rest[-1]
-    first_core, first_rows, last_rows = own_range(lengths, ndocs, rows)
+    first_core, first_rows, last_rows = own_range(table, rows)
     for h in range(heads):
         cols = slice(h * HEAD_DIM, (h + 1) * HEAD_DIM)
         at = slice(offset + h * HEAD_DIM, offset + (h + 1) * HEAD_DIM)
@@ -237,16 +239,13 @@
     deal(done, outs, rows, groups)
 
 
-def carry_rows_kernel(lengths, k, v, g, near, mine, got, *rest, ndocs, rows, offset, heads, groups, shifts):
+def carry_rows_kernel(table, k, v, g, near, mine, got, *rest, ndocs, rows, offset, heads, groups, shifts):
     outs = rest[-len(shifts):]
-    place, column, part = lax.axis_index("seq"), lax.axis_index("head"), rows // groups
-    first_core = lax.rem(place, 2) == 0
-    _, _, _, _, first, last = block_range(lengths, ndocs, place * rows, rows)
-    order = lax.broadcasted_iota(jnp.int32, (part, HEAD_DIM), 0)
+    column, part = lax.axis_index("head"), rows // groups
     for j, out in zip(shifts, outs):
         start = pl.multiple_of(lax.rem(column + j, groups) * part, part)
         lines = pl.ds(start, part)
-        first_rows, last_rows = order + start < first, order + start >= last
+        first_core, first_rows, last_rows = own_range(table, part, start)
         for h in range(heads):
             cols = slice(h * HEAD_DIM, (h + 1) * HEAD_DIM)
             at = slice(offset + h * HEAD_DIM, offset + (h + 1) * HEAD_DIM)
@@ -343,7 +342,7 @@
         heads = half // HEAD_DIM
         return call(
             "states", functools.partial(late_state_kernel, offset=offset, heads=heads, **sizes), inputs,
-            [shape_of(heads, *square)] * 2, after=after, limit=GRAD_LIMIT,
+            [shape_of(heads, *square)] * 2, after=after, limit=GRAD_LIMIT, known=table,
         )
 
     def pair_up(table, kept, got, copies, after):
@@ -366,20 +365,20 @@
         return call(
             "grads", functools.partial(grad_kernel, offset=offset, heads=cw // HEAD_DIM, groups=groups, **sizes),
             (*inputs, *masks, mine, theirs), [shape_of(3, part, cw, dtype=bf16)] * groups,
-            [pltpu.VMEM((3, rows, cw), bf16)], after, GRAD_LIMIT,
+            [pltpu.VMEM((3, rows, cw), bf16)], after, GRAD_LIMIT, table,
         )
 
     def local(masks, offset, cw):
         kernel = functools.partial(local_kernel, offset=offset, heads=cw // HEAD_DIM)
         return call(
-            "local", kernel, (*inputs, *masks), [shape_of(3, rows, cw), shape_of(8, HEAD_DIM)], limit=GRAD_LIMIT,
+            "local", kernel, (*inputs, *masks), [shape_of(3, rows, cw), shape_of(8, HEAD_DIM)], limit=GRAD_LIMIT, known=table,
         )
 
     def carry(near, offset, cw, mine, theirs, after):
         kernel = functools.partial(carry_kernel, offset=offset, heads=cw // HEAD_DIM, groups=groups, **sizes)
         return call(
             "carry", kernel, (*inputs[1:], near, mine, theirs), [shape_of(3, part, cw, dtype=bf16)] * groups,
-            [pltpu.VMEM((3, rows, cw), bf16)], after, GRAD_LIMIT,
+            [pltpu.VMEM((3, rows, cw), bf16)], after, GRAD_LIMIT, table,
         )
 
     def carry_rows(shifts, near, offset, cw, mine, theirs, after):
@@ -387,9 +386,9 @@
             carry_rows_kernel, offset=offset, heads=cw // HEAD_DIM, groups=groups, shifts=shifts, **sizes
         )
         outs = [shape_of(3, part, cw, dtype=bf16)] * len(shifts)
-        return call("carry", kernel, (*inputs[1:], near, mine, theirs), outs, after=after, limit=GRAD_LIMIT)
-
-    cuts, outs, arrived, totals, masks = [], [], [], [], None
+        return call("carry", kernel, (*inputs[1:], near, mine, theirs), outs, after=after, limit=GRAD_LIMIT, known=table)
+
+    cuts, outs, arrived, totals, masks, table = [], [], [], [], None, None
     for start, half, chunks in halves:
         if not totals:
             (sent,) = states(False, start, half)

time: 58.8 us -> 57.9 us (0.985)
  Pallas kernels: 19.6 us -> 15.2 us
  waiting for transfers between devices: 16.6 us -> 19.9 us
    pallas_call x13, Pallas kernels: 12.4 us -> 8.09 us  [call(): pl.pallas_call(kernel, in_specs=[in_smem if known is doc_lengths else in_...]
    ppermute x4, waiting for transfers between devices: 3.16 us -> 5.27 us  [swap_pairs(): lax.ppermute(sent[hop - 1], 'seq', perm + [(b, a) for a, b in perm])]
    ppermute x4, waiting for transfers between devices: 11.4 us -> 12.7 us  [send_rows(): lax.ppermute(outs[j], 'head', [(x, (x + j) % groups) for x in range(group...]
  transfers between devices with their start and end apart: 17 -> 17, of which waited for: 7 -> 7; matrix products, arithmetic and copies ran while one was open for 0% -> 0% of each run, Pallas kernels for 29% -> 22%
where the time goes in v12:
time: 57.9 us; the launch traced here: 57.6 us
  starting transfers between devices  20.9 us (36%)
  waiting for transfers between devices  19.9 us (34%)
  Pallas kernels  15.2 us (26%)
  between operations  0.87 us (2%)
  local copies, waits for them, and re-layouts  0.67 us (1%)
    ppermute x4, starting transfers between devices, swap_pairs(): lax.ppermute(sent[hop - 1], 'seq', perm + [(b, a) for a, b in perm])  13.8 us
    ppermute x4, waiting for transfers between devices, send_rows(): lax.ppermute(outs[j], 'head', [(x, (x + j) % groups) for x in range(group...  12.7 us
    pallas_call x13, Pallas kernels, call(): pl.pallas_call(kernel, in_specs=[in_smem if known is doc_lengths else in_...  8.09 us
    ppermute x4, waiting for transfers between devices, swap_pairs(): lax.ppermute(sent[hop - 1], 'seq', perm + [(b, a) for a, b in perm])  5.27 us
    ppermute x4, starting transfers between devices, send_rows(): lax.ppermute(outs[j], 'head', [(x, (x + j) % groups) for x in range(group...  4.69 us
    pallas_call x4, Pallas kernels, shards(): pl.pallas_call(functools.partial(place_kernel, groups=groups, plan=[where...  3.71 us
    pallas_call x2, Pallas kernels, states(): pl.pallas_call(functools.partial(state_kernel, offset=offset, heads=heads...  3.44 us
    ppermute x9, starting transfers between devices, swap_cores(): return lax.ppermute(a, 'seq', [(b, b ^ 1) for b in range(seq)])  2.37 us
  transfers between devices with their start and end apart: 17, of which 7 were waited for; matrix products, arithmetic and copies ran while one was open for 0% of the time, Pallas kernels for 22%

profile of v12, /device:TPU:0, one launch (start us, length us, event | category | flops | bytes accessed | tf_op | source)
XLA Modules:
  0.0 57.6 jit_solution(16766388186993704140)
XLA Ops:
  0.6 0.0 copy-start.4
  0.6 0.6 %copy-done.4 = s32[8]{0:T(128)S(1)} copy-done((s32[8]{0:T(128)S(1)}, s32[8]{0:T(128)}, u32[]{:S(2)}) %copy-start.4) | copy-done | bytes 56
  1.3 1.6 %states.5 = f32[8,128,128]{2,1,0:T(8,128)S(1)} custom-call(s32[8]{0:T(128)S(1)} %copy-done.4, bf16[256,2048]{1,0:T(8,128)(2,1)} %q.13, bf16[256,2048]{1,0:T(8,128)(2,1)} %k.19, bf16[256,2048]{1,0:T(8,128)(2,1)} %v.19, bf16[256,2048]{1,0:T(8,128)(2,1)} %g.19), custom_call_target="tpu_custom_call" | custom-call | bytes 1024 | tf_op jit(solution)/shard_map/states/pallas_call | solution.py:331
  2.9 0.5 collective-permute-start.2
  3.5 0.0 copy-start.1
  3.5 0.0 copy-start.2
  3.5 0.0 copy-start.3
  3.5 1.8 %states.3 = (f32[8,128,128]{2,1,0:T(8,128)S(1)}, bf16[256,256]{1,0:T(8,128)(2,1)S(1)}, bf16[256,256]{1,0:T(8,128)(2,1)S(1)}, f32[16,128]{1,0:T(8,128)S(1)}) custom-call(s32[8]{0:T(128)S(1)} %copy-done.4, bf16[256,2048]{1,0:T(8,128)(2,1)} %q.13, bf16[256,2048]{1,0:T(8,128)(2,1)} %k.19, bf16[256,2048]{1,0:T(8,128)(2,1)} %v.19, bf16[256,2048]{1,0:T(8,128)(2,1)} %g.19), custom_call_target="tpu_custom_call" | custom-call | bytes 1024 | tf_op jit(solution)/shard_map/states/pallas_call | solution.py:331
  5.3 0.0 copy-start
  5.3 0.0 collective-permute-done.2.got
  5.3 0.1 pair.2
  5.4 4.7 %collective-permute-start.4 = (bf16[1056,128]{1,0:T(8,128)(2,1)S(1)}, bf16[1056,128]{1,0:T(8,128)(2,1)S(1)}, u32[]{:S(2)}, u32[]{:S(2)}) collective-permute-start(bf16[1056,128]{1,0:T(8,128)(2,1)S(1)} %get-tuple-element.51), channel_id=1, source_target_pairs={{0,6},{4,10},{8,14},{12,18},{16,22},{20,26},{24,30},{6,0},{10,4},{... | collective-permute-start | bytes 811016 | tf_op jit(solution)/shard_map/ppermute | solution.py:316
  10.1 3.1 %collective-permute-start.5 = (bf16[1040,128]{1,0:T(8,128)(2,1)S(1)}, bf16[1040,128]{1,0:T(8,128)(2,1)S(1)}, u32[]{:S(2)}, u32[]{:S(2)}) collective-permute-start(bf16[1040,128]{1,0:T(8,128)(2,1)S(1)} %get-tuple-element.52), channel_id=1, source_target_pairs={{0,10},{4,14},{8,18},{12,22},{16,26},{20,30},{10,0},{14,4},{18,8},... | collective-permute-start | bytes 798728 | tf_op jit(solution)/shard_map/ppermute | solution.py:316
  13.1 0.1 collective-permute-start.3
  13.2 0.0 copy-done.1
  13.2 0.0 copy-done.2
  13.2 0.0 copy-done.3
  13.2 0.0 copy-done
  13.3 1.1 %local.2 = (f32[3,256,512]{2,1,0:T(8,128)S(1)}, f32[8,128]{1,0:T(8,128)S(1)}) custom-call(f32[16,128]{1,0:T(8,128)S(1)} %get-tuple-element.42.table, bf16[256,2048]{1,0:T(8,128)(2,1)S(1)} %copy-done.3, bf16[256,2048]{1,0:T(8,128)(2,1)S(1)} %copy-done, bf16[256,2048]{1,0:T(8,128)(2,1)S(1)} %copy-done.1, bf16[256,2048]{1,0:T(8,128)(2,1)S(1)} %copy-done.2, ...), custom_call_target="tpu_custom_call" | custom-call | bytes 1024 | tf_op jit(solution)/shard_map/local/pallas_call | solution.py:303
  14.3 0.6 %states.4 = (f32[8,128,128]{2,1,0:T(8,128)S(1)}, f32[8,128,128]{2,1,0:T(8,128)S(1)}) custom-call(f32[16,128]{1,0:T(8,128)S(1)} %get-tuple-element.42.table, bf16[256,2048]{1,0:T(8,128)(2,1)S(1)} %copy-done.3, bf16[256,2048]{1,0:T(8,128)(2,1)S(1)} %copy-done, bf16[256,2048]{1,0:T(8,128)(2,1)S(1)} %copy-done.1, bf16[256,2048]{1,0:T(8,128)(2,1)S(1)} %copy-done.2, ...), custom_call_target="tpu_custom_call" | custom-call | bytes 1024 | tf_op jit(solution)/shard_map/states/pallas_call | solution.py:303
  15.0 0.5 collective-permute-start.1
  15.5 1.1 %local.3 = (f32[3,256,512]{2,1,0:T(8,128)S(1)}, f32[8,128]{1,0:T(8,128)S(1)}) custom-call(f32[16,128]{1,0:T(8,128)S(1)} %get-tuple-element.42.table, bf16[256,2048]{1,0:T(8,128)(2,1)S(1)} %copy-done.3, bf16[256,2048]{1,0:T(8,128)(2,1)S(1)} %copy-done, bf16[256,2048]{1,0:T(8,128)(2,1)S(1)} %copy-done.1, bf16[256,2048]{1,0:T(8,128)(2,1)S(1)} %copy-done.2, ...), custom_call_target="tpu_custom_call" | custom-call | bytes 1024 | tf_op jit(solution)/shard_map/local/pallas_call | solution.py:303
  16.6 0.1 collective-permute-start.7
  16.7 0.0 collective-permute-done.3.rest_0_
  16.7 1.5 %collective-permute-done.5.rest_2_ = bf16[1040,128]{1,0:T(8,128)(2,1)S(1)} collective-permute-done((bf16[1040,128]{1,0:T(8,128)(2,1)S(1)}, bf16[1040,128]{1,0:T(8,128)(2,1)S(1)}, u32[]{:S(2)}, u32[]{:S(2)}) %collective-permute-start.5) | collective-permute-done | bytes 266272 | tf_op jit(solution)/shard_map/ppermute | solution.py:316
  18.2 0.0 collective-permute-done.4.rest_1_
  18.2 0.1 join.3
  18.3 0.1 collective-permute-start.6
  18.4 0.5 collective-permute-start
  18.9 0.0 collective-permute-done.7.rest_0_
  18.9 0.1 join.4
  19.0 0.9 %collective-permute-done.6.got = f32[4,128,128]{2,1,0:T(8,128)S(1)} collective-permute-done((f32[4,128,128]{2,1,0:T(8,128)S(1)}, f32[4,128,128]{2,1,0:T(8,128)S(1)}, u32[]{:S(2)}, u32[]{:S(2)}) %collective-permute-start.6) | collective-permute-done | bytes 262176 | tf_op jit(solution)/shard_map/ppermute | solution.py:310
  19.9 0.4 carry.3.rest_0_
  20.3 1.6 %collective-permute-start.10 = (bf16[3,128,512]{2,1,0:T(8,128)(2,1)S(1)}, bf16[3,128,512]{2,1,0:T(8,128)(2,1)S(1)}, u32[]{:S(2)}, u32[]{:S(2)}) collective-permute-start(bf16[3,128,512]{2,1,0:T(8,128)(2,1)S(1)} %carry.3.rest_0_), channel_id=1, source_target_pairs={{0,1},{1,0},{2,3},{3,2},{4,5},{5,4},{6,7},{7,6},{8,9},{9,8},{10,11... | collective-permute-start | bytes 1179656 | tf_op jit(solution)/shard_map/ppermute | solution.py:322
  21.9 0.0 collective-permute-start.13
  21.9 0.0 collective-permute-done.1.got
  21.9 0.1 pair.3
  22.0 3.1 %collective-permute-start.8 = (bf16[1056,128]{1,0:T(8,128)(2,1)S(1)}, bf16[1056,128]{1,0:T(8,128)(2,1)S(1)}, u32[]{:S(2)}, u32[]{:S(2)}) collective-permute-start(bf16[1056,128]{1,0:T(8,128)(2,1)S(1)} %get-tuple-element.58), channel_id=1, source_target_pairs={{0,6},{4,10},{8,14},{12,18},{16,22},{20,26},{24,30},{6,0},{10,4},{... | collective-permute-start | bytes 811016 | tf_op jit(solution)/shard_map/ppermute | solution.py:316
  25.1 3.0 %collective-permute-start.9 = (bf16[1040,128]{1,0:T(8,128)(2,1)S(1)}, bf16[1040,128]{1,0:T(8,128)(2,1)S(1)}, u32[]{:S(2)}, u32[]{:S(2)}) collective-permute-start(bf16[1040,128]{1,0:T(8,128)(2,1)S(1)} %get-tuple-element.59), channel_id=1, source_target_pairs={{0,10},{4,14},{8,18},{12,22},{16,26},{20,30},{10,0},{14,4},{18,8},... | collective-permute-start | bytes 798728 | tf_op jit(solution)/shard_map/ppermute | solution.py:316
  28.1 0.0 collective-permute-done.13.got
  28.1 0.8 %carry.4 = (bf16[3,128,512]{2,1,0:T(8,128)(2,1)S(1)}, bf16[3,128,512]{2,1,0:T(8,128)(2,1)S(1)}) custom-call(f32[16,128]{1,0:T(8,128)S(1)} %get-tuple-element.42.table, bf16[256,2048]{1,0:T(8,128)(2,1)S(1)} %copy-done, bf16[256,2048]{1,0:T(8,128)(2,1)S(1)} %copy-done.1, bf16[256,2048]{1,0:T(8,128)(2,1)S(1)} %copy-done.2, ...), custom_call_target="tpu_custom_call" | custom-call | bytes 1024 | tf_op jit(solution)/shard_map/carry/pallas_call | solution.py:303
  28.9 0.6 %collective-permute-start.14 = (bf16[3,128,512]{2,1,0:T(8,128)(2,1)S(1)}, bf16[3,128,512]{2,1,0:T(8,128)(2,1)S(1)}, u32[]{:S(2)}, u32[]{:S(2)}) collective-permute-start(bf16[3,128,512]{2,1,0:T(8,128)(2,1)S(1)} %get-tuple-element.66.rest_0_), channel_id=1, source_target_pairs={{0,1},{1,0},{2,3},{3,2},{4,5},{5,4},{6,7},{7,6},{8,9},{9,8},{10,11... | collective-permute-start | bytes 1179656 | tf_op jit(solution)/shard_map/ppermute | solution.py:322
  29.5 0.0 collective-permute-done.rest_0_.rest_1_
  29.5 3.7 %collective-permute-done.9.rest_3_ = bf16[1040,128]{1,0:T(8,128)(2,1)S(1)} collective-permute-done((bf16[1040,128]{1,0:T(8,128)(2,1)S(1)}, bf16[1040,128]{1,0:T(8,128)(2,1)S(1)}, u32[]{:S(2)}, u32[]{:S(2)}) %collective-permute-start.9) | collective-permute-done | bytes 266272 | tf_op jit(solution)/shard_map/ppermute | solution.py:316
  33.2 0.0 collective-permute-done.8.rest_2_
  33.2 0.0 collective-permute-done.10.rest_4_.refs_2_
  33.2 0.1 join.5
  33.4 0.1 collective-permute-start.12
  33.4 0.5 collective-permute-start.11
  33.9 1.0 %collective-permute-done.12.got = f32[4,128,128]{2,1,0:T(8,128)S(1)} collective-permute-done((f32[4,128,128]{2,1,0:T(8,128)S(1)}, f32[4,128,128]{2,1,0:T(8,128)S(1)}, u32[]{:S(2)}, u32[]{:S(2)}) %collective-permute-start.12) | collective-permute-done | bytes 262176 | tf_op jit(solution)/shard_map/ppermute | solution.py:310
  35.0 1.6 %grads.2 = (bf16[3,128,512]{2,1,0:T(8,128)(2,1)S(1)}, bf16[3,128,512]{2,1,0:T(8,128)(2,1)S(1)}) custom-call(f32[16,128]{1,0:T(8,128)S(1)} %get-tuple-element.42.table, bf16[256,2048]{1,0:T(8,128)(2,1)S(1)} %copy-done.3, bf16[256,2048]{1,0:T(8,128)(2,1)S(1)} %copy-done, bf16[256,2048]{1,0:T(8,128)(2,1)S(1)} %copy-done.1, bf16[256,2048]{1,0:T(8,128)(2,1)S(1)} %copy-done.2, ...), custom_call_target="tpu_custom_call" | custom-call | bytes 1024 | tf_op jit(solution)/shard_map/grads/pallas_call | solution.py:303
  36.6 0.7 %collective-permute-start.16 = (bf16[3,128,512]{2,1,0:T(8,128)(2,1)S(1)}, bf16[3,128,512]{2,1,0:T(8,128)(2,1)S(1)}, u32[]{:S(2)}, u32[]{:S(2)}) collective-permute-start(bf16[3,128,512]{2,1,0:T(8,128)(2,1)S(1)} %get-tuple-element.67.rest_0_), channel_id=1, source_target_pairs={{0,1},{1,0},{2,3},{3,2},{4,5},{5,4},{6,7},{7,6},{8,9},{9,8},{10,11... | collective-permute-start | bytes 1179656 | tf_op jit(solution)/shard_map/ppermute | solution.py:322
  37.3 3.2 %collective-permute-done.14.rest_1_.refs_1_ = bf16[3,128,512]{2,1,0:T(8,128)(2,1)S(1)} collective-permute-done((bf16[3,128,512]{2,1,0:T(8,128)(2,1)S(1)}, bf16[3,128,512]{2,1,0:T(8,128)(2,1)S(1)}, u32[]{:S(2)}, u32[]{:S(2)}) %collective-permute-start.14) | collective-permute-done | bytes 393248 | tf_op jit(solution)/shard_map/ppermute | solution.py:322
  40.5 0.0 collective-permute-done.11.got
  40.5 1.6 %grads.3 = (bf16[3,128,512]{2,1,0:T(8,128)(2,1)S(1)}, bf16[3,128,512]{2,1,0:T(8,128)(2,1)S(1)}) custom-call(f32[16,128]{1,0:T(8,128)S(1)} %get-tuple-element.42.table, bf16[256,2048]{1,0:T(8,128)(2,1)S(1)} %copy-done.3, bf16[256,2048]{1,0:T(8,128)(2,1)S(1)} %copy-done, bf16[256,2048]{1,0:T(8,128)(2,1)S(1)} %copy-done.1, bf16[256,2048]{1,0:T(8,128)(2,1)S(1)} %copy-done.2, ...), custom_call_target="tpu_custom_call" | custom-call | bytes 1024 | tf_op jit(solution)/shard_map/grads/pallas_call | solution.py:303
  42.1 1.8 %collective-permute-start.15 = (bf16[3,128,512]{2,1,0:T(8,128)(2,1)S(1)}, bf16[3,128,512]{2,1,0:T(8,128)(2,1)S(1)}, u32[]{:S(2)}, u32[]{:S(2)}) collective-permute-start(bf16[3,128,512]{2,1,0:T(8,128)(2,1)S(1)} %get-tuple-element.68), channel_id=1, source_target_pairs={{0,1},{1,0},{2,3},{3,2},{4,5},{5,4},{6,7},{7,6},{8,9},{9,8},{10,11... | collective-permute-start | bytes 1179656 | tf_op jit(solution)/shard_map/ppermute | solution.py:322
  44.0 0.4 carry.5.refs_0_
  44.4 1.1 %place.4 = (bf16[128,4096]{1,0:T(8,128)(2,1)}, bf16[128,4096]{1,0:T(8,128)(2,1)}, bf16[128,4096]{1,0:T(8,128)(2,1)}) custom-call(bf16[3,128,512]{2,1,0:T(8,128)(2,1)S(1)} %carry.5.refs_0_, bf16[3,128,512]{2,1,0:T(8,128)(2,1)S(1)} %get-tuple-element.71.refs_1_, bf16[3,128,512]{2,1,0:T(8,128)(2,1)S(1)} %collective-permute-done.10.rest_4_.refs_2_), custom_call_target="tpu_custom_call" | custom-call | bytes 1024 | tf_op jit(solution)/shard_map/place/pallas_call | solution.py:434
  45.5 0.9 %place.5 = (bf16[128,4096]{1,0:T(8,128)(2,1)}, bf16[128,4096]{1,0:T(8,128)(2,1)}, bf16[128,4096]{1,0:T(8,128)(2,1)}) custom-call(bf16[3,128,512]{2,1,0:T(8,128)(2,1)S(1)} %get-tuple-element.70.refs_0_, bf16[3,128,512]{2,1,0:T(8,128)(2,1)S(1)} %collective-permute-done.14.rest_1_.refs_1_, ...), custom_call_target="tpu_custom_call", output_to_operand_aliasing={{0}: (2, {}), {1}: (3, {}), {2}: (4, {})} | custom-call | bytes 1024 | tf_op jit(solution)/shard_map/place/pallas_call | solution.py:434
  46.4 2.5 %collective-permute-done.16.refs_1_ = bf16[3,128,512]{2,1,0:T(8,128)(2,1)S(1)} collective-permute-done((bf16[3,128,512]{2,1,0:T(8,128)(2,1)S(1)}, bf16[3,128,512]{2,1,0:T(8,128)(2,1)S(1)}, u32[]{:S(2)}, u32[]{:S(2)}) %collective-permute-start.16) | collective-permute-done | bytes 393248 | tf_op jit(solution)/shard_map/ppermute | solution.py:322
  48.9 0.9 %place.6 = (bf16[128,4096]{1,0:T(8,128)(2,1)}, bf16[128,4096]{1,0:T(8,128)(2,1)}, bf16[128,4096]{1,0:T(8,128)(2,1)}) custom-call(bf16[3,128,512]{2,1,0:T(8,128)(2,1)S(1)} %get-tuple-element.69.refs_0_, bf16[3,128,512]{2,1,0:T(8,128)(2,1)S(1)} %collective-permute-done.16.refs_1_, ...), custom_call_target="tpu_custom_call", output_to_operand_aliasing={{0}: (2, {}), {1}: (3, {}), {2}: (4, {})} | custom-call | bytes 1024 | tf_op jit(solution)/shard_map/place/pallas_call | solution.py:434
  49.9 7.0 %collective-permute-done.15.refs_0_ = bf16[3,128,512]{2,1,0:T(8,128)(2,1)S(1)} collective-permute-done((bf16[3,128,512]{2,1,0:T(8,128)(2,1)S(1)}, bf16[3,128,512]{2,1,0:T(8,128)(2,1)S(1)}, u32[]{:S(2)}, u32[]{:S(2)}) %collective-permute-start.15) | collective-permute-done | bytes 393248 | tf_op jit(solution)/shard_map/ppermute | solution.py:322
  56.8 0.8 %place.7 = (bf16[128,4096]{1,0:T(8,128)(2,1)}, bf16[128,4096]{1,0:T(8,128)(2,1)}, bf16[128,4096]{1,0:T(8,128)(2,1)}) custom-call(bf16[3,128,512]{2,1,0:T(8,128)(2,1)S(1)} %collective-permute-done.15.refs_0_, bf16[128,4096]{1,0:T(8,128)(2,1)} %get-tuple-element.78.refs_1_, ...), custom_call_target="tpu_custom_call", output_to_operand_aliasing={{0}: (1, {}), {1}: (2, {}), {2}: (3, {})} | custom-call | bytes 1024 | tf_op jit(solution)/shard_map/place/pallas_call | solution.py:434
Async XLA Ops:
  0.6 0.7 %copy-start.4 = (s32[8]{0:T(128)S(1)}, s32[8]{0:T(128)}, u32[]{:S(2)}) copy-start(s32[8]{0:T(128)} %lengths.3) | copy-start | bytes 100
  2.9 2.3 %collective-permute-start.2 = (f32[8,128,128]{2,1,0:T(8,128)S(1)}, f32[8,128,128]{2,1,0:T(8,128)S(1)}, u32[]{:S(2)}, u32[]{:S(2)}) collective-permute-start(f32[8,128,128]{2,1,0:T(8,128)S(1)} %states.5), channel_id=1, source_target_pairs={{0,2},{2,0},{4,6},{6,4},{8,10},{10,8},{12,14},{14,12},{16,18},{18,... | collective-permute-start | bytes 1572872 | tf_op jit(solution)/shard_map/ppermute | solution.py:310
  3.5 9.8 %copy-start.1 = (bf16[256,2048]{1,0:T(8,128)(2,1)S(1)}, bf16[256,2048]{1,0:T(8,128)(2,1)}, u32[]{:S(2)}) copy-start(bf16[256,2048]{1,0:T(8,128)(2,1)} %v.19) | copy-start | bytes 3145732
  3.5 9.8 %copy-start.2 = (bf16[256,2048]{1,0:T(8,128)(2,1)S(1)}, bf16[256,2048]{1,0:T(8,128)(2,1)}, u32[]{:S(2)}) copy-start(bf16[256,2048]{1,0:T(8,128)(2,1)} %g.19) | copy-start | bytes 3145732
  3.5 9.8 %copy-start.3 = (bf16[256,2048]{1,0:T(8,128)(2,1)S(1)}, bf16[256,2048]{1,0:T(8,128)(2,1)}, u32[]{:S(2)}) copy-start(bf16[256,2048]{1,0:T(8,128)(2,1)} %q.13) | copy-start | bytes 3145732
  5.3 8.0 %copy-start = (bf16[256,2048]{1,0:T(8,128)(2,1)S(1)}, bf16[256,2048]{1,0:T(8,128)(2,1)}, u32[]{:S(2)}) copy-start(bf16[256,2048]{1,0:T(8,128)(2,1)} %k.19) | copy-start | bytes 3145732
  5.4 12.8 %collective-permute-start.4 = (bf16[1056,128]{1,0:T(8,128)(2,1)S(1)}, bf16[1056,128]{1,0:T(8,128)(2,1)S(1)}, u32[]{:S(2)}, u32[]{:S(2)}) collective-permute-start(bf16[1056,128]{1,0:T(8,128)(2,1)S(1)} %get-tuple-element.51), channel_id=1, source_target_pairs={{0,6},{4,10},{8,14},{12,18},{16,22},{20,26},{24,30},{6,0},{10,4},{... | collective-permute-start | bytes 811016 | tf_op jit(solution)/shard_map/ppermute | solution.py:316
  10.1 8.2 %collective-permute-start.5 = (bf16[1040,128]{1,0:T(8,128)(2,1)S(1)}, bf16[1040,128]{1,0:T(8,128)(2,1)S(1)}, u32[]{:S(2)}, u32[]{:S(2)}) collective-permute-start(bf16[1040,128]{1,0:T(8,128)(2,1)S(1)} %get-tuple-element.52), channel_id=1, source_target_pairs={{0,10},{4,14},{8,18},{12,22},{16,26},{20,30},{10,0},{14,4},{18,8},... | collective-permute-start | bytes 798728 | tf_op jit(solution)/shard_map/ppermute | solution.py:316
  13.1 3.6 %collective-permute-start.3 = (f32[4,128,128]{2,1,0:T(8,128)S(1)}, f32[4,128,128]{2,1,0:T(8,128)S(1)}, u32[]{:S(2)}, u32[]{:S(2)}) collective-permute-start(f32[4,128,128]{2,1,0:T(8,128)S(1)} %get-tuple-element.50), channel_id=1, source_target_pairs={{0,2},{2,0},{4,6},{6,4},{8,10},{10,8},{12,14},{14,12},{16,18},{18,... | collective-permute-start | bytes 786440 | tf_op jit(solution)/shard_map/ppermute | solution.py:310
  15.0 6.9 %collective-permute-start.1 = (f32[8,128,128]{2,1,0:T(8,128)S(1)}, f32[8,128,128]{2,1,0:T(8,128)S(1)}, u32[]{:S(2)}, u32[]{:S(2)}) collective-permute-start(f32[8,128,128]{2,1,0:T(8,128)S(1)} %get-tuple-element.47), channel_id=1, source_target_pairs={{0,2},{2,0},{4,6},{6,4},{8,10},{10,8},{12,14},{14,12},{16,18},{18,... | collective-permute-start | bytes 1572872 | tf_op jit(solution)/shard_map/ppermute | solution.py:310
  16.6 2.3 %collective-permute-start.7 = (f32[4,128,128]{2,1,0:T(8,128)S(1)}, f32[4,128,128]{2,1,0:T(8,128)S(1)}, u32[]{:S(2)}, u32[]{:S(2)}) collective-permute-start(f32[4,128,128]{2,1,0:T(8,128)S(1)} %get-tuple-element.56), channel_id=1, source_target_pairs={{0,2},{2,0},{4,6},{6,4},{8,10},{10,8},{12,14},{14,12},{16,18},{18,... | collective-permute-start | bytes 786440 | tf_op jit(solution)/shard_map/ppermute | solution.py:310
  18.3 1.6 %collective-permute-start.6 = (f32[4,128,128]{2,1,0:T(8,128)S(1)}, f32[4,128,128]{2,1,0:T(8,128)S(1)}, u32[]{:S(2)}, u32[]{:S(2)}) collective-permute-start(f32[4,128,128]{2,1,0:T(8,128)S(1)} %get-tuple-element.55), channel_id=1, source_target_pairs={{0,2},{2,0},{4,6},{6,4},{8,10},{10,8},{12,14},{14,12},{16,18},{18,... | collective-permute-start | bytes 786440 | tf_op jit(solution)/shard_map/ppermute | solution.py:310
  18.4 11.1 %collective-permute-start = (f32[8,128,128]{2,1,0:T(8,128)S(1)}, f32[8,128,128]{2,1,0:T(8,128)S(1)}, u32[]{:S(2)}, u32[]{:S(2)}) collective-permute-start(f32[8,128,128]{2,1,0:T(8,128)S(1)} %get-tuple-element.46.kept), channel_id=1, source_target_pairs={{0,2},{2,0},{4,6},{6,4},{8,10},{10,8},{12,14},{14,12},{16,18},{18,... | collective-permute-start | bytes 1572872 | tf_op jit(solution)/shard_map/ppermute | solution.py:310
  20.3 12.9 %collective-permute-start.10 = (bf16[3,128,512]{2,1,0:T(8,128)(2,1)S(1)}, bf16[3,128,512]{2,1,0:T(8,128)(2,1)S(1)}, u32[]{:S(2)}, u32[]{:S(2)}) collective-permute-start(bf16[3,128,512]{2,1,0:T(8,128)(2,1)S(1)} %carry.3.rest_0_), channel_id=1, source_target_pairs={{0,1},{1,0},{2,3},{3,2},{4,5},{5,4},{6,7},{7,6},{8,9},{9,8},{10,11... | collective-permute-start | bytes 1179656 | tf_op jit(solution)/shard_map/ppermute | solution.py:322
  21.9 6.2 %collective-permute-start.13 = (f32[4,128,128]{2,1,0:T(8,128)S(1)}, f32[4,128,128]{2,1,0:T(8,128)S(1)}, u32[]{:S(2)}, u32[]{:S(2)}) collective-permute-start(f32[4,128,128]{2,1,0:T(8,128)S(1)} %get-tuple-element.65), channel_id=1, source_target_pairs={{0,2},{2,0},{4,6},{6,4},{8,10},{10,8},{12,14},{14,12},{16,18},{18,... | collective-permute-start | bytes 786440 | tf_op jit(solution)/shard_map/ppermute | solution.py:310
  22.0 11.2 %collective-permute-start.8 = (bf16[1056,128]{1,0:T(8,128)(2,1)S(1)}, bf16[1056,128]{1,0:T(8,128)(2,1)S(1)}, u32[]{:S(2)}, u32[]{:S(2)}) collective-permute-start(bf16[1056,128]{1,0:T(8,128)(2,1)S(1)} %get-tuple-element.58), channel_id=1, source_target_pairs={{0,6},{4,10},{8,14},{12,18},{16,22},{20,26},{24,30},{6,0},{10,4},{... | collective-permute-start | bytes 811016 | tf_op jit(solution)/shard_map/ppermute | solution.py:316
  25.1 8.1 %collective-permute-start.9 = (bf16[1040,128]{1,0:T(8,128)(2,1)S(1)}, bf16[1040,128]{1,0:T(8,128)(2,1)S(1)}, u32[]{:S(2)}, u32[]{:S(2)}) collective-permute-start(bf16[1040,128]{1,0:T(8,128)(2,1)S(1)} %get-tuple-element.59), channel_id=1, source_target_pairs={{0,10},{4,14},{8,18},{12,22},{16,26},{20,30},{10,0},{14,4},{18,8},... | collective-permute-start | bytes 798728 | tf_op jit(solution)/shard_map/ppermute | solution.py:316
  28.9 11.6 %collective-permute-start.14 = (bf16[3,128,512]{2,1,0:T(8,128)(2,1)S(1)}, bf16[3,128,512]{2,1,0:T(8,128)(2,1)S(1)}, u32[]{:S(2)}, u32[]{:S(2)}) collective-permute-start(bf16[3,128,512]{2,1,0:T(8,128)(2,1)S(1)} %get-tuple-element.66.rest_0_), channel_id=1, source_target_pairs={{0,1},{1,0},{2,3},{3,2},{4,5},{5,4},{6,7},{7,6},{8,9},{9,8},{10,11... | collective-permute-start | bytes 1179656 | tf_op jit(solution)/shard_map/ppermute | solution.py:322
  33.4 1.6 %collective-permute-start.12 = (f32[4,128,128]{2,1,0:T(8,128)S(1)}, f32[4,128,128]{2,1,0:T(8,128)S(1)}, u32[]{:S(2)}, u32[]{:S(2)}) collective-permute-start(f32[4,128,128]{2,1,0:T(8,128)S(1)} %get-tuple-element.63), channel_id=1, source_target_pairs={{0,2},{2,0},{4,6},{6,4},{8,10},{10,8},{12,14},{14,12},{16,18},{18,... | collective-permute-start | bytes 786440 | tf_op jit(solution)/shard_map/ppermute | solution.py:310
  33.4 7.1 %collective-permute-start.11 = (f32[4,128,128]{2,1,0:T(8,128)S(1)}, f32[4,128,128]{2,1,0:T(8,128)S(1)}, u32[]{:S(2)}, u32[]{:S(2)}) collective-permute-start(f32[4,128,128]{2,1,0:T(8,128)S(1)} %get-tuple-element.61), channel_id=1, source_target_pairs={{0,2},{2,0},{4,6},{6,4},{8,10},{10,8},{12,14},{14,12},{16,18},{18,... | collective-permute-start | bytes 786440 | tf_op jit(solution)/shard_map/ppermute | solution.py:310
  36.6 12.4 %collective-permute-start.16 = (bf16[3,128,512]{2,1,0:T(8,128)(2,1)S(1)}, bf16[3,128,512]{2,1,0:T(8,128)(2,1)S(1)}, u32[]{:S(2)}, u32[]{:S(2)}) collective-permute-start(bf16[3,128,512]{2,1,0:T(8,128)(2,1)S(1)} %get-tuple-element.67.rest_0_), channel_id=1, source_target_pairs={{0,1},{1,0},{2,3},{3,2},{4,5},{5,4},{6,7},{7,6},{8,9},{9,8},{10,11... | collective-permute-start | bytes 1179656 | tf_op jit(solution)/shard_map/ppermute | solution.py:322
  42.1 14.7 %collective-permute-start.15 = (bf16[3,128,512]{2,1,0:T(8,128)(2,1)S(1)}, bf16[3,128,512]{2,1,0:T(8,128)(2,1)S(1)}, u32[]{:S(2)}, u32[]{:S(2)}) collective-permute-start(bf16[3,128,512]{2,1,0:T(8,128)(2,1)S(1)} %get-tuple-element.68), channel_id=1, source_target_pairs={{0,1},{1,0},{2,3},{3,2},{4,5},{5,4},{6,7},{7,6},{8,9},{9,8},{10,11... | collective-permute-start | bytes 1179656 | tf_op jit(solution)/shard_map/ppermute | solution.py:322

commit v13 on v12

--- a/solution.py
+++ b/solution.py
@@ -396,15 +396,15 @@
         else:
             kept, sent = late_states(start, half, [token])
         total, came, others = pair_up(
-            table, kept, swap_cores(sent), 0 if totals else len(chunks), [made[-1] for made in outs[:1]]
+            table, kept, swap_cores(sent), len(chunks), [made[-1] for made in outs[:1]]
         )
         if not totals:
             near = [local(masks, *chunk) for chunk in chunks]
             token = near[0][1]
         count = chunks[0][1] // HEAD_DIM
         if totals:
-            spans = [(c * count, c * count, count) for c in range(len(chunks))]
-            joined = join(table, spans, [swap_cores(kept)] * len(chunks), came, [arrived[0][1]])
+            spans = [(0, c * count, count) for c in range(len(chunks))]
+            joined = join(table, spans, others, came, [arrived[0][1]])
         else:
             joined, after = [], [made[1] for made in near]
             for c in range(len(chunks)):

time: 57.9 us -> 58.5 us (1.010)
  waiting for transfers between devices: 19.9 us -> 21.6 us
  starting transfers between devices: 20.9 us -> 19.8 us
    ppermute x4, waiting for transfers between devices: 12.7 us -> 14.4 us  [send_rows(): lax.ppermute(outs[j], 'head', [(x, (x + j) % groups) for x in range(group...]
    ppermute x4, starting transfers between devices: 4.69 us -> 3.49 us  [send_rows(): lax.ppermute(outs[j], 'head', [(x, (x + j) % groups) for x in range(group...]
    ppermute x9 -> x10, starting transfers between devices: 2.37 us -> 2.53 us  [swap_cores(): return lax.ppermute(a, 'seq', [(b, b ^ 1) for b in range(seq)])]
    ppermute x9 -> x10, waiting for transfers between devices: 1.99 us -> 2.07 us  [swap_cores(): return lax.ppermute(a, 'seq', [(b, b ^ 1) for b in range(seq)])]
  transfers between devices with their start and end apart: 17 -> 18, of which waited for: 7 -> 8; matrix products, arithmetic and copies ran while one was open for 0% -> 0% of each run, Pallas kernels for 22% -> 22%
where the time goes in v13:
time: 58.5 us; the launch traced here: 58.2 us
  waiting for transfers between devices  21.6 us (37%)
  starting transfers between devices  19.8 us (34%)
  Pallas kernels  15.3 us (26%)
  between operations  0.91 us (2%)
  local copies, waits for them, and re-layouts  0.67 us (1%)
    ppermute x4, waiting for transfers between devices, send_rows(): lax.ppermute(outs[j], 'head', [(x, (x + j) % groups) for x in range(group...  14.4 us
    ppermute x4, starting transfers between devices, swap_pairs(): lax.ppermute(sent[hop - 1], 'seq', perm + [(b, a) for a, b in perm])  13.8 us
    pallas_call x13, Pallas kernels, call(): pl.pallas_call(kernel, in_specs=[in_smem if known is doc_lengths else in_...  8.12 us
    ppermute x4, waiting for transfers between devices, swap_pairs(): lax.ppermute(sent[hop - 1], 'seq', perm + [(b, a) for a, b in perm])  5.06 us
    pallas_call x4, Pallas kernels, shards(): pl.pallas_call(functools.partial(place_kernel, groups=groups, plan=[where...  3.71 us
    ppermute x4, starting transfers between devices, send_rows(): lax.ppermute(outs[j], 'head', [(x, (x + j) % groups) for x in range(group...  3.49 us
    pallas_call x2, Pallas kernels, states(): pl.pallas_call(functools.partial(state_kernel, offset=offset, heads=heads...  3.44 us
    ppermute x10, starting transfers between devices, swap_cores(): return lax.ppermute(a, 'seq', [(b, b ^ 1) for b in range(seq)])  2.53 us
  transfers between devices with their start and end apart: 18, of which 8 were waited for; matrix products, arithmetic and copies ran while one was open for 0% of the time, Pallas kernels for 22%

profile of v13, /device:TPU:0, one launch (start us, length us, event | category | flops | bytes accessed | tf_op | source)
XLA Modules:
  0.0 58.2 jit_solution(8538692025144669493)
XLA Ops:
  0.6 0.0 copy-start.4
  0.6 0.6 %copy-done.4 = s32[8]{0:T(128)S(1)} copy-done((s32[8]{0:T(128)S(1)}, s32[8]{0:T(128)}, u32[]{:S(2)}) %copy-start.4) | copy-done | bytes 56
  1.3 1.6 %states.5 = f32[8,128,128]{2,1,0:T(8,128)S(1)} custom-call(s32[8]{0:T(128)S(1)} %copy-done.4, bf16[256,2048]{1,0:T(8,128)(2,1)} %q.13, bf16[256,2048]{1,0:T(8,128)(2,1)} %k.19, bf16[256,2048]{1,0:T(8,128)(2,1)} %v.19, bf16[256,2048]{1,0:T(8,128)(2,1)} %g.19), custom_call_target="tpu_custom_call" | custom-call | bytes 1024 | tf_op jit(solution)/shard_map/states/pallas_call | solution.py:331
  2.9 0.5 collective-permute-start.1
  3.5 0.0 copy-start.1
  3.5 0.0 copy-start.2
  3.5 1.8 %states.3 = (f32[8,128,128]{2,1,0:T(8,128)S(1)}, bf16[256,256]{1,0:T(8,128)(2,1)S(1)}, bf16[256,256]{1,0:T(8,128)(2,1)S(1)}, f32[16,128]{1,0:T(8,128)S(1)}) custom-call(s32[8]{0:T(128)S(1)} %copy-done.4, bf16[256,2048]{1,0:T(8,128)(2,1)} %q.13, bf16[256,2048]{1,0:T(8,128)(2,1)} %k.19, bf16[256,2048]{1,0:T(8,128)(2,1)} %v.19, bf16[256,2048]{1,0:T(8,128)(2,1)} %g.19), custom_call_target="tpu_custom_call" | custom-call | bytes 1024 | tf_op jit(solution)/shard_map/states/pallas_call | solution.py:331
  5.3 0.0 copy-start
  5.3 0.0 collective-permute-done.1.got
  5.3 0.1 pair.2
  5.4 4.7 %collective-permute-start.3 = (bf16[1056,128]{1,0:T(8,128)(2,1)S(1)}, bf16[1056,128]{1,0:T(8,128)(2,1)S(1)}, u32[]{:S(2)}, u32[]{:S(2)}) collective-permute-start(bf16[1056,128]{1,0:T(8,128)(2,1)S(1)} %get-tuple-element.53), channel_id=1, source_target_pairs={{0,6},{4,10},{8,14},{12,18},{16,22},{20,26},{24,30},{6,0},{10,4},{... | collective-permute-start | bytes 811016 | tf_op jit(solution)/shard_map/ppermute | solution.py:316
  10.1 3.1 %collective-permute-start.4 = (bf16[1040,128]{1,0:T(8,128)(2,1)S(1)}, bf16[1040,128]{1,0:T(8,128)(2,1)S(1)}, u32[]{:S(2)}, u32[]{:S(2)}) collective-permute-start(bf16[1040,128]{1,0:T(8,128)(2,1)S(1)} %get-tuple-element.54), channel_id=1, source_target_pairs={{0,10},{4,14},{8,18},{12,22},{16,26},{20,30},{10,0},{14,4},{18,8},... | collective-permute-start | bytes 798728 | tf_op jit(solution)/shard_map/ppermute | solution.py:316
  13.1 0.1 collective-permute-start.2
  13.2 0.0 copy-done.1
  13.2 0.0 copy-done.2
  13.2 0.0 copy-done.3
  13.2 0.0 copy-done
  13.3 1.1 %local.2 = (f32[3,256,512]{2,1,0:T(8,128)S(1)}, f32[8,128]{1,0:T(8,128)S(1)}) custom-call(f32[16,128]{1,0:T(8,128)S(1)} %get-tuple-element.44.table, bf16[256,2048]{1,0:T(8,128)(2,1)S(1)} %copy-done.3, bf16[256,2048]{1,0:T(8,128)(2,1)S(1)} %copy-done, bf16[256,2048]{1,0:T(8,128)(2,1)S(1)} %copy-done.1, bf16[256,2048]{1,0:T(8,128)(2,1)S(1)} %copy-done.2, ...), custom_call_target="tpu_custom_call" | custom-call | bytes 1024 | tf_op jit(solution)/shard_map/local/pallas_call | solution.py:303
  14.3 0.6 %states.4 = (f32[8,128,128]{2,1,0:T(8,128)S(1)}, f32[8,128,128]{2,1,0:T(8,128)S(1)}) custom-call(f32[16,128]{1,0:T(8,128)S(1)} %get-tuple-element.44.table, bf16[256,2048]{1,0:T(8,128)(2,1)S(1)} %copy-done.3, bf16[256,2048]{1,0:T(8,128)(2,1)S(1)} %copy-done, bf16[256,2048]{1,0:T(8,128)(2,1)S(1)} %copy-done.1, bf16[256,2048]{1,0:T(8,128)(2,1)S(1)} %copy-done.2, ...), custom_call_target="tpu_custom_call" | custom-call | bytes 1024 | tf_op jit(solution)/shard_map/states/pallas_call | solution.py:303
  15.0 0.5 collective-permute-start
  15.5 0.1 collective-permute-start.6
  15.6 1.1 %local.3 = (f32[3,256,512]{2,1,0:T(8,128)S(1)}, f32[8,128]{1,0:T(8,128)S(1)}) custom-call(f32[16,128]{1,0:T(8,128)S(1)} %get-tuple-element.44.table, bf16[256,2048]{1,0:T(8,128)(2,1)S(1)} %copy-done.3, bf16[256,2048]{1,0:T(8,128)(2,1)S(1)} %copy-done, bf16[256,2048]{1,0:T(8,128)(2,1)S(1)} %copy-done.1, bf16[256,2048]{1,0:T(8,128)(2,1)S(1)} %copy-done.2, ...), custom_call_target="tpu_custom_call" | custom-call | bytes 1024 | tf_op jit(solution)/shard_map/local/pallas_call | solution.py:303
  16.7 0.0 collective-permute-done.2.rest_0_
  16.7 1.6 %collective-permute-done.4.rest_2_ = bf16[1040,128]{1,0:T(8,128)(2,1)S(1)} collective-permute-done((bf16[1040,128]{1,0:T(8,128)(2,1)S(1)}, bf16[1040,128]{1,0:T(8,128)(2,1)S(1)}, u32[]{:S(2)}, u32[]{:S(2)}) %collective-permute-start.4) | collective-permute-done | bytes 266272 | tf_op jit(solution)/shard_map/ppermute | solution.py:316
  18.2 0.0 collective-permute-done.3.rest_1_
  18.2 0.1 join.3
  18.3 0.1 collective-permute-start.5
  18.4 0.0 collective-permute-done.6.rest_0_
  18.4 0.1 join.4
  18.5 0.6 collective-permute-start.14
  19.0 0.9 %collective-permute-done.5.got = f32[4,128,128]{2,1,0:T(8,128)S(1)} collective-permute-done((f32[4,128,128]{2,1,0:T(8,128)S(1)}, f32[4,128,128]{2,1,0:T(8,128)S(1)}, u32[]{:S(2)}, u32[]{:S(2)}) %collective-permute-start.5) | collective-permute-done | bytes 262176 | tf_op jit(solution)/shard_map/ppermute | solution.py:310
  19.9 0.4 carry.3.rest_0_
  20.3 1.6 %collective-permute-start.11 = (bf16[3,128,512]{2,1,0:T(8,128)(2,1)S(1)}, bf16[3,128,512]{2,1,0:T(8,128)(2,1)S(1)}, u32[]{:S(2)}, u32[]{:S(2)}) collective-permute-start(bf16[3,128,512]{2,1,0:T(8,128)(2,1)S(1)} %carry.3.rest_0_), channel_id=1, source_target_pairs={{0,1},{1,0},{2,3},{3,2},{4,5},{5,4},{6,7},{7,6},{8,9},{9,8},{10,11... | collective-permute-start | bytes 1179656 | tf_op jit(solution)/shard_map/ppermute | solution.py:322
  21.9 0.0 collective-permute-done.got
  21.9 0.1 pair.3
  22.0 0.1 collective-permute-start.7
  22.1 3.1 %collective-permute-start.9 = (bf16[1056,128]{1,0:T(8,128)(2,1)S(1)}, bf16[1056,128]{1,0:T(8,128)(2,1)S(1)}, u32[]{:S(2)}, u32[]{:S(2)}) collective-permute-start(bf16[1056,128]{1,0:T(8,128)(2,1)S(1)} %get-tuple-element.62), channel_id=1, source_target_pairs={{0,6},{4,10},{8,14},{12,18},{16,22},{20,26},{24,30},{6,0},{10,4},{... | collective-permute-start | bytes 811016 | tf_op jit(solution)/shard_map/ppermute | solution.py:316
  25.2 3.0 %collective-permute-start.10 = (bf16[1040,128]{1,0:T(8,128)(2,1)S(1)}, bf16[1040,128]{1,0:T(8,128)(2,1)S(1)}, u32[]{:S(2)}, u32[]{:S(2)}) collective-permute-start(bf16[1040,128]{1,0:T(8,128)(2,1)S(1)} %get-tuple-element.63), channel_id=1, source_target_pairs={{0,10},{4,14},{8,18},{12,22},{16,26},{20,30},{10,0},{14,4},{18,8},... | collective-permute-start | bytes 798728 | tf_op jit(solution)/shard_map/ppermute | solution.py:316
  28.2 0.0 collective-permute-done.14.got
  28.2 0.1 collective-permute-start.8
  28.3 0.8 %carry.4 = (bf16[3,128,512]{2,1,0:T(8,128)(2,1)S(1)}, bf16[3,128,512]{2,1,0:T(8,128)(2,1)S(1)}) custom-call(f32[16,128]{1,0:T(8,128)S(1)} %get-tuple-element.44.table, bf16[256,2048]{1,0:T(8,128)(2,1)S(1)} %copy-done, bf16[256,2048]{1,0:T(8,128)(2,1)S(1)} %copy-done.1, bf16[256,2048]{1,0:T(8,128)(2,1)S(1)} %copy-done.2, ...), custom_call_target="tpu_custom_call" | custom-call | bytes 1024 | tf_op jit(solution)/shard_map/carry/pallas_call | solution.py:303
  29.0 0.0 collective-permute-done.7.rest_0_
  29.1 0.6 %collective-permute-start.15 = (bf16[3,128,512]{2,1,0:T(8,128)(2,1)S(1)}, bf16[3,128,512]{2,1,0:T(8,128)(2,1)S(1)}, u32[]{:S(2)}, u32[]{:S(2)}) collective-permute-start(bf16[3,128,512]{2,1,0:T(8,128)(2,1)S(1)} %get-tuple-element.70.rest_0_), channel_id=1, source_target_pairs={{0,1},{1,0},{2,3},{3,2},{4,5},{5,4},{6,7},{7,6},{8,9},{9,8},{10,11... | collective-permute-start | bytes 1179656 | tf_op jit(solution)/shard_map/ppermute | solution.py:322
  29.7 0.1 collective-permute-done.8.rest_1_
  29.8 3.5 %collective-permute-done.10.rest_3_ = bf16[1040,128]{1,0:T(8,128)(2,1)S(1)} collective-permute-done((bf16[1040,128]{1,0:T(8,128)(2,1)S(1)}, bf16[1040,128]{1,0:T(8,128)(2,1)S(1)}, u32[]{:S(2)}, u32[]{:S(2)}) %collective-permute-start.10) | collective-permute-done | bytes 266272 | tf_op jit(solution)/shard_map/ppermute | solution.py:316
  33.3 0.0 collective-permute-done.9.rest_2_
  33.3 0.0 collective-permute-done.11.rest_4_.refs_2_
  33.3 0.1 join.5
  33.4 0.1 collective-permute-start.13
  33.5 0.5 collective-permute-start.12
  34.0 1.0 %collective-permute-done.13.got = f32[4,128,128]{2,1,0:T(8,128)S(1)} collective-permute-done((f32[4,128,128]{2,1,0:T(8,128)S(1)}, f32[4,128,128]{2,1,0:T(8,128)S(1)}, u32[]{:S(2)}, u32[]{:S(2)}) %collective-permute-start.13) | collective-permute-done | bytes 262176 | tf_op jit(solution)/shard_map/ppermute | solution.py:310
  35.0 1.6 %grads.2 = (bf16[3,128,512]{2,1,0:T(8,128)(2,1)S(1)}, bf16[3,128,512]{2,1,0:T(8,128)(2,1)S(1)}) custom-call(f32[16,128]{1,0:T(8,128)S(1)} %get-tuple-element.44.table, bf16[256,2048]{1,0:T(8,128)(2,1)S(1)} %copy-done.3, bf16[256,2048]{1,0:T(8,128)(2,1)S(1)} %copy-done, bf16[256,2048]{1,0:T(8,128)(2,1)S(1)} %copy-done.1, bf16[256,2048]{1,0:T(8,128)(2,1)S(1)} %copy-done.2, ...), custom_call_target="tpu_custom_call" | custom-call | bytes 1024 | tf_op jit(solution)/shard_map/grads/pallas_call | solution.py:303
  36.7 0.6 %collective-permute-start.17 = (bf16[3,128,512]{2,1,0:T(8,128)(2,1)S(1)}, bf16[3,128,512]{2,1,0:T(8,128)(2,1)S(1)}, u32[]{:S(2)}, u32[]{:S(2)}) collective-permute-start(bf16[3,128,512]{2,1,0:T(8,128)(2,1)S(1)} %get-tuple-element.71.rest_0_), channel_id=1, source_target_pairs={{0,1},{1,0},{2,3},{3,2},{4,5},{5,4},{6,7},{7,6},{8,9},{9,8},{10,11... | collective-permute-start | bytes 1179656 | tf_op jit(solution)/shard_map/ppermute | solution.py:322
  37.3 3.8 %collective-permute-done.15.rest_1_.refs_1_ = bf16[3,128,512]{2,1,0:T(8,128)(2,1)S(1)} collective-permute-done((bf16[3,128,512]{2,1,0:T(8,128)(2,1)S(1)}, bf16[3,128,512]{2,1,0:T(8,128)(2,1)S(1)}, u32[]{:S(2)}, u32[]{:S(2)}) %collective-permute-start.15) | collective-permute-done | bytes 393248 | tf_op jit(solution)/shard_map/ppermute | solution.py:322
  41.0 0.0 collective-permute-done.12.got
  41.0 1.6 %grads.3 = (bf16[3,128,512]{2,1,0:T(8,128)(2,1)S(1)}, bf16[3,128,512]{2,1,0:T(8,128)(2,1)S(1)}) custom-call(f32[16,128]{1,0:T(8,128)S(1)} %get-tuple-element.44.table, bf16[256,2048]{1,0:T(8,128)(2,1)S(1)} %copy-done.3, bf16[256,2048]{1,0:T(8,128)(2,1)S(1)} %copy-done, bf16[256,2048]{1,0:T(8,128)(2,1)S(1)} %copy-done.1, bf16[256,2048]{1,0:T(8,128)(2,1)S(1)} %copy-done.2, ...), custom_call_target="tpu_custom_call" | custom-call | bytes 1024 | tf_op jit(solution)/shard_map/grads/pallas_call | solution.py:303
  42.7 0.7 %collective-permute-start.16 = (bf16[3,128,512]{2,1,0:T(8,128)(2,1)S(1)}, bf16[3,128,512]{2,1,0:T(8,128)(2,1)S(1)}, u32[]{:S(2)}, u32[]{:S(2)}) collective-permute-start(bf16[3,128,512]{2,1,0:T(8,128)(2,1)S(1)} %get-tuple-element.72), channel_id=1, source_target_pairs={{0,1},{1,0},{2,3},{3,2},{4,5},{5,4},{6,7},{7,6},{8,9},{9,8},{10,11... | collective-permute-start | bytes 1179656 | tf_op jit(solution)/shard_map/ppermute | solution.py:322
  43.4 0.4 carry.5.refs_0_
  43.8 1.1 %place.4 = (bf16[128,4096]{1,0:T(8,128)(2,1)}, bf16[128,4096]{1,0:T(8,128)(2,1)}, bf16[128,4096]{1,0:T(8,128)(2,1)}) custom-call(bf16[3,128,512]{2,1,0:T(8,128)(2,1)S(1)} %carry.5.refs_0_, bf16[3,128,512]{2,1,0:T(8,128)(2,1)S(1)} %get-tuple-element.75.refs_1_, bf16[3,128,512]{2,1,0:T(8,128)(2,1)S(1)} %collective-permute-done.11.rest_4_.refs_2_), custom_call_target="tpu_custom_call" | custom-call | bytes 1024 | tf_op jit(solution)/shard_map/place/pallas_call | solution.py:434
  44.9 0.9 %place.5 = (bf16[128,4096]{1,0:T(8,128)(2,1)}, bf16[128,4096]{1,0:T(8,128)(2,1)}, bf16[128,4096]{1,0:T(8,128)(2,1)}) custom-call(bf16[3,128,512]{2,1,0:T(8,128)(2,1)S(1)} %get-tuple-element.74.refs_0_, bf16[3,128,512]{2,1,0:T(8,128)(2,1)S(1)} %collective-permute-done.15.rest_1_.refs_1_, ...), custom_call_target="tpu_custom_call", output_to_operand_aliasing={{0}: (2, {}), {1}: (3, {}), {2}: (4, {})} | custom-call | bytes 1024 | tf_op jit(solution)/shard_map/place/pallas_call | solution.py:434
  45.9 3.6 %collective-permute-done.17.refs_1_ = bf16[3,128,512]{2,1,0:T(8,128)(2,1)S(1)} collective-permute-done((bf16[3,128,512]{2,1,0:T(8,128)(2,1)S(1)}, bf16[3,128,512]{2,1,0:T(8,128)(2,1)S(1)}, u32[]{:S(2)}, u32[]{:S(2)}) %collective-permute-start.17) | collective-permute-done | bytes 393248 | tf_op jit(solution)/shard_map/ppermute | solution.py:322
  49.5 0.9 %place.6 = (bf16[128,4096]{1,0:T(8,128)(2,1)}, bf16[128,4096]{1,0:T(8,128)(2,1)}, bf16[128,4096]{1,0:T(8,128)(2,1)}) custom-call(bf16[3,128,512]{2,1,0:T(8,128)(2,1)S(1)} %get-tuple-element.73.refs_0_, bf16[3,128,512]{2,1,0:T(8,128)(2,1)S(1)} %collective-permute-done.17.refs_1_, ...), custom_call_target="tpu_custom_call", output_to_operand_aliasing={{0}: (2, {}), {1}: (3, {}), {2}: (4, {})} | custom-call | bytes 1024 | tf_op jit(solution)/shard_map/place/pallas_call | solution.py:434
  50.4 7.1 %collective-permute-done.16.refs_0_ = bf16[3,128,512]{2,1,0:T(8,128)(2,1)S(1)} collective-permute-done((bf16[3,128,512]{2,1,0:T(8,128)(2,1)S(1)}, bf16[3,128,512]{2,1,0:T(8,128)(2,1)S(1)}, u32[]{:S(2)}, u32[]{:S(2)}) %collective-permute-start.16) | collective-permute-done | bytes 393248 | tf_op jit(solution)/shard_map/ppermute | solution.py:322
  57.5 0.8 %place.7 = (bf16[128,4096]{1,0:T(8,128)(2,1)}, bf16[128,4096]{1,0:T(8,128)(2,1)}, bf16[128,4096]{1,0:T(8,128)(2,1)}) custom-call(bf16[3,128,512]{2,1,0:T(8,128)(2,1)S(1)} %collective-permute-done.16.refs_0_, bf16[128,4096]{1,0:T(8,128)(2,1)} %get-tuple-element.82.refs_1_, ...), custom_call_target="tpu_custom_call", output_to_operand_aliasing={{0}: (1, {}), {1}: (2, {}), {2}: (3, {})} | custom-call | bytes 1024 | tf_op jit(solution)/shard_map/place/pallas_call | solution.py:434
  (1 shorter events, 0.0 us)
Async XLA Ops:
  0.6 0.7 %copy-start.4 = (s32[8]{0:T(128)S(1)}, s32[8]{0:T(128)}, u32[]{:S(2)}) copy-start(s32[8]{0:T(128)} %lengths.3) | copy-start | bytes 100
  2.9 2.3 %collective-permute-start.1 = (f32[8,128,128]{2,1,0:T(8,128)S(1)}, f32[8,128,128]{2,1,0:T(8,128)S(1)}, u32[]{:S(2)}, u32[]{:S(2)}) collective-permute-start(f32[8,128,128]{2,1,0:T(8,128)S(1)} %states.5), channel_id=1, source_target_pairs={{0,2},{2,0},{4,6},{6,4},{8,10},{10,8},{12,14},{14,12},{16,18},{18,... | collective-permute-start | bytes 1572872 | tf_op jit(solution)/shard_map/ppermute | solution.py:310
  3.5 9.8 %copy-start.1 = (bf16[256,2048]{1,0:T(8,128)(2,1)S(1)}, bf16[256,2048]{1,0:T(8,128)(2,1)}, u32[]{:S(2)}) copy-start(bf16[256,2048]{1,0:T(8,128)(2,1)} %v.19) | copy-start | bytes 3145732
  3.5 9.8 %copy-start.2 = (bf16[256,2048]{1,0:T(8,128)(2,1)S(1)}, bf16[256,2048]{1,0:T(8,128)(2,1)}, u32[]{:S(2)}) copy-start(bf16[256,2048]{1,0:T(8,128)(2,1)} %g.19) | copy-start | bytes 3145732
  3.5 9.8 %copy-start.3 = (bf16[256,2048]{1,0:T(8,128)(2,1)S(1)}, bf16[256,2048]{1,0:T(8,128)(2,1)}, u32[]{:S(2)}) copy-start(bf16[256,2048]{1,0:T(8,128)(2,1)} %q.13) | copy-start | bytes 3145732
  5.3 8.0 %copy-start = (bf16[256,2048]{1,0:T(8,128)(2,1)S(1)}, bf16[256,2048]{1,0:T(8,128)(2,1)}, u32[]{:S(2)}) copy-start(bf16[256,2048]{1,0:T(8,128)(2,1)} %k.19) | copy-start | bytes 3145732
  5.4 12.8 %collective-permute-start.3 = (bf16[1056,128]{1,0:T(8,128)(2,1)S(1)}, bf16[1056,128]{1,0:T(8,128)(2,1)S(1)}, u32[]{:S(2)}, u32[]{:S(2)}) collective-permute-start(bf16[1056,128]{1,0:T(8,128)(2,1)S(1)} %get-tuple-element.53), channel_id=1, source_target_pairs={{0,6},{4,10},{8,14},{12,18},{16,22},{20,26},{24,30},{6,0},{10,4},{... | collective-permute-start | bytes 811016 | tf_op jit(solution)/shard_map/ppermute | solution.py:316
  10.1 8.2 %collective-permute-start.4 = (bf16[1040,128]{1,0:T(8,128)(2,1)S(1)}, bf16[1040,128]{1,0:T(8,128)(2,1)S(1)}, u32[]{:S(2)}, u32[]{:S(2)}) collective-permute-start(bf16[1040,128]{1,0:T(8,128)(2,1)S(1)} %get-tuple-element.54), channel_id=1, source_target_pairs={{0,10},{4,14},{8,18},{12,22},{16,26},{20,30},{10,0},{14,4},{18,8},... | collective-permute-start | bytes 798728 | tf_op jit(solution)/shard_map/ppermute | solution.py:316
  13.1 3.5 %collective-permute-start.2 = (f32[4,128,128]{2,1,0:T(8,128)S(1)}, f32[4,128,128]{2,1,0:T(8,128)S(1)}, u32[]{:S(2)}, u32[]{:S(2)}) collective-permute-start(f32[4,128,128]{2,1,0:T(8,128)S(1)} %get-tuple-element.52), channel_id=1, source_target_pairs={{0,2},{2,0},{4,6},{6,4},{8,10},{10,8},{12,14},{14,12},{16,18},{18,... | collective-permute-start | bytes 786440 | tf_op jit(solution)/shard_map/ppermute | solution.py:310
  15.0 6.9 %collective-permute-start = (f32[8,128,128]{2,1,0:T(8,128)S(1)}, f32[8,128,128]{2,1,0:T(8,128)S(1)}, u32[]{:S(2)}, u32[]{:S(2)}) collective-permute-start(f32[8,128,128]{2,1,0:T(8,128)S(1)} %get-tuple-element.49), channel_id=1, source_target_pairs={{0,2},{2,0},{4,6},{6,4},{8,10},{10,8},{12,14},{14,12},{16,18},{18,... | collective-permute-start | bytes 1572872 | tf_op jit(solution)/shard_map/ppermute | solution.py:310
  15.5 2.9 %collective-permute-start.6 = (f32[4,128,128]{2,1,0:T(8,128)S(1)}, f32[4,128,128]{2,1,0:T(8,128)S(1)}, u32[]{:S(2)}, u32[]{:S(2)}) collective-permute-start(f32[4,128,128]{2,1,0:T(8,128)S(1)} %get-tuple-element.58), channel_id=1, source_target_pairs={{0,2},{2,0},{4,6},{6,4},{8,10},{10,8},{12,14},{14,12},{16,18},{18,... | collective-permute-start | bytes 786440 | tf_op jit(solution)/shard_map/ppermute | solution.py:310
  18.3 1.6 %collective-permute-start.5 = (f32[4,128,128]{2,1,0:T(8,128)S(1)}, f32[4,128,128]{2,1,0:T(8,128)S(1)}, u32[]{:S(2)}, u32[]{:S(2)}) collective-permute-start(f32[4,128,128]{2,1,0:T(8,128)S(1)} %get-tuple-element.57), channel_id=1, source_target_pairs={{0,2},{2,0},{4,6},{6,4},{8,10},{10,8},{12,14},{14,12},{16,18},{18,... | collective-permute-start | bytes 786440 | tf_op jit(solution)/shard_map/ppermute | solution.py:310
  18.5 9.7 %collective-permute-start.14 = (f32[4,128,128]{2,1,0:T(8,128)S(1)}, f32[4,128,128]{2,1,0:T(8,128)S(1)}, u32[]{:S(2)}, u32[]{:S(2)}) collective-permute-start(f32[4,128,128]{2,1,0:T(8,128)S(1)} %get-tuple-element.69), channel_id=1, source_target_pairs={{0,2},{2,0},{4,6},{6,4},{8,10},{10,8},{12,14},{14,12},{16,18},{18,... | collective-permute-start | bytes 786440 | tf_op jit(solution)/shard_map/ppermute | solution.py:310
  20.3 13.0 %collective-permute-start.11 = (bf16[3,128,512]{2,1,0:T(8,128)(2,1)S(1)}, bf16[3,128,512]{2,1,0:T(8,128)(2,1)S(1)}, u32[]{:S(2)}, u32[]{:S(2)}) collective-permute-start(bf16[3,128,512]{2,1,0:T(8,128)(2,1)S(1)} %carry.3.rest_0_), channel_id=1, source_target_pairs={{0,1},{1,0},{2,3},{3,2},{4,5},{5,4},{6,7},{7,6},{8,9},{9,8},{10,11... | collective-permute-start | bytes 1179656 | tf_op jit(solution)/shard_map/ppermute | solution.py:322
  22.0 7.1 %collective-permute-start.7 = (f32[4,128,128]{2,1,0:T(8,128)S(1)}, f32[4,128,128]{2,1,0:T(8,128)S(1)}, u32[]{:S(2)}, u32[]{:S(2)}) collective-permute-start(f32[4,128,128]{2,1,0:T(8,128)S(1)} %get-tuple-element.60), channel_id=1, source_target_pairs={{0,2},{2,0},{4,6},{6,4},{8,10},{10,8},{12,14},{14,12},{16,18},{18,... | collective-permute-start | bytes 786440 | tf_op jit(solution)/shard_map/ppermute | solution.py:310
  22.1 11.2 %collective-permute-start.9 = (bf16[1056,128]{1,0:T(8,128)(2,1)S(1)}, bf16[1056,128]{1,0:T(8,128)(2,1)S(1)}, u32[]{:S(2)}, u32[]{:S(2)}) collective-permute-start(bf16[1056,128]{1,0:T(8,128)(2,1)S(1)} %get-tuple-element.62), channel_id=1, source_target_pairs={{0,6},{4,10},{8,14},{12,18},{16,22},{20,26},{24,30},{6,0},{10,4},{... | collective-permute-start | bytes 811016 | tf_op jit(solution)/shard_map/ppermute | solution.py:316
  25.2 8.1 %collective-permute-start.10 = (bf16[1040,128]{1,0:T(8,128)(2,1)S(1)}, bf16[1040,128]{1,0:T(8,128)(2,1)S(1)}, u32[]{:S(2)}, u32[]{:S(2)}) collective-permute-start(bf16[1040,128]{1,0:T(8,128)(2,1)S(1)} %get-tuple-element.63), channel_id=1, source_target_pairs={{0,10},{4,14},{8,18},{12,22},{16,26},{20,30},{10,0},{14,4},{18,8},... | collective-permute-start | bytes 798728 | tf_op jit(solution)/shard_map/ppermute | solution.py:316
  28.2 1.6 %collective-permute-start.8 = (f32[4,128,128]{2,1,0:T(8,128)S(1)}, f32[4,128,128]{2,1,0:T(8,128)S(1)}, u32[]{:S(2)}, u32[]{:S(2)}) collective-permute-start(f32[4,128,128]{2,1,0:T(8,128)S(1)} %get-tuple-element.61), channel_id=1, source_target_pairs={{0,2},{2,0},{4,6},{6,4},{8,10},{10,8},{12,14},{14,12},{16,18},{18,... | collective-permute-start | bytes 786440 | tf_op jit(solution)/shard_map/ppermute | solution.py:310
  29.1 12.0 %collective-permute-start.15 = (bf16[3,128,512]{2,1,0:T(8,128)(2,1)S(1)}, bf16[3,128,512]{2,1,0:T(8,128)(2,1)S(1)}, u32[]{:S(2)}, u32[]{:S(2)}) collective-permute-start(bf16[3,128,512]{2,1,0:T(8,128)(2,1)S(1)} %get-tuple-element.70.rest_0_), channel_id=1, source_target_pairs={{0,1},{1,0},{2,3},{3,2},{4,5},{5,4},{6,7},{7,6},{8,9},{9,8},{10,11... | collective-permute-start | bytes 1179656 | tf_op jit(solution)/shard_map/ppermute | solution.py:322
  33.4 1.6 %collective-permute-start.13 = (f32[4,128,128]{2,1,0:T(8,128)S(1)}, f32[4,128,128]{2,1,0:T(8,128)S(1)}, u32[]{:S(2)}, u32[]{:S(2)}) collective-permute-start(f32[4,128,128]{2,1,0:T(8,128)S(1)} %get-tuple-element.67), channel_id=1, source_target_pairs={{0,2},{2,0},{4,6},{6,4},{8,10},{10,8},{12,14},{14,12},{16,18},{18,... | collective-permute-start | bytes 786440 | tf_op jit(solution)/shard_map/ppermute | solution.py:310
  33.5 7.5 %collective-permute-start.12 = (f32[4,128,128]{2,1,0:T(8,128)S(1)}, f32[4,128,128]{2,1,0:T(8,128)S(1)}, u32[]{:S(2)}, u32[]{:S(2)}) collective-permute-start(f32[4,128,128]{2,1,0:T(8,128)S(1)} %get-tuple-element.65), channel_id=1, source_target_pairs={{0,2},{2,0},{4,6},{6,4},{8,10},{10,8},{12,14},{14,12},{16,18},{18,... | collective-permute-start | bytes 786440 | tf_op jit(solution)/shard_map/ppermute | solution.py:310
  36.7 12.8 %collective-permute-start.17 = (bf16[3,128,512]{2,1,0:T(8,128)(2,1)S(1)}, bf16[3,128,512]{2,1,0:T(8,128)(2,1)S(1)}, u32[]{:S(2)}, u32[]{:S(2)}) collective-permute-start(bf16[3,128,512]{2,1,0:T(8,128)(2,1)S(1)} %get-tuple-element.71.rest_0_), channel_id=1, source_target_pairs={{0,1},{1,0},{2,3},{3,2},{4,5},{5,4},{6,7},{7,6},{8,9},{9,8},{10,11... | collective-permute-start | bytes 1179656 | tf_op jit(solution)/shard_map/ppermute | solution.py:322
  42.7 14.8 %collective-permute-start.16 = (bf16[3,128,512]{2,1,0:T(8,128)(2,1)S(1)}, bf16[3,128,512]{2,1,0:T(8,128)(2,1)S(1)}, u32[]{:S(2)}, u32[]{:S(2)}) collective-permute-start(bf16[3,128,512]{2,1,0:T(8,128)(2,1)S(1)} %get-tuple-element.72), channel_id=1, source_target_pairs={{0,1},{1,0},{2,3},{3,2},{4,5},{5,4},{6,7},{7,6},{8,9},{9,8},{10,11... | collective-permute-start | bytes 1179656 | tf_op jit(solution)/shard_map/ppermute | solution.py:322
